TPU v7x, 512 devices: a whole 4x8x8 slice. The times are simulated.
512 devices in a mesh: space: 64 (over x, z, core), freq: 8 (over y).
Axes of the slice: x: 4, y: 8, z: 8, core: 2. Of those that a mesh axis runs over, the one named last changes fastest.
Arguments:
- sketch: bfloat16 [16, 64, 5, 512, 128], P('freq', None, None, 'space'), may hold values from -160 to 160
- coupling: float32 [5, 5, 512, 128], P(None, None, 'space'), may hold values from -2.5 to 2.5
- velocity: float32 [512, 128], P('space'), may hold values from 0.5 to 2
- freq_index: int32 [8], replicated, may hold values from 1 to 15, as said below
Outputs:
- basis: float32 [8, 128, 5, 512, 128], P('freq', None, None, 'space')
- factor: float32 [8, 128, 128], P('freq')
Inputs may be any that keep to these rules, and one draw needn't show every extreme that they name: `freq_index`: 8 distinct indices, none equal to 0 or to half of 16.
All inputs are finite; a program needn't handle non-finite values.
Results may differ from a plain program's by a relative error of at most 0.0003.
Values may be sent and summed in bfloat16 or wider, within the bound.
No kernel may reach another device: no remote copies, remote signals or barrier semaphores. Data moves between devices by JAX's collectives and lax.ppermute only.
A program may use at most 128 MiB of HBM per device.

v0:
```python
from functools import partial
import math

import jax
import jax.numpy as jnp
from jax import lax
from jax.sharding import PartitionSpec as P

K = 64
FIELDS = 5
NT = 16
F = 8


STEP_DT = 0.25
VISCOSITY = 0.5


def with_halo(value, sides, width):
    for axis, dim in sides:
        count, length = (lax.axis_size(axis), value.shape[dim])
        up = [(i, (i + 1) % count) for i in range(count - 1)]
        down = [(j, i) for i, j in up]
        last = lax.slice_in_dim(value, length - width, length, axis=dim)
        leading = lax.slice_in_dim(value, 0, width, axis=dim)
        before = lax.ppermute(last, axis, up)
        after = lax.ppermute(leading, axis, down)
        value = jnp.concatenate([before, value, after], axis=dim)
    return value


def make_table(indices, slots):
    times = jnp.arange(slots, dtype=jnp.int32)
    phases = indices[:, None] * times[None, :] % slots
    angles = phases.astype(jnp.float32) * (2.0 * math.pi / slots)
    return jnp.stack([jnp.cos(angles), -jnp.sin(angles)], axis=1).reshape(
        2 * indices.shape[0], slots
    )


def advance(padded, velocity, coupling, angular):
    centre = padded[..., 2:-2, :]
    far_plus = padded[..., 4:, :]
    near_plus = padded[..., 3:-1, :]
    near_minus = padded[..., 1:-3, :]
    far_minus = padded[..., :-4, :]
    slope_x = (8.0 * (near_plus - near_minus) - (far_plus - far_minus)) / 12.0
    curve_x = (16.0 * (near_plus + near_minus) - (far_plus + far_minus) - 30.0 * centre) / 12.0
    radial_pad = jnp.pad(centre, [(0, 0)] * (centre.ndim - 1) + [(1, 1)])
    radial = radial_pad[..., 2:] + radial_pad[..., :-2] - 2.0 * centre
    coupled = coupling[0] * centre[:, :, :, 0:1]
    for source in range(1, coupling.shape[0]):
        coupled = coupled + coupling[source] * centre[:, :, :, source : source + 1]
    tendency = velocity * slope_x + VISCOSITY * (curve_x + radial) + coupled
    rotation = (
        jnp.stack([centre[:, 1], -centre[:, 0]], axis=1) * angular[:, None, None, None, None, None]
    )
    return centre + STEP_DT * (tendency + rotation)


def local(sketch, coupling, velocity, freq_index):
    group_size = lax.axis_size("freq")
    per_group = F // group_size
    row_count = sketch.shape[3]
    radial_count = sketch.shape[4]
    own_index = lax.dynamic_slice_in_dim(freq_index, lax.axis_index("freq") * per_group, per_group)
    angular = math.pi / NT * own_index.astype(jnp.float32)
    cosines = make_table(freq_index, NT)
    spectra = jnp.einsum(
        "ct,tkvxr->ckvxr",
        cosines,
        lax.all_to_all(sketch, "freq", split_axis=3, concat_axis=0, tiled=True).astype(jnp.float32),
        precision=lax.Precision.HIGHEST,
    )
    fields = lax.all_to_all(spectra, "freq", split_axis=0, concat_axis=3, tiled=True)
    fields = fields.reshape(per_group, 2, K, FIELDS, row_count, radial_count)
    for repeat in range(2):
        padded = with_halo(fields, (("space", 4),), 2)
        fields = advance(padded, velocity, coupling, angular)
    columns = fields.reshape(per_group, 2 * K, FIELDS * row_count * radial_count)
    partial_gram = jnp.einsum("fir,fjr->fij", columns, columns, precision=lax.Precision.HIGHEST)
    gram_total = lax.psum(partial_gram, "space")
    chol_factor = jnp.linalg.cholesky(gram_total)
    row_scale = math.sqrt(FIELDS * row_count * lax.axis_size("space") * radial_count)
    solved = jax.vmap(partial(jax.scipy.linalg.solve_triangular, lower=True))(chol_factor, columns)
    basis_out = (solved * row_scale).reshape(per_group, 2 * K, FIELDS, row_count, radial_count)
    return (basis_out, chol_factor / row_scale)


def solution(mesh):
    return jax.shard_map(
        local,
        mesh=mesh,
        in_specs=(
            P("freq", None, None, "space", None),
            P(None, None, "space", None),
            P("space", None),
            P(),
        ),
        out_specs=(P("freq", None, None, "space", None), P("freq", None, None)),
        check_vma=False,
    )
```

profile of v0, /device:TPU:1, one launch (start us, length us, event | category | flops | bytes accessed | tf_op | source)
XLA Modules:
  0.0 395.3 jit_solution(16415143378156558418)
XLA Ops:
  7.2 0.0 copy-start.3
  7.2 2.7 copy.32
  9.9 7.7 %all-to-all-start = ((bf16[2,64,5,8,128]{4,1,2,0,3:T(8,128)(2,1)}), bf16[2,64,5,8,128]{4,1,2,0,3:T(8,128)(2,1)S(1)}, u32[]{:S(2)}, u32[]{:S(2)}) async-start(bf16[2,64,5,8,128]{4,1,2,0,3:T(8,128)(2,1)} %copy.32), calls=%async_computation | async-start | bytes 2621440 | tf_op jit(solution)/shard_map/all_to_all | solution.py:72
  17.5 0.0 copy-done.3
  17.5 0.1 fusion.32
  17.7 34.7 %all-to-all-done = bf16[2,64,5,8,128]{4,1,2,0,3:T(8,128)(2,1)S(1)} async-done(((bf16[2,64,5,8,128]{4,1,2,0,3:T(8,128)(2,1)}), bf16[2,64,5,8,128]{4,1,2,0,3:T(8,128)(2,1)S(1)}, u32[]{:S(2)}, u32[]{:S(2)}) %all-to-all-start) | async-done | bytes 1310752 | tf_op jit(solution)/shard_map/all_to_all | solution.py:72
  52.4 1.3 copy.33
  53.7 1.2 convolution_bitcast_fusion
  54.9 2.3 copy.34
  57.2 0.0 copy-start.1
  57.2 3.8 all-to-all-start.1
  61.0 0.0 all-reduce.4.cloned.1.call-start
  61.0 0.0 copy-done.1
  61.0 62.8 %all-to-all-done.1 = f32[16,64,5,1,128]{4,1,3,2,0:T(8,128)S(1)} async-done(((f32[16,64,5,1,128]{4,1,3,2,0:T(8,128)}), f32[16,64,5,1,128]{4,1,3,2,0:T(8,128)S(1)}, u32[]{:S(2)}, u32[]{:S(2)}) %all-to-all-start.1) | async-done | bytes 2621472 | tf_op jit(solution)/shard_map/all_to_all | solution.py:75
  123.8 0.0 copy-start
  123.8 1.5 copy-done
  125.3 3.3 copy.42
  128.6 0.0 copy-start.2
  128.6 1.2 fusion.35
  129.8 4.5 %collective-permute-start.1 = (f32[1,2,64,5,2,128]{5,4,3,2,1,0:T(2,128)}, f32[1,2,64,5,2,128]{5,4,3,2,1,0:T(2,128)}, u32[]{:S(2)}, u32[]{:S(2)}) collective-permute-start(f32[1,2,64,5,2,128]{5,4,3,2,1,0:T(2,128)} %get-tuple-element.16), channel_id=1, source_target_pairs={{0,8},{8,16},{16,24},{24,32},{32,40},{40,48},{48,56},{56,64},{64,7... | collective-permute-start | bytes 1966088 | tf_op jit(solution)/shard_map/ppermute | solution.py:26
  134.3 1.9 collective-permute-start
  136.2 0.0 copy-done.2
  136.3 0.6 dynamic_slice.3
  137.5 0.2 slice_bitcast_fusion.9
  137.7 0.2 fusion.36
  137.9 4.2 %collective-permute-done.1 = f32[1,2,64,5,2,128]{5,4,3,2,1,0:T(2,128)} collective-permute-done((f32[1,2,64,5,2,128]{5,4,3,2,1,0:T(2,128)}, f32[1,2,64,5,2,128]{5,4,3,2,1,0:T(2,128)}, u32[]{:S(2)}, u32[]{:S(2)}) %collective-permute-start.1) | collective-permute-done | bytes 655392 | tf_op jit(solution)/shard_map/ppermute | solution.py:26
  142.1 4.2 %collective-permute-done = f32[1,2,64,5,2,128]{5,4,3,2,1,0:T(2,128)} collective-permute-done((f32[1,2,64,5,2,128]{5,4,3,2,1,0:T(2,128)S(1)}, f32[1,2,64,5,2,128]{5,4,3,2,1,0:T(2,128)}, u32[]{:S(2)}, u32[]{:S(2)}) %collective-permute-start) | collective-permute-done | bytes 655392 | tf_op jit(solution)/shard_map/ppermute | solution.py:27
  146.3 6.1 %fusion.12 = f32[1,2,64,5,8,128]{5,4,3,2,1,0:T(8,128)S(1)} fusion(f32[1,2,64,5,8,128]{5,4,3,2,1,0:T(8,128)S(1)} %bitcast.73, f32[1,1,64,5,8,128]{5,4,3,2,1,0:T(8,128)S(1)} %get-tuple-element.19, f32[1,1,64,5,8,128]{5,4,3,2,1,0:T(8,128)S(1)} %get-tuple-element.18, f32[1,2,64,5,2,128]{5,4,3,2,1,0:T(2,128)} %collective-permute-done, ...), kind=kLoop, calls=%fused_computation.25 | loop fusion | flops 24248320 | bytes 11902980 | tf_op jit(solution)/shard_map/add | solution.py:58
  152.4 0.4 fusion.33
  152.8 1.9 collective-permute-start.3
  154.7 2.4 collective-permute-start.2
  157.2 0.2 slice_bitcast_fusion.4
  157.4 0.2 fusion.34
  157.6 4.6 %collective-permute-done.3 = f32[1,2,64,5,2,128]{5,4,3,2,1,0:T(2,128)S(1)} collective-permute-done((f32[1,2,64,5,2,128]{5,4,3,2,1,0:T(2,128)S(1)}, f32[1,2,64,5,2,128]{5,4,3,2,1,0:T(2,128)S(1)}, u32[]{:S(2)}, u32[]{:S(2)}) %collective-permute-start.3) | collective-permute-done | bytes 655392 | tf_op jit(solution)/shard_map/ppermute | solution.py:26
  162.3 5.1 %collective-permute-done.2 = f32[1,2,64,5,2,128]{5,4,3,2,1,0:T(2,128)S(1)} collective-permute-done((f32[1,2,64,5,2,128]{5,4,3,2,1,0:T(2,128)S(1)}, f32[1,2,64,5,2,128]{5,4,3,2,1,0:T(2,128)S(1)}, u32[]{:S(2)}, u32[]{:S(2)}) %collective-permute-start.2) | collective-permute-done | bytes 655392 | tf_op jit(solution)/shard_map/ppermute | solution.py:27
  167.4 5.7 %fusion.21 = f32[1,2,64,5,8,128]{5,4,3,2,1,0:T(8,128)} fusion(f32[1,2,64,5,8,128]{5,4,3,2,1,0:T(8,128)S(1)} %fusion.12, f32[1,1,64,5,8,128]{5,4,3,2,1,0:T(8,128)S(1)} %get-tuple-element.10, f32[1,1,64,5,8,128]{5,4,3,2,1,0:T(8,128)S(1)} %get-tuple-element.9, f32[1,2,64,5,2,128]{5,4,3,2,1,0:T(2,128)S(1)} %collective-permute-done.2, ...), kind=kLoop, calls=%fused_computation.34 | loop fusion | flops 24248320 | bytes 11902980 | tf_op jit(solution)/shard_map/add | solution.py:58
  173.1 2.7 reshape.378
  175.9 2.8 convolution_bitcast_fusion.1
  178.7 0.0 all-reduce.4.cloned.1.call-update
  178.7 180.0 %all-reduce.4.cloned.1.call-done = f32[1,128,128]{1,2,0:T(8,128)} async-done(((f32[1,128,128]{1,2,0:T(8,128)}), f32[1,128,128]{1,2,0:T(8,128)}) %all-reduce.4.cloned.1.call-update) | async-done | bytes 65552 | tf_op jit(solution)/shard_map/psum | solution.py:82
  358.7 0.9 copy.37
  359.7 0.9 fusion.24
  360.5 11.7 %custom-call.8 = f32[1,128,128]{2,1,0:T(8,128)S(1)} custom-call(f32[1,128,128]{2,1,0:T(8,128)S(1)} %fusion.24), custom_call_target="Cholesky" | custom-call | tf_op jit(solution)/shard_map/jit(cholesky)/cholesky | solution.py:83
  372.3 0.6 compare_reduce_fusion
  372.9 1.3 fusion.25
  374.2 9.8 %custom-call.9 = f32[1,1,128,128]{2,3,1,0:T(8,128)S(1)} custom-call(f32[1,1,128,128]{3,2,1,0:T(8,128)S(1)} %get-tuple-element.26), custom_call_target="InvertDiagBlocksLowerTriangular" | custom-call | tf_op jit(solution)/shard_map/vmap(jit(_solve_triangular))/triangular_solve | solution.py:85
  384.0 2.5 fusion.22
  386.5 1.9 copy.40
  (5 shorter events, 0.1 us)
Async XLA Ops:
  7.2 10.4 %copy-start.3 = (s32[8]{0:T(128)S(1)}, s32[8]{0:T(128)}, u32[]{:S(2)}) copy-start(s32[8]{0:T(128)} %param.7) | copy-start | bytes 100
  9.9 42.5 %all-to-all-start = ((bf16[2,64,5,8,128]{4,1,2,0,3:T(8,128)(2,1)}), bf16[2,64,5,8,128]{4,1,2,0,3:T(8,128)(2,1)S(1)}, u32[]{:S(2)}, u32[]{:S(2)}) async-start(bf16[2,64,5,8,128]{4,1,2,0,3:T(8,128)(2,1)} %copy.32), calls=%async_computation | async-start | bytes 2621440 | tf_op jit(solution)/shard_map/all_to_all | solution.py:72
  57.2 3.8 copy-start.1
  57.2 66.6 %all-to-all-start.1 = ((f32[16,64,5,1,128]{4,1,3,2,0:T(8,128)}), f32[16,64,5,1,128]{4,1,3,2,0:T(8,128)S(1)}, u32[]{:S(2)}, u32[]{:S(2)}) async-start(f32[16,64,5,1,128]{4,1,3,2,0:T(8,128)} %copy.34), calls=%async_computation.1 | async-start | bytes 5242880 | tf_op jit(solution)/shard_map/all_to_all | solution.py:75
  61.0 297.8 %all-reduce.4.cloned.1.call-start = ((), (), s32[]{:S(2)}) async-start(), calls=%async_computation.2 | async-start | bytes 131072 | tf_op jit(solution)/shard_map/psum | solution.py:82
  123.8 1.5 copy-start
  128.6 7.6 %copy-start.2 = (f32[8,128]{1,0:T(8,128)S(1)}, f32[8,128]{1,0:T(8,128)}, u32[]{:S(2)}) copy-start(f32[8,128]{1,0:T(8,128)} %param.6) | copy-start | bytes 12292
  129.8 12.3 %collective-permute-start.1 = (f32[1,2,64,5,2,128]{5,4,3,2,1,0:T(2,128)}, f32[1,2,64,5,2,128]{5,4,3,2,1,0:T(2,128)}, u32[]{:S(2)}, u32[]{:S(2)}) collective-permute-start(f32[1,2,64,5,2,128]{5,4,3,2,1,0:T(2,128)} %get-tuple-element.16), channel_id=1, source_target_pairs={{0,8},{8,16},{16,24},{24,32},{32,40},{40,48},{48,56},{56,64},{64,7... | collective-permute-start | bytes 1966088 | tf_op jit(solution)/shard_map/ppermute | solution.py:26
  134.3 12.0 %collective-permute-start = (f32[1,2,64,5,2,128]{5,4,3,2,1,0:T(2,128)S(1)}, f32[1,2,64,5,2,128]{5,4,3,2,1,0:T(2,128)}, u32[]{:S(2)}, u32[]{:S(2)}) collective-permute-start(f32[1,2,64,5,2,128]{5,4,3,2,1,0:T(2,128)S(1)} %get-tuple-element.17), channel_id=1, source_target_pairs={{8,0},{16,8},{24,16},{32,24},{40,32},{48,40},{56,48},{64,56},{72,6... | collective-permute-start | bytes 1966088 | tf_op jit(solution)/shard_map/ppermute | solution.py:27
  152.8 9.4 %collective-permute-start.3 = (f32[1,2,64,5,2,128]{5,4,3,2,1,0:T(2,128)S(1)}, f32[1,2,64,5,2,128]{5,4,3,2,1,0:T(2,128)S(1)}, u32[]{:S(2)}, u32[]{:S(2)}) collective-permute-start(f32[1,2,64,5,2,128]{5,4,3,2,1,0:T(2,128)S(1)} %get-tuple-element.7), channel_id=1, source_target_pairs={{0,8},{8,16},{16,24},{24,32},{32,40},{40,48},{48,56},{56,64},{64,7... | collective-permute-start | bytes 1966088 | tf_op jit(solution)/shard_map/ppermute | solution.py:26
  154.7 12.6 %collective-permute-start.2 = (f32[1,2,64,5,2,128]{5,4,3,2,1,0:T(2,128)S(1)}, f32[1,2,64,5,2,128]{5,4,3,2,1,0:T(2,128)S(1)}, u32[]{:S(2)}, u32[]{:S(2)}) collective-permute-start(f32[1,2,64,5,2,128]{5,4,3,2,1,0:T(2,128)S(1)} %get-tuple-element.8), channel_id=1, source_target_pairs={{8,0},{16,8},{24,16},{32,24},{40,32},{48,40},{56,48},{64,56},{72,6... | collective-permute-start | bytes 1966088 | tf_op jit(solution)/shard_map/ppermute | solution.py:27
Sparse Core Ops, SparseCore 0:
  178.8 179.8 all-reduce.3
where the time goes:
time: 396 us; the launch traced here: 395 us
  waiting for transfers between devices  296 us (75%)
  other arithmetic  36.6 us (9%)
  starting transfers between devices  22.2 us (6%)
  local copies, waits for them, and re-layouts  19.4 us (5%)
  between operations  14.9 us (4%)
  matrix products  6.55 us (2%)
    psum x1, waiting for transfers between devices, local(): gram_total = lax.psum(partial_gram, 'space')  180 us
    all_to_all x1, waiting for transfers between devices, local(): lax.all_to_all(spectra, 'freq', split_axis=0, concat_axis=3, tiled=True)  62.8 us
    all_to_all x1, waiting for transfers between devices, local(): lax.all_to_all(sketch, 'freq', split_axis=3, concat_axis=0, tiled=True)  34.7 us
    another operation x3, other arithmetic, local(): chol_factor = jnp.linalg.cholesky(gram_total)  12.4 us
    add x2, other arithmetic, advance(): return centre + STEP_DT * (tendency + rotation)  11.8 us
    another operation x1, other arithmetic, local(): jax.vmap(partial(jax.scipy.linalg.solve_triangular, lower=True))  9.81 us
    ppermute x2, waiting for transfers between devices, with_halo(): after = lax.ppermute(leading, axis, down)  9.33 us
    ppermute x2, waiting for transfers between devices, with_halo(): before = lax.ppermute(last, axis, up)  8.85 us
  transfers between devices with their start and end apart: 7, of which 7 were waited for; matrix products, arithmetic and copies ran while one was open for 0% of the time, Pallas kernels for 0%

commit v1 on v0

--- a/solution.py
+++ b/solution.py
@@ -26,6 +26,15 @@
         before = lax.ppermute(last, axis, up)
         after = lax.ppermute(leading, axis, down)
         value = jnp.concatenate([before, value, after], axis=dim)
+    return value
+
+
+def butterfly_sum(value, axis):
+    count = lax.axis_size(axis)
+    stride = 1
+    while stride < count:
+        value = value + lax.ppermute(value, axis, [(i, i ^ stride) for i in range(count)])
+        stride *= 2
     return value
 
 
@@ -79,7 +88,7 @@
         fields = advance(padded, velocity, coupling, angular)
     columns = fields.reshape(per_group, 2 * K, FIELDS * row_count * radial_count)
     partial_gram = jnp.einsum("fir,fjr->fij", columns, columns, precision=lax.Precision.HIGHEST)
-    gram_total = lax.psum(partial_gram, "space")
+    gram_total = butterfly_sum(partial_gram, "space")
     chol_factor = jnp.linalg.cholesky(gram_total)
     row_scale = math.sqrt(FIELDS * row_count * lax.axis_size("space") * radial_count)
     solved = jax.vmap(partial(jax.scipy.linalg.solve_triangular, lower=True))(chol_factor, columns)

time: 396 us -> 247 us (0.62)
  the two profiles are of different devices: /device:TPU:1 before, /device:TPU:6 now
where the time goes in v1:
time: 247 us; the launch traced here: 246 us
  waiting for transfers between devices  136 us (55%)
  starting transfers between devices  47.8 us (19%)
  other arithmetic  35.9 us (15%)
  local copies, waits for them, and re-layouts  18.4 us (7%)
  matrix products  5.92 us (2%)
    all_to_all x1, waiting for transfers between devices, local(): lax.all_to_all(spectra, 'freq', split_axis=0, concat_axis=3, tiled=True)  62.8 us
    all_to_all x1, waiting for transfers between devices, local(): lax.all_to_all(sketch, 'freq', split_axis=3, concat_axis=0, tiled=True)  34.3 us
    ppermute x6, waiting for transfers between devices, butterfly_sum(): lax.ppermute(value, axis, [(i, i ^ stride) for i in range(count)])  25.3 us
    ppermute x2, starting transfers between devices, with_halo(): after = lax.ppermute(leading, axis, down)  17 us
    ppermute x6, starting transfers between devices, butterfly_sum(): lax.ppermute(value, axis, [(i, i ^ stride) for i in range(count)])  16 us
    another operation x3, other arithmetic, local(): chol_factor = jnp.linalg.cholesky(gram_total)  12.4 us
    add x2, other arithmetic, advance(): return centre + STEP_DT * (tendency + rotation)  11.8 us
    ppermute x2, waiting for transfers between devices, with_halo(): before = lax.ppermute(last, axis, up)  10.7 us
  transfers between devices with their start and end apart: 12, of which 12 were waited for; matrix products, arithmetic and copies ran while one was open for 1% of the time, Pallas kernels for 0%

profile of v1, /device:TPU:6, one launch (start us, length us, event | category | flops | bytes accessed | tf_op | source)
XLA Modules:
  0.0 245.9 jit_solution(16042466661425459955)
XLA Ops:
  0.6 2.7 %copy.32 = bf16[2,64,5,8,128]{4,1,2,0,3:T(8,128)(2,1)} copy(bf16[2,64,5,8,128]{4,3,2,1,0:T(8,128)(2,1)} %param.4) | data formatting | bytes 2621440 | tf_op args[0]
  3.4 7.1 %all-to-all-start = ((bf16[2,64,5,8,128]{4,1,2,0,3:T(8,128)(2,1)}), bf16[2,64,5,8,128]{4,1,2,0,3:T(8,128)(2,1)S(1)}, u32[]{:S(2)}, u32[]{:S(2)}) async-start(bf16[2,64,5,8,128]{4,1,2,0,3:T(8,128)(2,1)} %copy.32), calls=%async_computation | async-start | bytes 2621440 | tf_op jit(solution)/shard_map/all_to_all | solution.py:81
  10.5 0.1 fusion.32
  10.6 34.3 %all-to-all-done = bf16[2,64,5,8,128]{4,1,2,0,3:T(8,128)(2,1)S(1)} async-done(((bf16[2,64,5,8,128]{4,1,2,0,3:T(8,128)(2,1)}), bf16[2,64,5,8,128]{4,1,2,0,3:T(8,128)(2,1)S(1)}, u32[]{:S(2)}, u32[]{:S(2)}) %all-to-all-start) | async-done | bytes 1310752 | tf_op jit(solution)/shard_map/all_to_all | solution.py:81
  44.9 1.3 copy.33
  46.2 1.2 convolution_bitcast_fusion
  47.5 2.3 copy.34
  49.8 3.8 %all-to-all-start.1 = ((f32[16,64,5,1,128]{4,1,3,2,0:T(8,128)}), f32[16,64,5,1,128]{4,1,3,2,0:T(8,128)S(1)}, u32[]{:S(2)}, u32[]{:S(2)}) async-start(f32[16,64,5,1,128]{4,1,3,2,0:T(8,128)} %copy.34), calls=%async_computation.1 | async-start | bytes 5242880 | tf_op jit(solution)/shard_map/all_to_all | solution.py:84
  53.5 62.8 %all-to-all-done.1 = f32[16,64,5,1,128]{4,1,3,2,0:T(8,128)S(1)} async-done(((f32[16,64,5,1,128]{4,1,3,2,0:T(8,128)}), f32[16,64,5,1,128]{4,1,3,2,0:T(8,128)S(1)}, u32[]{:S(2)}, u32[]{:S(2)}) %all-to-all-start.1) | async-done | bytes 2621472 | tf_op jit(solution)/shard_map/all_to_all | solution.py:84
  116.4 1.5 copy-done
  117.9 3.3 %copy.42 = f32[8,2,64,5,1,128]{5,0,3,2,1,4:T(8,128)S(1)} copy(f32[8,2,64,5,1,128]{5,2,3,1,0,4:T(8,128)} %bitcast.74) | data formatting | bytes 5242880 | tf_op jit(solution)/shard_map/all_to_all | solution.py:84
  121.1 1.2 fusion.35
  122.4 1.9 collective-permute-start.1
  124.3 10.8 %collective-permute-start = (f32[1,2,64,5,2,128]{5,4,3,2,1,0:T(2,128)S(1)}, f32[1,2,64,5,2,128]{5,4,3,2,1,0:T(2,128)}, u32[]{:S(2)}, u32[]{:S(2)}) collective-permute-start(f32[1,2,64,5,2,128]{5,4,3,2,1,0:T(2,128)S(1)} %get-tuple-element.17), channel_id=1, source_target_pairs={{8,0},{16,8},{24,16},{32,24},{40,32},{48,40},{56,48},{64,56},{72,6... | collective-permute-start | bytes 1966088 | tf_op jit(solution)/shard_map/ppermute | solution.py:27
  135.2 0.6 dynamic_slice.3
  136.4 0.2 slice_bitcast_fusion.9
  136.6 0.2 fusion.36
  136.8 5.0 %collective-permute-done.1 = f32[1,2,64,5,2,128]{5,4,3,2,1,0:T(2,128)} collective-permute-done((f32[1,2,64,5,2,128]{5,4,3,2,1,0:T(2,128)}, f32[1,2,64,5,2,128]{5,4,3,2,1,0:T(2,128)}, u32[]{:S(2)}, u32[]{:S(2)}) %collective-permute-start.1) | collective-permute-done | bytes 655392 | tf_op jit(solution)/shard_map/ppermute | solution.py:26
  141.8 1.4 collective-permute-done
  143.2 6.1 %fusion.12 = f32[1,2,64,5,8,128]{5,4,3,2,1,0:T(8,128)S(1)} fusion(f32[1,2,64,5,8,128]{5,4,3,2,1,0:T(8,128)S(1)} %bitcast.73, f32[1,1,64,5,8,128]{5,4,3,2,1,0:T(8,128)S(1)} %get-tuple-element.19, f32[1,1,64,5,8,128]{5,4,3,2,1,0:T(8,128)S(1)} %get-tuple-element.18, f32[1,2,64,5,2,128]{5,4,3,2,1,0:T(2,128)} %collective-permute-done, ...), kind=kLoop, calls=%fused_computation.25 | loop fusion | flops 24248320 | bytes 11902980 | tf_op jit(solution)/shard_map/add | solution.py:67
  149.3 0.4 fusion.33
  149.7 1.9 collective-permute-start.3
  151.7 6.2 %collective-permute-start.2 = (f32[1,2,64,5,2,128]{5,4,3,2,1,0:T(2,128)S(1)}, f32[1,2,64,5,2,128]{5,4,3,2,1,0:T(2,128)S(1)}, u32[]{:S(2)}, u32[]{:S(2)}) collective-permute-start(f32[1,2,64,5,2,128]{5,4,3,2,1,0:T(2,128)S(1)} %get-tuple-element.8), channel_id=1, source_target_pairs={{8,0},{16,8},{24,16},{32,24},{40,32},{48,40},{56,48},{64,56},{72,6... | collective-permute-start | bytes 1966088 | tf_op jit(solution)/shard_map/ppermute | solution.py:27
  157.9 0.2 slice_bitcast_fusion.4
  158.1 0.2 fusion.34
  158.3 5.7 %collective-permute-done.3 = f32[1,2,64,5,2,128]{5,4,3,2,1,0:T(2,128)S(1)} collective-permute-done((f32[1,2,64,5,2,128]{5,4,3,2,1,0:T(2,128)S(1)}, f32[1,2,64,5,2,128]{5,4,3,2,1,0:T(2,128)S(1)}, u32[]{:S(2)}, u32[]{:S(2)}) %collective-permute-start.3) | collective-permute-done | bytes 655392 | tf_op jit(solution)/shard_map/ppermute | solution.py:26
  164.0 1.8 collective-permute-done.2
  165.8 5.7 %fusion.21 = f32[1,2,64,5,8,128]{5,4,3,2,1,0:T(8,128)} fusion(f32[1,2,64,5,8,128]{5,4,3,2,1,0:T(8,128)S(1)} %fusion.12, f32[1,1,64,5,8,128]{5,4,3,2,1,0:T(8,128)S(1)} %get-tuple-element.10, f32[1,1,64,5,8,128]{5,4,3,2,1,0:T(8,128)S(1)} %get-tuple-element.9, f32[1,2,64,5,2,128]{5,4,3,2,1,0:T(2,128)S(1)} %collective-permute-done.2, ...), kind=kLoop, calls=%fused_computation.34 | loop fusion | flops 24248320 | bytes 11902980 | tf_op jit(solution)/shard_map/add | solution.py:67
  171.5 2.5 %reshape.378 = f32[128,5120]{1,0:T(8,128)S(1)} reshape(f32[1,2,64,5,8,128]{5,4,3,2,1,0:T(8,128)} %fusion.21) | data formatting | bytes 5242880 | tf_op jit(solution)/shard_map/reshape.42
  174.1 2.2 convolution_bitcast_fusion.1
  176.3 1.9 collective-permute-start.4
  178.2 1.2 collective-permute-done.4
  179.4 1.9 collective-permute-start.5
  181.4 4.2 %collective-permute-done.5 = f32[1,128,128]{1,2,0:T(8,128)S(1)} collective-permute-done((f32[1,128,128]{1,2,0:T(8,128)S(1)}, f32[1,128,128]{1,2,0:T(8,128)S(1)}, u32[]{:S(2)}, u32[]{:S(2)}) %collective-permute-start.5) | collective-permute-done | bytes 65568 | tf_op jit(solution)/shard_map/ppermute | solution.py:36
  185.6 3.4 %collective-permute-start.6 = (f32[1,128,128]{1,2,0:T(8,128)S(1)}, f32[1,128,128]{1,2,0:T(8,128)S(1)}, u32[]{:S(2)}, u32[]{:S(2)}) collective-permute-start(f32[1,128,128]{1,2,0:T(8,128)S(1)} %add.217), channel_id=1, source_target_pairs={{0,32},{8,40},{16,48},{24,56},{32,0},{40,8},{48,16},{56,24},{64,96... | collective-permute-start | bytes 196616 | tf_op jit(solution)/shard_map/ppermute | solution.py:36
  189.0 4.1 %collective-permute-done.6 = f32[1,128,128]{1,2,0:T(8,128)S(1)} collective-permute-done((f32[1,128,128]{1,2,0:T(8,128)S(1)}, f32[1,128,128]{1,2,0:T(8,128)S(1)}, u32[]{:S(2)}, u32[]{:S(2)}) %collective-permute-start.6) | collective-permute-done | bytes 65568 | tf_op jit(solution)/shard_map/ppermute | solution.py:36
  193.2 4.2 %collective-permute-start.7 = (f32[1,128,128]{1,2,0:T(8,128)S(1)}, f32[1,128,128]{1,2,0:T(8,128)S(1)}, u32[]{:S(2)}, u32[]{:S(2)}) collective-permute-start(f32[1,128,128]{1,2,0:T(8,128)S(1)} %add.218), channel_id=1, source_target_pairs={{0,64},{8,72},{16,80},{24,88},{32,96},{40,104},{48,112},{56,120},{... | collective-permute-start | bytes 196616 | tf_op jit(solution)/shard_map/ppermute | solution.py:36
  197.4 6.5 %collective-permute-done.7 = f32[1,128,128]{1,2,0:T(8,128)S(1)} collective-permute-done((f32[1,128,128]{1,2,0:T(8,128)S(1)}, f32[1,128,128]{1,2,0:T(8,128)S(1)}, u32[]{:S(2)}, u32[]{:S(2)}) %collective-permute-start.7) | collective-permute-done | bytes 65568 | tf_op jit(solution)/shard_map/ppermute | solution.py:36
  203.9 2.0 collective-permute-start.8
  205.9 4.2 %collective-permute-done.8 = f32[1,128,128]{1,2,0:T(8,128)S(1)} collective-permute-done((f32[1,128,128]{1,2,0:T(8,128)S(1)}, f32[1,128,128]{1,2,0:T(8,128)S(1)}, u32[]{:S(2)}, u32[]{:S(2)}) %collective-permute-start.8) | collective-permute-done | bytes 65568 | tf_op jit(solution)/shard_map/ppermute | solution.py:36
  210.1 2.6 %collective-permute-start.9 = (f32[1,128,128]{1,2,0:T(8,128)S(1)}, f32[1,128,128]{1,2,0:T(8,128)S(1)}, u32[]{:S(2)}, u32[]{:S(2)}) collective-permute-start(f32[1,128,128]{1,2,0:T(8,128)S(1)} %add.220), channel_id=1, source_target_pairs={{0,256},{8,264},{16,272},{24,280},{32,288},{40,296},{48,304},{56,3... | collective-permute-start | bytes 196616 | tf_op jit(solution)/shard_map/ppermute | solution.py:36
  212.7 5.1 %collective-permute-done.9 = f32[1,128,128]{1,2,0:T(8,128)S(1)} collective-permute-done((f32[1,128,128]{1,2,0:T(8,128)S(1)}, f32[1,128,128]{1,2,0:T(8,128)S(1)}, u32[]{:S(2)}, u32[]{:S(2)}) %collective-permute-start.9) | collective-permute-done | bytes 65568 | tf_op jit(solution)/shard_map/ppermute | solution.py:36
  217.9 11.7 %custom-call.8 = f32[1,128,128]{2,1,0:T(8,128)S(1)} custom-call(f32[1,128,128]{2,1,0:T(8,128)S(1)} %fusion.24), custom_call_target="Cholesky" | custom-call | tf_op jit(solution)/shard_map/jit(cholesky)/cholesky | solution.py:92
  229.6 0.6 compare_reduce_fusion
  230.3 1.3 fusion.25
  231.6 9.8 %custom-call.9 = f32[1,1,128,128]{2,3,1,0:T(8,128)S(1)} custom-call(f32[1,1,128,128]{3,2,1,0:T(8,128)S(1)} %get-tuple-element.26), custom_call_target="InvertDiagBlocksLowerTriangular" | custom-call | tf_op jit(solution)/shard_map/vmap(jit(_solve_triangular))/triangular_solve | solution.py:94
  241.4 2.5 %fusion.22 = f32[16,8,40,128]{3,1,2,0:T(8,128)S(1)} fusion(f32[128,5120]{1,0:T(8,128)S(1)} %reshape.378, f32[1,1,128,128]{2,3,1,0:T(8,128)S(1)} %custom-call.9), kind=kOutput, calls=%fused_computation.42 | convolution fusion | flops 1007288320 | bytes 5308416 | tf_op jit(solution)/shard_map/vmap(jit(_solve_triangular))/triangular_solve | solution.py:94
  243.9 1.9 copy.40
  (20 shorter events, 0.2 us)
Async XLA Ops:
  0.6 9.8 %copy-start.3 = (s32[8]{0:T(128)S(1)}, s32[8]{0:T(128)}, u32[]{:S(2)}) copy-start(s32[8]{0:T(128)} %param.7) | copy-start | bytes 100
  3.4 41.5 %all-to-all-start = ((bf16[2,64,5,8,128]{4,1,2,0,3:T(8,128)(2,1)}), bf16[2,64,5,8,128]{4,1,2,0,3:T(8,128)(2,1)S(1)}, u32[]{:S(2)}, u32[]{:S(2)}) async-start(bf16[2,64,5,8,128]{4,1,2,0,3:T(8,128)(2,1)} %copy.32), calls=%async_computation | async-start | bytes 2621440 | tf_op jit(solution)/shard_map/all_to_all | solution.py:81
  49.8 3.8 %copy-start.1 = (f32[5,5,8,128]{3,2,1,0:T(8,128)S(1)}, f32[5,5,8,128]{3,2,1,0:T(8,128)}, u32[]{:S(2)}) copy-start(f32[5,5,8,128]{3,2,1,0:T(8,128)} %param.5) | copy-start | bytes 307204
  49.8 66.6 %all-to-all-start.1 = ((f32[16,64,5,1,128]{4,1,3,2,0:T(8,128)}), f32[16,64,5,1,128]{4,1,3,2,0:T(8,128)S(1)}, u32[]{:S(2)}, u32[]{:S(2)}) async-start(f32[16,64,5,1,128]{4,1,3,2,0:T(8,128)} %copy.34), calls=%async_computation.1 | async-start | bytes 5242880 | tf_op jit(solution)/shard_map/all_to_all | solution.py:84
  116.4 1.5 copy-start
  121.1 14.0 %copy-start.2 = (f32[8,128]{1,0:T(8,128)S(1)}, f32[8,128]{1,0:T(8,128)}, u32[]{:S(2)}) copy-start(f32[8,128]{1,0:T(8,128)} %param.6) | copy-start | bytes 12292
  122.4 19.4 %collective-permute-start.1 = (f32[1,2,64,5,2,128]{5,4,3,2,1,0:T(2,128)}, f32[1,2,64,5,2,128]{5,4,3,2,1,0:T(2,128)}, u32[]{:S(2)}, u32[]{:S(2)}) collective-permute-start(f32[1,2,64,5,2,128]{5,4,3,2,1,0:T(2,128)} %get-tuple-element.16), channel_id=1, source_target_pairs={{0,8},{8,16},{16,24},{24,32},{32,40},{40,48},{48,56},{56,64},{64,7... | collective-permute-start | bytes 1966088 | tf_op jit(solution)/shard_map/ppermute | solution.py:26
  124.3 18.9 %collective-permute-start = (f32[1,2,64,5,2,128]{5,4,3,2,1,0:T(2,128)S(1)}, f32[1,2,64,5,2,128]{5,4,3,2,1,0:T(2,128)}, u32[]{:S(2)}, u32[]{:S(2)}) collective-permute-start(f32[1,2,64,5,2,128]{5,4,3,2,1,0:T(2,128)S(1)} %get-tuple-element.17), channel_id=1, source_target_pairs={{8,0},{16,8},{24,16},{32,24},{40,32},{48,40},{56,48},{64,56},{72,6... | collective-permute-start | bytes 1966088 | tf_op jit(solution)/shard_map/ppermute | solution.py:27
  149.7 14.3 %collective-permute-start.3 = (f32[1,2,64,5,2,128]{5,4,3,2,1,0:T(2,128)S(1)}, f32[1,2,64,5,2,128]{5,4,3,2,1,0:T(2,128)S(1)}, u32[]{:S(2)}, u32[]{:S(2)}) collective-permute-start(f32[1,2,64,5,2,128]{5,4,3,2,1,0:T(2,128)S(1)} %get-tuple-element.7), channel_id=1, source_target_pairs={{0,8},{8,16},{16,24},{24,32},{32,40},{40,48},{48,56},{56,64},{64,7... | collective-permute-start | bytes 1966088 | tf_op jit(solution)/shard_map/ppermute | solution.py:26
  151.7 14.1 %collective-permute-start.2 = (f32[1,2,64,5,2,128]{5,4,3,2,1,0:T(2,128)S(1)}, f32[1,2,64,5,2,128]{5,4,3,2,1,0:T(2,128)S(1)}, u32[]{:S(2)}, u32[]{:S(2)}) collective-permute-start(f32[1,2,64,5,2,128]{5,4,3,2,1,0:T(2,128)S(1)} %get-tuple-element.8), channel_id=1, source_target_pairs={{8,0},{16,8},{24,16},{32,24},{40,32},{48,40},{56,48},{64,56},{72,6... | collective-permute-start | bytes 1966088 | tf_op jit(solution)/shard_map/ppermute | solution.py:27
  176.3 3.1 %collective-permute-start.4 = (f32[1,128,128]{1,2,0:T(8,128)S(1)}, f32[1,128,128]{1,2,0:T(8,128)S(1)}, u32[]{:S(2)}, u32[]{:S(2)}) collective-permute-start(f32[1,128,128]{1,2,0:T(8,128)S(1)} %convolution_bitcast_fusion.1), channel_id=1, source_target_pairs={{0,8},{8,0},{16,24},{24,16},{32,40},{40,32},{48,56},{56,48},{64,72... | collective-permute-start | bytes 196616 | tf_op jit(solution)/shard_map/ppermute | solution.py:36
  179.4 6.2 %collective-permute-start.5 = (f32[1,128,128]{1,2,0:T(8,128)S(1)}, f32[1,128,128]{1,2,0:T(8,128)S(1)}, u32[]{:S(2)}, u32[]{:S(2)}) collective-permute-start(f32[1,128,128]{1,2,0:T(8,128)S(1)} %add.216), channel_id=1, source_target_pairs={{0,16},{8,24},{16,0},{24,8},{32,48},{40,56},{48,32},{56,40},{64,80... | collective-permute-start | bytes 196616 | tf_op jit(solution)/shard_map/ppermute | solution.py:36
  185.6 7.5 %collective-permute-start.6 = (f32[1,128,128]{1,2,0:T(8,128)S(1)}, f32[1,128,128]{1,2,0:T(8,128)S(1)}, u32[]{:S(2)}, u32[]{:S(2)}) collective-permute-start(f32[1,128,128]{1,2,0:T(8,128)S(1)} %add.217), channel_id=1, source_target_pairs={{0,32},{8,40},{16,48},{24,56},{32,0},{40,8},{48,16},{56,24},{64,96... | collective-permute-start | bytes 196616 | tf_op jit(solution)/shard_map/ppermute | solution.py:36
  193.2 10.8 %collective-permute-start.7 = (f32[1,128,128]{1,2,0:T(8,128)S(1)}, f32[1,128,128]{1,2,0:T(8,128)S(1)}, u32[]{:S(2)}, u32[]{:S(2)}) collective-permute-start(f32[1,128,128]{1,2,0:T(8,128)S(1)} %add.218), channel_id=1, source_target_pairs={{0,64},{8,72},{16,80},{24,88},{32,96},{40,104},{48,112},{56,120},{... | collective-permute-start | bytes 196616 | tf_op jit(solution)/shard_map/ppermute | solution.py:36
  203.9 6.2 %collective-permute-start.8 = (f32[1,128,128]{1,2,0:T(8,128)S(1)}, f32[1,128,128]{1,2,0:T(8,128)S(1)}, u32[]{:S(2)}, u32[]{:S(2)}) collective-permute-start(f32[1,128,128]{1,2,0:T(8,128)S(1)} %add.219), channel_id=1, source_target_pairs={{0,128},{8,136},{16,144},{24,152},{32,160},{40,168},{48,176},{56,1... | collective-permute-start | bytes 196616 | tf_op jit(solution)/shard_map/ppermute | solution.py:36
  210.1 7.7 %collective-permute-start.9 = (f32[1,128,128]{1,2,0:T(8,128)S(1)}, f32[1,128,128]{1,2,0:T(8,128)S(1)}, u32[]{:S(2)}, u32[]{:S(2)}) collective-permute-start(f32[1,128,128]{1,2,0:T(8,128)S(1)} %add.220), channel_id=1, source_target_pairs={{0,256},{8,264},{16,272},{24,280},{32,288},{40,296},{48,304},{56,3... | collective-permute-start | bytes 196616 | tf_op jit(solution)/shard_map/ppermute | solution.py:36

commit v2 on v1

v2 whole, which is shorter than its diff:
```python
from functools import partial
import math

import jax
import jax.numpy as jnp
from jax import lax
from jax.experimental import pallas as pl
from jax.experimental.pallas import tpu as pltpu
from jax.sharding import PartitionSpec as P

K = 64
FIELDS = 5
NT = 16
F = 8
STEP_DT = 0.25
VISCOSITY = 0.5
LANES = 2 * K
HALF = 4
RH = 2
VMEM_LIMIT = 50 * 1024 * 1024


def butterfly_sum(value, axis):
    count = lax.axis_size(axis)
    stride = 1
    while stride < count:
        value = value + lax.ppermute(value, axis, [(i, i ^ stride) for i in range(count)])
        stride *= 2
    return value


def spread_body(sketch_ref, low_ref, high_ref, rows_ref, turned_ref):
    groups = low_ref.shape[0]
    radial = sketch_ref.shape[4]
    per = radial // groups
    rows_ref[...] = sketch_ref[...].astype(jnp.float32).reshape(LANES * 8, radial)
    edge = jnp.zeros((RH * HALF, LANES), jnp.float32)
    for half in range(2):
        turned_ref[half, 0 : RH * HALF, :] = edge
        turned_ref[half, (radial + RH) * HALF :, :] = edge
    for x in range(8):
        block = rows_ref[pl.ds(x, LANES, stride=8), :]
        turned_ref[x // HALF, pl.ds(RH * HALF + x % HALF, radial, stride=HALF), :] = block.T
    count = (per + 2 * RH) * HALF
    for half, ref in ((0, low_ref), (1, high_ref)):
        for group in range(groups):
            start = group * per * HALF
            ref[group] = turned_ref[half, start : start + count, :].astype(jnp.bfloat16)


def spread(sketch, groups):
    radial = sketch.shape[4]
    rows = (radial // groups + 2 * RH) * HALF
    shape = jax.ShapeDtypeStruct((groups, FIELDS * rows, LANES), jnp.bfloat16)
    return pl.pallas_call(
        spread_body,
        grid=(FIELDS,),
        in_specs=[pl.BlockSpec((2, K, 1, 8, radial), lambda i: (0, 0, i, 0, 0))],
        out_specs=[pl.BlockSpec((groups, rows, LANES), lambda i: (0, i, 0))] * 2,
        out_shape=[shape, shape],
        scratch_shapes=[
            pltpu.VMEM((LANES * 8, radial), jnp.float32),
            pltpu.VMEM((2, (radial + 2 * RH) * HALF, LANES), jnp.float32),
        ],
        compiler_params=pltpu.CompilerParams(vmem_limit_bytes=VMEM_LIMIT),
        name="spread",
    )(sketch)


def evolve_body(
    parity_ref, low_ref, high_ref, right_ref, left_ref, table_ref, coef_ref, mask_ref, turn_ref,
    out_ref, gram_ref, pair_ref, z_ref, s_ref,
):
    per = z_ref.shape[2] - 2 * RH
    rows = FIELDS * (per + 2 * RH) * HALF
    lane = lax.broadcasted_iota(jnp.int32, (16, LANES), 1)
    first = lane < K

    for quarter, ref in enumerate((low_ref, high_ref, right_ref, left_ref)):

        @pl.loop(0, rows // 16)
        def _(step):
            start = pl.multiple_of(step * 16, 16)
            for d in range(4):
                a = ref[d, pl.ds(start, 16), :].astype(jnp.float32)
                b = ref[d + 4, pl.ds(start, 16), :].astype(jnp.float32)
                pair_ref[0, d] = a + b
                pair_ref[1, d] = a - b
            line = step * 4
            field = line // (per + 2 * RH)
            cell = line % (per + 2 * RH)
            for f in range(F):
                parity = parity_ref[f]
                p = [pair_ref[parity, d] for d in range(4)]
                u = p[0] * table_ref[f, 0, 0:1]
                v = p[0] * table_ref[f, 1, 0:1]
                for d in range(1, 4):
                    u = u + p[d] * table_ref[f, 0, d : d + 1]
                    v = v + p[d] * table_ref[f, 1, d : d + 1]
                z = jnp.where(first, u, v) + pltpu.roll(jnp.where(first, v, u), K, 1)
                for c in range(4):
                    z_ref[f, field, cell + c, quarter * HALF : (quarter + 1) * HALF, :] = z[
                        c * HALF : (c + 1) * HALF
                    ]

    def advance(q, before, after, f, r):
        turn = turn_ref[f]
        values = []
        for i in range(FIELDS):
            value = coef_ref[i, r] * q[0]
            for j in range(1, FIELDS):
                value = value + coef_ref[j * FIELDS + i, r] * q[j]
            here = q[i]
            value = value + coef_ref[25, r] * pltpu.roll(here, 15, 0)
            value = value + coef_ref[26, r] * pltpu.roll(here, 1, 0)
            value = value + coef_ref[27, r] * pltpu.roll(here, 14, 0)
            value = value + coef_ref[28, r] * pltpu.roll(here, 2, 0)
            value = value + (STEP_DT * VISCOSITY) * (before[i] + after[i])
            value = value + turn * pltpu.roll(here, K, 1)
            values.append(value)
        return values

    @pl.loop(0, per + 2)
    def _(r):
        mask = mask_ref[r]

        @pl.loop(0, F)
        def _(f):
            q = [z_ref[f, i, r + 1] for i in range(FIELDS)]
            before = [z_ref[f, i, r] for i in range(FIELDS)]
            after = [z_ref[f, i, r + 2] for i in range(FIELDS)]
            for i, value in enumerate(advance(q, before, after, f, r)):
                s_ref[f, i, r] = value * mask

    @pl.loop(0, per)
    def _(r):
        @pl.loop(0, F)
        def _(f):
            q = [s_ref[f, i, r + 1] for i in range(FIELDS)]
            before = [s_ref[f, i, r] for i in range(FIELDS)]
            after = [s_ref[f, i, r + 2] for i in range(FIELDS)]
            for i, value in enumerate(advance(q, before, after, f, r + 1)):
                out_ref[f, pl.ds(i * 8 * per + r, 8, stride=per), :] = value[0:8]

    @pl.loop(0, F)
    def _(f):
        block = out_ref[f]
        gram_ref[f] = lax.dot_general(
            block, block, (((0,), (0,)), ((), ())),
            precision=lax.Precision.HIGHEST, preferred_element_type=jnp.float32,
        )


def evolve(parity, low, high, right, left, table, coef, mask, turn):
    per = coef.shape[1] - 2
    vmem = pl.BlockSpec(memory_space=pltpu.VMEM)
    return pl.pallas_call(
        evolve_body,
        in_specs=[pl.BlockSpec(memory_space=pltpu.SMEM)] + [vmem] * 8,
        out_specs=[vmem, vmem],
        out_shape=[
            jax.ShapeDtypeStruct((F, FIELDS * 8 * per, LANES), jnp.float32),
            jax.ShapeDtypeStruct((F, LANES, LANES), jnp.float32),
        ],
        scratch_shapes=[
            pltpu.VMEM((2, 4, 16, LANES), jnp.float32),
            pltpu.VMEM((F, FIELDS, per + 2 * RH, 16, LANES), jnp.float32),
            pltpu.VMEM((F, FIELDS, per + 2, 16, LANES), jnp.float32),
        ],
        compiler_params=pltpu.CompilerParams(vmem_limit_bytes=VMEM_LIMIT),
        name="evolve",
    )(parity, low, high, right, left, table, coef, mask, turn)


def apply_body(place_ref, inverse_ref, *refs):
    chunks = refs[:F]
    out_ref, rows_ref, all_ref = refs[F:]
    per = chunks[0].shape[0] // 8
    radial = per * F
    inverse = inverse_ref[...]
    for x in range(8):
        for d in range(F):
            spot = pl.multiple_of(place_ref[d] * per, per)
            all_ref[x, pl.ds(spot, per), :] = chunks[d][x * per : (x + 1) * per, :]
    for x in range(8):
        rows_ref[pl.ds(x, LANES, stride=8), :] = lax.dot_general(
            inverse, all_ref[x], (((1,), (1,)), ((), ())),
            precision=lax.Precision.HIGHEST, preferred_element_type=jnp.float32,
        )
    out_ref[...] = rows_ref[...].reshape(out_ref.shape)


def apply(place, inverse, chunks):
    per = chunks[0].shape[0] // (8 * FIELDS)
    radial = per * F
    return pl.pallas_call(
        apply_body,
        grid=(FIELDS,),
        in_specs=[
            pl.BlockSpec(memory_space=pltpu.SMEM),
            pl.BlockSpec((LANES, LANES), lambda i: (0, 0)),
        ]
        + [pl.BlockSpec((8 * per, LANES), lambda i: (i, 0))] * F,
        out_specs=pl.BlockSpec((1, LANES, 1, 8, radial), lambda i: (0, 0, i, 0, 0)),
        out_shape=jax.ShapeDtypeStruct((1, LANES, FIELDS, 8, radial), jnp.float32),
        scratch_shapes=[
            pltpu.VMEM((LANES * 8, radial), jnp.float32),
            pltpu.VMEM((8, radial, LANES), jnp.float32),
        ],
        compiler_params=pltpu.CompilerParams(vmem_limit_bytes=VMEM_LIMIT),
        name="apply",
    )(place, inverse, *chunks)


def make_table(indices, slots):
    times = jnp.arange(slots, dtype=jnp.int32)
    phases = indices[:, None] * times[None, :] % slots
    angles = phases.astype(jnp.float32) * (2.0 * math.pi / slots)
    return jnp.stack([jnp.cos(angles), -jnp.sin(angles)], axis=1)


def stencil(coupling, velocity, per):
    count = lax.axis_size("space")
    mine = lax.axis_index("space")
    start = lax.axis_index("freq") * per
    radial = velocity.shape[1]
    up = [(i, i + 1) for i in range(count - 1)]
    down = [(i + 1, i) for i in range(count - 1)]
    both = jnp.concatenate([coupling.reshape(FIELDS * FIELDS, 8, radial), velocity[None]], axis=0)
    right = lax.ppermute(both[:, :2], "space", down)
    left = lax.ppermute(both[:, 6:], "space", up)
    gap = jnp.zeros((both.shape[0], 4, radial), jnp.float32)
    full = jnp.concatenate([both, right, gap, left], axis=1)
    full = jnp.pad(full, ((0, 0), (0, 0), (1, 1)))
    full = lax.dynamic_slice_in_dim(full, start, per + 2, axis=2).transpose(0, 2, 1)
    speed = full[FIELDS * FIELDS]
    coupled = STEP_DT * full[: FIELDS * FIELDS]
    centre = 1.0 - STEP_DT * VISCOSITY * (30.0 / 12.0 + 2.0)
    diagonal = jnp.eye(FIELDS, dtype=jnp.float32).reshape(-1) * centre
    coupled = coupled + diagonal[:, None, None]
    near_d, near_c = STEP_DT * 8.0 / 12.0, STEP_DT * VISCOSITY * 16.0 / 12.0
    far_d, far_c = STEP_DT / 12.0, STEP_DT * VISCOSITY / 12.0
    shifts = jnp.stack(
        [near_d * speed + near_c, near_c - near_d * speed, -far_d * speed - far_c, far_d * speed - far_c]
    )
    coef = jnp.concatenate([coupled, shifts], axis=0)
    coef = jnp.broadcast_to(coef[..., None], coef.shape + (LANES,))
    r = start - 1 + jnp.arange(per + 2)
    place = jnp.arange(16)
    inside = (place < 8) | ((place < 12) & (mine < count - 1)) | ((place >= 12) & (mine > 0))
    mask = ((r >= 0) & (r < radial))[:, None] & inside[None, :]
    mask = jnp.broadcast_to(mask.astype(jnp.float32)[..., None], mask.shape + (LANES,))
    return coef, mask


def local(sketch, coupling, velocity, freq_index):
    groups = lax.axis_size("freq")
    count = lax.axis_size("space")
    radial = sketch.shape[4]
    per = radial // groups
    mine = lax.axis_index("freq")
    low, high = spread(sketch, groups)
    low = lax.all_to_all(low, "freq", split_axis=0, concat_axis=0, tiled=True)
    high = lax.all_to_all(high, "freq", split_axis=0, concat_axis=0, tiled=True)
    right = lax.ppermute(low, "space", [(i + 1, i) for i in range(count - 1)])
    left = lax.ppermute(high, "space", [(i, i + 1) for i in range(count - 1)])

    waves = make_table(freq_index, NT)[:, :, : NT // 2].reshape(F, 2, 4, 2)
    waves = jnp.repeat(waves, K, axis=3)
    coef, mask = stencil(coupling, velocity, per)
    angular = math.pi / NT * STEP_DT * freq_index.astype(jnp.float32)
    sign = jnp.where(jnp.arange(LANES) < K, 1.0, -1.0).astype(jnp.float32)
    turn = jnp.broadcast_to((angular[:, None] * sign)[:, None, :], (F, 16, LANES))
    columns, grams = evolve(freq_index % 2, low, high, right, left, waves, coef, mask, turn)

    parts = lax.all_to_all(grams, "freq", split_axis=0, concat_axis=0, tiled=True)
    gram = jnp.sum(parts, axis=0)
    columns, gram = lax.optimization_barrier((columns, gram))
    chunks = []
    for shift in range(groups):
        chunk = lax.dynamic_index_in_dim(columns, (mine + shift) % groups, 0, keepdims=False)
        if shift:
            chunk = lax.ppermute(chunk, "freq", [(i, (i + shift) % groups) for i in range(groups)])
        chunks.append(chunk)
    gram = butterfly_sum(gram, "space")
    chol = jnp.linalg.cholesky(gram)
    row_scale = math.sqrt(FIELDS * 8 * count * radial)
    inverse = jax.scipy.linalg.solve_triangular(chol, row_scale * jnp.eye(LANES, dtype=jnp.float32), lower=True)
    place = (mine - jnp.arange(groups)) % groups
    basis = apply(place.astype(jnp.int32), inverse, chunks)
    return basis, (chol / row_scale)[None]


def solution(mesh):
    return jax.shard_map(
        local,
        mesh=mesh,
        in_specs=(
            P("freq", None, None, "space", None),
            P(None, None, "space", None),
            P("space", None),
            P(),
        ),
        out_specs=(P("freq", None, None, "space", None), P("freq", None, None)),
        check_vma=False,
    )
```

time: 247 us -> 262 us (1.061)
  the two profiles are of different devices: /device:TPU:6 before, /device:TPU:1 now
where the time goes in v2:
time: 262 us; the launch traced here: 261 us
  starting transfers between devices  88.4 us (34%)
  waiting for transfers between devices  63.6 us (24%)
  Pallas kernels  52.4 us (20%)
  other arithmetic  29.8 us (11%)
  blocking collectives  14.8 us (6%)
  local copies, waits for them, and re-layouts  10.4 us (4%)
    pallas_call x1, Pallas kernels, evolve(): pl.pallas_call(evolve_body, in_specs=[pl.BlockSpec(memory_space=pltpu.SME...  41.5 us
    ppermute x6, starting transfers between devices, butterfly_sum(): lax.ppermute(value, axis, [(i, i ^ stride) for i in range(count)])  32.5 us
    ppermute x7, starting transfers between devices, local(): lax.ppermute(chunk, 'freq', [(i, (i + shift) % groups) for i in range(gro...  23.3 us
    ppermute x7, waiting for transfers between devices, local(): lax.ppermute(chunk, 'freq', [(i, (i + shift) % groups) for i in range(gro...  23 us
    all_to_all x1, waiting for transfers between devices, local(): low = lax.all_to_all(low, 'freq', split_axis=0, concat_axis=0, tiled=True)  14.8 us
    all_to_all x1, blocking collectives, local(): lax.all_to_all(grams, 'freq', split_axis=0, concat_axis=0, tiled=True)  14.8 us
    all_to_all x1, waiting for transfers between devices, local(): high = lax.all_to_all(high, 'freq', split_axis=0, concat_axis=0, tiled=True)  14 us
    another operation x3, other arithmetic, local(): chol = jnp.linalg.cholesky(gram)  12.4 us
  transfers between devices with their start and end apart: 19, of which 10 were waited for; matrix products, arithmetic and copies ran while one was open for 13% of the time, Pallas kernels for 0%

profile of v2, /device:TPU:1, one launch (start us, length us, event | category | flops | bytes accessed | tf_op | source)
XLA Modules:
  0.0 260.8 jit_solution(7411995320874530788)
XLA Ops:
  0.6 1.3 copy-done
  2.0 3.1 %spread.1 = (bf16[8,400,128]{2,1,0:T(8,128)(2,1)}, bf16[8,400,128]{2,1,0:T(8,128)(2,1)}) custom-call(bf16[2,64,5,8,128]{4,3,2,1,0:T(8,128)(2,1)S(1)} %copy-done), custom_call_target="tpu_custom_call" | custom-call | tf_op jit(solution)/shard_map/spread/pallas_call | solution.py:55
  5.1 7.7 %all-to-all-start = ((bf16[8,400,128]{2,1,0:T(8,128)(2,1)}), bf16[8,400,128]{2,1,0:T(8,128)(2,1)S(1)}, u32[]{:S(2)}, u32[]{:S(2)}) async-start(bf16[8,400,128]{2,1,0:T(8,128)(2,1)} %get-tuple-element.8), calls=%async_computation | async-start | bytes 1638400 | tf_op jit(solution)/shard_map/all_to_all | solution.py:263
  12.8 4.7 %collective-permute-start.2 = (f32[26,2,128]{2,1,0:T(2,128)S(1)}, f32[26,2,128]{2,1,0:T(2,128)S(1)}, u32[]{:S(2)}, u32[]{:S(2)}) collective-permute-start(f32[26,2,128]{2,1,0:T(2,128)S(1)} %get-tuple-element.22), channel_id=1, source_target_pairs={{8,0},{16,8},{24,16},{32,24},{40,32},{48,40},{56,48},{64,56},{72,6... | collective-permute-start | bytes 79880 | tf_op jit(solution)/shard_map/ppermute | solution.py:230
  17.5 2.1 collective-permute-start.3
  19.7 14.8 %all-to-all-done.low_ref = bf16[8,400,128]{2,1,0:T(8,128)(2,1)S(1)} async-done(((bf16[8,400,128]{2,1,0:T(8,128)(2,1)}), bf16[8,400,128]{2,1,0:T(8,128)(2,1)S(1)}, u32[]{:S(2)}, u32[]{:S(2)}) %all-to-all-start) | async-done | bytes 819232 | tf_op jit(solution)/shard_map/all_to_all | solution.py:263
  34.5 3.5 %all-to-all-start.1 = ((bf16[8,400,128]{2,1,0:T(8,128)(2,1)}), bf16[8,400,128]{2,1,0:T(8,128)(2,1)S(1)}, u32[]{:S(2)}, u32[]{:S(2)}) async-start(bf16[8,400,128]{2,1,0:T(8,128)(2,1)} %get-tuple-element.9), calls=%async_computation.1 | async-start | bytes 1638400 | tf_op jit(solution)/shard_map/all_to_all | solution.py:264
  39.0 0.7 copy-done.2
  39.7 0.8 fusion.2
  40.5 5.0 %collective-permute-start = (bf16[8,400,128]{2,1,0:T(8,128)(2,1)S(1)}, bf16[8,400,128]{2,1,0:T(8,128)(2,1)S(1)}, u32[]{:S(2)}, u32[]{:S(2)}) collective-permute-start(bf16[8,400,128]{2,1,0:T(8,128)(2,1)S(1)} %all-to-all-done.low_ref), channel_id=1, source_target_pairs={{8,0},{16,8},{24,16},{32,24},{40,32},{48,40},{56,48},{64,56},{72,6... | collective-permute-start | bytes 2457608 | tf_op jit(solution)/shard_map/ppermute | solution.py:265
  45.4 14.0 %all-to-all-done.1.high_ref = bf16[8,400,128]{2,1,0:T(8,128)(2,1)S(1)} async-done(((bf16[8,400,128]{2,1,0:T(8,128)(2,1)}), bf16[8,400,128]{2,1,0:T(8,128)(2,1)S(1)}, u32[]{:S(2)}, u32[]{:S(2)}) %all-to-all-start.1) | async-done | bytes 819232 | tf_op jit(solution)/shard_map/all_to_all | solution.py:264
  59.4 9.8 %collective-permute-start.1 = (bf16[8,400,128]{2,1,0:T(8,128)(2,1)S(1)}, bf16[8,400,128]{2,1,0:T(8,128)(2,1)S(1)}, u32[]{:S(2)}, u32[]{:S(2)}) collective-permute-start(bf16[8,400,128]{2,1,0:T(8,128)(2,1)S(1)} %all-to-all-done.1.high_ref), channel_id=1, source_target_pairs={{0,8},{8,16},{16,24},{24,32},{32,40},{40,48},{48,56},{56,64},{64,7... | collective-permute-start | bytes 2457608 | tf_op jit(solution)/shard_map/ppermute | solution.py:266
  69.2 1.3 constant_dynamic-update-slice_fusion.3
  70.5 1.3 constant_dynamic-update-slice_fusion.2
  71.7 1.3 constant_dynamic-update-slice_fusion.1
  73.0 1.3 constant_dynamic-update-slice_fusion
  74.3 1.9 copy.21
  76.3 2.1 collective-permute-done.1.left_ref
  78.4 4.2 %broadcast_in_dim.26.coef_ref = f32[29,18,16,128]{3,2,1,0:T(8,128)} broadcast(f32[29,18,16]{2,1,0:T(8,128)} %copy.21), dimensions={0,1,2} | broadcast | bytes 4309632 | tf_op jit(solution)/shard_map/broadcast_in_dim | solution.py:247
  82.7 41.5 %evolve.1 = (f32[8,640,128]{2,1,0:T(8,128)}, f32[8,128,128]{2,1,0:T(8,128)S(1)}) custom-call(s32[8]{0:T(128)S(1)} %and_select_fusion.parity_ref, bf16[8,400,128]{2,1,0:T(8,128)(2,1)S(1)} %all-to-all-done.low_ref, bf16[8,400,128]{2,1,0:T(8,128)(2,1)S(1)} %all-to-all-done.1.high_ref, bf16[8,400,128]{2,1,0:T(8,128)(2,1)S(1)} %collective-permute-done.right_ref, ...), custom_call_target="tpu_custom_call" | custom-call | tf_op jit(solution)/shard_map/evolve/pallas_call | solution.py:157
  124.2 14.8 %all_to_all.15 = f32[8,128,128]{2,1,0:T(8,128)S(1)} all-to-all(f32[8,128,128]{2,1,0:T(8,128)S(1)} %get-tuple-element.11), channel_id=1, replica_groups=mesh['space'=64,'freq'=8] {'freq'}, dimensions={0} | all-to-all | bytes 1048576 | tf_op jit(solution)/shard_map/all_to_all | solution.py:276
  139.1 1.9 collective-permute-start.4
  141.0 1.2 collective-permute-done.4
  142.3 10.0 %collective-permute-start.5 = (f32[128,128]{0,1:T(8,128)S(1)}, f32[128,128]{0,1:T(8,128)S(1)}, u32[]{:S(2)}, u32[]{:S(2)}) collective-permute-start(f32[128,128]{0,1:T(8,128)S(1)} %add.169), channel_id=1, source_target_pairs={{0,16},{8,24},{16,0},{24,8},{32,48},{40,56},{48,32},{56,40},{64,80... | collective-permute-start | bytes 196616 | tf_op jit(solution)/shard_map/ppermute | solution.py:27
  152.2 2.2 collective-permute-done.5
  154.4 6.7 %collective-permute-start.6 = (f32[128,128]{0,1:T(8,128)S(1)}, f32[128,128]{0,1:T(8,128)S(1)}, u32[]{:S(2)}, u32[]{:S(2)}) collective-permute-start(f32[128,128]{0,1:T(8,128)S(1)} %add.170), channel_id=1, source_target_pairs={{0,32},{8,40},{16,48},{24,56},{32,0},{40,8},{48,16},{56,24},{64,96... | collective-permute-start | bytes 196616 | tf_op jit(solution)/shard_map/ppermute | solution.py:27
  161.2 1.7 collective-permute-done.6
  162.8 6.1 %collective-permute-start.7 = (f32[128,128]{0,1:T(8,128)S(1)}, f32[128,128]{0,1:T(8,128)S(1)}, u32[]{:S(2)}, u32[]{:S(2)}) collective-permute-start(f32[128,128]{0,1:T(8,128)S(1)} %add.171), channel_id=1, source_target_pairs={{0,64},{8,72},{16,80},{24,88},{32,96},{40,104},{48,112},{56,120},{... | collective-permute-start | bytes 196616 | tf_op jit(solution)/shard_map/ppermute | solution.py:27
  169.0 2.8 %collective-permute-done.7 = f32[128,128]{0,1:T(8,128)S(1)} collective-permute-done((f32[128,128]{0,1:T(8,128)S(1)}, f32[128,128]{0,1:T(8,128)S(1)}, u32[]{:S(2)}, u32[]{:S(2)}) %collective-permute-start.7) | collective-permute-done | bytes 65568 | tf_op jit(solution)/shard_map/ppermute | solution.py:27
  171.8 3.1 %collective-permute-start.8 = (f32[128,128]{0,1:T(8,128)S(1)}, f32[128,128]{0,1:T(8,128)S(1)}, u32[]{:S(2)}, u32[]{:S(2)}) collective-permute-start(f32[128,128]{0,1:T(8,128)S(1)} %add.172), channel_id=1, source_target_pairs={{0,128},{8,136},{16,144},{24,152},{32,160},{40,168},{48,176},{56,1... | collective-permute-start | bytes 196616 | tf_op jit(solution)/shard_map/ppermute | solution.py:27
  174.9 1.9 collective-permute-done.8
  176.8 4.7 %collective-permute-start.9 = (f32[128,128]{0,1:T(8,128)S(1)}, f32[128,128]{0,1:T(8,128)S(1)}, u32[]{:S(2)}, u32[]{:S(2)}) collective-permute-start(f32[128,128]{0,1:T(8,128)S(1)} %add.173), channel_id=1, source_target_pairs={{0,256},{8,264},{16,272},{24,280},{32,288},{40,296},{48,304},{56,3... | collective-permute-start | bytes 196616 | tf_op jit(solution)/shard_map/ppermute | solution.py:27
  181.5 1.3 dynamic-slice_bitcast_fusion
  182.8 2.0 collective-permute-start.10
  184.8 2.6 collective-permute-start.11
  187.3 3.4 %collective-permute-start.12 = (f32[640,128]{1,0:T(8,128)}, f32[640,128]{1,0:T(8,128)S(1)}, u32[]{:S(2)}, u32[]{:S(2)}) collective-permute-start(f32[640,128]{1,0:T(8,128)} %get-tuple-element.18), channel_id=1, source_target_pairs={{0,3},{1,4},{2,5},{3,6},{4,7},{5,0},{6,1},{7,2},{8,11},{9,12},{10,... | collective-permute-start | bytes 983048 | tf_op jit(solution)/shard_map/ppermute | solution.py:283
  190.8 6.0 %collective-permute-start.13 = (f32[640,128]{1,0:T(8,128)}, f32[640,128]{1,0:T(8,128)S(1)}, u32[]{:S(2)}, u32[]{:S(2)}) collective-permute-start(f32[640,128]{1,0:T(8,128)} %get-tuple-element.17), channel_id=1, source_target_pairs={{0,4},{1,5},{2,6},{3,7},{4,0},{5,1},{6,2},{7,3},{8,12},{9,13},{10,... | collective-permute-start | bytes 983048 | tf_op jit(solution)/shard_map/ppermute | solution.py:283
  196.8 2.0 collective-permute-start.14
  199.0 11.7 %cholesky.17 = f32[128,128]{1,0:T(8,128)S(1)} custom-call(f32[128,128]{1,0:T(8,128)S(1)} %fusion.5), custom_call_target="Cholesky" | custom-call | tf_op jit(solution)/shard_map/jit(cholesky)/cholesky | solution.py:286
  210.7 0.6 compare_reduce_fusion
  211.3 4.7 %collective-permute-start.15 = (f32[640,128]{1,0:T(8,128)}, f32[640,128]{1,0:T(8,128)S(1)}, u32[]{:S(2)}, u32[]{:S(2)}) collective-permute-start(f32[640,128]{1,0:T(8,128)} %get-tuple-element.15), channel_id=1, source_target_pairs={{0,6},{1,7},{2,0},{3,1},{4,2},{5,3},{6,4},{7,5},{8,14},{9,15},{10,... | collective-permute-start | bytes 983048 | tf_op jit(solution)/shard_map/ppermute | solution.py:283
  216.1 2.6 collective-permute-start.16
  218.7 1.2 multiply_bitcast_fusion
  219.9 9.8 %custom-call.7 = f32[1,128,128]{1,2,0:T(8,128)S(1)} custom-call(f32[1,128,128]{2,1,0:T(8,128)S(1)} %get-tuple-element.25), custom_call_target="InvertDiagBlocksLowerTriangular" | custom-call | tf_op jit(solution)/shard_map/jit(_solve_triangular)/triangular_solve | solution.py:288
  229.7 0.3 fusion.3.inverse_ref
  230.0 14.3 %collective-permute-done.15.refs_6_ = f32[640,128]{1,0:T(8,128)S(1)} collective-permute-done((f32[640,128]{1,0:T(8,128)}, f32[640,128]{1,0:T(8,128)S(1)}, u32[]{:S(2)}, u32[]{:S(2)}) %collective-permute-start.15) | collective-permute-done | bytes 327712 | tf_op jit(solution)/shard_map/ppermute | solution.py:283
  244.3 8.6 %collective-permute-done.16.refs_7_ = f32[640,128]{1,0:T(8,128)S(1)} collective-permute-done((f32[640,128]{1,0:T(8,128)S(1)}, f32[640,128]{1,0:T(8,128)S(1)}, u32[]{:S(2)}, u32[]{:S(2)}) %collective-permute-start.16) | collective-permute-done | bytes 327712 | tf_op jit(solution)/shard_map/ppermute | solution.py:283
  252.9 7.9 %apply.1 = f32[1,128,5,8,128]{4,3,2,1,0:T(8,128)} custom-call(s32[8]{0:T(128)S(1)} %and_select_fusion.1.place_ref, f32[128,128]{1,0:T(8,128)S(1)} %fusion.3.inverse_ref, f32[640,128]{1,0:T(8,128)S(1)} %get-tuple-element.21.refs_0_, f32[640,128]{1,0:T(8,128)S(1)} %collective-permute-done.10.refs_1_, f32[640,128]{1,0:T(8,128)S(1)} %collective-permute-done.11.refs_2_, ...), custom_call_target="tpu_custom_call" | custom-call | tf_op jit(solution)/shard_map/apply/pallas_call | solution.py:196
  (52 shorter events, 1.5 us)
Async XLA Ops:
  0.6 1.3 copy-start
  1.9 10.8 %copy-start.3 = (f32[5,5,8,128]{3,2,1,0:T(8,128)S(1)}, f32[5,5,8,128]{3,2,1,0:T(8,128)}, u32[]{:S(2)}) copy-start(f32[5,5,8,128]{3,2,1,0:T(8,128)} %param.5) | copy-start | bytes 307204
  1.9 10.8 %copy-start.4 = (f32[8,128]{1,0:T(8,128)S(1)}, f32[8,128]{1,0:T(8,128)}, u32[]{:S(2)}) copy-start(f32[8,128]{1,0:T(8,128)} %param.6) | copy-start | bytes 12292
  2.0 17.6 %copy-start.5 = (s32[8]{0:T(128)S(1)}, s32[8]{0:T(128)}, u32[]{:S(2)}) copy-start(s32[8]{0:T(128)} %param.7) | copy-start | bytes 100
  5.1 29.4 %all-to-all-start = ((bf16[8,400,128]{2,1,0:T(8,128)(2,1)}), bf16[8,400,128]{2,1,0:T(8,128)(2,1)S(1)}, u32[]{:S(2)}, u32[]{:S(2)}) async-start(bf16[8,400,128]{2,1,0:T(8,128)(2,1)} %get-tuple-element.8), calls=%async_computation | async-start | bytes 1638400 | tf_op jit(solution)/shard_map/all_to_all | solution.py:263
  12.8 26.0 %collective-permute-start.2 = (f32[26,2,128]{2,1,0:T(2,128)S(1)}, f32[26,2,128]{2,1,0:T(2,128)S(1)}, u32[]{:S(2)}, u32[]{:S(2)}) collective-permute-start(f32[26,2,128]{2,1,0:T(2,128)S(1)} %get-tuple-element.22), channel_id=1, source_target_pairs={{8,0},{16,8},{24,16},{32,24},{40,32},{48,40},{56,48},{64,56},{72,6... | collective-permute-start | bytes 79880 | tf_op jit(solution)/shard_map/ppermute | solution.py:230
  17.5 21.3 %collective-permute-start.3 = (f32[26,2,128]{2,1,0:T(2,128)S(1)}, f32[26,2,128]{2,1,0:T(2,128)S(1)}, u32[]{:S(2)}, u32[]{:S(2)}) collective-permute-start(f32[26,2,128]{2,1,0:T(2,128)S(1)} %get-tuple-element.23), channel_id=1, source_target_pairs={{0,8},{8,16},{16,24},{24,32},{32,40},{40,48},{48,56},{56,64},{64,7... | collective-permute-start | bytes 79880 | tf_op jit(solution)/shard_map/ppermute | solution.py:231
  34.5 24.9 %all-to-all-start.1 = ((bf16[8,400,128]{2,1,0:T(8,128)(2,1)}), bf16[8,400,128]{2,1,0:T(8,128)(2,1)S(1)}, u32[]{:S(2)}, u32[]{:S(2)}) async-start(bf16[8,400,128]{2,1,0:T(8,128)(2,1)} %get-tuple-element.9), calls=%async_computation.1 | async-start | bytes 1638400 | tf_op jit(solution)/shard_map/all_to_all | solution.py:264
  39.0 0.7 copy-start.2
  40.5 35.8 %collective-permute-start = (bf16[8,400,128]{2,1,0:T(8,128)(2,1)S(1)}, bf16[8,400,128]{2,1,0:T(8,128)(2,1)S(1)}, u32[]{:S(2)}, u32[]{:S(2)}) collective-permute-start(bf16[8,400,128]{2,1,0:T(8,128)(2,1)S(1)} %all-to-all-done.low_ref), channel_id=1, source_target_pairs={{8,0},{16,8},{24,16},{32,24},{40,32},{48,40},{56,48},{64,56},{72,6... | collective-permute-start | bytes 2457608 | tf_op jit(solution)/shard_map/ppermute | solution.py:265
  59.4 19.0 %collective-permute-start.1 = (bf16[8,400,128]{2,1,0:T(8,128)(2,1)S(1)}, bf16[8,400,128]{2,1,0:T(8,128)(2,1)S(1)}, u32[]{:S(2)}, u32[]{:S(2)}) collective-permute-start(bf16[8,400,128]{2,1,0:T(8,128)(2,1)S(1)} %all-to-all-done.1.high_ref), channel_id=1, source_target_pairs={{0,8},{8,16},{16,24},{24,32},{32,40},{40,48},{48,56},{56,64},{64,7... | collective-permute-start | bytes 2457608 | tf_op jit(solution)/shard_map/ppermute | solution.py:266
  124.2 57.3 %copy-start.1 = (f32[8,640,128]{2,1,0:T(8,128)S(1)}, f32[8,640,128]{2,1,0:T(8,128)}, u32[]{:S(2)}) copy-start(f32[8,640,128]{2,1,0:T(8,128)} %get-tuple-element.13) | copy-start | bytes 7864324
  139.1 3.1 %collective-permute-start.4 = (f32[128,128]{0,1:T(8,128)S(1)}, f32[128,128]{0,1:T(8,128)S(1)}, u32[]{:S(2)}, u32[]{:S(2)}) collective-permute-start(f32[128,128]{0,1:T(8,128)S(1)} %copy.23), channel_id=1, source_target_pairs={{0,8},{8,0},{16,24},{24,16},{32,40},{40,32},{48,56},{56,48},{64,72... | collective-permute-start | bytes 196616 | tf_op jit(solution)/shard_map/ppermute | solution.py:27
  142.3 12.1 %collective-permute-start.5 = (f32[128,128]{0,1:T(8,128)S(1)}, f32[128,128]{0,1:T(8,128)S(1)}, u32[]{:S(2)}, u32[]{:S(2)}) collective-permute-start(f32[128,128]{0,1:T(8,128)S(1)} %add.169), channel_id=1, source_target_pairs={{0,16},{8,24},{16,0},{24,8},{32,48},{40,56},{48,32},{56,40},{64,80... | collective-permute-start | bytes 196616 | tf_op jit(solution)/shard_map/ppermute | solution.py:27
  154.4 8.4 %collective-permute-start.6 = (f32[128,128]{0,1:T(8,128)S(1)}, f32[128,128]{0,1:T(8,128)S(1)}, u32[]{:S(2)}, u32[]{:S(2)}) collective-permute-start(f32[128,128]{0,1:T(8,128)S(1)} %add.170), channel_id=1, source_target_pairs={{0,32},{8,40},{16,48},{24,56},{32,0},{40,8},{48,16},{56,24},{64,96... | collective-permute-start | bytes 196616 | tf_op jit(solution)/shard_map/ppermute | solution.py:27
  162.8 8.9 %collective-permute-start.7 = (f32[128,128]{0,1:T(8,128)S(1)}, f32[128,128]{0,1:T(8,128)S(1)}, u32[]{:S(2)}, u32[]{:S(2)}) collective-permute-start(f32[128,128]{0,1:T(8,128)S(1)} %add.171), channel_id=1, source_target_pairs={{0,64},{8,72},{16,80},{24,88},{32,96},{40,104},{48,112},{56,120},{... | collective-permute-start | bytes 196616 | tf_op jit(solution)/shard_map/ppermute | solution.py:27
  171.8 5.0 %collective-permute-start.8 = (f32[128,128]{0,1:T(8,128)S(1)}, f32[128,128]{0,1:T(8,128)S(1)}, u32[]{:S(2)}, u32[]{:S(2)}) collective-permute-start(f32[128,128]{0,1:T(8,128)S(1)} %add.172), channel_id=1, source_target_pairs={{0,128},{8,136},{16,144},{24,152},{32,160},{40,168},{48,176},{56,1... | collective-permute-start | bytes 196616 | tf_op jit(solution)/shard_map/ppermute | solution.py:27
  176.8 20.0 %collective-permute-start.9 = (f32[128,128]{0,1:T(8,128)S(1)}, f32[128,128]{0,1:T(8,128)S(1)}, u32[]{:S(2)}, u32[]{:S(2)}) collective-permute-start(f32[128,128]{0,1:T(8,128)S(1)} %add.173), channel_id=1, source_target_pairs={{0,256},{8,264},{16,272},{24,280},{32,288},{40,296},{48,304},{56,3... | collective-permute-start | bytes 196616 | tf_op jit(solution)/shard_map/ppermute | solution.py:27
  182.8 28.5 %collective-permute-start.10 = (f32[640,128]{1,0:T(8,128)}, f32[640,128]{1,0:T(8,128)S(1)}, u32[]{:S(2)}, u32[]{:S(2)}) collective-permute-start(f32[640,128]{1,0:T(8,128)} %get-tuple-element.20), channel_id=1, source_target_pairs={{0,1},{1,2},{2,3},{3,4},{4,5},{5,6},{6,7},{7,0},{8,9},{9,10},{10,1... | collective-permute-start | bytes 983048 | tf_op jit(solution)/shard_map/ppermute | solution.py:283
  184.8 31.3 %collective-permute-start.11 = (f32[640,128]{1,0:T(8,128)}, f32[640,128]{1,0:T(8,128)S(1)}, u32[]{:S(2)}, u32[]{:S(2)}) collective-permute-start(f32[640,128]{1,0:T(8,128)} %get-tuple-element.19), channel_id=1, source_target_pairs={{0,2},{1,3},{2,4},{3,5},{4,6},{5,7},{6,0},{7,1},{8,10},{9,11},{10,... | collective-permute-start | bytes 983048 | tf_op jit(solution)/shard_map/ppermute | solution.py:283
  187.3 42.6 %collective-permute-start.12 = (f32[640,128]{1,0:T(8,128)}, f32[640,128]{1,0:T(8,128)S(1)}, u32[]{:S(2)}, u32[]{:S(2)}) collective-permute-start(f32[640,128]{1,0:T(8,128)} %get-tuple-element.18), channel_id=1, source_target_pairs={{0,3},{1,4},{2,5},{3,6},{4,7},{5,0},{6,1},{7,2},{8,11},{9,12},{10,... | collective-permute-start | bytes 983048 | tf_op jit(solution)/shard_map/ppermute | solution.py:283
  190.8 39.2 %collective-permute-start.13 = (f32[640,128]{1,0:T(8,128)}, f32[640,128]{1,0:T(8,128)S(1)}, u32[]{:S(2)}, u32[]{:S(2)}) collective-permute-start(f32[640,128]{1,0:T(8,128)} %get-tuple-element.17), channel_id=1, source_target_pairs={{0,4},{1,5},{2,6},{3,7},{4,0},{5,1},{6,2},{7,3},{8,12},{9,13},{10,... | collective-permute-start | bytes 983048 | tf_op jit(solution)/shard_map/ppermute | solution.py:283
  196.8 33.2 %collective-permute-start.14 = (f32[640,128]{1,0:T(8,128)}, f32[640,128]{1,0:T(8,128)S(1)}, u32[]{:S(2)}, u32[]{:S(2)}) collective-permute-start(f32[640,128]{1,0:T(8,128)} %get-tuple-element.16), channel_id=1, source_target_pairs={{0,5},{1,6},{2,7},{3,0},{4,1},{5,2},{6,3},{7,4},{8,13},{9,14},{10,... | collective-permute-start | bytes 983048 | tf_op jit(solution)/shard_map/ppermute | solution.py:283
  211.3 33.0 %collective-permute-start.15 = (f32[640,128]{1,0:T(8,128)}, f32[640,128]{1,0:T(8,128)S(1)}, u32[]{:S(2)}, u32[]{:S(2)}) collective-permute-start(f32[640,128]{1,0:T(8,128)} %get-tuple-element.15), channel_id=1, source_target_pairs={{0,6},{1,7},{2,0},{3,1},{4,2},{5,3},{6,4},{7,5},{8,14},{9,15},{10,... | collective-permute-start | bytes 983048 | tf_op jit(solution)/shard_map/ppermute | solution.py:283
  216.1 36.9 %collective-permute-start.16 = (f32[640,128]{1,0:T(8,128)S(1)}, f32[640,128]{1,0:T(8,128)S(1)}, u32[]{:S(2)}, u32[]{:S(2)}) collective-permute-start(f32[640,128]{1,0:T(8,128)S(1)} %get-tuple-element.14), channel_id=1, source_target_pairs={{0,7},{1,0},{2,1},{3,2},{4,3},{5,4},{6,5},{7,6},{8,15},{9,8},{10,9... | collective-permute-start | bytes 983048 | tf_op jit(solution)/shard_map/ppermute | solution.py:283

commit v3 on v2

v3 whole, which is shorter than its diff:
```python
from functools import partial
import math

import jax
import jax.numpy as jnp
from jax import lax
from jax.experimental import pallas as pl
from jax.experimental.pallas import tpu as pltpu
from jax.sharding import PartitionSpec as P

K = 64
FIELDS = 5
NT = 16
F = 8
STEP_DT = 0.25
VISCOSITY = 0.5
LANES = 2 * K
HALF = 4
RH = 2
VMEM_LIMIT = 50 * 1024 * 1024


def quad_sum(value, axis, bit):
    count = lax.axis_size(axis)
    others = [m << bit for m in (2, 3, 1)]
    return [value] + [lax.ppermute(value, axis, [(i, i ^ m) for i in range(count)]) for m in others]


def spread_body(sketch_ref, out_ref, rows_ref, turned_ref):
    groups = out_ref.shape[0]
    radial = sketch_ref.shape[4]
    per = radial // groups
    rows_ref[...] = sketch_ref[...].astype(jnp.float32).reshape(LANES * 8, radial)
    edge = jnp.zeros((RH * HALF, LANES), jnp.float32)
    for half in range(2):
        turned_ref[half, 0 : RH * HALF, :] = edge
        turned_ref[half, (radial + RH) * HALF :, :] = edge
    for x in range(8):
        block = rows_ref[pl.ds(x, LANES, stride=8), :]
        turned_ref[x // HALF, pl.ds(RH * HALF + x % HALF, radial, stride=HALF), :] = block.T
    count = (per + 2 * RH) * HALF
    for half in range(2):
        for group in range(groups):
            start = group * per * HALF
            out_ref[group, half] = turned_ref[half, start : start + count, :].astype(jnp.bfloat16)


def spread(sketch, groups):
    radial = sketch.shape[4]
    rows = (radial // groups + 2 * RH) * HALF
    return pl.pallas_call(
        spread_body,
        grid=(FIELDS,),
        in_specs=[pl.BlockSpec((2, K, 1, 8, radial), lambda i: (0, 0, i, 0, 0))],
        out_specs=pl.BlockSpec((groups, 2, rows, LANES), lambda i: (0, 0, i, 0)),
        out_shape=jax.ShapeDtypeStruct((groups, 2, FIELDS * rows, LANES), jnp.bfloat16),
        scratch_shapes=[
            pltpu.VMEM((LANES * 8, radial), jnp.float32),
            pltpu.VMEM((2, (radial + 2 * RH) * HALF, LANES), jnp.float32),
        ],
        compiler_params=pltpu.CompilerParams(vmem_limit_bytes=VMEM_LIMIT),
        name="spread",
    )(sketch)


def fourier_body(parity_ref, rows_ref, table_ref, z_ref, pair_ref):
    size = pair_ref.shape[2]
    first = lax.broadcasted_iota(jnp.int32, (8, LANES), 1) < K

    @pl.loop(0, rows_ref.shape[2] // size)
    def _(step):
        start = pl.multiple_of(step * size, size)
        for d in range(4):
            a = rows_ref[d, 0, pl.ds(start, size), :].astype(jnp.float32)
            b = rows_ref[d + 4, 0, pl.ds(start, size), :].astype(jnp.float32)
            pair_ref[0, d] = a + b
            pair_ref[1, d] = a - b
        for f in range(F):
            parity = parity_ref[f]
            wave = [[jnp.broadcast_to(table_ref[f, c, d : d + 1], (8, LANES)) for d in range(4)] for c in range(2)]
            for line in range(0, size, 8):
                p = [pair_ref[parity, d, line : line + 8] for d in range(4)]
                u = (p[0] * wave[0][0] + p[1] * wave[0][1]) + (p[2] * wave[0][2] + p[3] * wave[0][3])
                v = (p[0] * wave[1][0] + p[1] * wave[1][1]) + (p[2] * wave[1][2] + p[3] * wave[1][3])
                z_ref[f, pl.ds(start + line, 8), :] = jnp.where(first, u, v) + pltpu.roll(
                    jnp.where(first, v, u), K, 1
                )


def fourier(parity, rows, part, table):
    slots, _, count, _ = rows.shape
    return pl.pallas_call(
        fourier_body,
        grid=(1,),
        in_specs=[
            pl.BlockSpec(memory_space=pltpu.SMEM),
            pl.BlockSpec((slots, 1, count, LANES), lambda i: (0, part, 0, 0)),
            pl.BlockSpec(table.shape, lambda i: (0, 0, 0, 0)),
        ],
        out_specs=pl.BlockSpec((F, count, LANES), lambda i: (0, 0, 0)),
        out_shape=jax.ShapeDtypeStruct((F, count, LANES), jnp.float32),
        scratch_shapes=[pltpu.VMEM((2, 4, count // 5, LANES), jnp.float32)],
        compiler_params=pltpu.CompilerParams(vmem_limit_bytes=VMEM_LIMIT),
        name="fourier",
    )(parity, rows, table)


def evolve_body(order_ref, *refs):
    layers, (coef_ref, mask_ref, turn_a, turn_b, out_ref, gram_ref, z_ref, s_ref) = refs[:8], refs[8:]
    wide = z_ref.shape[2]
    per = wide - 2 * RH
    sub = lax.broadcasted_iota(jnp.int32, (8, LANES), 0)

    @pl.loop(0, layers[0].shape[1] // 8, unroll=5)
    def _(step):
        here = pl.ds(pl.multiple_of(step * 8, 8), 8)
        line = step * 2
        field = line // wide
        cell = line % wide
        for n in range(2):
            for tile in range(2):
                a = layers[4 * n + 2 * tile][0, here, :]
                b = layers[4 * n + 2 * tile + 1][0, here, :]
                z_ref[n, field, cell, tile] = jnp.where(sub < HALF, a, pltpu.roll(b, HALF, 0))
                z_ref[n, field, cell + 1, tile] = jnp.where(sub < HALF, pltpu.roll(a, HALF, 0), b)

    turns = [turn_a[0], turn_b[0]]

    def shifted(tiles, shift, t):
        keep = (sub < 8 - shift) if shift > 0 else (sub >= -shift)
        turned = [pltpu.roll(v, (-shift) % 8, 0) for v in tiles]
        return jnp.where(keep, turned[t], turned[1 - t])

    def advance(ref, r, place, t, store):
        q = [[ref[n, j, r, t] for j in range(FIELDS)] for n in range(2)]
        for i in range(FIELDS):
            coupled = [coef_ref[j * FIELDS + i, place, t] for j in range(FIELDS)]
            moves = [coef_ref[FIELDS * FIELDS + m, place, t] for m in range(4)]
            for n in range(2):
                value = coupled[0] * q[n][0]
                for j in range(1, FIELDS):
                    value = value + coupled[j] * q[n][j]
                pair = [None, None]
                pair[t] = q[n][i]
                pair[1 - t] = ref[n, i, r, 1 - t]
                for m, shift in enumerate((1, -1, 2, -2)):
                    value = value + moves[m] * shifted(pair, shift, t)
                value = value + (STEP_DT * VISCOSITY) * (ref[n, i, r - 1, t] + ref[n, i, r + 1, t])
                store(n, i, value + turns[n] * pltpu.roll(q[n][i], K, 1))

    @pl.loop(0, per + 2)
    def _(r):
        for t in range(2):
            mask = mask_ref[r, t]

            def store(n, i, value):
                s_ref[n, i, r, t] = value * mask

            advance(z_ref, r + 1, r, t, store)

    @pl.loop(0, per, unroll=2)
    def _(r):
        def store(n, i, value):
            out_ref[n, pl.ds(i * 8 * per + r, 8, stride=per), :] = value

        advance(s_ref, r + 1, r + 1, 0, store)

    for n in range(2):
        block = out_ref[n]
        gram_ref[n] = lax.dot_general(
            block, block, (((0,), (0,)), ((), ())),
            precision=lax.Precision.HIGHEST, preferred_element_type=jnp.float32,
        )


def evolve(order, low, high, right, left, coef, mask, turn):
    count = order.shape[0]
    per = coef.shape[1] - 2
    rows = low.shape[1]
    whole = lambda shape: pl.BlockSpec(shape, lambda i, order: (0,) * len(shape))
    pick = lambda shape, n: pl.BlockSpec((1,) + shape, lambda i, order: (order[2 * i + n], 0, 0))
    layers = [pick((rows, LANES), n) for n in range(2) for _ in range(4)]
    return pl.pallas_call(
        evolve_body,
        grid_spec=pltpu.PrefetchScalarGridSpec(
            num_scalar_prefetch=1,
            grid=(count // 2,),
            in_specs=layers
            + [whole(coef.shape), whole(mask.shape), pick((8, LANES), 0), pick((8, LANES), 1)],
            out_specs=[
                pl.BlockSpec((2, FIELDS * 8 * per, LANES), lambda i, order: (i, 0, 0)),
                pl.BlockSpec((2, LANES, LANES), lambda i, order: (i, 0, 0)),
            ],
            scratch_shapes=[
                pltpu.VMEM((2, FIELDS, per + 2 * RH, 2, 8, LANES), jnp.float32),
                pltpu.VMEM((2, FIELDS, per + 2, 2, 8, LANES), jnp.float32),
            ],
        ),
        out_shape=[
            jax.ShapeDtypeStruct((count, FIELDS * 8 * per, LANES), jnp.float32),
            jax.ShapeDtypeStruct((count, LANES, LANES), jnp.float32),
        ],
        compiler_params=pltpu.CompilerParams(vmem_limit_bytes=VMEM_LIMIT),
        name="evolve",
    )(order, *([low, high, right, left] * 2), coef, mask, turn, turn)


def factor_body(scale, *refs):
    parts = refs[:-2]
    inverse_ref, factor_ref = refs[-2:]
    blocks = LANES // 8
    lane = lax.broadcasted_iota(jnp.int32, (8, LANES), 1)
    sub = lax.broadcasted_iota(jnp.int32, (8, LANES), 0)
    w = []
    for b in range(blocks):
        here = slice(8 * b, 8 * b + 8)
        w.append(sum(ref[here, :] for ref in parts))
    full = lambda v: jnp.broadcast_to(v, (8, LANES))
    for b in range(blocks):
        columns = [[full(w[i][:, 8 * b + k : 8 * b + k + 1]) for k in range(8)] for i in range(b, blocks)]
        rows = [full(w[b][k : k + 1, :]) for k in range(8)]
        a = [[full(columns[0][k][i : i + 1, :]) for k in range(i + 1)] for i in range(8)]
        low = [[None] * 8 for _ in range(8)]
        m = [[None] * 8 for _ in range(8)]
        for j in range(8):
            root = lax.rsqrt(a[j][j])
            root = root * (1.5 - 0.5 * (a[j][j] * root) * root)
            m[j][j] = root
            for i in range(j + 1, 8):
                low[i][j] = a[i][j] * root
            for i in range(j + 1, 8):
                for k in range(j + 1, i + 1):
                    a[i][k] = a[i][k] - low[i][j] * low[k][j]
            for k in range(j):
                total = low[j][k] * m[k][k]
                for n in range(k + 1, j):
                    total = total + low[j][n] * m[n][k]
                m[j][k] = -(total * root)
        inside = (lane >= 8 * b) & (lane < 8 * b + 8)
        ones = [jnp.where(inside, jnp.where(lane == 8 * b + k, 1.0, 0.0), rows[k]) for k in range(8)]
        final = [None] * 8
        upper = None
        lower = None
        for i in range(8):
            top = m[i][0] * rows[0]
            final[i] = m[i][0] * ones[0]
            for k in range(1, i + 1):
                top = top + m[i][k] * rows[k]
                final[i] = final[i] + m[i][k] * ones[k]
            upper = top if i == 0 else jnp.where(sub == i, top, upper)
            lower = final[i] if i == 0 else jnp.where(sub == i, final[i], lower)
        inverse_ref[8 * b : 8 * b + 8, :] = jnp.where(lane <= sub + 8 * b, lower * scale, 0.0)
        factor_ref[8 * b : 8 * b + 8, :] = jnp.where(lane >= sub + 8 * b, upper * (1.0 / scale), 0.0)
        if b + 1 < blocks:
            solved = []
            for k in range(8):
                total = m[k][k] * final[k]
                for i in range(k + 1, 8):
                    total = total + m[i][k] * final[i]
                solved.append(total)
            for i in range(b + 1, blocks):
                c = columns[i - b]
                products = [c[k] * solved[k] for k in range(8)]
                while len(products) > 1:
                    products = [products[n] + products[n + 1] for n in range(0, len(products), 2)]
                w[i] = jnp.where(inside, 0.0, w[i]) - products[0]
    factor_ref[...] = factor_ref[...].T


def factorize(parts, scale):
    vmem = pl.BlockSpec(memory_space=pltpu.VMEM)
    shape = jax.ShapeDtypeStruct((LANES, LANES), jnp.float32)
    return pl.pallas_call(
        partial(factor_body, scale),
        in_specs=[vmem] * len(parts),
        out_specs=[vmem, vmem],
        out_shape=[shape, shape],
        name="factorize",
    )(*parts)


def split(value):
    one = value.astype(jnp.bfloat16)
    rest = value - one.astype(jnp.float32)
    two = rest.astype(jnp.bfloat16)
    three = (rest - two.astype(jnp.float32)).astype(jnp.bfloat16)
    return one, two, three


def apply_body(inverse_ref, columns_ref, out_ref, rows_ref, all_ref):
    per = columns_ref.shape[1] // 8
    one, two, three = split(inverse_ref[...].T)
    main = jnp.concatenate([jnp.concatenate([one, two], axis=1)] * 2, axis=0)
    rest = jnp.concatenate([one, three], axis=0)
    for x in range(8):
        for d in range(F):
            all_ref[x, d * per : (d + 1) * per, :] = columns_ref[d, x * per : (x + 1) * per, :]
    for x in range(8):
        a, b, c = split(all_ref[x])
        wide = jnp.dot(jnp.concatenate([a, b], axis=1), main, preferred_element_type=jnp.float32)
        tail = jnp.dot(jnp.concatenate([c, a], axis=1), rest, preferred_element_type=jnp.float32)
        value = wide[:, :LANES] + (wide[:, LANES:] + tail)
        rows_ref[pl.ds(x, LANES, stride=8), :] = value.T
    out_ref[...] = rows_ref[...].reshape(out_ref.shape)


def apply(inverse, columns):
    per = columns.shape[1] // (8 * FIELDS)
    radial = per * F
    return pl.pallas_call(
        apply_body,
        grid=(FIELDS,),
        in_specs=[
            pl.BlockSpec((LANES, LANES), lambda i: (0, 0)),
            pl.BlockSpec((F, 8 * per, LANES), lambda i: (0, i, 0)),
        ],
        out_specs=pl.BlockSpec((1, LANES, 1, 8, radial), lambda i: (0, 0, i, 0, 0)),
        out_shape=jax.ShapeDtypeStruct((1, LANES, FIELDS, 8, radial), jnp.float32),
        scratch_shapes=[
            pltpu.VMEM((LANES * 8, radial), jnp.float32),
            pltpu.VMEM((8, radial, LANES), jnp.float32),
        ],
        compiler_params=pltpu.CompilerParams(vmem_limit_bytes=VMEM_LIMIT),
        name="apply",
    )(inverse, columns)


def make_table(indices, slots):
    times = jnp.arange(slots, dtype=jnp.int32)
    phases = indices[:, None] * times[None, :] % slots
    angles = phases.astype(jnp.float32) * (2.0 * math.pi / slots)
    return jnp.stack([jnp.cos(angles), -jnp.sin(angles)], axis=1)


def stencil(coupling, velocity, per):
    count = lax.axis_size("space")
    mine = lax.axis_index("space")
    start = lax.axis_index("freq") * per
    radial = velocity.shape[1]
    up = [(i, i + 1) for i in range(count - 1)]
    down = [(i + 1, i) for i in range(count - 1)]
    both = jnp.concatenate([coupling.reshape(FIELDS * FIELDS, 8, radial), velocity[None]], axis=0)
    right = lax.ppermute(both[:, :2], "space", down)
    left = lax.ppermute(both[:, 6:], "space", up)
    gap = jnp.zeros((both.shape[0], 4, radial), jnp.float32)
    full = jnp.concatenate([both, right, gap, left], axis=1)
    full = jnp.pad(full, ((0, 0), (0, 0), (1, 1)))
    full = lax.dynamic_slice_in_dim(full, start, per + 2, axis=2).transpose(0, 2, 1)
    speed = full[FIELDS * FIELDS]
    coupled = STEP_DT * full[: FIELDS * FIELDS]
    centre = 1.0 - STEP_DT * VISCOSITY * (30.0 / 12.0 + 2.0)
    diagonal = jnp.eye(FIELDS, dtype=jnp.float32).reshape(-1) * centre
    coupled = coupled + diagonal[:, None, None]
    near_d, near_c = STEP_DT * 8.0 / 12.0, STEP_DT * VISCOSITY * 16.0 / 12.0
    far_d, far_c = STEP_DT / 12.0, STEP_DT * VISCOSITY / 12.0
    shifts = jnp.stack(
        [near_d * speed + near_c, near_c - near_d * speed, -far_d * speed - far_c, far_d * speed - far_c]
    )
    coef = jnp.concatenate([coupled, shifts], axis=0)
    coef = jnp.broadcast_to(coef.reshape(-1, per + 2, 2, 8)[..., None], (coef.shape[0], per + 2, 2, 8, LANES))
    r = start - 1 + jnp.arange(per + 2)
    place = jnp.arange(16)
    inside = (place < 8) | ((place < 12) & (mine < count - 1)) | ((place >= 12) & (mine > 0))
    mask = ((r >= 0) & (r < radial))[:, None] & inside[None, :]
    mask = mask.astype(jnp.float32).reshape(per + 2, 2, 8)
    mask = jnp.broadcast_to(mask[..., None], mask.shape + (LANES,))
    return coef, mask


def local(sketch, coupling, velocity, freq_index):
    groups = lax.axis_size("freq")
    count = lax.axis_size("space")
    radial = sketch.shape[4]
    per = radial // groups
    mine = lax.axis_index("freq")

    rows = spread(sketch, groups)
    coupling, velocity, rows = lax.optimization_barrier((coupling, velocity, rows))
    rows = lax.all_to_all(rows, "freq", split_axis=0, concat_axis=0, tiled=True)

    parity = freq_index % 2
    waves = make_table(freq_index, NT)[:, :, : NT // 2].reshape(F, 2, 4, 2)
    waves = jnp.repeat(waves, K, axis=3)
    angular = math.pi / NT * STEP_DT * freq_index.astype(jnp.float32)
    sign = jnp.where(jnp.arange(LANES) < K, 1.0, -1.0).astype(jnp.float32)
    turn = jnp.broadcast_to((angular[:, None] * sign)[:, None, :], (F, 8, LANES))
    coef, mask = stencil(coupling, velocity, per)

    right = lax.ppermute(rows[:, 0], "space", [(i + 1, i) for i in range(count - 1)])
    left = lax.ppermute(rows[:, 1], "space", [(i, i + 1) for i in range(count - 1)])
    low, high = fourier(parity, rows, 0, waves), fourier(parity, rows, 1, waves)
    right, left = fourier(parity, right[:, None], 0, waves), fourier(parity, left[:, None], 0, waves)

    columns, grams = evolve(jnp.arange(F, dtype=jnp.int32), low, high, right, left, coef, mask, turn)
    parts = lax.all_to_all(grams, "freq", split_axis=0, concat_axis=0, tiled=True)
    gram = jnp.sum(parts, axis=0)
    columns, gram = lax.optimization_barrier((columns, gram))
    columns = lax.all_to_all(columns, "freq", split_axis=0, concat_axis=0, tiled=True)
    for bit in (0, 2, 4):
        parts = quad_sum(gram, "space", bit)
        gram = sum(parts)
    row_scale = math.sqrt(FIELDS * 8 * count * radial)
    inverse, factor = factorize(parts, row_scale)
    return apply(inverse, columns), factor[None]


def solution(mesh):
    return jax.shard_map(
        local,
        mesh=mesh,
        in_specs=(
            P("freq", None, None, "space", None),
            P(None, None, "space", None),
            P("space", None),
            P(),
        ),
        out_specs=(P("freq", None, None, "space", None), P("freq", None, None)),
        check_vma=False,
    )
```

time: 262 us -> 202 us (0.77)
  starting transfers between devices: 88.4 us -> 58.2 us
  other arithmetic: 29.8 us -> 2.8 us
  local copies, waits for them, and re-layouts: 10.4 us -> 23.5 us
  waiting for transfers between devices: 63.6 us -> 52.2 us
  Pallas kernels: 52.4 us -> 42.4 us
  blocking collectives: 14.8 us -> 18.1 us
    ppermute x15 -> x11, starting transfers between devices: 70.5 us -> 40 us  [the longest x9 33.7 us: quad_sum(): lax.ppermute(value, axis, [(i, i ^ m) for i in range(count)])]
    another operation x4 -> x0, other arithmetic: 22.2 us -> none  [the longest x3 12.4 us: local(): chol = jnp.linalg.cholesky(gram)]
    ppermute x15 -> x11, waiting for transfers between devices: 34.8 us -> 14.2 us  [the longest x9 14.2 us: quad_sum(): lax.ppermute(value, axis, [(i, i ^ m) for i in range(count)])]
    pallas_call x2 -> x7, Pallas kernels: 49.3 us -> 39.3 us  [the longest x1 19.7 us: evolve(): pl.pallas_call(evolve_body, grid_spec=pltpu.PrefetchScalarGridSpec(num_sc...]
    all_to_all x2, waiting for transfers between devices: 28.8 us -> 38 us  [the longest x1 33.1 us: local(): rows = lax.all_to_all(rows, 'freq', split_axis=0, concat_axis=0, tiled=True)]
    unnamed x4 -> x0, other arithmetic: 4.66 us -> none
    sub x0 -> x3, local copies, waits for them, and re-layouts: none -> 3.32 us  [the longest x1 1.11 us: stencil(): far_d * speed - far_c]
    all_to_all x1, blocking collectives: 14.8 us -> 18.1 us  [local(): lax.all_to_all(grams, 'freq', split_axis=0, concat_axis=0, tiled=True)]
  transfers between devices with their start and end apart: 19 -> 15, of which waited for: 10 -> 6; matrix products, arithmetic and copies ran while one was open for 13% -> 9% of each run, Pallas kernels for 0% -> 7%
where the time goes in v3:
time: 202 us; the launch traced here: 198 us
  starting transfers between devices  58.2 us (29%)
  waiting for transfers between devices  52.2 us (26%)
  Pallas kernels  42.4 us (21%)
  local copies, waits for them, and re-layouts  23.5 us (12%)
  blocking collectives  18.1 us (9%)
  other arithmetic  2.8 us (1%)
    ppermute x9, starting transfers between devices, quad_sum(): lax.ppermute(value, axis, [(i, i ^ m) for i in range(count)])  33.7 us
    all_to_all x1, waiting for transfers between devices, local(): rows = lax.all_to_all(rows, 'freq', split_axis=0, concat_axis=0, tiled=True)  33.1 us
    pallas_call x1, Pallas kernels, evolve(): pl.pallas_call(evolve_body, grid_spec=pltpu.PrefetchScalarGridSpec(num_sc...  19.7 us
    all_to_all x1, blocking collectives, local(): lax.all_to_all(grams, 'freq', split_axis=0, concat_axis=0, tiled=True)  18.1 us
    ppermute x9, waiting for transfers between devices, quad_sum(): lax.ppermute(value, axis, [(i, i ^ m) for i in range(count)])  14.2 us
    all_to_all x1, starting transfers between devices, local(): rows = lax.all_to_all(rows, 'freq', split_axis=0, concat_axis=0, tiled=True)  7.78 us
    pallas_call x1, Pallas kernels, factorize(): pl.pallas_call(partial(factor_body, scale), in_specs=[vmem] * len(parts),...  7.69 us
    pallas_call x4, Pallas kernels, fourier(): pl.pallas_call(fourier_body, grid=(1,), in_specs=[pl.BlockSpec(memory_spa...  7.58 us
  transfers between devices with their start and end apart: 15, of which 6 were waited for; matrix products, arithmetic and copies ran while one was open for 9% of the time, Pallas kernels for 7%

profile of v3, /device:TPU:1, one launch (start us, length us, event | category | flops | bytes accessed | tf_op | source)
XLA Modules:
  0.0 198.2 jit_solution(14698013947935550788)
XLA Ops:
  0.6 1.3 copy-done.2
  1.9 3.1 %spread.1 = bf16[8,2,400,128]{3,2,1,0:T(8,128)(2,1)} custom-call(bf16[2,64,5,8,128]{4,3,2,1,0:T(8,128)(2,1)S(1)} %copy-done.2), custom_call_target="tpu_custom_call" | custom-call | tf_op jit(solution)/shard_map/spread/pallas_call | solution.py:51
  5.0 7.8 %all-to-all-start = ((bf16[8,2,400,128]{3,2,1,0:T(8,128)(2,1)}), bf16[8,2,400,128]{3,2,1,0:T(8,128)(2,1)S(1)}, u32[]{:S(2)}, u32[]{:S(2)}) async-start(bf16[8,2,400,128]{3,2,1,0:T(8,128)(2,1)} %spread.1), calls=%async_computation | async-start | bytes 3276800 | tf_op jit(solution)/shard_map/all_to_all | solution.py:379
  12.9 4.7 %collective-permute-start.2 = (f32[26,2,128]{2,1,0:T(2,128)S(1)}, f32[26,2,128]{2,1,0:T(2,128)S(1)}, u32[]{:S(2)}, u32[]{:S(2)}) collective-permute-start(f32[26,2,128]{2,1,0:T(2,128)S(1)} %get-tuple-element.26), channel_id=1, source_target_pairs={{8,0},{16,8},{24,16},{32,24},{40,32},{48,40},{56,48},{64,56},{72,6... | collective-permute-start | bytes 79880 | tf_op jit(solution)/shard_map/ppermute | solution.py:343
  17.6 2.0 %collective-permute-start.3 = (f32[26,2,128]{2,1,0:T(2,128)S(1)}, f32[26,2,128]{2,1,0:T(2,128)}, u32[]{:S(2)}, u32[]{:S(2)}) collective-permute-start(f32[26,2,128]{2,1,0:T(2,128)S(1)} %get-tuple-element.27), channel_id=1, source_target_pairs={{0,8},{8,16},{16,24},{24,32},{32,40},{40,48},{48,56},{56,64},{64,7... | collective-permute-start | bytes 79880 | tf_op jit(solution)/shard_map/ppermute | solution.py:344
  21.6 33.1 %all-to-all-done.rows_ref = bf16[8,2,400,128]{3,2,1,0:T(8,128)(2,1)S(1)} async-done(((bf16[8,2,400,128]{3,2,1,0:T(8,128)(2,1)}), bf16[8,2,400,128]{3,2,1,0:T(8,128)(2,1)S(1)}, u32[]{:S(2)}, u32[]{:S(2)}) %all-to-all-start) | async-done | bytes 1638432 | tf_op jit(solution)/shard_map/all_to_all | solution.py:379
  54.7 1.3 slice_bitcast_fusion
  55.9 4.4 %collective-permute-start.1 = (bf16[8,400,128]{2,1,0:T(8,128)(2,1)}, bf16[8,400,128]{2,1,0:T(8,128)(2,1)S(1)}, u32[]{:S(2)}, u32[]{:S(2)}) collective-permute-start(bf16[8,400,128]{2,1,0:T(8,128)(2,1)} %get-tuple-element.20), channel_id=1, source_target_pairs={{0,8},{8,16},{16,24},{24,32},{32,40},{40,48},{48,56},{56,64},{64,7... | collective-permute-start | bytes 2457608 | tf_op jit(solution)/shard_map/ppermute | solution.py:390
  60.3 1.9 collective-permute-start
  62.9 0.8 pad_maximum_fusion
  63.7 1.4 copy.69
  65.2 0.9 fusion
  66.1 0.9 multiply_add_fusion
  67.0 1.1 copy.73
  68.1 1.1 copy.72
  69.2 1.1 copy.71
  70.3 1.1 copy.70
  71.4 0.9 copy.74
  72.3 0.9 copy.75
  73.2 0.9 copy.76
  74.0 0.9 copy.77
  75.5 1.4 concatenate.27
  77.0 1.1 copy.78
  78.1 1.9 fourier.5.refs_1_.refs_5_
  80.0 1.9 fourier.4.refs_0_.refs_4_
  81.9 1.9 fourier.7.refs_3_.refs_7_
  83.8 1.2 copy-done
  85.0 1.9 fourier.6.refs_2_.refs_6_
  87.0 3.2 %broadcast_in_dim.57.refs_8_ = f32[29,18,2,8,128]{4,3,2,1,0:T(8,128)} broadcast(f32[29,18,2,8]{3,2,1,0:T(2,128)S(1)} %copy-done.4), dimensions={0,1,2,3} | broadcast | bytes 4309632 | tf_op jit(solution)/shard_map/broadcast_in_dim | solution.py:360
  90.2 19.7 %evolve.1 = (f32[8,640,128]{2,1,0:T(8,128)}, f32[8,128,128]{2,1,0:T(8,128)S(1)}) custom-call(s32[8]{0:T(128)S(1)} %iota.73.order_ref, f32[8,400,128]{2,1,0:T(8,128)S(1)} %fourier.4.refs_0_.refs_4_, f32[8,400,128]{2,1,0:T(8,128)S(1)} %fourier.5.refs_1_.refs_5_, f32[8,400,128]{2,1,0:T(8,128)} %copy-done.1, f32[8,400,128]{2,1,0:T(8,128)} %copy-done, ...), custom_call_target="tpu_custom_call" | custom-call | tf_op jit(solution)/shard_map/evolve/pallas_call | solution.py:183
  109.9 18.1 %all_to_all.15 = f32[8,128,128]{2,1,0:T(8,128)S(1)} all-to-all(f32[8,128,128]{2,1,0:T(8,128)S(1)} %get-tuple-element.15), channel_id=1, replica_groups=mesh['space'=64,'freq'=8] {'freq'}, dimensions={0} | all-to-all | bytes 1048576 | tf_op jit(solution)/shard_map/all_to_all | solution.py:395
  128.0 3.6 %all-to-all-start.2 = ((f32[8,640,128]{2,1,0:T(8,128)}), f32[8,640,128]{2,1,0:T(8,128)S(1)}, u32[]{:S(2)}, u32[]{:S(2)}) async-start(f32[8,640,128]{2,1,0:T(8,128)} %get-tuple-element.18), calls=%async_computation.2 | async-start | bytes 5242880 | tf_op jit(solution)/shard_map/all_to_all | solution.py:398
  131.6 1.9 collective-permute-start.6
  133.6 6.7 %collective-permute-start.5 = (f32[128,128]{1,0:T(8,128)S(1)}, f32[128,128]{1,0:T(8,128)S(1)}, u32[]{:S(2)}, u32[]{:S(2)}) collective-permute-start(f32[128,128]{1,0:T(8,128)S(1)} %reduce_sum.9), channel_id=1, source_target_pairs={{0,24},{8,16},{16,8},{24,0},{32,56},{40,48},{48,40},{56,32},{64,88... | collective-permute-start | bytes 196616 | tf_op jit(solution)/shard_map/ppermute | solution.py:26
  140.3 2.0 collective-permute-start.4
  143.0 2.7 %collective-permute-done.4 = f32[128,128]{1,0:T(8,128)S(1)} collective-permute-done((f32[128,128]{1,0:T(8,128)S(1)}, f32[128,128]{1,0:T(8,128)S(1)}, u32[]{:S(2)}, u32[]{:S(2)}) %collective-permute-start.4) | collective-permute-done | bytes 65568 | tf_op jit(solution)/shard_map/ppermute | solution.py:26
  145.7 6.0 %collective-permute-start.9 = (f32[128,128]{1,0:T(8,128)S(1)}, f32[128,128]{1,0:T(8,128)S(1)}, u32[]{:S(2)}, u32[]{:S(2)}) collective-permute-start(f32[128,128]{1,0:T(8,128)S(1)} %add_add_fusion.1), channel_id=1, source_target_pairs={{0,32},{8,40},{16,48},{24,56},{32,0},{40,8},{48,16},{56,24},{64,96... | collective-permute-start | bytes 196616 | tf_op jit(solution)/shard_map/ppermute | solution.py:26
  151.7 4.9 %collective-permute-start.8 = (f32[128,128]{1,0:T(8,128)S(1)}, f32[128,128]{1,0:T(8,128)S(1)}, u32[]{:S(2)}, u32[]{:S(2)}) collective-permute-start(f32[128,128]{1,0:T(8,128)S(1)} %add_add_fusion.1), channel_id=1, source_target_pairs={{0,96},{8,104},{16,112},{24,120},{32,64},{40,72},{48,80},{56,88},{... | collective-permute-start | bytes 196616 | tf_op jit(solution)/shard_map/ppermute | solution.py:26
  156.6 2.7 %collective-permute-start.7 = (f32[128,128]{1,0:T(8,128)S(1)}, f32[128,128]{1,0:T(8,128)S(1)}, u32[]{:S(2)}, u32[]{:S(2)}) collective-permute-start(f32[128,128]{1,0:T(8,128)S(1)} %add_add_fusion.1), channel_id=1, source_target_pairs={{0,64},{8,72},{16,80},{24,88},{32,96},{40,104},{48,112},{56,120},{... | collective-permute-start | bytes 196616 | tf_op jit(solution)/shard_map/ppermute | solution.py:26
  159.3 6.7 %collective-permute-done.7 = f32[128,128]{1,0:T(8,128)S(1)} collective-permute-done((f32[128,128]{1,0:T(8,128)S(1)}, f32[128,128]{1,0:T(8,128)S(1)}, u32[]{:S(2)}, u32[]{:S(2)}) %collective-permute-start.7) | collective-permute-done | bytes 65568 | tf_op jit(solution)/shard_map/ppermute | solution.py:26
  166.1 3.1 %collective-permute-start.12 = (f32[128,128]{1,0:T(8,128)S(1)}, f32[128,128]{1,0:T(8,128)S(1)}, u32[]{:S(2)}, u32[]{:S(2)}) collective-permute-start(f32[128,128]{1,0:T(8,128)S(1)} %add_add_fusion.refs_0_), channel_id=1, source_target_pairs={{0,128},{8,136},{16,144},{24,152},{32,160},{40,168},{48,176},{56,1... | collective-permute-start | bytes 196616 | tf_op jit(solution)/shard_map/ppermute | solution.py:26
  169.2 3.7 %collective-permute-start.11 = (f32[128,128]{1,0:T(8,128)S(1)}, f32[128,128]{1,0:T(8,128)S(1)}, u32[]{:S(2)}, u32[]{:S(2)}) collective-permute-start(f32[128,128]{1,0:T(8,128)S(1)} %add_add_fusion.refs_0_), channel_id=1, source_target_pairs={{0,384},{8,392},{16,400},{24,408},{32,416},{40,424},{48,432},{56,4... | collective-permute-start | bytes 196616 | tf_op jit(solution)/shard_map/ppermute | solution.py:26
  172.9 2.6 %collective-permute-start.10 = (f32[128,128]{1,0:T(8,128)S(1)}, f32[128,128]{1,0:T(8,128)S(1)}, u32[]{:S(2)}, u32[]{:S(2)}) collective-permute-start(f32[128,128]{1,0:T(8,128)S(1)} %add_add_fusion.refs_0_), channel_id=1, source_target_pairs={{0,256},{8,264},{16,272},{24,280},{32,288},{40,296},{48,304},{56,3... | collective-permute-start | bytes 196616 | tf_op jit(solution)/shard_map/ppermute | solution.py:26
  175.6 4.1 %collective-permute-done.10.refs_1_ = f32[128,128]{1,0:T(8,128)S(1)} collective-permute-done((f32[128,128]{1,0:T(8,128)S(1)}, f32[128,128]{1,0:T(8,128)S(1)}, u32[]{:S(2)}, u32[]{:S(2)}) %collective-permute-start.10) | collective-permute-done | bytes 65568 | tf_op jit(solution)/shard_map/ppermute | solution.py:26
  180.4 7.7 %factorize.1 = (f32[128,128]{1,0:T(8,128)}, f32[128,128]{1,0:T(8,128)}) custom-call(f32[128,128]{1,0:T(8,128)} %copy-done.7, f32[128,128]{1,0:T(8,128)} %copy-done.10, f32[128,128]{1,0:T(8,128)} %copy-done.9, f32[128,128]{1,0:T(8,128)} %copy-done.8), custom_call_target="tpu_custom_call" | custom-call | tf_op jit(solution)/shard_map/factorize/pallas_call | solution.py:273
  188.1 4.9 %all-to-all-done.2.columns_ref = f32[8,640,128]{2,1,0:T(8,128)S(1)} async-done(((f32[8,640,128]{2,1,0:T(8,128)}), f32[8,640,128]{2,1,0:T(8,128)S(1)}, u32[]{:S(2)}, u32[]{:S(2)}) %all-to-all-start.2) | async-done | bytes 2621472 | tf_op jit(solution)/shard_map/all_to_all | solution.py:398
  193.0 0.8 copy-done.3
  193.8 4.4 %apply.1 = f32[1,128,5,8,128]{4,3,2,1,0:T(8,128)} custom-call(f32[128,128]{1,0:T(8,128)S(1)} %copy-done.3, f32[8,640,128]{2,1,0:T(8,128)S(1)} %all-to-all-done.2.columns_ref), custom_call_target="tpu_custom_call" | custom-call | tf_op jit(solution)/shard_map/apply/pallas_call | solution.py:310
  (63 shorter events, 4.7 us)
Async XLA Ops:
  0.6 1.3 copy-start.2
  5.0 7.8 %copy-start.5 = (f32[5,5,8,128]{3,2,1,0:T(8,128)S(1)}, f32[5,5,8,128]{3,2,1,0:T(8,128)}, u32[]{:S(2)}) copy-start(f32[5,5,8,128]{3,2,1,0:T(8,128)} %param.5) | copy-start | bytes 307204
  5.0 7.8 %copy-start.12 = (f32[8,128]{1,0:T(8,128)S(1)}, f32[8,128]{1,0:T(8,128)}, u32[]{:S(2)}) copy-start(f32[8,128]{1,0:T(8,128)} %param.6) | copy-start | bytes 12292
  5.0 15.2 %copy-start.15 = (s32[8]{0:T(128)S(1)}, s32[8]{0:T(128)}, u32[]{:S(2)}) copy-start(s32[8]{0:T(128)} %param.7) | copy-start | bytes 100
  5.0 49.6 %all-to-all-start = ((bf16[8,2,400,128]{3,2,1,0:T(8,128)(2,1)}), bf16[8,2,400,128]{3,2,1,0:T(8,128)(2,1)S(1)}, u32[]{:S(2)}, u32[]{:S(2)}) async-start(bf16[8,2,400,128]{3,2,1,0:T(8,128)(2,1)} %spread.1), calls=%async_computation | async-start | bytes 3276800 | tf_op jit(solution)/shard_map/all_to_all | solution.py:379
  12.9 49.4 %collective-permute-start.2 = (f32[26,2,128]{2,1,0:T(2,128)S(1)}, f32[26,2,128]{2,1,0:T(2,128)S(1)}, u32[]{:S(2)}, u32[]{:S(2)}) collective-permute-start(f32[26,2,128]{2,1,0:T(2,128)S(1)} %get-tuple-element.26), channel_id=1, source_target_pairs={{8,0},{16,8},{24,16},{32,24},{40,32},{48,40},{56,48},{64,56},{72,6... | collective-permute-start | bytes 79880 | tf_op jit(solution)/shard_map/ppermute | solution.py:343
  17.6 45.3 %collective-permute-start.3 = (f32[26,2,128]{2,1,0:T(2,128)S(1)}, f32[26,2,128]{2,1,0:T(2,128)}, u32[]{:S(2)}, u32[]{:S(2)}) collective-permute-start(f32[26,2,128]{2,1,0:T(2,128)S(1)} %get-tuple-element.27), channel_id=1, source_target_pairs={{0,8},{8,16},{16,24},{24,32},{32,40},{40,48},{48,56},{56,64},{64,7... | collective-permute-start | bytes 79880 | tf_op jit(solution)/shard_map/ppermute | solution.py:344
  54.7 8.2 %copy-start.6 = (f32[5,5,8,128]{3,2,1,0:T(8,128)S(1)}, f32[5,5,8,128]{3,2,1,0:T(8,128)}, u32[]{:S(2)}) copy-start(f32[5,5,8,128]{3,2,1,0:T(8,128)} %param.5) | copy-start | bytes 307204
  54.7 8.2 %copy-start.14 = (f32[16]{0:T(128)S(1)}, f32[16]{0:T(128)}, u32[]{:S(2)}) copy-start(f32[16]{0:T(128)} %pad.8.clone) | copy-start | bytes 196
  55.9 26.0 %collective-permute-start.1 = (bf16[8,400,128]{2,1,0:T(8,128)(2,1)}, bf16[8,400,128]{2,1,0:T(8,128)(2,1)S(1)}, u32[]{:S(2)}, u32[]{:S(2)}) collective-permute-start(bf16[8,400,128]{2,1,0:T(8,128)(2,1)} %get-tuple-element.20), channel_id=1, source_target_pairs={{0,8},{8,16},{16,24},{24,32},{32,40},{40,48},{48,56},{56,64},{64,7... | collective-permute-start | bytes 2457608 | tf_op jit(solution)/shard_map/ppermute | solution.py:390
  60.3 24.7 %collective-permute-start = (bf16[8,400,128]{2,1,0:T(8,128)(2,1)}, bf16[8,400,128]{2,1,0:T(8,128)(2,1)S(1)}, u32[]{:S(2)}, u32[]{:S(2)}) collective-permute-start(bf16[8,400,128]{2,1,0:T(8,128)(2,1)} %get-tuple-element.21), channel_id=1, source_target_pairs={{8,0},{16,8},{24,16},{32,24},{40,32},{48,40},{56,48},{64,56},{72,6... | collective-permute-start | bytes 2457608 | tf_op jit(solution)/shard_map/ppermute | solution.py:389
  62.3 0.6 copy-start.11
  65.2 9.7 %copy-start.13 = (f32[25]{0:T(128)S(1)}, f32[25]{0:T(128)}, u32[]{:S(2)}) copy-start(f32[25]{0:T(128)} %mul.105) | copy-start | bytes 304
  83.8 1.2 copy-start
  85.0 2.0 %copy-start.4 = (f32[29,18,2,8]{3,2,1,0:T(2,128)S(1)}, f32[29,18,2,8]{3,2,1,0:T(2,128)}, u32[]{:S(2)}) copy-start(f32[29,18,2,8]{3,2,1,0:T(2,128)} %copy.78) | copy-start | bytes 100228
  86.9 3.3 %copy-start.1 = (f32[8,400,128]{2,1,0:T(8,128)}, f32[8,400,128]{2,1,0:T(8,128)S(1)}, u32[]{:S(2)}) copy-start(f32[8,400,128]{2,1,0:T(8,128)S(1)} %fourier.6.refs_2_.refs_6_) | copy-start | bytes 4915204
  128.0 65.0 %all-to-all-start.2 = ((f32[8,640,128]{2,1,0:T(8,128)}), f32[8,640,128]{2,1,0:T(8,128)S(1)}, u32[]{:S(2)}, u32[]{:S(2)}) async-start(f32[8,640,128]{2,1,0:T(8,128)} %get-tuple-element.18), calls=%async_computation.2 | async-start | bytes 5242880 | tf_op jit(solution)/shard_map/all_to_all | solution.py:398
  131.6 10.7 %collective-permute-start.6 = (f32[128,128]{1,0:T(8,128)S(1)}, f32[128,128]{1,0:T(8,128)S(1)}, u32[]{:S(2)}, u32[]{:S(2)}) collective-permute-start(f32[128,128]{1,0:T(8,128)S(1)} %reduce_sum.9), channel_id=1, source_target_pairs={{0,8},{8,0},{16,24},{24,16},{32,40},{40,32},{48,56},{56,48},{64,72... | collective-permute-start | bytes 196616 | tf_op jit(solution)/shard_map/ppermute | solution.py:26
  133.6 9.4 %collective-permute-start.5 = (f32[128,128]{1,0:T(8,128)S(1)}, f32[128,128]{1,0:T(8,128)S(1)}, u32[]{:S(2)}, u32[]{:S(2)}) collective-permute-start(f32[128,128]{1,0:T(8,128)S(1)} %reduce_sum.9), channel_id=1, source_target_pairs={{0,24},{8,16},{16,8},{24,0},{32,56},{40,48},{48,40},{56,32},{64,88... | collective-permute-start | bytes 196616 | tf_op jit(solution)/shard_map/ppermute | solution.py:26
  140.3 5.3 %collective-permute-start.4 = (f32[128,128]{1,0:T(8,128)S(1)}, f32[128,128]{1,0:T(8,128)S(1)}, u32[]{:S(2)}, u32[]{:S(2)}) collective-permute-start(f32[128,128]{1,0:T(8,128)S(1)} %reduce_sum.9), channel_id=1, source_target_pairs={{0,16},{8,24},{16,0},{24,8},{32,48},{40,56},{48,32},{56,40},{64,80... | collective-permute-start | bytes 196616 | tf_op jit(solution)/shard_map/ppermute | solution.py:26
  145.7 13.6 %collective-permute-start.9 = (f32[128,128]{1,0:T(8,128)S(1)}, f32[128,128]{1,0:T(8,128)S(1)}, u32[]{:S(2)}, u32[]{:S(2)}) collective-permute-start(f32[128,128]{1,0:T(8,128)S(1)} %add_add_fusion.1), channel_id=1, source_target_pairs={{0,32},{8,40},{16,48},{24,56},{32,0},{40,8},{48,16},{56,24},{64,96... | collective-permute-start | bytes 196616 | tf_op jit(solution)/shard_map/ppermute | solution.py:26
  151.7 7.6 %collective-permute-start.8 = (f32[128,128]{1,0:T(8,128)S(1)}, f32[128,128]{1,0:T(8,128)S(1)}, u32[]{:S(2)}, u32[]{:S(2)}) collective-permute-start(f32[128,128]{1,0:T(8,128)S(1)} %add_add_fusion.1), channel_id=1, source_target_pairs={{0,96},{8,104},{16,112},{24,120},{32,64},{40,72},{48,80},{56,88},{... | collective-permute-start | bytes 196616 | tf_op jit(solution)/shard_map/ppermute | solution.py:26
  156.6 9.4 %collective-permute-start.7 = (f32[128,128]{1,0:T(8,128)S(1)}, f32[128,128]{1,0:T(8,128)S(1)}, u32[]{:S(2)}, u32[]{:S(2)}) collective-permute-start(f32[128,128]{1,0:T(8,128)S(1)} %add_add_fusion.1), channel_id=1, source_target_pairs={{0,64},{8,72},{16,80},{24,88},{32,96},{40,104},{48,112},{56,120},{... | collective-permute-start | bytes 196616 | tf_op jit(solution)/shard_map/ppermute | solution.py:26
  166.1 13.7 %copy-start.7 = (f32[128,128]{1,0:T(8,128)}, f32[128,128]{1,0:T(8,128)S(1)}, u32[]{:S(2)}) copy-start(f32[128,128]{1,0:T(8,128)S(1)} %add_add_fusion.refs_0_) | copy-start | bytes 196612
  166.1 9.5 %collective-permute-start.12 = (f32[128,128]{1,0:T(8,128)S(1)}, f32[128,128]{1,0:T(8,128)S(1)}, u32[]{:S(2)}, u32[]{:S(2)}) collective-permute-start(f32[128,128]{1,0:T(8,128)S(1)} %add_add_fusion.refs_0_), channel_id=1, source_target_pairs={{0,128},{8,136},{16,144},{24,152},{32,160},{40,168},{48,176},{56,1... | collective-permute-start | bytes 196616 | tf_op jit(solution)/shard_map/ppermute | solution.py:26
  169.2 6.4 %collective-permute-start.11 = (f32[128,128]{1,0:T(8,128)S(1)}, f32[128,128]{1,0:T(8,128)S(1)}, u32[]{:S(2)}, u32[]{:S(2)}) collective-permute-start(f32[128,128]{1,0:T(8,128)S(1)} %add_add_fusion.refs_0_), channel_id=1, source_target_pairs={{0,384},{8,392},{16,400},{24,408},{32,416},{40,424},{48,432},{56,4... | collective-permute-start | bytes 196616 | tf_op jit(solution)/shard_map/ppermute | solution.py:26
  172.9 6.8 %collective-permute-start.10 = (f32[128,128]{1,0:T(8,128)S(1)}, f32[128,128]{1,0:T(8,128)S(1)}, u32[]{:S(2)}, u32[]{:S(2)}) collective-permute-start(f32[128,128]{1,0:T(8,128)S(1)} %add_add_fusion.refs_0_), channel_id=1, source_target_pairs={{0,256},{8,264},{16,272},{24,280},{32,288},{40,296},{48,304},{56,3... | collective-permute-start | bytes 196616 | tf_op jit(solution)/shard_map/ppermute | solution.py:26
  175.6 4.2 %copy-start.8 = (f32[128,128]{1,0:T(8,128)}, f32[128,128]{1,0:T(8,128)S(1)}, u32[]{:S(2)}) copy-start(f32[128,128]{1,0:T(8,128)S(1)} %collective-permute-done.12.refs_3_) | copy-start | bytes 196612
  175.6 4.1 %copy-start.9 = (f32[128,128]{1,0:T(8,128)}, f32[128,128]{1,0:T(8,128)S(1)}, u32[]{:S(2)}) copy-start(f32[128,128]{1,0:T(8,128)S(1)} %collective-permute-done.11.refs_2_) | copy-start | bytes 196612
  179.8 0.6 copy-start.10
  193.0 0.8 copy-start.3

commit v4 on v3

--- a/solution.py
+++ b/solution.py
@@ -105,6 +105,28 @@
     )(parity, rows, table)
 
 
+def pack(gram, ref, n):
+    line = lax.broadcasted_iota(jnp.int32, (K, LANES), 0)
+    lane = lax.broadcasted_iota(jnp.int32, (K, LANES), 1)
+    last = pltpu.roll(gram[K:], K, 1)
+    ref[n, 0:K, :] = jnp.where(lane >= line, gram[:K], last)
+    diagonal = jnp.sum(jnp.where(lane == line, last, 0.0), axis=0, keepdims=True)
+    ref[n, K : K + 8, :] = jnp.broadcast_to(diagonal, (8, LANES))
+
+
+def unpack(packed):
+    line = lax.broadcasted_iota(jnp.int32, (K, LANES), 0)
+    lane = lax.broadcasted_iota(jnp.int32, (K, LANES), 1)
+    top = packed[:K]
+    last = pltpu.roll(jnp.where(lane < line, top, 0.0), K, 1)
+    half = jnp.concatenate([jnp.where(lane >= line, top, 0.0), last], axis=0)
+    diagonal = pltpu.roll(packed[K : K + 8], K, 1)
+    diagonal = jnp.concatenate([top] + [diagonal] * (K // 8), axis=0)
+    line = lax.broadcasted_iota(jnp.int32, (LANES, LANES), 0)
+    lane = lax.broadcasted_iota(jnp.int32, (LANES, LANES), 1)
+    return jnp.where(line == lane, diagonal, half + half.T)
+
+
 def evolve_body(order_ref, *refs):
     layers, (coef_ref, mask_ref, turn_a, turn_b, out_ref, gram_ref, z_ref, s_ref) = refs[:8], refs[8:]
     wide = z_ref.shape[2]
@@ -167,10 +189,11 @@
 
     for n in range(2):
         block = out_ref[n]
-        gram_ref[n] = lax.dot_general(
+        gram = lax.dot_general(
             block, block, (((0,), (0,)), ((), ())),
             precision=lax.Precision.HIGHEST, preferred_element_type=jnp.float32,
         )
+        pack(gram, gram_ref, n)
 
 
 def evolve(order, low, high, right, left, coef, mask, turn):
@@ -189,7 +212,7 @@
             + [whole(coef.shape), whole(mask.shape), pick((8, LANES), 0), pick((8, LANES), 1)],
             out_specs=[
                 pl.BlockSpec((2, FIELDS * 8 * per, LANES), lambda i, order: (i, 0, 0)),
-                pl.BlockSpec((2, LANES, LANES), lambda i, order: (i, 0, 0)),
+                pl.BlockSpec((2, K + 8, LANES), lambda i, order: (i, 0, 0)),
             ],
             scratch_shapes=[
                 pltpu.VMEM((2, FIELDS, per + 2 * RH, 2, 8, LANES), jnp.float32),
@@ -198,7 +221,7 @@
         ),
         out_shape=[
             jax.ShapeDtypeStruct((count, FIELDS * 8 * per, LANES), jnp.float32),
-            jax.ShapeDtypeStruct((count, LANES, LANES), jnp.float32),
+            jax.ShapeDtypeStruct((count, K + 8, LANES), jnp.float32),
         ],
         compiler_params=pltpu.CompilerParams(vmem_limit_bytes=VMEM_LIMIT),
         name="evolve",
@@ -211,10 +234,8 @@
     blocks = LANES // 8
     lane = lax.broadcasted_iota(jnp.int32, (8, LANES), 1)
     sub = lax.broadcasted_iota(jnp.int32, (8, LANES), 0)
-    w = []
-    for b in range(blocks):
-        here = slice(8 * b, 8 * b + 8)
-        w.append(sum(ref[here, :] for ref in parts))
+    gram = unpack(sum(ref[...] for ref in parts))
+    w = [gram[8 * b : 8 * b + 8] for b in range(blocks)]
     full = lambda v: jnp.broadcast_to(v, (8, LANES))
     for b in range(blocks):
         columns = [[full(w[i][:, 8 * b + k : 8 * b + k + 1]) for k in range(8)] for i in range(b, blocks)]
@@ -386,6 +407,7 @@
     turn = jnp.broadcast_to((angular[:, None] * sign)[:, None, :], (F, 8, LANES))
     coef, mask = stencil(coupling, velocity, per)
 
+    rows, coef, mask, turn, waves, parity = lax.optimization_barrier((rows, coef, mask, turn, waves, parity))
     right = lax.ppermute(rows[:, 0], "space", [(i + 1, i) for i in range(count - 1)])
     left = lax.ppermute(rows[:, 1], "space", [(i, i + 1) for i in range(count - 1)])
     low, high = fourier(parity, rows, 0, waves), fourier(parity, rows, 1, waves)

time: 202 us -> 186 us (0.921)
  the two profiles are of different devices: /device:TPU:1 before, /device:TPU:64 now
where the time goes in v4:
time: 186 us; the launch traced here: 185 us
  waiting for transfers between devices  57.7 us (31%)
  starting transfers between devices  54.8 us (29%)
  Pallas kernels  42.8 us (23%)
  blocking collectives  16.3 us (9%)
  local copies, waits for them, and re-layouts  11.8 us (6%)
    ppermute x9, starting transfers between devices, quad_sum(): lax.ppermute(value, axis, [(i, i ^ m) for i in range(count)])  34.1 us
    all_to_all x1, waiting for transfers between devices, local(): rows = lax.all_to_all(rows, 'freq', split_axis=0, concat_axis=0, tiled=True)  31.2 us
    pallas_call x1, Pallas kernels, evolve(): pl.pallas_call(evolve_body, grid_spec=pltpu.PrefetchScalarGridSpec(num_sc...  20 us
    all_to_all x1, blocking collectives, local(): lax.all_to_all(grams, 'freq', split_axis=0, concat_axis=0, tiled=True)  16.3 us
    ppermute x9, waiting for transfers between devices, quad_sum(): lax.ppermute(value, axis, [(i, i ^ m) for i in range(count)])  12.8 us
    pallas_call x1, Pallas kernels, factorize(): pl.pallas_call(partial(factor_body, scale), in_specs=[vmem] * len(parts),...  7.72 us
    all_to_all x1, waiting for transfers between devices, local(): lax.all_to_all(columns, 'freq', split_axis=0, concat_axis=0, tiled=True)  7.58 us
    pallas_call x4, Pallas kernels, fourier(): pl.pallas_call(fourier_body, grid=(1,), in_specs=[pl.BlockSpec(memory_spa...  7.58 us
  transfers between devices with their start and end apart: 15, of which 8 were waited for; matrix products, arithmetic and copies ran while one was open for 2% of the time, Pallas kernels for 7%

profile of v4, /device:TPU:64, one launch (start us, length us, event | category | flops | bytes accessed | tf_op | source)
XLA Modules:
  0.0 185.1 jit_solution(12806104160014478510)
XLA Ops:
  0.6 1.3 copy-done.2
  1.9 3.1 %spread.1 = bf16[8,2,400,128]{3,2,1,0:T(8,128)(2,1)} custom-call(bf16[2,64,5,8,128]{4,3,2,1,0:T(8,128)(2,1)S(1)} %copy-done.2), custom_call_target="tpu_custom_call" | custom-call | tf_op jit(solution)/shard_map/spread/pallas_call | solution.py:51
  5.0 7.2 %all-to-all-start = ((bf16[8,2,400,128]{3,2,1,0:T(8,128)(2,1)}), bf16[8,2,400,128]{3,2,1,0:T(8,128)(2,1)S(1)}, u32[]{:S(2)}, u32[]{:S(2)}) async-start(bf16[8,2,400,128]{3,2,1,0:T(8,128)(2,1)} %spread.1), calls=%async_computation | async-start | bytes 3276800 | tf_op jit(solution)/shard_map/all_to_all | solution.py:400
  12.3 1.9 %collective-permute-start = (f32[26,2,128]{2,1,0:T(2,128)S(1)}, f32[26,2,128]{2,1,0:T(2,128)S(1)}, u32[]{:S(2)}, u32[]{:S(2)}) collective-permute-start(f32[26,2,128]{2,1,0:T(2,128)S(1)} %get-tuple-element.38), channel_id=1, source_target_pairs={{8,0},{16,8},{24,16},{32,24},{40,32},{48,40},{56,48},{64,56},{72,6... | collective-permute-start | bytes 79880 | tf_op jit(solution)/shard_map/ppermute | solution.py:364
  14.2 2.4 %collective-permute-start.1 = (f32[26,2,128]{2,1,0:T(2,128)S(1)}, f32[26,2,128]{2,1,0:T(2,128)S(1)}, u32[]{:S(2)}, u32[]{:S(2)}) collective-permute-start(f32[26,2,128]{2,1,0:T(2,128)S(1)} %get-tuple-element.39), channel_id=1, source_target_pairs={{0,8},{8,16},{16,24},{24,32},{32,40},{40,48},{48,56},{56,64},{64,7... | collective-permute-start | bytes 79880 | tf_op jit(solution)/shard_map/ppermute | solution.py:365
  17.5 1.9 %collective-permute-done.1 = f32[26,2,128]{2,1,0:T(2,128)S(1)} collective-permute-done((f32[26,2,128]{2,1,0:T(2,128)S(1)}, f32[26,2,128]{2,1,0:T(2,128)S(1)}, u32[]{:S(2)}, u32[]{:S(2)}) %collective-permute-start.1) | collective-permute-done | bytes 26656 | tf_op jit(solution)/shard_map/ppermute | solution.py:365
  19.5 0.5 copy.66
  20.2 0.2 copy.70
  20.6 0.2 copy.68
  20.8 0.2 copy.67
  21.0 0.2 copy.71
  21.2 0.2 copy.72
  21.4 0.2 copy.73
  21.6 0.2 copy.74
  21.9 0.2 concatenate.27
  22.1 0.4 copy.75
  22.5 31.2 %all-to-all-done.rows_ref = bf16[8,2,400,128]{3,2,1,0:T(8,128)(2,1)S(1)} async-done(((bf16[8,2,400,128]{3,2,1,0:T(8,128)(2,1)}), bf16[8,2,400,128]{3,2,1,0:T(8,128)(2,1)S(1)}, u32[]{:S(2)}, u32[]{:S(2)}) %all-to-all-start) | async-done | bytes 1638432 | tf_op jit(solution)/shard_map/all_to_all | solution.py:400
  53.7 3.2 %broadcast_in_dim.54.refs_8_ = f32[29,18,2,8,128]{4,3,2,1,0:T(8,128)} broadcast(f32[29,18,2,8]{3,2,1,0:T(2,128)S(1)} %copy.75), dimensions={0,1,2,3} | broadcast | bytes 4309632 | tf_op jit(solution)/shard_map/broadcast_in_dim | solution.py:381
  57.0 1.9 %collective-permute-start.3 = (bf16[8,400,128]{2,1,0:T(8,128)(2,1)S(1)}, bf16[8,400,128]{2,1,0:T(8,128)(2,1)S(1)}, u32[]{:S(2)}, u32[]{:S(2)}) collective-permute-start(bf16[8,400,128]{2,1,0:T(8,128)(2,1)S(1)} %get-tuple-element.32), channel_id=1, source_target_pairs={{0,8},{8,16},{16,24},{24,32},{32,40},{40,48},{48,56},{56,64},{64,7... | collective-permute-start | bytes 2457608 | tf_op jit(solution)/shard_map/ppermute | solution.py:412
  58.9 3.6 %collective-permute-start.2 = (bf16[8,400,128]{2,1,0:T(8,128)(2,1)S(1)}, bf16[8,400,128]{2,1,0:T(8,128)(2,1)S(1)}, u32[]{:S(2)}, u32[]{:S(2)}) collective-permute-start(bf16[8,400,128]{2,1,0:T(8,128)(2,1)S(1)} %get-tuple-element.33), channel_id=1, source_target_pairs={{8,0},{16,8},{24,16},{32,24},{40,32},{48,40},{56,48},{64,56},{72,6... | collective-permute-start | bytes 2457608 | tf_op jit(solution)/shard_map/ppermute | solution.py:411
  62.6 1.9 %fourier.5.refs_1_.refs_5_ = f32[8,400,128]{2,1,0:T(8,128)S(1)} custom-call(s32[8]{0:T(128)S(1)} %and_select_fusion.parity_ref, bf16[8,2,400,128]{3,2,1,0:T(8,128)(2,1)S(1)} %all-to-all-done.rows_ref, f32[8,2,4,128]{3,2,1,0:T(4,128)S(1)} %reshape.194.table_ref), custom_call_target="tpu_custom_call" | custom-call | tf_op jit(solution)/shard_map/fourier/pallas_call | solution.py:92
  64.5 1.9 %fourier.4.refs_0_.refs_4_ = f32[8,400,128]{2,1,0:T(8,128)S(1)} custom-call(s32[8]{0:T(128)S(1)} %and_select_fusion.parity_ref, bf16[8,2,400,128]{3,2,1,0:T(8,128)(2,1)S(1)} %all-to-all-done.rows_ref, f32[8,2,4,128]{3,2,1,0:T(4,128)S(1)} %reshape.194.table_ref), custom_call_target="tpu_custom_call" | custom-call | tf_op jit(solution)/shard_map/fourier/pallas_call | solution.py:92
  66.4 4.3 %collective-permute-done.3 = bf16[8,400,128]{2,1,0:T(8,128)(2,1)S(1)} collective-permute-done((bf16[8,400,128]{2,1,0:T(8,128)(2,1)S(1)}, bf16[8,400,128]{2,1,0:T(8,128)(2,1)S(1)}, u32[]{:S(2)}, u32[]{:S(2)}) %collective-permute-start.3) | collective-permute-done | bytes 819232 | tf_op jit(solution)/shard_map/ppermute | solution.py:412
  70.7 1.9 %fourier.7.refs_3_.refs_7_ = f32[8,400,128]{2,1,0:T(8,128)S(1)} custom-call(s32[8]{0:T(128)S(1)} %and_select_fusion.parity_ref, bf16[8,1,400,128]{3,2,1,0:T(8,128)(2,1)S(1)} %bitcast.20, f32[8,2,4,128]{3,2,1,0:T(4,128)S(1)} %reshape.194.table_ref), custom_call_target="tpu_custom_call" | custom-call | tf_op jit(solution)/shard_map/fourier/pallas_call | solution.py:92
  72.6 1.2 copy-done
  73.7 1.9 %fourier.6.refs_2_.refs_6_ = f32[8,400,128]{2,1,0:T(8,128)S(1)} custom-call(s32[8]{0:T(128)S(1)} %and_select_fusion.parity_ref, bf16[8,1,400,128]{3,2,1,0:T(8,128)(2,1)S(1)} %bitcast.19, f32[8,2,4,128]{3,2,1,0:T(4,128)S(1)} %reshape.194.table_ref), custom_call_target="tpu_custom_call" | custom-call | tf_op jit(solution)/shard_map/fourier/pallas_call | solution.py:92
  75.6 1.2 copy-done.1
  76.8 20.0 %evolve.1 = (f32[8,640,128]{2,1,0:T(8,128)}, f32[8,72,128]{2,1,0:T(8,128)S(1)}) custom-call(s32[8]{0:T(128)S(1)} %iota.73.order_ref, f32[8,400,128]{2,1,0:T(8,128)S(1)} %fourier.4.refs_0_.refs_4_, f32[8,400,128]{2,1,0:T(8,128)S(1)} %fourier.5.refs_1_.refs_5_, f32[8,400,128]{2,1,0:T(8,128)} %copy-done.1, f32[8,400,128]{2,1,0:T(8,128)} %copy-done, ...), custom_call_target="tpu_custom_call" | custom-call | tf_op jit(solution)/shard_map/evolve/pallas_call | solution.py:206
  96.9 16.3 %all_to_all.15 = f32[8,72,128]{2,1,0:T(8,128)S(1)} all-to-all(f32[8,72,128]{2,1,0:T(8,128)S(1)} %get-tuple-element.27), channel_id=1, replica_groups=mesh['space'=64,'freq'=8] {'freq'}, dimensions={0} | all-to-all | bytes 589824 | tf_op jit(solution)/shard_map/all_to_all | solution.py:417
  113.2 3.6 %all-to-all-start.2 = ((f32[8,640,128]{2,1,0:T(8,128)}), f32[8,640,128]{2,1,0:T(8,128)S(1)}, u32[]{:S(2)}, u32[]{:S(2)}) async-start(f32[8,640,128]{2,1,0:T(8,128)} %get-tuple-element.30), calls=%async_computation.2 | async-start | bytes 5242880 | tf_op jit(solution)/shard_map/all_to_all | solution.py:420
  116.9 2.0 %collective-permute-start.6 = (f32[72,128]{1,0:T(8,128)S(1)}, f32[72,128]{1,0:T(8,128)S(1)}, u32[]{:S(2)}, u32[]{:S(2)}) collective-permute-start(f32[72,128]{1,0:T(8,128)S(1)} %reduce_sum.9), channel_id=1, source_target_pairs={{0,8},{8,0},{16,24},{24,16},{32,40},{40,32},{48,56},{56,48},{64,72... | collective-permute-start | bytes 110600 | tf_op jit(solution)/shard_map/ppermute | solution.py:26
  118.9 1.9 %collective-permute-start.5 = (f32[72,128]{1,0:T(8,128)S(1)}, f32[72,128]{1,0:T(8,128)S(1)}, u32[]{:S(2)}, u32[]{:S(2)}) collective-permute-start(f32[72,128]{1,0:T(8,128)S(1)} %reduce_sum.9), channel_id=1, source_target_pairs={{0,24},{8,16},{16,8},{24,0},{32,56},{40,48},{48,40},{56,32},{64,88... | collective-permute-start | bytes 110600 | tf_op jit(solution)/shard_map/ppermute | solution.py:26
  120.8 3.9 %collective-permute-start.4 = (f32[72,128]{1,0:T(8,128)S(1)}, f32[72,128]{1,0:T(8,128)S(1)}, u32[]{:S(2)}, u32[]{:S(2)}) collective-permute-start(f32[72,128]{1,0:T(8,128)S(1)} %reduce_sum.9), channel_id=1, source_target_pairs={{0,16},{8,24},{16,0},{24,8},{32,48},{40,56},{48,32},{56,40},{64,80... | collective-permute-start | bytes 110600 | tf_op jit(solution)/shard_map/ppermute | solution.py:26
  124.8 1.9 %collective-permute-done.4 = f32[72,128]{1,0:T(8,128)S(1)} collective-permute-done((f32[72,128]{1,0:T(8,128)S(1)}, f32[72,128]{1,0:T(8,128)S(1)}, u32[]{:S(2)}, u32[]{:S(2)}) %collective-permute-start.4) | collective-permute-done | bytes 36896 | tf_op jit(solution)/shard_map/ppermute | solution.py:26
  126.7 5.8 %collective-permute-start.9 = (f32[72,128]{1,0:T(8,128)S(1)}, f32[72,128]{1,0:T(8,128)S(1)}, u32[]{:S(2)}, u32[]{:S(2)}) collective-permute-start(f32[72,128]{1,0:T(8,128)S(1)} %add_add_fusion.1), channel_id=1, source_target_pairs={{0,32},{8,40},{16,48},{24,56},{32,0},{40,8},{48,16},{56,24},{64,96... | collective-permute-start | bytes 110600 | tf_op jit(solution)/shard_map/ppermute | solution.py:26
  132.5 6.7 %collective-permute-start.8 = (f32[72,128]{1,0:T(8,128)S(1)}, f32[72,128]{1,0:T(8,128)S(1)}, u32[]{:S(2)}, u32[]{:S(2)}) collective-permute-start(f32[72,128]{1,0:T(8,128)S(1)} %add_add_fusion.1), channel_id=1, source_target_pairs={{0,96},{8,104},{16,112},{24,120},{32,64},{40,72},{48,80},{56,88},{... | collective-permute-start | bytes 110600 | tf_op jit(solution)/shard_map/ppermute | solution.py:26
  139.2 3.7 %collective-permute-start.7 = (f32[72,128]{1,0:T(8,128)S(1)}, f32[72,128]{1,0:T(8,128)S(1)}, u32[]{:S(2)}, u32[]{:S(2)}) collective-permute-start(f32[72,128]{1,0:T(8,128)S(1)} %add_add_fusion.1), channel_id=1, source_target_pairs={{0,64},{8,72},{16,80},{24,88},{32,96},{40,104},{48,112},{56,120},{... | collective-permute-start | bytes 110600 | tf_op jit(solution)/shard_map/ppermute | solution.py:26
  143.0 6.1 %collective-permute-done.7 = f32[72,128]{1,0:T(8,128)S(1)} collective-permute-done((f32[72,128]{1,0:T(8,128)S(1)}, f32[72,128]{1,0:T(8,128)S(1)}, u32[]{:S(2)}, u32[]{:S(2)}) %collective-permute-start.7) | collective-permute-done | bytes 36896 | tf_op jit(solution)/shard_map/ppermute | solution.py:26
  149.2 3.4 %collective-permute-start.12 = (f32[72,128]{1,0:T(8,128)S(1)}, f32[72,128]{1,0:T(8,128)S(1)}, u32[]{:S(2)}, u32[]{:S(2)}) collective-permute-start(f32[72,128]{1,0:T(8,128)S(1)} %add_add_fusion.refs_0_), channel_id=1, source_target_pairs={{0,128},{8,136},{16,144},{24,152},{32,160},{40,168},{48,176},{56,1... | collective-permute-start | bytes 110600 | tf_op jit(solution)/shard_map/ppermute | solution.py:26
  152.6 4.0 %collective-permute-start.11 = (f32[72,128]{1,0:T(8,128)S(1)}, f32[72,128]{1,0:T(8,128)S(1)}, u32[]{:S(2)}, u32[]{:S(2)}) collective-permute-start(f32[72,128]{1,0:T(8,128)S(1)} %add_add_fusion.refs_0_), channel_id=1, source_target_pairs={{0,384},{8,392},{16,400},{24,408},{32,416},{40,424},{48,432},{56,4... | collective-permute-start | bytes 110600 | tf_op jit(solution)/shard_map/ppermute | solution.py:26
  156.6 2.6 %collective-permute-start.10 = (f32[72,128]{1,0:T(8,128)S(1)}, f32[72,128]{1,0:T(8,128)S(1)}, u32[]{:S(2)}, u32[]{:S(2)}) collective-permute-start(f32[72,128]{1,0:T(8,128)S(1)} %add_add_fusion.refs_0_), channel_id=1, source_target_pairs={{0,256},{8,264},{16,272},{24,280},{32,288},{40,296},{48,304},{56,3... | collective-permute-start | bytes 110600 | tf_op jit(solution)/shard_map/ppermute | solution.py:26
  159.2 0.9 collective-permute-done.11.refs_2_
  160.0 3.9 %collective-permute-done.10.refs_1_ = f32[72,128]{1,0:T(8,128)S(1)} collective-permute-done((f32[72,128]{1,0:T(8,128)S(1)}, f32[72,128]{1,0:T(8,128)S(1)}, u32[]{:S(2)}, u32[]{:S(2)}) %collective-permute-start.10) | collective-permute-done | bytes 36896 | tf_op jit(solution)/shard_map/ppermute | solution.py:26
  164.0 0.6 copy-done.8
  164.6 7.7 %factorize.1 = (f32[128,128]{1,0:T(8,128)}, f32[128,128]{1,0:T(8,128)}) custom-call(f32[72,128]{1,0:T(8,128)} %copy-done.5, f32[72,128]{1,0:T(8,128)} %copy-done.8, f32[72,128]{1,0:T(8,128)} %copy-done.7, f32[72,128]{1,0:T(8,128)} %copy-done.6), custom_call_target="tpu_custom_call" | custom-call | tf_op jit(solution)/shard_map/factorize/pallas_call | solution.py:294
  172.3 7.6 %all-to-all-done.2.columns_ref = f32[8,640,128]{2,1,0:T(8,128)S(1)} async-done(((f32[8,640,128]{2,1,0:T(8,128)}), f32[8,640,128]{2,1,0:T(8,128)S(1)}, u32[]{:S(2)}, u32[]{:S(2)}) %all-to-all-start.2) | async-done | bytes 2621472 | tf_op jit(solution)/shard_map/all_to_all | solution.py:420
  179.9 0.8 copy-done.3
  180.7 4.4 %apply.1 = f32[1,128,5,8,128]{4,3,2,1,0:T(8,128)} custom-call(f32[128,128]{1,0:T(8,128)S(1)} %copy-done.3, f32[8,640,128]{2,1,0:T(8,128)S(1)} %all-to-all-done.2.columns_ref), custom_call_target="tpu_custom_call" | custom-call | tf_op jit(solution)/shard_map/apply/pallas_call | solution.py:331
  (53 shorter events, 1.6 us)
Async XLA Ops:
  0.6 1.3 copy-start.2
  5.0 7.2 %copy-start.4 = (f32[5,5,8,128]{3,2,1,0:T(8,128)S(1)}, f32[5,5,8,128]{3,2,1,0:T(8,128)}, u32[]{:S(2)}) copy-start(f32[5,5,8,128]{3,2,1,0:T(8,128)} %param.5) | copy-start | bytes 307204
  5.0 7.2 %copy-start.9 = (f32[8,128]{1,0:T(8,128)S(1)}, f32[8,128]{1,0:T(8,128)}, u32[]{:S(2)}) copy-start(f32[8,128]{1,0:T(8,128)} %param.6) | copy-start | bytes 12292
  5.0 11.7 %copy-start.10 = (s32[8]{0:T(128)S(1)}, s32[8]{0:T(128)}, u32[]{:S(2)}) copy-start(s32[8]{0:T(128)} %param.7) | copy-start | bytes 100
  5.0 48.6 %all-to-all-start = ((bf16[8,2,400,128]{3,2,1,0:T(8,128)(2,1)}), bf16[8,2,400,128]{3,2,1,0:T(8,128)(2,1)S(1)}, u32[]{:S(2)}, u32[]{:S(2)}) async-start(bf16[8,2,400,128]{3,2,1,0:T(8,128)(2,1)} %spread.1), calls=%async_computation | async-start | bytes 3276800 | tf_op jit(solution)/shard_map/all_to_all | solution.py:400
  12.3 5.2 %collective-permute-start = (f32[26,2,128]{2,1,0:T(2,128)S(1)}, f32[26,2,128]{2,1,0:T(2,128)S(1)}, u32[]{:S(2)}, u32[]{:S(2)}) collective-permute-start(f32[26,2,128]{2,1,0:T(2,128)S(1)} %get-tuple-element.38), channel_id=1, source_target_pairs={{8,0},{16,8},{24,16},{32,24},{40,32},{48,40},{56,48},{64,56},{72,6... | collective-permute-start | bytes 79880 | tf_op jit(solution)/shard_map/ppermute | solution.py:364
  14.2 5.2 %collective-permute-start.1 = (f32[26,2,128]{2,1,0:T(2,128)S(1)}, f32[26,2,128]{2,1,0:T(2,128)S(1)}, u32[]{:S(2)}, u32[]{:S(2)}) collective-permute-start(f32[26,2,128]{2,1,0:T(2,128)S(1)} %get-tuple-element.39), channel_id=1, source_target_pairs={{0,8},{8,16},{16,24},{24,32},{32,40},{40,48},{48,56},{56,64},{64,7... | collective-permute-start | bytes 79880 | tf_op jit(solution)/shard_map/ppermute | solution.py:365
  57.0 13.7 %collective-permute-start.3 = (bf16[8,400,128]{2,1,0:T(8,128)(2,1)S(1)}, bf16[8,400,128]{2,1,0:T(8,128)(2,1)S(1)}, u32[]{:S(2)}, u32[]{:S(2)}) collective-permute-start(bf16[8,400,128]{2,1,0:T(8,128)(2,1)S(1)} %get-tuple-element.32), channel_id=1, source_target_pairs={{0,8},{8,16},{16,24},{24,32},{32,40},{40,48},{48,56},{56,64},{64,7... | collective-permute-start | bytes 2457608 | tf_op jit(solution)/shard_map/ppermute | solution.py:412
  58.9 14.8 %collective-permute-start.2 = (bf16[8,400,128]{2,1,0:T(8,128)(2,1)S(1)}, bf16[8,400,128]{2,1,0:T(8,128)(2,1)S(1)}, u32[]{:S(2)}, u32[]{:S(2)}) collective-permute-start(bf16[8,400,128]{2,1,0:T(8,128)(2,1)S(1)} %get-tuple-element.33), channel_id=1, source_target_pairs={{8,0},{16,8},{24,16},{32,24},{40,32},{48,40},{56,48},{64,56},{72,6... | collective-permute-start | bytes 2457608 | tf_op jit(solution)/shard_map/ppermute | solution.py:411
  72.6 1.2 copy-start
  75.6 1.2 copy-start.1
  113.2 66.6 %all-to-all-start.2 = ((f32[8,640,128]{2,1,0:T(8,128)}), f32[8,640,128]{2,1,0:T(8,128)S(1)}, u32[]{:S(2)}, u32[]{:S(2)}) async-start(f32[8,640,128]{2,1,0:T(8,128)} %get-tuple-element.30), calls=%async_computation.2 | async-start | bytes 5242880 | tf_op jit(solution)/shard_map/all_to_all | solution.py:420
  116.9 7.9 %collective-permute-start.6 = (f32[72,128]{1,0:T(8,128)S(1)}, f32[72,128]{1,0:T(8,128)S(1)}, u32[]{:S(2)}, u32[]{:S(2)}) collective-permute-start(f32[72,128]{1,0:T(8,128)S(1)} %reduce_sum.9), channel_id=1, source_target_pairs={{0,8},{8,0},{16,24},{24,16},{32,40},{40,32},{48,56},{56,48},{64,72... | collective-permute-start | bytes 110600 | tf_op jit(solution)/shard_map/ppermute | solution.py:26
  118.9 5.9 %collective-permute-start.5 = (f32[72,128]{1,0:T(8,128)S(1)}, f32[72,128]{1,0:T(8,128)S(1)}, u32[]{:S(2)}, u32[]{:S(2)}) collective-permute-start(f32[72,128]{1,0:T(8,128)S(1)} %reduce_sum.9), channel_id=1, source_target_pairs={{0,24},{8,16},{16,8},{24,0},{32,56},{40,48},{48,40},{56,32},{64,88... | collective-permute-start | bytes 110600 | tf_op jit(solution)/shard_map/ppermute | solution.py:26
  120.8 5.9 %collective-permute-start.4 = (f32[72,128]{1,0:T(8,128)S(1)}, f32[72,128]{1,0:T(8,128)S(1)}, u32[]{:S(2)}, u32[]{:S(2)}) collective-permute-start(f32[72,128]{1,0:T(8,128)S(1)} %reduce_sum.9), channel_id=1, source_target_pairs={{0,16},{8,24},{16,0},{24,8},{32,48},{40,56},{48,32},{56,40},{64,80... | collective-permute-start | bytes 110600 | tf_op jit(solution)/shard_map/ppermute | solution.py:26
  126.7 16.3 %collective-permute-start.9 = (f32[72,128]{1,0:T(8,128)S(1)}, f32[72,128]{1,0:T(8,128)S(1)}, u32[]{:S(2)}, u32[]{:S(2)}) collective-permute-start(f32[72,128]{1,0:T(8,128)S(1)} %add_add_fusion.1), channel_id=1, source_target_pairs={{0,32},{8,40},{16,48},{24,56},{32,0},{40,8},{48,16},{56,24},{64,96... | collective-permute-start | bytes 110600 | tf_op jit(solution)/shard_map/ppermute | solution.py:26
  132.5 10.5 %collective-permute-start.8 = (f32[72,128]{1,0:T(8,128)S(1)}, f32[72,128]{1,0:T(8,128)S(1)}, u32[]{:S(2)}, u32[]{:S(2)}) collective-permute-start(f32[72,128]{1,0:T(8,128)S(1)} %add_add_fusion.1), channel_id=1, source_target_pairs={{0,96},{8,104},{16,112},{24,120},{32,64},{40,72},{48,80},{56,88},{... | collective-permute-start | bytes 110600 | tf_op jit(solution)/shard_map/ppermute | solution.py:26
  139.2 9.9 %collective-permute-start.7 = (f32[72,128]{1,0:T(8,128)S(1)}, f32[72,128]{1,0:T(8,128)S(1)}, u32[]{:S(2)}, u32[]{:S(2)}) collective-permute-start(f32[72,128]{1,0:T(8,128)S(1)} %add_add_fusion.1), channel_id=1, source_target_pairs={{0,64},{8,72},{16,80},{24,88},{32,96},{40,104},{48,112},{56,120},{... | collective-permute-start | bytes 110600 | tf_op jit(solution)/shard_map/ppermute | solution.py:26
  149.2 14.8 %copy-start.5 = (f32[72,128]{1,0:T(8,128)}, f32[72,128]{1,0:T(8,128)S(1)}, u32[]{:S(2)}) copy-start(f32[72,128]{1,0:T(8,128)S(1)} %add_add_fusion.refs_0_) | copy-start | bytes 110596
  149.2 10.0 %collective-permute-start.12 = (f32[72,128]{1,0:T(8,128)S(1)}, f32[72,128]{1,0:T(8,128)S(1)}, u32[]{:S(2)}, u32[]{:S(2)}) collective-permute-start(f32[72,128]{1,0:T(8,128)S(1)} %add_add_fusion.refs_0_), channel_id=1, source_target_pairs={{0,128},{8,136},{16,144},{24,152},{32,160},{40,168},{48,176},{56,1... | collective-permute-start | bytes 110600 | tf_op jit(solution)/shard_map/ppermute | solution.py:26
  152.6 7.5 %collective-permute-start.11 = (f32[72,128]{1,0:T(8,128)S(1)}, f32[72,128]{1,0:T(8,128)S(1)}, u32[]{:S(2)}, u32[]{:S(2)}) collective-permute-start(f32[72,128]{1,0:T(8,128)S(1)} %add_add_fusion.refs_0_), channel_id=1, source_target_pairs={{0,384},{8,392},{16,400},{24,408},{32,416},{40,424},{48,432},{56,4... | collective-permute-start | bytes 110600 | tf_op jit(solution)/shard_map/ppermute | solution.py:26
  156.6 7.4 %collective-permute-start.10 = (f32[72,128]{1,0:T(8,128)S(1)}, f32[72,128]{1,0:T(8,128)S(1)}, u32[]{:S(2)}, u32[]{:S(2)}) collective-permute-start(f32[72,128]{1,0:T(8,128)S(1)} %add_add_fusion.refs_0_), channel_id=1, source_target_pairs={{0,256},{8,264},{16,272},{24,280},{32,288},{40,296},{48,304},{56,3... | collective-permute-start | bytes 110600 | tf_op jit(solution)/shard_map/ppermute | solution.py:26
  159.2 4.8 %copy-start.6 = (f32[72,128]{1,0:T(8,128)}, f32[72,128]{1,0:T(8,128)S(1)}, u32[]{:S(2)}) copy-start(f32[72,128]{1,0:T(8,128)S(1)} %collective-permute-done.12.refs_3_) | copy-start | bytes 110596
  160.0 3.9 %copy-start.7 = (f32[72,128]{1,0:T(8,128)}, f32[72,128]{1,0:T(8,128)S(1)}, u32[]{:S(2)}) copy-start(f32[72,128]{1,0:T(8,128)S(1)} %collective-permute-done.11.refs_2_) | copy-start | bytes 110596
  163.9 0.6 copy-start.8
  179.9 0.8 copy-start.3

commit v5 on v4

--- a/solution.py
+++ b/solution.py
@@ -63,16 +63,13 @@
     )(sketch)
 
 
-def fourier_body(parity_ref, rows_ref, table_ref, z_ref, pair_ref):
+def fourier_body(parity_ref, one_ref, two_ref, table_ref, z_one, z_two, pair_ref):
     size = pair_ref.shape[2]
     first = lax.broadcasted_iota(jnp.int32, (8, LANES), 1) < K
-
-    @pl.loop(0, rows_ref.shape[2] // size)
-    def _(step):
-        start = pl.multiple_of(step * size, size)
+    for rows_ref, z_ref in ((one_ref, z_one), (two_ref, z_two)):
         for d in range(4):
-            a = rows_ref[d, 0, pl.ds(start, size), :].astype(jnp.float32)
-            b = rows_ref[d + 4, 0, pl.ds(start, size), :].astype(jnp.float32)
+            a = rows_ref[d, 0].astype(jnp.float32)
+            b = rows_ref[d + 4, 0].astype(jnp.float32)
             pair_ref[0, d] = a + b
             pair_ref[1, d] = a - b
         for f in range(F):
@@ -82,27 +79,40 @@
                 p = [pair_ref[parity, d, line : line + 8] for d in range(4)]
                 u = (p[0] * wave[0][0] + p[1] * wave[0][1]) + (p[2] * wave[0][2] + p[3] * wave[0][3])
                 v = (p[0] * wave[1][0] + p[1] * wave[1][1]) + (p[2] * wave[1][2] + p[3] * wave[1][3])
-                z_ref[f, pl.ds(start + line, 8), :] = jnp.where(first, u, v) + pltpu.roll(
-                    jnp.where(first, v, u), K, 1
-                )
-
-
-def fourier(parity, rows, part, table):
-    slots, _, count, _ = rows.shape
+                z_ref[f, line : line + 8, :] = jnp.where(first, u, v) + pltpu.roll(jnp.where(first, v, u), K, 1)
+
+
+def fourier(parity, one, two, table, parts):
+    slots, _, count, _ = one.shape
+    size = count // FIELDS
+    z_spec = pl.BlockSpec((F, size, LANES), lambda i: (0, i, 0))
+    z_shape = jax.ShapeDtypeStruct((F, count, LANES), jnp.float32)
     return pl.pallas_call(
         fourier_body,
-        grid=(1,),
+        grid=(FIELDS,),
         in_specs=[
             pl.BlockSpec(memory_space=pltpu.SMEM),
-            pl.BlockSpec((slots, 1, count, LANES), lambda i: (0, part, 0, 0)),
+            pl.BlockSpec((slots, 1, size, LANES), lambda i: (0, parts[0], i, 0)),
+            pl.BlockSpec((slots, 1, size, LANES), lambda i: (0, parts[1], i, 0)),
             pl.BlockSpec(table.shape, lambda i: (0, 0, 0, 0)),
         ],
-        out_specs=pl.BlockSpec((F, count, LANES), lambda i: (0, 0, 0)),
-        out_shape=jax.ShapeDtypeStruct((F, count, LANES), jnp.float32),
-        scratch_shapes=[pltpu.VMEM((2, 4, count // 5, LANES), jnp.float32)],
+        out_specs=[z_spec, z_spec],
+        out_shape=[z_shape, z_shape],
+        scratch_shapes=[pltpu.VMEM((2, 4, size, LANES), jnp.float32)],
         compiler_params=pltpu.CompilerParams(vmem_limit_bytes=VMEM_LIMIT),
         name="fourier",
-    )(parity, rows, table)
+    )(parity, one, two, table)
+
+
+CODE = 8388000.0
+
+
+def encode(block, scale):
+    number = jnp.round(block * (CODE / scale)).astype(jnp.int32)
+    half = block.shape[0] // 2
+    low = number & 255
+    both = (low[:half] << 8) + low[half:] - 32768
+    return (number >> 8).astype(jnp.int16), both.astype(jnp.int16)
 
 
 def pack(gram, ref, n):
@@ -120,7 +130,7 @@
     top = packed[:K]
     last = pltpu.roll(jnp.where(lane < line, top, 0.0), K, 1)
     half = jnp.concatenate([jnp.where(lane >= line, top, 0.0), last], axis=0)
-    diagonal = pltpu.roll(packed[K : K + 8], K, 1)
+    diagonal = pltpu.roll(jnp.broadcast_to(packed[K : K + 1], (8, LANES)), K, 1)
     diagonal = jnp.concatenate([top] + [diagonal] * (K // 8), axis=0)
     line = lax.broadcasted_iota(jnp.int32, (LANES, LANES), 0)
     lane = lax.broadcasted_iota(jnp.int32, (LANES, LANES), 1)
@@ -128,7 +138,7 @@
 
 
 def evolve_body(order_ref, *refs):
-    layers, (coef_ref, mask_ref, turn_a, turn_b, out_ref, gram_ref, z_ref, s_ref) = refs[:8], refs[8:]
+    layers, (coef_ref, mask_ref, turn_a, turn_b, code_ref, gram_ref, z_ref, s_ref, out_ref) = refs[:8], refs[8:]
     wide = z_ref.shape[2]
     per = wide - 2 * RH
     sub = lax.broadcasted_iota(jnp.int32, (8, LANES), 0)
@@ -194,6 +204,10 @@
             precision=lax.Precision.HIGHEST, preferred_element_type=jnp.float32,
         )
         pack(gram, gram_ref, n)
+        scale = jnp.maximum(jnp.max(jnp.abs(block), axis=0, keepdims=True), 1e-30)
+        gram_ref[n, K + 1 : K + 2, :] = scale
+        count = block.shape[0]
+        code_ref[n, 0:count, :], code_ref[n, count : count + count // 2, :] = encode(block, scale)
 
 
 def evolve(order, low, high, right, left, coef, mask, turn):
@@ -211,16 +225,17 @@
             in_specs=layers
             + [whole(coef.shape), whole(mask.shape), pick((8, LANES), 0), pick((8, LANES), 1)],
             out_specs=[
-                pl.BlockSpec((2, FIELDS * 8 * per, LANES), lambda i, order: (i, 0, 0)),
+                pl.BlockSpec((2, FIELDS * 12 * per, LANES), lambda i, order: (i, 0, 0)),
                 pl.BlockSpec((2, K + 8, LANES), lambda i, order: (i, 0, 0)),
             ],
             scratch_shapes=[
                 pltpu.VMEM((2, FIELDS, per + 2 * RH, 2, 8, LANES), jnp.float32),
                 pltpu.VMEM((2, FIELDS, per + 2, 2, 8, LANES), jnp.float32),
+                pltpu.VMEM((2, FIELDS * 8 * per, LANES), jnp.float32),
             ],
         ),
         out_shape=[
-            jax.ShapeDtypeStruct((count, FIELDS * 8 * per, LANES), jnp.float32),
+            jax.ShapeDtypeStruct((count, FIELDS * 12 * per, LANES), jnp.int16),
             jax.ShapeDtypeStruct((count, K + 8, LANES), jnp.float32),
         ],
         compiler_params=pltpu.CompilerParams(vmem_limit_bytes=VMEM_LIMIT),
@@ -308,14 +323,24 @@
     return one, two, three
 
 
-def apply_body(inverse_ref, columns_ref, out_ref, rows_ref, all_ref):
-    per = columns_ref.shape[1] // 8
+def apply_body(inverse_ref, scale_ref, code_ref, out_ref, rows_ref, all_ref):
+    per = code_ref.shape[1] // (12 * FIELDS)
+    total = 8 * FIELDS * per
+    field = pl.program_id(0)
     one, two, three = split(inverse_ref[...].T)
     main = jnp.concatenate([jnp.concatenate([one, two], axis=1)] * 2, axis=0)
     rest = jnp.concatenate([one, three], axis=0)
     for x in range(8):
+        line = (field * 8 + x) * per
+        late = line >= total // 2
+        other = jnp.where(late, line - total // 2, line)
+        shift = jnp.where(late, 0, 8)
         for d in range(F):
-            all_ref[x, d * per : (d + 1) * per, :] = columns_ref[d, x * per : (x + 1) * per, :]
+            high = code_ref[d, pl.ds(pl.multiple_of(line, 16), per), :].astype(jnp.int32)
+            low = code_ref[d, pl.ds(pl.multiple_of(total + other, 16), per), :].astype(jnp.int32) + 32768
+            low = lax.shift_right_logical(low, jnp.full(low.shape, shift, jnp.int32)) & 255
+            value = ((high << 8) + low).astype(jnp.float32) * (scale_ref[d : d + 1, :] * (1.0 / CODE))
+            all_ref[x, d * per : (d + 1) * per, :] = value
     for x in range(8):
         a, b, c = split(all_ref[x])
         wide = jnp.dot(jnp.concatenate([a, b], axis=1), main, preferred_element_type=jnp.float32)
@@ -325,16 +350,14 @@
     out_ref[...] = rows_ref[...].reshape(out_ref.shape)
 
 
-def apply(inverse, columns):
-    per = columns.shape[1] // (8 * FIELDS)
+def apply(inverse, scales, columns):
+    per = columns.shape[1] // (12 * FIELDS)
     radial = per * F
+    vmem = pl.BlockSpec(memory_space=pltpu.VMEM)
     return pl.pallas_call(
         apply_body,
         grid=(FIELDS,),
-        in_specs=[
-            pl.BlockSpec((LANES, LANES), lambda i: (0, 0)),
-            pl.BlockSpec((F, 8 * per, LANES), lambda i: (0, i, 0)),
-        ],
+        in_specs=[vmem, vmem, vmem],
         out_specs=pl.BlockSpec((1, LANES, 1, 8, radial), lambda i: (0, 0, i, 0, 0)),
         out_shape=jax.ShapeDtypeStruct((1, LANES, FIELDS, 8, radial), jnp.float32),
         scratch_shapes=[
@@ -343,7 +366,7 @@
         ],
         compiler_params=pltpu.CompilerParams(vmem_limit_bytes=VMEM_LIMIT),
         name="apply",
-    )(inverse, columns)
+    )(inverse, scales, columns)
 
 
 def make_table(indices, slots):
@@ -353,39 +376,67 @@
     return jnp.stack([jnp.cos(angles), -jnp.sin(angles)], axis=1)
 
 
+def stencil_body(place_ref, coupling_ref, velocity_ref, right_ref, left_ref, coef_ref, mask_ref):
+    cells, radial = coef_ref.shape[1], velocity_ref.shape[1]
+    start = place_ref[0]
+    turn = lax.rem(radial + 1 - start, radial)
+    sub = lax.broadcasted_iota(jnp.int32, (8, LANES), 0)
+
+    def tiles(index, own):
+        gap = jnp.zeros((4, radial), jnp.float32)
+        other = jnp.concatenate([right_ref[index], gap, left_ref[index]], axis=0)
+        return [pltpu.roll(value, turn, 1) for value in (own, other)]
+
+    def spread_lanes(index, t, value):
+        for r in range(cells):
+            coef_ref[index, r, t] = jnp.broadcast_to(value[:, r : r + 1], (8, LANES))
+
+    centre = 1.0 - STEP_DT * VISCOSITY * (30.0 / 12.0 + 2.0)
+
+    @pl.loop(0, FIELDS * FIELDS)
+    def _(index):
+        diagonal = jnp.where(lax.rem(index, FIELDS + 1) == 0, centre, 0.0)
+        for t, value in enumerate(tiles(index, coupling_ref[index])):
+            spread_lanes(index, t, STEP_DT * value + diagonal)
+
+    near_d, near_c = STEP_DT * 8.0 / 12.0, STEP_DT * VISCOSITY * 16.0 / 12.0
+    far_d, far_c = STEP_DT / 12.0, STEP_DT * VISCOSITY / 12.0
+    for t, speed in enumerate(tiles(FIELDS * FIELDS, velocity_ref[...])):
+        spread_lanes(FIELDS * FIELDS, t, near_d * speed + near_c)
+        spread_lanes(FIELDS * FIELDS + 1, t, near_c - near_d * speed)
+        spread_lanes(FIELDS * FIELDS + 2, t, -far_d * speed - far_c)
+        spread_lanes(FIELDS * FIELDS + 3, t, far_d * speed - far_c)
+    sides = jnp.where(sub < HALF, place_ref[2], place_ref[1])
+    for r in range(cells):
+        here = start - 1 + r
+        inside = jnp.where((here >= 0) & (here < radial), 1, 0)
+        mask_ref[r, 0] = jnp.full((8, LANES), inside, jnp.int32).astype(jnp.float32)
+        mask_ref[r, 1] = (sides * inside).astype(jnp.float32)
+
+
 def stencil(coupling, velocity, per):
     count = lax.axis_size("space")
     mine = lax.axis_index("space")
-    start = lax.axis_index("freq") * per
     radial = velocity.shape[1]
     up = [(i, i + 1) for i in range(count - 1)]
     down = [(i + 1, i) for i in range(count - 1)]
-    both = jnp.concatenate([coupling.reshape(FIELDS * FIELDS, 8, radial), velocity[None]], axis=0)
-    right = lax.ppermute(both[:, :2], "space", down)
-    left = lax.ppermute(both[:, 6:], "space", up)
-    gap = jnp.zeros((both.shape[0], 4, radial), jnp.float32)
-    full = jnp.concatenate([both, right, gap, left], axis=1)
-    full = jnp.pad(full, ((0, 0), (0, 0), (1, 1)))
-    full = lax.dynamic_slice_in_dim(full, start, per + 2, axis=2).transpose(0, 2, 1)
-    speed = full[FIELDS * FIELDS]
-    coupled = STEP_DT * full[: FIELDS * FIELDS]
-    centre = 1.0 - STEP_DT * VISCOSITY * (30.0 / 12.0 + 2.0)
-    diagonal = jnp.eye(FIELDS, dtype=jnp.float32).reshape(-1) * centre
-    coupled = coupled + diagonal[:, None, None]
-    near_d, near_c = STEP_DT * 8.0 / 12.0, STEP_DT * VISCOSITY * 16.0 / 12.0
-    far_d, far_c = STEP_DT / 12.0, STEP_DT * VISCOSITY / 12.0
-    shifts = jnp.stack(
-        [near_d * speed + near_c, near_c - near_d * speed, -far_d * speed - far_c, far_d * speed - far_c]
-    )
-    coef = jnp.concatenate([coupled, shifts], axis=0)
-    coef = jnp.broadcast_to(coef.reshape(-1, per + 2, 2, 8)[..., None], (coef.shape[0], per + 2, 2, 8, LANES))
-    r = start - 1 + jnp.arange(per + 2)
-    place = jnp.arange(16)
-    inside = (place < 8) | ((place < 12) & (mine < count - 1)) | ((place >= 12) & (mine > 0))
-    mask = ((r >= 0) & (r < radial))[:, None] & inside[None, :]
-    mask = mask.astype(jnp.float32).reshape(per + 2, 2, 8)
-    mask = jnp.broadcast_to(mask[..., None], mask.shape + (LANES,))
-    return coef, mask
+    coupling = coupling.reshape(FIELDS * FIELDS, 8, radial)
+    edges = [jnp.concatenate([coupling[:, s], velocity[None, s]], axis=0) for s in (slice(0, 2), slice(6, 8))]
+    right = lax.ppermute(edges[0], "space", down)
+    left = lax.ppermute(edges[1], "space", up)
+    place = jnp.stack([lax.axis_index("freq") * per, (mine > 0).astype(jnp.int32), (mine < count - 1).astype(jnp.int32)])
+    vmem = pl.BlockSpec(memory_space=pltpu.VMEM)
+    return pl.pallas_call(
+        stencil_body,
+        in_specs=[pl.BlockSpec(memory_space=pltpu.SMEM)] + [vmem] * 4,
+        out_specs=[vmem, vmem],
+        out_shape=[
+            jax.ShapeDtypeStruct((FIELDS * FIELDS + 4, per + 2, 2, 8, LANES), jnp.float32),
+            jax.ShapeDtypeStruct((per + 2, 2, 8, LANES), jnp.float32),
+        ],
+        compiler_params=pltpu.CompilerParams(vmem_limit_bytes=VMEM_LIMIT),
+        name="stencil",
+    )(place, coupling, velocity, right, left)
 
 
 def local(sketch, coupling, velocity, freq_index):
@@ -410,12 +461,13 @@
     rows, coef, mask, turn, waves, parity = lax.optimization_barrier((rows, coef, mask, turn, waves, parity))
     right = lax.ppermute(rows[:, 0], "space", [(i + 1, i) for i in range(count - 1)])
     left = lax.ppermute(rows[:, 1], "space", [(i, i + 1) for i in range(count - 1)])
-    low, high = fourier(parity, rows, 0, waves), fourier(parity, rows, 1, waves)
-    right, left = fourier(parity, right[:, None], 0, waves), fourier(parity, left[:, None], 0, waves)
+    low, high = fourier(parity, rows, rows, waves, (0, 1))
+    right, left = fourier(parity, right[:, None], left[:, None], waves, (0, 0))
 
     columns, grams = evolve(jnp.arange(F, dtype=jnp.int32), low, high, right, left, coef, mask, turn)
     parts = lax.all_to_all(grams, "freq", split_axis=0, concat_axis=0, tiled=True)
     gram = jnp.sum(parts, axis=0)
+    scales = parts[:, K + 1]
     columns, gram = lax.optimization_barrier((columns, gram))
     columns = lax.all_to_all(columns, "freq", split_axis=0, concat_axis=0, tiled=True)
     for bit in (0, 2, 4):
@@ -423,7 +475,7 @@
         gram = sum(parts)
     row_scale = math.sqrt(FIELDS * 8 * count * radial)
     inverse, factor = factorize(parts, row_scale)
-    return apply(inverse, columns), factor[None]
+    return apply(inverse, scales, columns), factor[None]
 
 
 def solution(mesh):

time: 186 us -> 181 us (0.973)
  the two profiles are of different devices: /device:TPU:64 before, /device:TPU:8 now
where the time goes in v5:
time: 181 us; the launch traced here: 180 us
  starting transfers between devices  66.4 us (37%)
  Pallas kernels  53 us (29%)
  waiting for transfers between devices  40.4 us (22%)
  blocking collectives  13.2 us (7%)
  local copies, waits for them, and re-layouts  5.51 us (3%)
    ppermute x9, starting transfers between devices, quad_sum(): lax.ppermute(value, axis, [(i, i ^ m) for i in range(count)])  45.1 us
    all_to_all x1, waiting for transfers between devices, local(): rows = lax.all_to_all(rows, 'freq', split_axis=0, concat_axis=0, tiled=True)  25.1 us
    pallas_call x1, Pallas kernels, evolve(): pl.pallas_call(evolve_body, grid_spec=pltpu.PrefetchScalarGridSpec(num_sc...  21.2 us
    ppermute x9, waiting for transfers between devices, quad_sum(): lax.ppermute(value, axis, [(i, i ^ m) for i in range(count)])  14.4 us
    all_to_all x1, blocking collectives, local(): lax.all_to_all(grams, 'freq', split_axis=0, concat_axis=0, tiled=True)  13.2 us
    all_to_all x1, starting transfers between devices, local(): rows = lax.all_to_all(rows, 'freq', split_axis=0, concat_axis=0, tiled=True)  9.44 us
    pallas_call x2, Pallas kernels, fourier(): pl.pallas_call(fourier_body, grid=(FIELDS,), in_specs=[pl.BlockSpec(memor...  8.97 us
    pallas_call x1, Pallas kernels, stencil(): pl.pallas_call(stencil_body, in_specs=[pl.BlockSpec(memory_space=pltpu.SM...  7.83 us
  transfers between devices with their start and end apart: 15, of which 7 were waited for; matrix products, arithmetic and copies ran while one was open for 0% of the time, Pallas kernels for 11%

profile of v5, /device:TPU:8, one launch (start us, length us, event | category | flops | bytes accessed | tf_op | source)
XLA Modules:
  0.0 179.9 jit_solution(3273660633162564843)
XLA Ops:
  0.6 1.3 copy-done.1
  1.9 3.1 %spread.1 = bf16[8,2,400,128]{3,2,1,0:T(8,128)(2,1)} custom-call(bf16[2,64,5,8,128]{4,3,2,1,0:T(8,128)(2,1)S(1)} %copy-done.1), custom_call_target="tpu_custom_call" | custom-call | tf_op jit(solution)/shard_map/spread/pallas_call | solution.py:51
  5.0 9.4 %all-to-all-start = ((bf16[8,2,400,128]{3,2,1,0:T(8,128)(2,1)}), bf16[8,2,400,128]{3,2,1,0:T(8,128)(2,1)S(1)}, u32[]{:S(2)}, u32[]{:S(2)}) async-start(bf16[8,2,400,128]{3,2,1,0:T(8,128)(2,1)} %spread.1), calls=%async_computation | async-start | bytes 3276800 | tf_op jit(solution)/shard_map/all_to_all | solution.py:451
  14.5 1.3 collective-permute-start
  15.9 3.0 %collective-permute-start.1 = (f32[26,2,128]{2,1,0:T(2,128)S(1)}, f32[26,2,128]{2,1,0:T(2,128)S(1)}, u32[]{:S(2)}, u32[]{:S(2)}) collective-permute-start(f32[26,2,128]{2,1,0:T(2,128)S(1)} %pad_maximum_fusion.1), channel_id=1, source_target_pairs={{0,8},{8,16},{16,24},{24,32},{32,40},{40,48},{48,56},{56,64},{64,7... | collective-permute-start | bytes 79880 | tf_op jit(solution)/shard_map/ppermute | solution.py:426
  18.9 0.1 fusion.6
  19.0 0.1 broadcast_multiply_fusion
  19.1 0.1 pad_add_fusion.place_ref
  19.2 0.1 copy.12
  19.3 0.1 broadcast_in_dim.41
  19.5 0.1 reshape.137.table_ref
  19.6 0.0 collective-permute-done.right_ref
  19.6 0.2 collective-permute-done.1.left_ref
  19.7 7.8 %stencil.1 = (f32[29,18,2,8,128]{4,3,2,1,0:T(8,128)}, f32[18,2,8,128]{3,2,1,0:T(8,128)S(1)}) custom-call(s32[3]{0:T(128)S(1)} %pad_add_fusion.place_ref, f32[25,8,128]{2,1,0:T(8,128)S(1)} %bitcast.22, f32[8,128]{1,0:T(8,128)S(1)} %copy-done.4, f32[26,2,128]{2,1,0:T(2,128)S(1)} %collective-permute-done.right_ref, ...), custom_call_target="tpu_custom_call" | custom-call | tf_op jit(solution)/shard_map/stencil/pallas_call | solution.py:429
  27.6 25.1 %all-to-all-done.one_ref.two_ref = bf16[8,2,400,128]{3,2,1,0:T(8,128)(2,1)S(1)} async-done(((bf16[8,2,400,128]{3,2,1,0:T(8,128)(2,1)}), bf16[8,2,400,128]{3,2,1,0:T(8,128)(2,1)S(1)}, u32[]{:S(2)}, u32[]{:S(2)}) %all-to-all-start) | async-done | bytes 1638432 | tf_op jit(solution)/shard_map/all_to_all | solution.py:451
  52.6 0.1 slice_bitcast_fusion
  52.7 1.0 copy-done.5
  53.8 1.3 collective-permute-start.3
  55.1 1.3 collective-permute-start.2
  56.4 4.6 %fourier.2 = (f32[8,400,128]{2,1,0:T(8,128)S(1)}, f32[8,400,128]{2,1,0:T(8,128)S(1)}) custom-call(s32[8]{0:T(128)S(1)} %and_select_fusion.parity_ref, bf16[8,2,400,128]{3,2,1,0:T(8,128)(2,1)} %copy-done.5, bf16[8,2,400,128]{3,2,1,0:T(8,128)(2,1)} %copy-done.5, f32[8,2,4,128]{3,2,1,0:T(4,128)S(1)} %reshape.137.table_ref), custom_call_target="tpu_custom_call" | custom-call | tf_op jit(solution)/shard_map/fourier/pallas_call | solution.py:90
  61.1 0.0 collective-permute-done.3
  61.1 0.8 collective-permute-done.2
  61.9 4.3 %fourier.3 = (f32[8,400,128]{2,1,0:T(8,128)S(1)}, f32[8,400,128]{2,1,0:T(8,128)}) custom-call(s32[8]{0:T(128)S(1)} %and_select_fusion.parity_ref, bf16[8,1,400,128]{3,2,1,0:T(8,128)(2,1)S(1)} %bitcast.20, bf16[8,1,400,128]{3,2,1,0:T(8,128)(2,1)S(1)} %bitcast.19, f32[8,2,4,128]{3,2,1,0:T(4,128)S(1)} %reshape.137.table_ref), custom_call_target="tpu_custom_call" | custom-call | tf_op jit(solution)/shard_map/fourier/pallas_call | solution.py:90
  66.3 1.2 copy-done
  67.4 21.2 %evolve.1 = (s16[8,960,128]{2,1,0:T(8,128)(2,1)}, f32[8,72,128]{2,1,0:T(8,128)S(1)}) custom-call(s32[8]{0:T(128)S(1)} %iota.17.order_ref, f32[8,400,128]{2,1,0:T(8,128)S(1)} %get-tuple-element.31.refs_0_.refs_4_, f32[8,400,128]{2,1,0:T(8,128)S(1)} %get-tuple-element.32.refs_1_.refs_5_, f32[8,400,128]{2,1,0:T(8,128)} %copy-done, ...), custom_call_target="tpu_custom_call" | custom-call | tf_op jit(solution)/shard_map/evolve/pallas_call | solution.py:220
  88.6 13.2 %all_to_all.15 = f32[8,72,128]{2,1,0:T(8,128)S(1)} all-to-all(f32[8,72,128]{2,1,0:T(8,128)S(1)} %get-tuple-element.39), channel_id=1, replica_groups=mesh['space'=64,'freq'=8] {'freq'}, dimensions={0} | all-to-all | bytes 589824 | tf_op jit(solution)/shard_map/all_to_all | solution.py:468
  101.8 5.0 %all-to-all-start.2 = ((s16[8,960,128]{2,1,0:T(8,128)(2,1)}), s16[8,960,128]{2,1,0:T(8,128)(2,1)S(1)}, u32[]{:S(2)}, u32[]{:S(2)}) async-start(s16[8,960,128]{2,1,0:T(8,128)(2,1)} %get-tuple-element.42), calls=%async_computation.2 | async-start | bytes 3932160 | tf_op jit(solution)/shard_map/all_to_all | solution.py:472
  106.8 10.4 %collective-permute-start.6 = (f32[72,128]{1,0:T(8,128)S(1)}, f32[72,128]{1,0:T(8,128)S(1)}, u32[]{:S(2)}, u32[]{:S(2)}) collective-permute-start(f32[72,128]{1,0:T(8,128)S(1)} %reduce_sum.9), channel_id=1, source_target_pairs={{0,8},{8,0},{16,24},{24,16},{32,40},{40,32},{48,56},{56,48},{64,72... | collective-permute-start | bytes 110600 | tf_op jit(solution)/shard_map/ppermute | solution.py:26
  117.2 5.4 %collective-permute-start.5 = (f32[72,128]{1,0:T(8,128)S(1)}, f32[72,128]{1,0:T(8,128)S(1)}, u32[]{:S(2)}, u32[]{:S(2)}) collective-permute-start(f32[72,128]{1,0:T(8,128)S(1)} %reduce_sum.9), channel_id=1, source_target_pairs={{0,24},{8,16},{16,8},{24,0},{32,56},{40,48},{48,40},{56,32},{64,88... | collective-permute-start | bytes 110600 | tf_op jit(solution)/shard_map/ppermute | solution.py:26
  122.6 2.3 %collective-permute-start.4 = (f32[72,128]{1,0:T(8,128)S(1)}, f32[72,128]{1,0:T(8,128)S(1)}, u32[]{:S(2)}, u32[]{:S(2)}) collective-permute-start(f32[72,128]{1,0:T(8,128)S(1)} %reduce_sum.9), channel_id=1, source_target_pairs={{0,16},{8,24},{16,0},{24,8},{32,48},{40,56},{48,32},{56,40},{64,80... | collective-permute-start | bytes 110600 | tf_op jit(solution)/shard_map/ppermute | solution.py:26
  124.9 0.0 collective-permute-done.6
  124.9 3.5 %collective-permute-done.4 = f32[72,128]{1,0:T(8,128)S(1)} collective-permute-done((f32[72,128]{1,0:T(8,128)S(1)}, f32[72,128]{1,0:T(8,128)S(1)}, u32[]{:S(2)}, u32[]{:S(2)}) %collective-permute-start.4) | collective-permute-done | bytes 36896 | tf_op jit(solution)/shard_map/ppermute | solution.py:26
  128.5 7.0 %collective-permute-start.9 = (f32[72,128]{1,0:T(8,128)S(1)}, f32[72,128]{1,0:T(8,128)S(1)}, u32[]{:S(2)}, u32[]{:S(2)}) collective-permute-start(f32[72,128]{1,0:T(8,128)S(1)} %add_add_fusion.1), channel_id=1, source_target_pairs={{0,32},{8,40},{16,48},{24,56},{32,0},{40,8},{48,16},{56,24},{64,96... | collective-permute-start | bytes 110600 | tf_op jit(solution)/shard_map/ppermute | solution.py:26
  135.5 5.9 %collective-permute-start.8 = (f32[72,128]{1,0:T(8,128)S(1)}, f32[72,128]{1,0:T(8,128)S(1)}, u32[]{:S(2)}, u32[]{:S(2)}) collective-permute-start(f32[72,128]{1,0:T(8,128)S(1)} %add_add_fusion.1), channel_id=1, source_target_pairs={{0,96},{8,104},{16,112},{24,120},{32,64},{40,72},{48,80},{56,88},{... | collective-permute-start | bytes 110600 | tf_op jit(solution)/shard_map/ppermute | solution.py:26
  141.4 4.3 %collective-permute-start.7 = (f32[72,128]{1,0:T(8,128)S(1)}, f32[72,128]{1,0:T(8,128)S(1)}, u32[]{:S(2)}, u32[]{:S(2)}) collective-permute-start(f32[72,128]{1,0:T(8,128)S(1)} %add_add_fusion.1), channel_id=1, source_target_pairs={{0,64},{8,72},{16,80},{24,88},{32,96},{40,104},{48,112},{56,120},{... | collective-permute-start | bytes 110600 | tf_op jit(solution)/shard_map/ppermute | solution.py:26
  145.7 0.0 collective-permute-done.9
  145.7 0.0 collective-permute-done.8
  145.7 6.0 %collective-permute-done.7 = f32[72,128]{1,0:T(8,128)S(1)} collective-permute-done((f32[72,128]{1,0:T(8,128)S(1)}, f32[72,128]{1,0:T(8,128)S(1)}, u32[]{:S(2)}, u32[]{:S(2)}) %collective-permute-start.7) | collective-permute-done | bytes 36896 | tf_op jit(solution)/shard_map/ppermute | solution.py:26
  151.7 3.4 %collective-permute-start.12 = (f32[72,128]{1,0:T(8,128)S(1)}, f32[72,128]{1,0:T(8,128)S(1)}, u32[]{:S(2)}, u32[]{:S(2)}) collective-permute-start(f32[72,128]{1,0:T(8,128)S(1)} %add_add_fusion.refs_0_), channel_id=1, source_target_pairs={{0,128},{8,136},{16,144},{24,152},{32,160},{40,168},{48,176},{56,1... | collective-permute-start | bytes 110600 | tf_op jit(solution)/shard_map/ppermute | solution.py:26
  155.1 4.0 %collective-permute-start.11 = (f32[72,128]{1,0:T(8,128)S(1)}, f32[72,128]{1,0:T(8,128)S(1)}, u32[]{:S(2)}, u32[]{:S(2)}) collective-permute-start(f32[72,128]{1,0:T(8,128)S(1)} %add_add_fusion.refs_0_), channel_id=1, source_target_pairs={{0,384},{8,392},{16,400},{24,408},{32,416},{40,424},{48,432},{56,4... | collective-permute-start | bytes 110600 | tf_op jit(solution)/shard_map/ppermute | solution.py:26
  159.1 2.4 %collective-permute-start.10 = (f32[72,128]{1,0:T(8,128)S(1)}, f32[72,128]{1,0:T(8,128)S(1)}, u32[]{:S(2)}, u32[]{:S(2)}) collective-permute-start(f32[72,128]{1,0:T(8,128)S(1)} %add_add_fusion.refs_0_), channel_id=1, source_target_pairs={{0,256},{8,264},{16,272},{24,280},{32,288},{40,296},{48,304},{56,3... | collective-permute-start | bytes 110600 | tf_op jit(solution)/shard_map/ppermute | solution.py:26
  161.5 0.6 collective-permute-done.11.refs_2_
  162.2 4.3 %collective-permute-done.10.refs_1_ = f32[72,128]{1,0:T(8,128)S(1)} collective-permute-done((f32[72,128]{1,0:T(8,128)S(1)}, f32[72,128]{1,0:T(8,128)S(1)}, u32[]{:S(2)}, u32[]{:S(2)}) %collective-permute-start.10) | collective-permute-done | bytes 36896 | tf_op jit(solution)/shard_map/ppermute | solution.py:26
  166.5 0.6 copy-done.9
  167.1 7.7 %factorize.1 = (f32[128,128]{1,0:T(8,128)}, f32[128,128]{1,0:T(8,128)}) custom-call(f32[72,128]{1,0:T(8,128)} %copy-done.6, f32[72,128]{1,0:T(8,128)} %copy-done.9, f32[72,128]{1,0:T(8,128)} %copy-done.8, f32[72,128]{1,0:T(8,128)} %copy-done.7), custom_call_target="tpu_custom_call" | custom-call | tf_op jit(solution)/shard_map/factorize/pallas_call | solution.py:309
  174.8 0.0 all-to-all-done.2.code_ref
  174.8 0.8 copy-done.3
  175.6 4.3 %apply.1 = f32[1,128,5,8,128]{4,3,2,1,0:T(8,128)} custom-call(f32[128,128]{1,0:T(8,128)S(1)} %copy-done.3, f32[8,128]{1,0:T(8,128)S(1)} %bitcast.23, s16[8,960,128]{2,1,0:T(8,128)(2,1)S(1)} %all-to-all-done.2.code_ref), custom_call_target="tpu_custom_call" | custom-call | tf_op jit(solution)/shard_map/apply/pallas_call | solution.py:357
  (33 shorter events, 0.2 us)
Async XLA Ops:
  0.6 1.3 copy-start.1
  5.0 9.4 %copy-start.4 = (f32[8,128]{1,0:T(8,128)S(1)}, f32[8,128]{1,0:T(8,128)}, u32[]{:S(2)}) copy-start(f32[8,128]{1,0:T(8,128)} %velocity_ref) | copy-start | bytes 12292
  5.0 9.5 %copy-start.2 = (f32[5,5,8,128]{3,2,1,0:T(8,128)S(1)}, f32[5,5,8,128]{3,2,1,0:T(8,128)}, u32[]{:S(2)}) copy-start(f32[5,5,8,128]{3,2,1,0:T(8,128)} %param.5) | copy-start | bytes 307204
  5.0 13.9 %copy-start.10 = (s32[8]{0:T(128)S(1)}, s32[8]{0:T(128)}, u32[]{:S(2)}) copy-start(s32[8]{0:T(128)} %param.7) | copy-start | bytes 100
  5.0 47.6 %all-to-all-start = ((bf16[8,2,400,128]{3,2,1,0:T(8,128)(2,1)}), bf16[8,2,400,128]{3,2,1,0:T(8,128)(2,1)S(1)}, u32[]{:S(2)}, u32[]{:S(2)}) async-start(bf16[8,2,400,128]{3,2,1,0:T(8,128)(2,1)} %spread.1), calls=%async_computation | async-start | bytes 3276800 | tf_op jit(solution)/shard_map/all_to_all | solution.py:451
  14.5 5.0 %collective-permute-start = (f32[26,2,128]{2,1,0:T(2,128)S(1)}, f32[26,2,128]{2,1,0:T(2,128)S(1)}, u32[]{:S(2)}, u32[]{:S(2)}) collective-permute-start(f32[26,2,128]{2,1,0:T(2,128)S(1)} %pad_maximum_fusion), channel_id=1, source_target_pairs={{8,0},{16,8},{24,16},{32,24},{40,32},{48,40},{56,48},{64,56},{72,6... | collective-permute-start | bytes 79880 | tf_op jit(solution)/shard_map/ppermute | solution.py:425
  15.9 3.9 %collective-permute-start.1 = (f32[26,2,128]{2,1,0:T(2,128)S(1)}, f32[26,2,128]{2,1,0:T(2,128)S(1)}, u32[]{:S(2)}, u32[]{:S(2)}) collective-permute-start(f32[26,2,128]{2,1,0:T(2,128)S(1)} %pad_maximum_fusion.1), channel_id=1, source_target_pairs={{0,8},{8,16},{16,24},{24,32},{32,40},{40,48},{48,56},{56,64},{64,7... | collective-permute-start | bytes 79880 | tf_op jit(solution)/shard_map/ppermute | solution.py:426
  52.6 1.2 copy-start.5
  53.8 7.3 %collective-permute-start.3 = (bf16[8,400,128]{2,1,0:T(8,128)(2,1)S(1)}, bf16[8,400,128]{2,1,0:T(8,128)(2,1)S(1)}, u32[]{:S(2)}, u32[]{:S(2)}) collective-permute-start(bf16[8,400,128]{2,1,0:T(8,128)(2,1)S(1)} %get-tuple-element.44), channel_id=1, source_target_pairs={{0,8},{8,16},{16,24},{24,32},{32,40},{40,48},{48,56},{56,64},{64,7... | collective-permute-start | bytes 2457608 | tf_op jit(solution)/shard_map/ppermute | solution.py:463
  55.1 6.8 %collective-permute-start.2 = (bf16[8,400,128]{2,1,0:T(8,128)(2,1)S(1)}, bf16[8,400,128]{2,1,0:T(8,128)(2,1)S(1)}, u32[]{:S(2)}, u32[]{:S(2)}) collective-permute-start(bf16[8,400,128]{2,1,0:T(8,128)(2,1)S(1)} %get-tuple-element.45), channel_id=1, source_target_pairs={{8,0},{16,8},{24,16},{32,24},{40,32},{48,40},{56,48},{64,56},{72,6... | collective-permute-start | bytes 2457608 | tf_op jit(solution)/shard_map/ppermute | solution.py:462
  66.3 1.2 copy-start
  101.8 73.0 %all-to-all-start.2 = ((s16[8,960,128]{2,1,0:T(8,128)(2,1)}), s16[8,960,128]{2,1,0:T(8,128)(2,1)S(1)}, u32[]{:S(2)}, u32[]{:S(2)}) async-start(s16[8,960,128]{2,1,0:T(8,128)(2,1)} %get-tuple-element.42), calls=%async_computation.2 | async-start | bytes 3932160 | tf_op jit(solution)/shard_map/all_to_all | solution.py:472
  106.8 18.1 %collective-permute-start.6 = (f32[72,128]{1,0:T(8,128)S(1)}, f32[72,128]{1,0:T(8,128)S(1)}, u32[]{:S(2)}, u32[]{:S(2)}) collective-permute-start(f32[72,128]{1,0:T(8,128)S(1)} %reduce_sum.9), channel_id=1, source_target_pairs={{0,8},{8,0},{16,24},{24,16},{32,40},{40,32},{48,56},{56,48},{64,72... | collective-permute-start | bytes 110600 | tf_op jit(solution)/shard_map/ppermute | solution.py:26
  117.2 7.7 %collective-permute-start.5 = (f32[72,128]{1,0:T(8,128)S(1)}, f32[72,128]{1,0:T(8,128)S(1)}, u32[]{:S(2)}, u32[]{:S(2)}) collective-permute-start(f32[72,128]{1,0:T(8,128)S(1)} %reduce_sum.9), channel_id=1, source_target_pairs={{0,24},{8,16},{16,8},{24,0},{32,56},{40,48},{48,40},{56,32},{64,88... | collective-permute-start | bytes 110600 | tf_op jit(solution)/shard_map/ppermute | solution.py:26
  122.6 5.9 %collective-permute-start.4 = (f32[72,128]{1,0:T(8,128)S(1)}, f32[72,128]{1,0:T(8,128)S(1)}, u32[]{:S(2)}, u32[]{:S(2)}) collective-permute-start(f32[72,128]{1,0:T(8,128)S(1)} %reduce_sum.9), channel_id=1, source_target_pairs={{0,16},{8,24},{16,0},{24,8},{32,48},{40,56},{48,32},{56,40},{64,80... | collective-permute-start | bytes 110600 | tf_op jit(solution)/shard_map/ppermute | solution.py:26
  128.5 17.2 %collective-permute-start.9 = (f32[72,128]{1,0:T(8,128)S(1)}, f32[72,128]{1,0:T(8,128)S(1)}, u32[]{:S(2)}, u32[]{:S(2)}) collective-permute-start(f32[72,128]{1,0:T(8,128)S(1)} %add_add_fusion.1), channel_id=1, source_target_pairs={{0,32},{8,40},{16,48},{24,56},{32,0},{40,8},{48,16},{56,24},{64,96... | collective-permute-start | bytes 110600 | tf_op jit(solution)/shard_map/ppermute | solution.py:26
  135.5 10.2 %collective-permute-start.8 = (f32[72,128]{1,0:T(8,128)S(1)}, f32[72,128]{1,0:T(8,128)S(1)}, u32[]{:S(2)}, u32[]{:S(2)}) collective-permute-start(f32[72,128]{1,0:T(8,128)S(1)} %add_add_fusion.1), channel_id=1, source_target_pairs={{0,96},{8,104},{16,112},{24,120},{32,64},{40,72},{48,80},{56,88},{... | collective-permute-start | bytes 110600 | tf_op jit(solution)/shard_map/ppermute | solution.py:26
  141.4 10.3 %collective-permute-start.7 = (f32[72,128]{1,0:T(8,128)S(1)}, f32[72,128]{1,0:T(8,128)S(1)}, u32[]{:S(2)}, u32[]{:S(2)}) collective-permute-start(f32[72,128]{1,0:T(8,128)S(1)} %add_add_fusion.1), channel_id=1, source_target_pairs={{0,64},{8,72},{16,80},{24,88},{32,96},{40,104},{48,112},{56,120},{... | collective-permute-start | bytes 110600 | tf_op jit(solution)/shard_map/ppermute | solution.py:26
  151.7 14.8 %copy-start.6 = (f32[72,128]{1,0:T(8,128)}, f32[72,128]{1,0:T(8,128)S(1)}, u32[]{:S(2)}) copy-start(f32[72,128]{1,0:T(8,128)S(1)} %add_add_fusion.refs_0_) | copy-start | bytes 110596
  151.7 9.9 %collective-permute-start.12 = (f32[72,128]{1,0:T(8,128)S(1)}, f32[72,128]{1,0:T(8,128)S(1)}, u32[]{:S(2)}, u32[]{:S(2)}) collective-permute-start(f32[72,128]{1,0:T(8,128)S(1)} %add_add_fusion.refs_0_), channel_id=1, source_target_pairs={{0,128},{8,136},{16,144},{24,152},{32,160},{40,168},{48,176},{56,1... | collective-permute-start | bytes 110600 | tf_op jit(solution)/shard_map/ppermute | solution.py:26
  155.1 7.1 %collective-permute-start.11 = (f32[72,128]{1,0:T(8,128)S(1)}, f32[72,128]{1,0:T(8,128)S(1)}, u32[]{:S(2)}, u32[]{:S(2)}) collective-permute-start(f32[72,128]{1,0:T(8,128)S(1)} %add_add_fusion.refs_0_), channel_id=1, source_target_pairs={{0,384},{8,392},{16,400},{24,408},{32,416},{40,424},{48,432},{56,4... | collective-permute-start | bytes 110600 | tf_op jit(solution)/shard_map/ppermute | solution.py:26
  159.1 7.4 %collective-permute-start.10 = (f32[72,128]{1,0:T(8,128)S(1)}, f32[72,128]{1,0:T(8,128)S(1)}, u32[]{:S(2)}, u32[]{:S(2)}) collective-permute-start(f32[72,128]{1,0:T(8,128)S(1)} %add_add_fusion.refs_0_), channel_id=1, source_target_pairs={{0,256},{8,264},{16,272},{24,280},{32,288},{40,296},{48,304},{56,3... | collective-permute-start | bytes 110600 | tf_op jit(solution)/shard_map/ppermute | solution.py:26
  161.5 4.9 %copy-start.7 = (f32[72,128]{1,0:T(8,128)}, f32[72,128]{1,0:T(8,128)S(1)}, u32[]{:S(2)}) copy-start(f32[72,128]{1,0:T(8,128)S(1)} %collective-permute-done.12.refs_3_) | copy-start | bytes 110596
  162.2 4.3 %copy-start.8 = (f32[72,128]{1,0:T(8,128)}, f32[72,128]{1,0:T(8,128)S(1)}, u32[]{:S(2)}) copy-start(f32[72,128]{1,0:T(8,128)S(1)} %collective-permute-done.11.refs_2_) | copy-start | bytes 110596
  166.5 0.6 copy-start.9
  174.8 0.8 copy-start.3

commit v6 on v5

--- a/solution.py
+++ b/solution.py
@@ -16,14 +16,16 @@
 VISCOSITY = 0.5
 LANES = 2 * K
 HALF = 4
+SPACE = ("chip", "core")
 RH = 2
-VMEM_LIMIT = 50 * 1024 * 1024
-
-
-def quad_sum(value, axis, bit):
+VMEM_LIMIT = 28 * 1024 * 1024
+
+
+def xor_sum(value, axis, masks):
     count = lax.axis_size(axis)
-    others = [m << bit for m in (2, 3, 1)]
-    return [value] + [lax.ppermute(value, axis, [(i, i ^ m) for i in range(count)]) for m in others]
+    for other in [lax.ppermute(value, axis, [(i, i ^ m) for i in range(count)]) for m in masks]:
+        value = value + other
+    return value
 
 
 def spread_body(sketch_ref, out_ref, rows_ref, turned_ref):
@@ -67,33 +69,39 @@
     size = pair_ref.shape[2]
     first = lax.broadcasted_iota(jnp.int32, (8, LANES), 1) < K
     for rows_ref, z_ref in ((one_ref, z_one), (two_ref, z_two)):
-        for d in range(4):
-            a = rows_ref[d, 0].astype(jnp.float32)
-            b = rows_ref[d + 4, 0].astype(jnp.float32)
-            pair_ref[0, d] = a + b
-            pair_ref[1, d] = a - b
-        for f in range(F):
-            parity = parity_ref[f]
-            wave = [[jnp.broadcast_to(table_ref[f, c, d : d + 1], (8, LANES)) for d in range(4)] for c in range(2)]
-            for line in range(0, size, 8):
-                p = [pair_ref[parity, d, line : line + 8] for d in range(4)]
-                u = (p[0] * wave[0][0] + p[1] * wave[0][1]) + (p[2] * wave[0][2] + p[3] * wave[0][3])
-                v = (p[0] * wave[1][0] + p[1] * wave[1][1]) + (p[2] * wave[1][2] + p[3] * wave[1][3])
-                z_ref[f, line : line + 8, :] = jnp.where(first, u, v) + pltpu.roll(jnp.where(first, v, u), K, 1)
+
+        @pl.loop(0, rows_ref.shape[2] // size)
+        def _(step):
+            start = pl.multiple_of(step * size, size)
+            for d in range(4):
+                a = rows_ref[d, 0, pl.ds(start, size), :].astype(jnp.float32)
+                b = rows_ref[d + 4, 0, pl.ds(start, size), :].astype(jnp.float32)
+                pair_ref[0, d] = a + b
+                pair_ref[1, d] = a - b
+            for f in range(F):
+                parity = parity_ref[f]
+                wave = [[jnp.broadcast_to(table_ref[f, c, d : d + 1], (8, LANES)) for d in range(4)] for c in range(2)]
+                for line in range(0, size, 8):
+                    p = [pair_ref[parity, d, line : line + 8] for d in range(4)]
+                    u = (p[0] * wave[0][0] + p[1] * wave[0][1]) + (p[2] * wave[0][2] + p[3] * wave[0][3])
+                    v = (p[0] * wave[1][0] + p[1] * wave[1][1]) + (p[2] * wave[1][2] + p[3] * wave[1][3])
+                    z_ref[f, pl.ds(start + line, 8), :] = jnp.where(first, u, v) + pltpu.roll(
+                        jnp.where(first, v, u), K, 1
+                    )
 
 
 def fourier(parity, one, two, table, parts):
     slots, _, count, _ = one.shape
     size = count // FIELDS
-    z_spec = pl.BlockSpec((F, size, LANES), lambda i: (0, i, 0))
+    z_spec = pl.BlockSpec((F, count, LANES), lambda i: (0, 0, 0))
     z_shape = jax.ShapeDtypeStruct((F, count, LANES), jnp.float32)
     return pl.pallas_call(
         fourier_body,
-        grid=(FIELDS,),
+        grid=(1,),
         in_specs=[
             pl.BlockSpec(memory_space=pltpu.SMEM),
-            pl.BlockSpec((slots, 1, size, LANES), lambda i: (0, parts[0], i, 0)),
-            pl.BlockSpec((slots, 1, size, LANES), lambda i: (0, parts[1], i, 0)),
+            pl.BlockSpec((slots, 1, count, LANES), lambda i: (0, parts[0], 0, 0)),
+            pl.BlockSpec((slots, 1, count, LANES), lambda i: (0, parts[1], 0, 0)),
             pl.BlockSpec(table.shape, lambda i: (0, 0, 0, 0)),
         ],
         out_specs=[z_spec, z_spec],
@@ -115,22 +123,28 @@
     return (number >> 8).astype(jnp.int16), both.astype(jnp.int16)
 
 
-def pack(gram, ref, n):
+HALF_ROWS = K // 2 + 8
+
+
+def pack(gram, scale, ref, n):
     line = lax.broadcasted_iota(jnp.int32, (K, LANES), 0)
     lane = lax.broadcasted_iota(jnp.int32, (K, LANES), 1)
     last = pltpu.roll(gram[K:], K, 1)
-    ref[n, 0:K, :] = jnp.where(lane >= line, gram[:K], last)
+    both = jnp.where(lane >= line, gram[:K], last)
     diagonal = jnp.sum(jnp.where(lane == line, last, 0.0), axis=0, keepdims=True)
-    ref[n, K : K + 8, :] = jnp.broadcast_to(diagonal, (8, LANES))
-
-
-def unpack(packed):
+    sub = lax.broadcasted_iota(jnp.int32, (8, LANES), 0)
+    for h in range(2):
+        ref[n, h, 0 : K // 2, :] = both[h * K // 2 : (h + 1) * K // 2]
+        ref[n, h, K // 2 :, :] = jnp.where(sub == 0, diagonal, scale)
+
+
+def unpack(one, two):
     line = lax.broadcasted_iota(jnp.int32, (K, LANES), 0)
     lane = lax.broadcasted_iota(jnp.int32, (K, LANES), 1)
-    top = packed[:K]
+    top = jnp.concatenate([one[: K // 2], two[: K // 2]], axis=0)
     last = pltpu.roll(jnp.where(lane < line, top, 0.0), K, 1)
     half = jnp.concatenate([jnp.where(lane >= line, top, 0.0), last], axis=0)
-    diagonal = pltpu.roll(jnp.broadcast_to(packed[K : K + 1], (8, LANES)), K, 1)
+    diagonal = pltpu.roll(jnp.broadcast_to(one[K // 2 : K // 2 + 1], (8, LANES)), K, 1)
     diagonal = jnp.concatenate([top] + [diagonal] * (K // 8), axis=0)
     line = lax.broadcasted_iota(jnp.int32, (LANES, LANES), 0)
     lane = lax.broadcasted_iota(jnp.int32, (LANES, LANES), 1)
@@ -203,9 +217,8 @@
             block, block, (((0,), (0,)), ((), ())),
             precision=lax.Precision.HIGHEST, preferred_element_type=jnp.float32,
         )
-        pack(gram, gram_ref, n)
         scale = jnp.maximum(jnp.max(jnp.abs(block), axis=0, keepdims=True), 1e-30)
-        gram_ref[n, K + 1 : K + 2, :] = scale
+        pack(gram, scale, gram_ref, n)
         count = block.shape[0]
         code_ref[n, 0:count, :], code_ref[n, count : count + count // 2, :] = encode(block, scale)
 
@@ -226,7 +239,7 @@
             + [whole(coef.shape), whole(mask.shape), pick((8, LANES), 0), pick((8, LANES), 1)],
             out_specs=[
                 pl.BlockSpec((2, FIELDS * 12 * per, LANES), lambda i, order: (i, 0, 0)),
-                pl.BlockSpec((2, K + 8, LANES), lambda i, order: (i, 0, 0)),
+                pl.BlockSpec((2, 2, HALF_ROWS, LANES), lambda i, order: (i, 0, 0, 0)),
             ],
             scratch_shapes=[
                 pltpu.VMEM((2, FIELDS, per + 2 * RH, 2, 8, LANES), jnp.float32),
@@ -236,7 +249,7 @@
         ),
         out_shape=[
             jax.ShapeDtypeStruct((count, FIELDS * 12 * per, LANES), jnp.int16),
-            jax.ShapeDtypeStruct((count, K + 8, LANES), jnp.float32),
+            jax.ShapeDtypeStruct((count, 2, HALF_ROWS, LANES), jnp.float32),
         ],
         compiler_params=pltpu.CompilerParams(vmem_limit_bytes=VMEM_LIMIT),
         name="evolve",
@@ -249,7 +262,7 @@
     blocks = LANES // 8
     lane = lax.broadcasted_iota(jnp.int32, (8, LANES), 1)
     sub = lax.broadcasted_iota(jnp.int32, (8, LANES), 0)
-    gram = unpack(sum(ref[...] for ref in parts))
+    gram = unpack(parts[0][...], parts[1][...])
     w = [gram[8 * b : 8 * b + 8] for b in range(blocks)]
     full = lambda v: jnp.broadcast_to(v, (8, LANES))
     for b in range(blocks):
@@ -415,15 +428,15 @@
 
 
 def stencil(coupling, velocity, per):
-    count = lax.axis_size("space")
-    mine = lax.axis_index("space")
+    count = lax.axis_size(SPACE)
+    mine = lax.axis_index(SPACE)
     radial = velocity.shape[1]
     up = [(i, i + 1) for i in range(count - 1)]
     down = [(i + 1, i) for i in range(count - 1)]
     coupling = coupling.reshape(FIELDS * FIELDS, 8, radial)
     edges = [jnp.concatenate([coupling[:, s], velocity[None, s]], axis=0) for s in (slice(0, 2), slice(6, 8))]
-    right = lax.ppermute(edges[0], "space", down)
-    left = lax.ppermute(edges[1], "space", up)
+    right = lax.ppermute(edges[0], SPACE, down)
+    left = lax.ppermute(edges[1], SPACE, up)
     place = jnp.stack([lax.axis_index("freq") * per, (mine > 0).astype(jnp.int32), (mine < count - 1).astype(jnp.int32)])
     vmem = pl.BlockSpec(memory_space=pltpu.VMEM)
     return pl.pallas_call(
@@ -441,7 +454,7 @@
 
 def local(sketch, coupling, velocity, freq_index):
     groups = lax.axis_size("freq")
-    count = lax.axis_size("space")
+    count = lax.axis_size(SPACE)
     radial = sketch.shape[4]
     per = radial // groups
     mine = lax.axis_index("freq")
@@ -459,35 +472,44 @@
     coef, mask = stencil(coupling, velocity, per)
 
     rows, coef, mask, turn, waves, parity = lax.optimization_barrier((rows, coef, mask, turn, waves, parity))
-    right = lax.ppermute(rows[:, 0], "space", [(i + 1, i) for i in range(count - 1)])
-    left = lax.ppermute(rows[:, 1], "space", [(i, i + 1) for i in range(count - 1)])
+    right = lax.ppermute(rows[:, 0], SPACE, [(i + 1, i) for i in range(count - 1)])
+    left = lax.ppermute(rows[:, 1], SPACE, [(i, i + 1) for i in range(count - 1)])
     low, high = fourier(parity, rows, rows, waves, (0, 1))
     right, left = fourier(parity, right[:, None], left[:, None], waves, (0, 0))
 
     columns, grams = evolve(jnp.arange(F, dtype=jnp.int32), low, high, right, left, coef, mask, turn)
-    parts = lax.all_to_all(grams, "freq", split_axis=0, concat_axis=0, tiled=True)
+    core = lax.axis_index("core")
+    grams = grams.reshape(groups * 2, HALF_ROWS, LANES)
+    parts = lax.all_to_all(grams, ("freq", "core"), split_axis=0, concat_axis=0, tiled=True)
     gram = jnp.sum(parts, axis=0)
-    scales = parts[:, K + 1]
+    parts = parts.reshape(groups, 2, HALF_ROWS, LANES)[:, :, K // 2 + 1]
+    scales = jnp.where(core == 0, parts[:, 0], parts[:, 1])
     columns, gram = lax.optimization_barrier((columns, gram))
     columns = lax.all_to_all(columns, "freq", split_axis=0, concat_axis=0, tiled=True)
-    for bit in (0, 2, 4):
-        parts = quad_sum(gram, "space", bit)
-        gram = sum(parts)
+    gram = xor_sum(gram, "chip", (16, 8, 24))
+    gram = xor_sum(gram, "chip", (2, 1, 3))
+    gram = xor_sum(gram, "chip", (4,))
+    other = lax.ppermute(gram, "core", [(0, 1), (1, 0)])
+    parts = [jnp.where(core == 0, gram, other), jnp.where(core == 0, other, gram)]
     row_scale = math.sqrt(FIELDS * 8 * count * radial)
     inverse, factor = factorize(parts, row_scale)
     return apply(inverse, scales, columns), factor[None]
 
 
 def solution(mesh):
+    devices = mesh.devices
+    split_mesh = jax.sharding.Mesh(
+        devices.reshape(devices.shape[0] // 2, 2, devices.shape[1]), ("chip", "core", "freq")
+    )
     return jax.shard_map(
         local,
-        mesh=mesh,
+        mesh=split_mesh,
         in_specs=(
-            P("freq", None, None, "space", None),
-            P(None, None, "space", None),
-            P("space", None),
+            P("freq", None, None, SPACE, None),
+            P(None, None, SPACE, None),
+            P(SPACE, None),
             P(),
         ),
-        out_specs=(P("freq", None, None, "space", None), P("freq", None, None)),
+        out_specs=(P("freq", None, None, SPACE, None), P("freq", None, None)),
         check_vma=False,
     )

time: 181 us -> 172 us (0.950)
  the two profiles are of different devices: /device:TPU:8 before, /device:TPU:1 now
where the time goes in v6:
time: 172 us
  starting transfers between devices  57.4 us (33%)
  waiting for transfers between devices  46.4 us (27%)
  Pallas kernels  45 us (26%)
  blocking collectives  14.9 us (9%)
  local copies, waits for them, and re-layouts  5.93 us (3%)
    ppermute x7, starting transfers between devices, xor_sum(): lax.ppermute(value, axis, [(i, i ^ m) for i in range(count)])  28.3 us
    all_to_all x1, waiting for transfers between devices, local(): rows = lax.all_to_all(rows, 'freq', split_axis=0, concat_axis=0, tiled=True)  26.1 us
    pallas_call x1, Pallas kernels, evolve(): pl.pallas_call(evolve_body, grid_spec=pltpu.PrefetchScalarGridSpec(num_sc...  17.7 us
    all_to_all x1, blocking collectives, local(): lax.all_to_all(grams, ('freq', 'core'), split_axis=0, concat_axis=0, tile...  14.9 us
    ppermute x7, waiting for transfers between devices, xor_sum(): lax.ppermute(value, axis, [(i, i ^ m) for i in range(count)])  10.7 us
    all_to_all x1, starting transfers between devices, local(): rows = lax.all_to_all(rows, 'freq', split_axis=0, concat_axis=0, tiled=True)  7.78 us
    pallas_call x1, Pallas kernels, factorize(): pl.pallas_call(partial(factor_body, scale), in_specs=[vmem] * len(parts),...  7.64 us
    pallas_call x2, Pallas kernels, fourier(): pl.pallas_call(fourier_body, grid=(1,), in_specs=[pl.BlockSpec(memory_spa...  6.49 us
  transfers between devices with their start and end apart: 14, of which 9 were waited for; matrix products, arithmetic and copies ran while one was open for 1% of the time, Pallas kernels for 10%

profile of v6, /device:TPU:1, one launch (start us, length us, event | category | flops | bytes accessed | tf_op | source)
XLA Modules:
  0.0 171.6 jit_solution(7564029173283174883)
XLA Ops:
  0.6 1.3 copy-done.3
  1.9 3.1 %spread.1 = bf16[8,2,400,128]{3,2,1,0:T(8,128)(2,1)} custom-call(bf16[2,64,5,8,128]{4,3,2,1,0:T(8,128)(2,1)S(1)} %copy-done.3), custom_call_target="tpu_custom_call" | custom-call | tf_op jit(solution)/shard_map/spread/pallas_call | solution.py:53
  5.0 7.8 %all-to-all-start = ((bf16[8,2,400,128]{3,2,1,0:T(8,128)(2,1)}), bf16[8,2,400,128]{3,2,1,0:T(8,128)(2,1)S(1)}, u32[]{:S(2)}, u32[]{:S(2)}) async-start(bf16[8,2,400,128]{3,2,1,0:T(8,128)(2,1)} %spread.1), calls=%async_computation | async-start | bytes 3276800 | tf_op jit(solution)/shard_map/all_to_all | solution.py:464
  12.9 4.7 %collective-permute-start = (f32[26,2,128]{2,1,0:T(2,128)S(1)}, f32[26,2,128]{2,1,0:T(2,128)S(1)}, u32[]{:S(2)}, u32[]{:S(2)}) collective-permute-start(f32[26,2,128]{2,1,0:T(2,128)S(1)} %pad_maximum_fusion), channel_id=1, source_target_pairs={{8,0},{16,8},{24,16},{32,24},{40,32},{48,40},{56,48},{64,56},{72,6... | collective-permute-start | bytes 79880 | tf_op jit(solution)/shard_map/ppermute | solution.py:438
  17.7 2.0 %collective-permute-start.1 = (f32[26,2,128]{2,1,0:T(2,128)S(1)}, f32[26,2,128]{2,1,0:T(2,128)S(1)}, u32[]{:S(2)}, u32[]{:S(2)}) collective-permute-start(f32[26,2,128]{2,1,0:T(2,128)S(1)} %pad_maximum_fusion.1), channel_id=1, source_target_pairs={{0,8},{8,16},{16,24},{24,32},{32,40},{40,48},{48,56},{56,64},{64,7... | collective-permute-start | bytes 79880 | tf_op jit(solution)/shard_map/ppermute | solution.py:439
  19.7 0.1 fusion.7
  19.8 0.1 broadcast_multiply_fusion
  19.9 0.1 pad_add_fusion.place_ref
  20.0 0.1 copy.17
  20.1 0.1 broadcast_in_dim.41
  20.2 0.1 reshape.145.table_ref
  20.4 0.0 collective-permute-done.right_ref
  20.4 0.4 collective-permute-done.1.left_ref
  20.8 5.8 %stencil.1 = (f32[29,18,2,8,128]{4,3,2,1,0:T(8,128)S(1)}, f32[18,2,8,128]{3,2,1,0:T(8,128)S(1)}) custom-call(s32[3]{0:T(128)S(1)} %pad_add_fusion.place_ref, f32[25,8,128]{2,1,0:T(8,128)S(1)} %bitcast.27, f32[8,128]{1,0:T(8,128)S(1)} %copy-done.6, f32[26,2,128]{2,1,0:T(2,128)S(1)} %collective-permute-done.right_ref, ...), custom_call_target="tpu_custom_call" | custom-call | tf_op jit(solution)/shard_map/stencil/pallas_call | solution.py:442
  26.6 2.0 %copy-done = f32[29,18,2,8,128]{4,3,2,1,0:T(8,128)} copy-done((f32[29,18,2,8,128]{4,3,2,1,0:T(8,128)}, f32[29,18,2,8,128]{4,3,2,1,0:T(8,128)S(1)}, u32[]{:S(2)}) %copy-start) | copy-done | bytes 4276248
  28.6 26.1 %all-to-all-done.one_ref.two_ref = bf16[8,2,400,128]{3,2,1,0:T(8,128)(2,1)S(1)} async-done(((bf16[8,2,400,128]{3,2,1,0:T(8,128)(2,1)}), bf16[8,2,400,128]{3,2,1,0:T(8,128)(2,1)S(1)}, u32[]{:S(2)}, u32[]{:S(2)}) %all-to-all-start) | async-done | bytes 1638432 | tf_op jit(solution)/shard_map/all_to_all | solution.py:464
  54.7 0.1 slice_bitcast_fusion
  54.8 4.4 %collective-permute-start.3 = (bf16[8,400,128]{2,1,0:T(8,128)(2,1)S(1)}, bf16[8,400,128]{2,1,0:T(8,128)(2,1)S(1)}, u32[]{:S(2)}, u32[]{:S(2)}) collective-permute-start(bf16[8,400,128]{2,1,0:T(8,128)(2,1)S(1)} %get-tuple-element.44), channel_id=1, source_target_pairs={{0,8},{8,16},{16,24},{24,32},{32,40},{40,48},{48,56},{56,64},{64,7... | collective-permute-start | bytes 2457608 | tf_op jit(solution)/shard_map/ppermute | solution.py:476
  59.2 1.9 %collective-permute-start.2 = (bf16[8,400,128]{2,1,0:T(8,128)(2,1)S(1)}, bf16[8,400,128]{2,1,0:T(8,128)(2,1)S(1)}, u32[]{:S(2)}, u32[]{:S(2)}) collective-permute-start(bf16[8,400,128]{2,1,0:T(8,128)(2,1)S(1)} %get-tuple-element.45), channel_id=1, source_target_pairs={{8,0},{16,8},{24,16},{32,24},{40,32},{48,40},{56,48},{64,56},{72,6... | collective-permute-start | bytes 2457608 | tf_op jit(solution)/shard_map/ppermute | solution.py:475
  61.1 3.2 %fourier.2 = (f32[8,400,128]{2,1,0:T(8,128)S(1)}, f32[8,400,128]{2,1,0:T(8,128)S(1)}) custom-call(s32[8]{0:T(128)S(1)} %and_select_fusion.parity_ref, bf16[8,2,400,128]{3,2,1,0:T(8,128)(2,1)S(1)} %all-to-all-done.one_ref.two_ref, bf16[8,2,400,128]{3,2,1,0:T(8,128)(2,1)S(1)} %all-to-all-done.one_ref.two_ref, f32[8,2,4,128]{3,2,1,0:T(4,128)S(1)} %reshape.145.table_ref), custom_call_target="tpu_custom_call" | custom-call | tf_op jit(solution)/shard_map/fourier/pallas_call | solution.py:98
  64.3 4.1 %collective-permute-done.3 = bf16[8,400,128]{2,1,0:T(8,128)(2,1)S(1)} collective-permute-done((bf16[8,400,128]{2,1,0:T(8,128)(2,1)S(1)}, bf16[8,400,128]{2,1,0:T(8,128)(2,1)S(1)}, u32[]{:S(2)}, u32[]{:S(2)}) %collective-permute-start.3) | collective-permute-done | bytes 819232 | tf_op jit(solution)/shard_map/ppermute | solution.py:476
  68.4 4.4 %collective-permute-done.2 = bf16[8,400,128]{2,1,0:T(8,128)(2,1)S(1)} collective-permute-done((bf16[8,400,128]{2,1,0:T(8,128)(2,1)S(1)}, bf16[8,400,128]{2,1,0:T(8,128)(2,1)S(1)}, u32[]{:S(2)}, u32[]{:S(2)}) %collective-permute-start.2) | collective-permute-done | bytes 819232 | tf_op jit(solution)/shard_map/ppermute | solution.py:475
  72.8 3.2 %fourier.3 = (f32[8,400,128]{2,1,0:T(8,128)S(1)}, f32[8,400,128]{2,1,0:T(8,128)S(1)}) custom-call(s32[8]{0:T(128)S(1)} %and_select_fusion.parity_ref, bf16[8,1,400,128]{3,2,1,0:T(8,128)(2,1)S(1)} %bitcast.24, bf16[8,1,400,128]{3,2,1,0:T(8,128)(2,1)S(1)} %bitcast.23, f32[8,2,4,128]{3,2,1,0:T(4,128)S(1)} %reshape.145.table_ref), custom_call_target="tpu_custom_call" | custom-call | tf_op jit(solution)/shard_map/fourier/pallas_call | solution.py:98
  76.1 17.7 %evolve.1 = (s16[8,960,128]{2,1,0:T(8,128)(2,1)S(1)}, f32[8,2,40,128]{3,2,1,0:T(8,128)S(1)}) custom-call(s32[8]{0:T(128)S(1)} %iota.17.order_ref, f32[8,400,128]{2,1,0:T(8,128)S(1)} %get-tuple-element.31.refs_0_.refs_4_, f32[8,400,128]{2,1,0:T(8,128)S(1)} %get-tuple-element.32.refs_1_.refs_5_, f32[8,400,128]{2,1,0:T(8,128)S(1)} %get-tuple-element.33.refs_2_.refs_6_, ...), custom_call_target="tpu_custom_call" | custom-call | tf_op jit(solution)/shard_map/evolve/pallas_call | solution.py:233
  93.8 0.0 copy-start.2
  93.8 1.3 copy-done.2
  95.1 14.9 %all_to_all.15 = f32[16,40,128]{2,1,0:T(8,128)S(1)} all-to-all(f32[16,40,128]{2,1,0:T(8,128)S(1)} %bitcast.25), channel_id=1, replica_groups=mesh['chip'=32,'core'=2,'freq'=8] {'freq','core'}, dimensions={0} | all-to-all | bytes 655360 | tf_op jit(solution)/shard_map/all_to_all | solution.py:483
  110.0 3.6 %all-to-all-start.2 = ((s16[8,960,128]{2,1,0:T(8,128)(2,1)}), s16[8,960,128]{2,1,0:T(8,128)(2,1)S(1)}, u32[]{:S(2)}, u32[]{:S(2)}) async-start(s16[8,960,128]{2,1,0:T(8,128)(2,1)} %copy-done.2), calls=%async_computation.2 | async-start | bytes 3932160 | tf_op jit(solution)/shard_map/all_to_all | solution.py:488
  113.6 9.0 %collective-permute-start.6 = (f32[40,128]{1,0:T(8,128)S(1)}, f32[40,128]{1,0:T(8,128)S(1)}, u32[]{:S(2)}, u32[]{:S(2)}) collective-permute-start(f32[40,128]{1,0:T(8,128)S(1)} %reduce_sum.9), channel_id=1, source_target_pairs={{0,384},{16,400},{32,416},{48,432},{64,448},{80,464},{96,480},{112... | collective-permute-start | bytes 61448 | tf_op jit(solution)/shard_map/ppermute | solution.py:26
  122.6 1.9 %collective-permute-start.5 = (f32[40,128]{1,0:T(8,128)S(1)}, f32[40,128]{1,0:T(8,128)S(1)}, u32[]{:S(2)}, u32[]{:S(2)}) collective-permute-start(f32[40,128]{1,0:T(8,128)S(1)} %reduce_sum.9), channel_id=1, source_target_pairs={{0,128},{16,144},{32,160},{48,176},{64,192},{80,208},{96,224},{112... | collective-permute-start | bytes 61448 | tf_op jit(solution)/shard_map/ppermute | solution.py:26
  124.6 3.1 %collective-permute-start.4 = (f32[40,128]{1,0:T(8,128)S(1)}, f32[40,128]{1,0:T(8,128)S(1)}, u32[]{:S(2)}, u32[]{:S(2)}) collective-permute-start(f32[40,128]{1,0:T(8,128)S(1)} %reduce_sum.9), channel_id=1, source_target_pairs={{0,256},{16,272},{32,288},{48,304},{64,320},{80,336},{96,352},{112... | collective-permute-start | bytes 61448 | tf_op jit(solution)/shard_map/ppermute | solution.py:26
  127.7 0.0 collective-permute-done.6
  127.7 0.0 collective-permute-done.5
  127.7 3.3 %collective-permute-done.4 = f32[40,128]{1,0:T(8,128)S(1)} collective-permute-done((f32[40,128]{1,0:T(8,128)S(1)}, f32[40,128]{1,0:T(8,128)S(1)}, u32[]{:S(2)}, u32[]{:S(2)}) %collective-permute-start.4) | collective-permute-done | bytes 20512 | tf_op jit(solution)/shard_map/ppermute | solution.py:26
  131.0 5.3 %collective-permute-start.9 = (f32[40,128]{1,0:T(8,128)S(1)}, f32[40,128]{1,0:T(8,128)S(1)}, u32[]{:S(2)}, u32[]{:S(2)}) collective-permute-start(f32[40,128]{1,0:T(8,128)S(1)} %add_add_fusion.1), channel_id=1, source_target_pairs={{0,48},{16,32},{32,16},{48,0},{64,112},{80,96},{96,80},{112,64},{1... | collective-permute-start | bytes 61448 | tf_op jit(solution)/shard_map/ppermute | solution.py:26
  136.3 1.9 %collective-permute-start.8 = (f32[40,128]{1,0:T(8,128)S(1)}, f32[40,128]{1,0:T(8,128)S(1)}, u32[]{:S(2)}, u32[]{:S(2)}) collective-permute-start(f32[40,128]{1,0:T(8,128)S(1)} %add_add_fusion.1), channel_id=1, source_target_pairs={{0,16},{16,0},{32,48},{48,32},{64,80},{80,64},{96,112},{112,96},{1... | collective-permute-start | bytes 61448 | tf_op jit(solution)/shard_map/ppermute | solution.py:26
  138.2 2.2 %collective-permute-start.7 = (f32[40,128]{1,0:T(8,128)S(1)}, f32[40,128]{1,0:T(8,128)S(1)}, u32[]{:S(2)}, u32[]{:S(2)}) collective-permute-start(f32[40,128]{1,0:T(8,128)S(1)} %add_add_fusion.1), channel_id=1, source_target_pairs={{0,32},{16,48},{32,0},{48,16},{64,96},{80,112},{96,64},{112,80},{1... | collective-permute-start | bytes 61448 | tf_op jit(solution)/shard_map/ppermute | solution.py:26
  140.4 0.0 collective-permute-done.9
  140.5 0.7 collective-permute-done.8
  141.1 2.8 %collective-permute-done.7 = f32[40,128]{1,0:T(8,128)S(1)} collective-permute-done((f32[40,128]{1,0:T(8,128)S(1)}, f32[40,128]{1,0:T(8,128)S(1)}, u32[]{:S(2)}, u32[]{:S(2)}) %collective-permute-start.7) | collective-permute-done | bytes 20512 | tf_op jit(solution)/shard_map/ppermute | solution.py:26
  144.0 4.8 %collective-permute-start.10 = (f32[40,128]{1,0:T(8,128)S(1)}, f32[40,128]{1,0:T(8,128)S(1)}, u32[]{:S(2)}, u32[]{:S(2)}) collective-permute-start(f32[40,128]{1,0:T(8,128)S(1)} %add_add_fusion), channel_id=1, source_target_pairs={{0,64},{16,80},{32,96},{48,112},{64,0},{80,16},{96,32},{112,48},{1... | collective-permute-start | bytes 61448 | tf_op jit(solution)/shard_map/ppermute | solution.py:26
  148.8 3.9 %collective-permute-done.10 = f32[40,128]{1,0:T(8,128)S(1)} collective-permute-done((f32[40,128]{1,0:T(8,128)S(1)}, f32[40,128]{1,0:T(8,128)S(1)}, u32[]{:S(2)}, u32[]{:S(2)}) %collective-permute-start.10) | collective-permute-done | bytes 20512 | tf_op jit(solution)/shard_map/ppermute | solution.py:26
  152.7 4.7 %collective-permute-start.11 = (f32[40,128]{1,0:T(8,128)S(1)}, f32[40,128]{1,0:T(8,128)S(1)}, u32[]{:S(2)}, u32[]{:S(2)}) collective-permute-start(f32[40,128]{1,0:T(8,128)S(1)} %add.56), channel_id=1, source_target_pairs={{0,8},{8,0},{1,9},{9,1},{2,10},{10,2},{3,11},{11,3},{4,12},{12,4},... | collective-permute-start | bytes 61448 | tf_op jit(solution)/shard_map/ppermute | solution.py:492
  157.4 0.8 collective-permute-done.11
  158.2 0.6 broadcast_select_fusion
  158.8 7.6 %factorize.1 = (f32[128,128]{1,0:T(8,128)}, f32[128,128]{1,0:T(8,128)}) custom-call(f32[40,128]{1,0:T(8,128)} %get-tuple-element.49.refs_0_, f32[40,128]{1,0:T(8,128)} %get-tuple-element.48.refs_1_), custom_call_target="tpu_custom_call" | custom-call | tf_op jit(solution)/shard_map/factorize/pallas_call | solution.py:322
  166.5 0.8 copy-done.5
  167.3 4.3 %apply.1 = f32[1,128,5,8,128]{4,3,2,1,0:T(8,128)} custom-call(f32[128,128]{1,0:T(8,128)S(1)} %copy-done.5, f32[8,128]{1,0:T(8,128)S(1)} %fusion.6.scale_ref, s16[8,960,128]{2,1,0:T(8,128)(2,1)S(1)} %all-to-all-done.2.code_ref), custom_call_target="tpu_custom_call" | custom-call | tf_op jit(solution)/shard_map/apply/pallas_call | solution.py:370
  (29 shorter events, 0.2 us)
Async XLA Ops:
  0.6 1.3 copy-start.3
  5.0 7.8 %copy-start.6 = (f32[8,128]{1,0:T(8,128)S(1)}, f32[8,128]{1,0:T(8,128)}, u32[]{:S(2)}) copy-start(f32[8,128]{1,0:T(8,128)} %velocity_ref) | copy-start | bytes 12292
  5.0 7.8 %copy-start.4 = (f32[5,5,8,128]{3,2,1,0:T(8,128)S(1)}, f32[5,5,8,128]{3,2,1,0:T(8,128)}, u32[]{:S(2)}) copy-start(f32[5,5,8,128]{3,2,1,0:T(8,128)} %param.5) | copy-start | bytes 307204
  5.0 14.7 %copy-start.7 = (s32[8]{0:T(128)S(1)}, s32[8]{0:T(128)}, u32[]{:S(2)}) copy-start(s32[8]{0:T(128)} %param.7) | copy-start | bytes 100
  5.0 49.6 %all-to-all-start = ((bf16[8,2,400,128]{3,2,1,0:T(8,128)(2,1)}), bf16[8,2,400,128]{3,2,1,0:T(8,128)(2,1)S(1)}, u32[]{:S(2)}, u32[]{:S(2)}) async-start(bf16[8,2,400,128]{3,2,1,0:T(8,128)(2,1)} %spread.1), calls=%async_computation | async-start | bytes 3276800 | tf_op jit(solution)/shard_map/all_to_all | solution.py:464
  12.9 7.5 %collective-permute-start = (f32[26,2,128]{2,1,0:T(2,128)S(1)}, f32[26,2,128]{2,1,0:T(2,128)S(1)}, u32[]{:S(2)}, u32[]{:S(2)}) collective-permute-start(f32[26,2,128]{2,1,0:T(2,128)S(1)} %pad_maximum_fusion), channel_id=1, source_target_pairs={{8,0},{16,8},{24,16},{32,24},{40,32},{48,40},{56,48},{64,56},{72,6... | collective-permute-start | bytes 79880 | tf_op jit(solution)/shard_map/ppermute | solution.py:438
  17.7 3.1 %collective-permute-start.1 = (f32[26,2,128]{2,1,0:T(2,128)S(1)}, f32[26,2,128]{2,1,0:T(2,128)S(1)}, u32[]{:S(2)}, u32[]{:S(2)}) collective-permute-start(f32[26,2,128]{2,1,0:T(2,128)S(1)} %pad_maximum_fusion.1), channel_id=1, source_target_pairs={{0,8},{8,16},{16,24},{24,32},{32,40},{40,48},{48,56},{56,64},{64,7... | collective-permute-start | bytes 79880 | tf_op jit(solution)/shard_map/ppermute | solution.py:439
  26.6 2.0 %copy-start = (f32[29,18,2,8,128]{4,3,2,1,0:T(8,128)}, f32[29,18,2,8,128]{4,3,2,1,0:T(8,128)S(1)}, u32[]{:S(2)}) copy-start(f32[29,18,2,8,128]{4,3,2,1,0:T(8,128)S(1)} %get-tuple-element.35.refs_8_) | copy-start | bytes 12828676
  54.8 13.7 %collective-permute-start.3 = (bf16[8,400,128]{2,1,0:T(8,128)(2,1)S(1)}, bf16[8,400,128]{2,1,0:T(8,128)(2,1)S(1)}, u32[]{:S(2)}, u32[]{:S(2)}) collective-permute-start(bf16[8,400,128]{2,1,0:T(8,128)(2,1)S(1)} %get-tuple-element.44), channel_id=1, source_target_pairs={{0,8},{8,16},{16,24},{24,32},{32,40},{40,48},{48,56},{56,64},{64,7... | collective-permute-start | bytes 2457608 | tf_op jit(solution)/shard_map/ppermute | solution.py:476
  59.2 13.7 %collective-permute-start.2 = (bf16[8,400,128]{2,1,0:T(8,128)(2,1)S(1)}, bf16[8,400,128]{2,1,0:T(8,128)(2,1)S(1)}, u32[]{:S(2)}, u32[]{:S(2)}) collective-permute-start(bf16[8,400,128]{2,1,0:T(8,128)(2,1)S(1)} %get-tuple-element.45), channel_id=1, source_target_pairs={{8,0},{16,8},{24,16},{32,24},{40,32},{48,40},{56,48},{64,56},{72,6... | collective-permute-start | bytes 2457608 | tf_op jit(solution)/shard_map/ppermute | solution.py:475
  61.1 15.0 %copy-start.1 = (f32[29,18,2,8,128]{4,3,2,1,0:T(8,128)S(1)}, f32[29,18,2,8,128]{4,3,2,1,0:T(8,128)}, u32[]{:S(2)}) copy-start(f32[29,18,2,8,128]{4,3,2,1,0:T(8,128)} %copy-done) | copy-start | bytes 12828676
  93.8 1.3 copy-start.2
  110.0 56.5 %all-to-all-start.2 = ((s16[8,960,128]{2,1,0:T(8,128)(2,1)}), s16[8,960,128]{2,1,0:T(8,128)(2,1)S(1)}, u32[]{:S(2)}, u32[]{:S(2)}) async-start(s16[8,960,128]{2,1,0:T(8,128)(2,1)} %copy-done.2), calls=%async_computation.2 | async-start | bytes 3932160 | tf_op jit(solution)/shard_map/all_to_all | solution.py:488
  113.6 14.1 %collective-permute-start.6 = (f32[40,128]{1,0:T(8,128)S(1)}, f32[40,128]{1,0:T(8,128)S(1)}, u32[]{:S(2)}, u32[]{:S(2)}) collective-permute-start(f32[40,128]{1,0:T(8,128)S(1)} %reduce_sum.9), channel_id=1, source_target_pairs={{0,384},{16,400},{32,416},{48,432},{64,448},{80,464},{96,480},{112... | collective-permute-start | bytes 61448 | tf_op jit(solution)/shard_map/ppermute | solution.py:26
  122.6 5.0 %collective-permute-start.5 = (f32[40,128]{1,0:T(8,128)S(1)}, f32[40,128]{1,0:T(8,128)S(1)}, u32[]{:S(2)}, u32[]{:S(2)}) collective-permute-start(f32[40,128]{1,0:T(8,128)S(1)} %reduce_sum.9), channel_id=1, source_target_pairs={{0,128},{16,144},{32,160},{48,176},{64,192},{80,208},{96,224},{112... | collective-permute-start | bytes 61448 | tf_op jit(solution)/shard_map/ppermute | solution.py:26
  124.6 6.4 %collective-permute-start.4 = (f32[40,128]{1,0:T(8,128)S(1)}, f32[40,128]{1,0:T(8,128)S(1)}, u32[]{:S(2)}, u32[]{:S(2)}) collective-permute-start(f32[40,128]{1,0:T(8,128)S(1)} %reduce_sum.9), channel_id=1, source_target_pairs={{0,256},{16,272},{32,288},{48,304},{64,320},{80,336},{96,352},{112... | collective-permute-start | bytes 61448 | tf_op jit(solution)/shard_map/ppermute | solution.py:26
  131.0 9.5 %collective-permute-start.9 = (f32[40,128]{1,0:T(8,128)S(1)}, f32[40,128]{1,0:T(8,128)S(1)}, u32[]{:S(2)}, u32[]{:S(2)}) collective-permute-start(f32[40,128]{1,0:T(8,128)S(1)} %add_add_fusion.1), channel_id=1, source_target_pairs={{0,48},{16,32},{32,16},{48,0},{64,112},{80,96},{96,80},{112,64},{1... | collective-permute-start | bytes 61448 | tf_op jit(solution)/shard_map/ppermute | solution.py:26
  136.3 4.8 %collective-permute-start.8 = (f32[40,128]{1,0:T(8,128)S(1)}, f32[40,128]{1,0:T(8,128)S(1)}, u32[]{:S(2)}, u32[]{:S(2)}) collective-permute-start(f32[40,128]{1,0:T(8,128)S(1)} %add_add_fusion.1), channel_id=1, source_target_pairs={{0,16},{16,0},{32,48},{48,32},{64,80},{80,64},{96,112},{112,96},{1... | collective-permute-start | bytes 61448 | tf_op jit(solution)/shard_map/ppermute | solution.py:26
  138.2 5.7 %collective-permute-start.7 = (f32[40,128]{1,0:T(8,128)S(1)}, f32[40,128]{1,0:T(8,128)S(1)}, u32[]{:S(2)}, u32[]{:S(2)}) collective-permute-start(f32[40,128]{1,0:T(8,128)S(1)} %add_add_fusion.1), channel_id=1, source_target_pairs={{0,32},{16,48},{32,0},{48,16},{64,96},{80,112},{96,64},{112,80},{1... | collective-permute-start | bytes 61448 | tf_op jit(solution)/shard_map/ppermute | solution.py:26
  144.0 8.7 %collective-permute-start.10 = (f32[40,128]{1,0:T(8,128)S(1)}, f32[40,128]{1,0:T(8,128)S(1)}, u32[]{:S(2)}, u32[]{:S(2)}) collective-permute-start(f32[40,128]{1,0:T(8,128)S(1)} %add_add_fusion), channel_id=1, source_target_pairs={{0,64},{16,80},{32,96},{48,112},{64,0},{80,16},{96,32},{112,48},{1... | collective-permute-start | bytes 61448 | tf_op jit(solution)/shard_map/ppermute | solution.py:26
  152.7 5.5 %collective-permute-start.11 = (f32[40,128]{1,0:T(8,128)S(1)}, f32[40,128]{1,0:T(8,128)S(1)}, u32[]{:S(2)}, u32[]{:S(2)}) collective-permute-start(f32[40,128]{1,0:T(8,128)S(1)} %add.56), channel_id=1, source_target_pairs={{0,8},{8,0},{1,9},{9,1},{2,10},{10,2},{3,11},{11,3},{4,12},{12,4},... | collective-permute-start | bytes 61448 | tf_op jit(solution)/shard_map/ppermute | solution.py:492
  166.5 0.8 copy-start.5

commit v7 on v6

--- a/solution.py
+++ b/solution.py
@@ -18,6 +18,8 @@
 HALF = 4
 SPACE = ("chip", "core")
 RH = 2
+PITCH = 24
+TOGETHER = 4
 VMEM_LIMIT = 28 * 1024 * 1024
 
 
@@ -60,7 +62,7 @@
             pltpu.VMEM((LANES * 8, radial), jnp.float32),
             pltpu.VMEM((2, (radial + 2 * RH) * HALF, LANES), jnp.float32),
         ],
-        compiler_params=pltpu.CompilerParams(vmem_limit_bytes=VMEM_LIMIT),
+        compiler_params=pltpu.CompilerParams(vmem_limit_bytes=2 * VMEM_LIMIT),
         name="spread",
     )(sketch)
 
@@ -112,6 +114,14 @@
     )(parity, one, two, table)
 
 
+def split(value):
+    one = value.astype(jnp.bfloat16)
+    rest = value - one.astype(jnp.float32)
+    two = rest.astype(jnp.bfloat16)
+    three = (rest - two.astype(jnp.float32)).astype(jnp.bfloat16)
+    return one, two, three
+
+
 CODE = 8388000.0
 
 
@@ -152,71 +162,82 @@
 
 
 def evolve_body(order_ref, *refs):
-    layers, (coef_ref, mask_ref, turn_a, turn_b, code_ref, gram_ref, z_ref, s_ref, out_ref) = refs[:8], refs[8:]
-    wide = z_ref.shape[2]
-    per = wide - 2 * RH
-    sub = lax.broadcasted_iota(jnp.int32, (8, LANES), 0)
-
-    @pl.loop(0, layers[0].shape[1] // 8, unroll=5)
-    def _(step):
-        here = pl.ds(pl.multiple_of(step * 8, 8), 8)
-        line = step * 2
-        field = line // wide
-        cell = line % wide
-        for n in range(2):
-            for tile in range(2):
-                a = layers[4 * n + 2 * tile][0, here, :]
-                b = layers[4 * n + 2 * tile + 1][0, here, :]
-                z_ref[n, field, cell, tile] = jnp.where(sub < HALF, a, pltpu.roll(b, HALF, 0))
-                z_ref[n, field, cell + 1, tile] = jnp.where(sub < HALF, pltpu.roll(a, HALF, 0), b)
-
-    turns = [turn_a[0], turn_b[0]]
-
-    def shifted(tiles, shift, t):
-        keep = (sub < 8 - shift) if shift > 0 else (sub >= -shift)
-        turned = [pltpu.roll(v, (-shift) % 8, 0) for v in tiles]
-        return jnp.where(keep, turned[t], turned[1 - t])
-
-    def advance(ref, r, place, t, store):
-        q = [[ref[n, j, r, t] for j in range(FIELDS)] for n in range(2)]
+    layers, turn_refs = refs[: 4 * TOGETHER], refs[4 * TOGETHER : 5 * TOGETHER]
+    coef_ref, mask_ref, code_ref, gram_ref, z_ref, s_ref, out_ref = refs[5 * TOGETHER :]
+    per = out_ref.shape[1] // (8 * FIELDS)
+    wide = per + 2 * RH
+
+    for n in range(TOGETHER):
+        low, high, right, left = layers[4 * n : 4 * n + 4]
+
+        @pl.loop(0, FIELDS)
+        def _(field):
+            for group, ref in enumerate((left, low, high, right)):
+                for x in range(HALF):
+                    source = field * wide * HALF + x
+                    target = 8 + PITCH * (group * HALF + x)
+                    z_ref[n, field, target - RH : target, :] = ref[0, pl.ds(source, RH, stride=HALF), :]
+                    for r in range(0, per, 8):
+                        z_ref[n, field, target + r : target + r + 8, :] = ref[
+                            0, pl.ds(source + (r + RH) * HALF, 8, stride=HALF), :
+                        ]
+                    z_ref[n, field, target + per : target + per + RH, :] = ref[
+                        0, pl.ds(source + (per + RH) * HALF, RH, stride=HALF), :
+                    ]
+
+    turns = [ref[0] for ref in turn_refs]
+
+    def advance(ref, line, place, store):
+        q = [[ref[n, j, pl.ds(line, 8), :] for j in range(FIELDS)] for n in range(TOGETHER)]
         for i in range(FIELDS):
-            coupled = [coef_ref[j * FIELDS + i, place, t] for j in range(FIELDS)]
-            moves = [coef_ref[FIELDS * FIELDS + m, place, t] for m in range(4)]
-            for n in range(2):
+            coupled = [coef_ref[j * FIELDS + i, pl.ds(place, 8), :] for j in range(FIELDS)]
+            moves = [coef_ref[FIELDS * FIELDS + m, pl.ds(place, 8), :] for m in range(4)]
+            for n in range(TOGETHER):
                 value = coupled[0] * q[n][0]
                 for j in range(1, FIELDS):
                     value = value + coupled[j] * q[n][j]
-                pair = [None, None]
-                pair[t] = q[n][i]
-                pair[1 - t] = ref[n, i, r, 1 - t]
                 for m, shift in enumerate((1, -1, 2, -2)):
-                    value = value + moves[m] * shifted(pair, shift, t)
-                value = value + (STEP_DT * VISCOSITY) * (ref[n, i, r - 1, t] + ref[n, i, r + 1, t])
+                    value = value + moves[m] * ref[n, i, pl.ds(line + PITCH * shift, 8), :]
+                side = ref[n, i, pl.ds(line - 1, 8), :] + ref[n, i, pl.ds(line + 1, 8), :]
+                value = value + (STEP_DT * VISCOSITY) * side
                 store(n, i, value + turns[n] * pltpu.roll(q[n][i], K, 1))
 
-    @pl.loop(0, per + 2)
-    def _(r):
-        for t in range(2):
-            mask = mask_ref[r, t]
+    def first_step(place):
+        mask = mask_ref[pl.ds(place, 8), :]
+
+        def store(n, i, value):
+            s_ref[n, i, pl.ds(place, 8), :] = value * mask
+
+        advance(z_ref, pl.multiple_of(place + 2 * PITCH, 8), place, store)
+
+    @pl.loop(0, 12)
+    def _(x):
+        for r in range(0, per, 8):
+            first_step(pl.multiple_of(8 + PITCH * x + r, 8))
+
+    @pl.loop(1, 10)
+    def _(x):
+        first_step(pl.multiple_of(8 + PITCH * x + per, 8))
+
+    @pl.loop(0, 8)
+    def _(x):
+        for r in range(0, per, 8):
+            line = pl.multiple_of(8 + PITCH * (x + 2) + r, 8)
 
             def store(n, i, value):
-                s_ref[n, i, r, t] = value * mask
-
-            advance(z_ref, r + 1, r, t, store)
-
-    @pl.loop(0, per, unroll=2)
-    def _(r):
-        def store(n, i, value):
-            out_ref[n, pl.ds(i * 8 * per + r, 8, stride=per), :] = value
-
-        advance(s_ref, r + 1, r + 1, 0, store)
-
-    for n in range(2):
+                out_ref[n, pl.ds(pl.multiple_of((i * 8 + x) * per + r, 8), 8), :] = value
+
+            advance(s_ref, line, line, store)
+
+    for n in range(TOGETHER):
         block = out_ref[n]
-        gram = lax.dot_general(
-            block, block, (((0,), (0,)), ((), ())),
-            precision=lax.Precision.HIGHEST, preferred_element_type=jnp.float32,
-        )
+        one, two, three = split(block)
+        pair = jnp.concatenate([one, two], axis=1)
+        contract = (((0,), (0,)), ((), ()))
+        wide = lax.dot_general(pair, pair, contract, preferred_element_type=jnp.float32)
+        thin = lax.dot_general(one, three, contract, preferred_element_type=jnp.float32)
+        cross = wide[:LANES, LANES:] + thin
+        gram = wide[:LANES, :LANES] + (cross + cross.T + wide[LANES:, LANES:])
         scale = jnp.maximum(jnp.max(jnp.abs(block), axis=0, keepdims=True), 1e-30)
         pack(gram, scale, gram_ref, n)
         count = block.shape[0]
@@ -225,26 +246,27 @@
 
 def evolve(order, low, high, right, left, coef, mask, turn):
     count = order.shape[0]
-    per = coef.shape[1] - 2
     rows = low.shape[1]
+    per = rows // (FIELDS * HALF) - 2 * RH
     whole = lambda shape: pl.BlockSpec(shape, lambda i, order: (0,) * len(shape))
-    pick = lambda shape, n: pl.BlockSpec((1,) + shape, lambda i, order: (order[2 * i + n], 0, 0))
-    layers = [pick((rows, LANES), n) for n in range(2) for _ in range(4)]
+    pick = lambda shape, n: pl.BlockSpec((1,) + shape, lambda i, order: (order[TOGETHER * i + n], 0, 0))
+    layers = [pick((rows, LANES), n) for n in range(TOGETHER) for _ in range(4)]
     return pl.pallas_call(
         evolve_body,
         grid_spec=pltpu.PrefetchScalarGridSpec(
             num_scalar_prefetch=1,
-            grid=(count // 2,),
+            grid=(count // TOGETHER,),
             in_specs=layers
-            + [whole(coef.shape), whole(mask.shape), pick((8, LANES), 0), pick((8, LANES), 1)],
+            + [pick((8, LANES), n) for n in range(TOGETHER)]
+            + [whole(coef.shape), whole(mask.shape)],
             out_specs=[
-                pl.BlockSpec((2, FIELDS * 12 * per, LANES), lambda i, order: (i, 0, 0)),
-                pl.BlockSpec((2, 2, HALF_ROWS, LANES), lambda i, order: (i, 0, 0, 0)),
+                pl.BlockSpec((TOGETHER, FIELDS * 12 * per, LANES), lambda i, order: (i, 0, 0)),
+                pl.BlockSpec((TOGETHER, 2, HALF_ROWS, LANES), lambda i, order: (i, 0, 0, 0)),
             ],
             scratch_shapes=[
-                pltpu.VMEM((2, FIELDS, per + 2 * RH, 2, 8, LANES), jnp.float32),
-                pltpu.VMEM((2, FIELDS, per + 2, 2, 8, LANES), jnp.float32),
-                pltpu.VMEM((2, FIELDS * 8 * per, LANES), jnp.float32),
+                pltpu.VMEM((TOGETHER, FIELDS, 16 + 16 * PITCH, LANES), jnp.float32),
+                pltpu.VMEM((TOGETHER, FIELDS, 16 + 12 * PITCH, LANES), jnp.float32),
+                pltpu.VMEM((TOGETHER, FIELDS * 8 * per, LANES), jnp.float32),
             ],
         ),
         out_shape=[
@@ -253,7 +275,7 @@
         ],
         compiler_params=pltpu.CompilerParams(vmem_limit_bytes=VMEM_LIMIT),
         name="evolve",
-    )(order, *([low, high, right, left] * 2), coef, mask, turn, turn)
+    )(order, *([low, high, right, left] * TOGETHER), *([turn] * TOGETHER), coef, mask)
 
 
 def factor_body(scale, *refs):
@@ -328,14 +350,6 @@
     )(*parts)
 
 
-def split(value):
-    one = value.astype(jnp.bfloat16)
-    rest = value - one.astype(jnp.float32)
-    two = rest.astype(jnp.bfloat16)
-    three = (rest - two.astype(jnp.float32)).astype(jnp.bfloat16)
-    return one, two, three
-
-
 def apply_body(inverse_ref, scale_ref, code_ref, out_ref, rows_ref, all_ref):
     per = code_ref.shape[1] // (12 * FIELDS)
     total = 8 * FIELDS * per
@@ -390,19 +404,27 @@
 
 
 def stencil_body(place_ref, coupling_ref, velocity_ref, right_ref, left_ref, coef_ref, mask_ref):
-    cells, radial = coef_ref.shape[1], velocity_ref.shape[1]
+    radial = velocity_ref.shape[1]
+    cells = radial // F + 2
     start = place_ref[0]
     turn = lax.rem(radial + 1 - start, radial)
-    sub = lax.broadcasted_iota(jnp.int32, (8, LANES), 0)
 
     def tiles(index, own):
         gap = jnp.zeros((4, radial), jnp.float32)
         other = jnp.concatenate([right_ref[index], gap, left_ref[index]], axis=0)
         return [pltpu.roll(value, turn, 1) for value in (own, other)]
 
+    def put(ref, lead, t, r, value):
+        line = 8 + r - 1
+        if t == 0:
+            ref[lead + (pl.ds(line + 2 * PITCH, 8, stride=PITCH),)] = value
+        elif 1 <= r <= cells - 2:
+            ref[lead + (pl.ds(line + 10 * PITCH, 2, stride=PITCH),)] = value[0:2]
+            ref[lead + (pl.ds(line, 2, stride=PITCH),)] = value[6:8]
+
     def spread_lanes(index, t, value):
         for r in range(cells):
-            coef_ref[index, r, t] = jnp.broadcast_to(value[:, r : r + 1], (8, LANES))
+            put(coef_ref, (index,), t, r, jnp.broadcast_to(value[:, r : r + 1], (8, LANES)))
 
     centre = 1.0 - STEP_DT * VISCOSITY * (30.0 / 12.0 + 2.0)
 
@@ -419,12 +441,13 @@
         spread_lanes(FIELDS * FIELDS + 1, t, near_c - near_d * speed)
         spread_lanes(FIELDS * FIELDS + 2, t, -far_d * speed - far_c)
         spread_lanes(FIELDS * FIELDS + 3, t, far_d * speed - far_c)
+    sub = lax.broadcasted_iota(jnp.int32, (8, LANES), 0)
     sides = jnp.where(sub < HALF, place_ref[2], place_ref[1])
     for r in range(cells):
         here = start - 1 + r
         inside = jnp.where((here >= 0) & (here < radial), 1, 0)
-        mask_ref[r, 0] = jnp.full((8, LANES), inside, jnp.int32).astype(jnp.float32)
-        mask_ref[r, 1] = (sides * inside).astype(jnp.float32)
+        put(mask_ref, (), 0, r, jnp.full((8, LANES), inside, jnp.int32).astype(jnp.float32))
+        put(mask_ref, (), 1, r, (sides * inside).astype(jnp.float32))
 
 
 def stencil(coupling, velocity, per):
@@ -444,8 +467,8 @@
         in_specs=[pl.BlockSpec(memory_space=pltpu.SMEM)] + [vmem] * 4,
         out_specs=[vmem, vmem],
         out_shape=[
-            jax.ShapeDtypeStruct((FIELDS * FIELDS + 4, per + 2, 2, 8, LANES), jnp.float32),
-            jax.ShapeDtypeStruct((per + 2, 2, 8, LANES), jnp.float32),
+            jax.ShapeDtypeStruct((FIELDS * FIELDS + 4, 16 + 12 * PITCH, LANES), jnp.float32),
+            jax.ShapeDtypeStruct((16 + 12 * PITCH, LANES), jnp.float32),
         ],
         compiler_params=pltpu.CompilerParams(vmem_limit_bytes=VMEM_LIMIT),
         name="stencil",

time: 172 us -> 167 us (0.971)
  Pallas kernels: 45 us -> 41.1 us
    pallas_call x1, Pallas kernels: 17.7 us -> 12.3 us  [evolve(): pl.pallas_call(evolve_body, grid_spec=pltpu.PrefetchScalarGridSpec(num_sc...]
    unnamed x17 -> x15, local copies, waits for them, and re-layouts: 5.42 us -> 4.18 us
where the time goes in v7:
time: 167 us; the launch traced here: 166 us
  starting transfers between devices  57.4 us (34%)
  waiting for transfers between devices  46.4 us (28%)
  Pallas kernels  41.1 us (25%)
  blocking collectives  14.9 us (9%)
  local copies, waits for them, and re-layouts  4.69 us (3%)
    ppermute x7, starting transfers between devices, xor_sum(): lax.ppermute(value, axis, [(i, i ^ m) for i in range(count)])  28.3 us
    all_to_all x1, waiting for transfers between devices, local(): rows = lax.all_to_all(rows, 'freq', split_axis=0, concat_axis=0, tiled=True)  26.1 us
    all_to_all x1, blocking collectives, local(): lax.all_to_all(grams, ('freq', 'core'), split_axis=0, concat_axis=0, tile...  14.9 us
    pallas_call x1, Pallas kernels, evolve(): pl.pallas_call(evolve_body, grid_spec=pltpu.PrefetchScalarGridSpec(num_sc...  12.3 us
    ppermute x7, waiting for transfers between devices, xor_sum(): lax.ppermute(value, axis, [(i, i ^ m) for i in range(count)])  10.7 us
    all_to_all x1, starting transfers between devices, local(): rows = lax.all_to_all(rows, 'freq', split_axis=0, concat_axis=0, tiled=True)  7.79 us
    pallas_call x1, Pallas kernels, factorize(): pl.pallas_call(partial(factor_body, scale), in_specs=[vmem] * len(parts),...  7.64 us
    pallas_call x2, Pallas kernels, fourier(): pl.pallas_call(fourier_body, grid=(1,), in_specs=[pl.BlockSpec(memory_spa...  6.54 us
  transfers between devices with their start and end apart: 14, of which 9 were waited for; matrix products, arithmetic and copies ran while one was open for 1% of the time, Pallas kernels for 10%

profile of v7, /device:TPU:1, one launch (start us, length us, event | category | flops | bytes accessed | tf_op | source)
XLA Modules:
  0.0 166.4 jit_solution(3902571436495153305)
XLA Ops:
  0.6 4.6 %spread.1 = bf16[8,2,400,128]{3,2,1,0:T(8,128)(2,1)} custom-call(bf16[2,64,5,8,128]{4,3,2,1,0:T(8,128)(2,1)} %sketch_ref.1), custom_call_target="tpu_custom_call" | custom-call | tf_op jit(solution)/shard_map/spread/pallas_call | solution.py:55
  5.3 7.8 %all-to-all-start = ((bf16[8,2,400,128]{3,2,1,0:T(8,128)(2,1)}), bf16[8,2,400,128]{3,2,1,0:T(8,128)(2,1)S(1)}, u32[]{:S(2)}, u32[]{:S(2)}) async-start(bf16[8,2,400,128]{3,2,1,0:T(8,128)(2,1)} %spread.1), calls=%async_computation | async-start | bytes 3276800 | tf_op jit(solution)/shard_map/all_to_all | solution.py:487
  13.1 4.7 %collective-permute-start = (f32[26,2,128]{2,1,0:T(2,128)S(1)}, f32[26,2,128]{2,1,0:T(2,128)S(1)}, u32[]{:S(2)}, u32[]{:S(2)}) collective-permute-start(f32[26,2,128]{2,1,0:T(2,128)S(1)} %pad_maximum_fusion), channel_id=1, source_target_pairs={{8,0},{16,8},{24,16},{32,24},{40,32},{48,40},{56,48},{64,56},{72,6... | collective-permute-start | bytes 79880 | tf_op jit(solution)/shard_map/ppermute | solution.py:461
  17.9 2.0 %collective-permute-start.1 = (f32[26,2,128]{2,1,0:T(2,128)S(1)}, f32[26,2,128]{2,1,0:T(2,128)S(1)}, u32[]{:S(2)}, u32[]{:S(2)}) collective-permute-start(f32[26,2,128]{2,1,0:T(2,128)S(1)} %pad_maximum_fusion.1), channel_id=1, source_target_pairs={{0,8},{8,16},{16,24},{24,32},{32,40},{40,48},{48,56},{56,64},{64,7... | collective-permute-start | bytes 79880 | tf_op jit(solution)/shard_map/ppermute | solution.py:462
  20.0 0.1 fusion.7
  20.1 0.1 broadcast_multiply_fusion
  20.1 0.1 pad_add_fusion.place_ref
  20.2 0.1 copy.17
  20.3 0.1 broadcast_in_dim.41
  20.5 0.1 reshape.145.table_ref
  20.6 0.0 collective-permute-done.right_ref
  20.6 0.4 collective-permute-done.1.left_ref
  21.0 5.8 %stencil.1 = (f32[29,304,128]{2,1,0:T(8,128)S(1)}, f32[304,128]{1,0:T(8,128)S(1)}) custom-call(s32[3]{0:T(128)S(1)} %pad_add_fusion.place_ref, f32[25,8,128]{2,1,0:T(8,128)S(1)} %bitcast.27, f32[8,128]{1,0:T(8,128)S(1)} %copy-done.5, f32[26,2,128]{2,1,0:T(2,128)S(1)} %collective-permute-done.right_ref, f32[26,2,128]{2,1,0:T(2,128)S(1)} %collective-permute-done.1.left_ref), custom_call_target="tpu_custom_call" | custom-call | tf_op jit(solution)/shard_map/stencil/pallas_call | solution.py:465
  26.8 2.1 %copy-done = f32[29,304,128]{2,1,0:T(8,128)} copy-done((f32[29,304,128]{2,1,0:T(8,128)}, f32[29,304,128]{2,1,0:T(8,128)S(1)}, u32[]{:S(2)}) %copy-start) | copy-done | bytes 4513816
  28.8 26.1 %all-to-all-done.one_ref.two_ref = bf16[8,2,400,128]{3,2,1,0:T(8,128)(2,1)S(1)} async-done(((bf16[8,2,400,128]{3,2,1,0:T(8,128)(2,1)}), bf16[8,2,400,128]{3,2,1,0:T(8,128)(2,1)S(1)}, u32[]{:S(2)}, u32[]{:S(2)}) %all-to-all-start) | async-done | bytes 1638432 | tf_op jit(solution)/shard_map/all_to_all | solution.py:487
  54.9 0.1 slice_bitcast_fusion
  55.0 4.4 %collective-permute-start.3 = (bf16[8,400,128]{2,1,0:T(8,128)(2,1)S(1)}, bf16[8,400,128]{2,1,0:T(8,128)(2,1)S(1)}, u32[]{:S(2)}, u32[]{:S(2)}) collective-permute-start(bf16[8,400,128]{2,1,0:T(8,128)(2,1)S(1)} %get-tuple-element.44), channel_id=1, source_target_pairs={{0,8},{8,16},{16,24},{24,32},{32,40},{40,48},{48,56},{56,64},{64,7... | collective-permute-start | bytes 2457608 | tf_op jit(solution)/shard_map/ppermute | solution.py:499
  59.4 1.9 %collective-permute-start.2 = (bf16[8,400,128]{2,1,0:T(8,128)(2,1)S(1)}, bf16[8,400,128]{2,1,0:T(8,128)(2,1)S(1)}, u32[]{:S(2)}, u32[]{:S(2)}) collective-permute-start(bf16[8,400,128]{2,1,0:T(8,128)(2,1)S(1)} %get-tuple-element.45), channel_id=1, source_target_pairs={{8,0},{16,8},{24,16},{32,24},{40,32},{48,40},{56,48},{64,56},{72,6... | collective-permute-start | bytes 2457608 | tf_op jit(solution)/shard_map/ppermute | solution.py:498
  61.3 3.3 %fourier.2 = (f32[8,400,128]{2,1,0:T(8,128)S(1)}, f32[8,400,128]{2,1,0:T(8,128)S(1)}) custom-call(s32[8]{0:T(128)S(1)} %and_select_fusion.parity_ref, bf16[8,2,400,128]{3,2,1,0:T(8,128)(2,1)S(1)} %all-to-all-done.one_ref.two_ref, bf16[8,2,400,128]{3,2,1,0:T(8,128)(2,1)S(1)} %all-to-all-done.one_ref.two_ref, f32[8,2,4,128]{3,2,1,0:T(4,128)S(1)} %reshape.145.table_ref), custom_call_target="tpu_custom_call" | custom-call | tf_op jit(solution)/shard_map/fourier/pallas_call | solution.py:100
  64.6 4.1 %collective-permute-done.3 = bf16[8,400,128]{2,1,0:T(8,128)(2,1)S(1)} collective-permute-done((bf16[8,400,128]{2,1,0:T(8,128)(2,1)S(1)}, bf16[8,400,128]{2,1,0:T(8,128)(2,1)S(1)}, u32[]{:S(2)}, u32[]{:S(2)}) %collective-permute-start.3) | collective-permute-done | bytes 819232 | tf_op jit(solution)/shard_map/ppermute | solution.py:499
  68.6 4.4 %collective-permute-done.2 = bf16[8,400,128]{2,1,0:T(8,128)(2,1)S(1)} collective-permute-done((bf16[8,400,128]{2,1,0:T(8,128)(2,1)S(1)}, bf16[8,400,128]{2,1,0:T(8,128)(2,1)S(1)}, u32[]{:S(2)}, u32[]{:S(2)}) %collective-permute-start.2) | collective-permute-done | bytes 819232 | tf_op jit(solution)/shard_map/ppermute | solution.py:498
  73.0 3.3 %fourier.3 = (f32[8,400,128]{2,1,0:T(8,128)S(1)}, f32[8,400,128]{2,1,0:T(8,128)S(1)}) custom-call(s32[8]{0:T(128)S(1)} %and_select_fusion.parity_ref, bf16[8,1,400,128]{3,2,1,0:T(8,128)(2,1)S(1)} %bitcast.24, bf16[8,1,400,128]{3,2,1,0:T(8,128)(2,1)S(1)} %bitcast.23, f32[8,2,4,128]{3,2,1,0:T(4,128)S(1)} %reshape.145.table_ref), custom_call_target="tpu_custom_call" | custom-call | tf_op jit(solution)/shard_map/fourier/pallas_call | solution.py:100
  76.3 12.3 %evolve.1 = (s16[8,960,128]{2,1,0:T(8,128)(2,1)S(1)}, f32[8,2,40,128]{3,2,1,0:T(8,128)S(1)}) custom-call(s32[8]{0:T(128)S(1)} %iota.17.order_ref, f32[8,400,128]{2,1,0:T(8,128)S(1)} %get-tuple-element.31.refs_0_.refs_4_.refs_8_.refs_12_, f32[8,400,128]{2,1,0:T(8,128)S(1)} %get-tuple-element.32.refs_1_.refs_5_.refs_9_.refs_13_, ...), custom_call_target="tpu_custom_call" | custom-call | tf_op jit(solution)/shard_map/evolve/pallas_call | solution.py:254
  88.6 0.0 copy-start.2
  88.6 1.3 copy-done.2
  89.9 14.9 %all_to_all.15 = f32[16,40,128]{2,1,0:T(8,128)S(1)} all-to-all(f32[16,40,128]{2,1,0:T(8,128)S(1)} %bitcast.25), channel_id=1, replica_groups=mesh['chip'=32,'core'=2,'freq'=8] {'freq','core'}, dimensions={0} | all-to-all | bytes 655360 | tf_op jit(solution)/shard_map/all_to_all | solution.py:506
  104.8 3.6 %all-to-all-start.2 = ((s16[8,960,128]{2,1,0:T(8,128)(2,1)}), s16[8,960,128]{2,1,0:T(8,128)(2,1)S(1)}, u32[]{:S(2)}, u32[]{:S(2)}) async-start(s16[8,960,128]{2,1,0:T(8,128)(2,1)} %copy-done.2), calls=%async_computation.2 | async-start | bytes 3932160 | tf_op jit(solution)/shard_map/all_to_all | solution.py:511
  108.4 9.0 %collective-permute-start.6 = (f32[40,128]{1,0:T(8,128)S(1)}, f32[40,128]{1,0:T(8,128)S(1)}, u32[]{:S(2)}, u32[]{:S(2)}) collective-permute-start(f32[40,128]{1,0:T(8,128)S(1)} %reduce_sum.9), channel_id=1, source_target_pairs={{0,384},{16,400},{32,416},{48,432},{64,448},{80,464},{96,480},{112... | collective-permute-start | bytes 61448 | tf_op jit(solution)/shard_map/ppermute | solution.py:28
  117.5 1.9 %collective-permute-start.5 = (f32[40,128]{1,0:T(8,128)S(1)}, f32[40,128]{1,0:T(8,128)S(1)}, u32[]{:S(2)}, u32[]{:S(2)}) collective-permute-start(f32[40,128]{1,0:T(8,128)S(1)} %reduce_sum.9), channel_id=1, source_target_pairs={{0,128},{16,144},{32,160},{48,176},{64,192},{80,208},{96,224},{112... | collective-permute-start | bytes 61448 | tf_op jit(solution)/shard_map/ppermute | solution.py:28
  119.4 3.1 %collective-permute-start.4 = (f32[40,128]{1,0:T(8,128)S(1)}, f32[40,128]{1,0:T(8,128)S(1)}, u32[]{:S(2)}, u32[]{:S(2)}) collective-permute-start(f32[40,128]{1,0:T(8,128)S(1)} %reduce_sum.9), channel_id=1, source_target_pairs={{0,256},{16,272},{32,288},{48,304},{64,320},{80,336},{96,352},{112... | collective-permute-start | bytes 61448 | tf_op jit(solution)/shard_map/ppermute | solution.py:28
  122.5 0.0 collective-permute-done.6
  122.5 0.0 collective-permute-done.5
  122.5 3.3 %collective-permute-done.4 = f32[40,128]{1,0:T(8,128)S(1)} collective-permute-done((f32[40,128]{1,0:T(8,128)S(1)}, f32[40,128]{1,0:T(8,128)S(1)}, u32[]{:S(2)}, u32[]{:S(2)}) %collective-permute-start.4) | collective-permute-done | bytes 20512 | tf_op jit(solution)/shard_map/ppermute | solution.py:28
  125.8 5.3 %collective-permute-start.9 = (f32[40,128]{1,0:T(8,128)S(1)}, f32[40,128]{1,0:T(8,128)S(1)}, u32[]{:S(2)}, u32[]{:S(2)}) collective-permute-start(f32[40,128]{1,0:T(8,128)S(1)} %add_add_fusion.1), channel_id=1, source_target_pairs={{0,48},{16,32},{32,16},{48,0},{64,112},{80,96},{96,80},{112,64},{1... | collective-permute-start | bytes 61448 | tf_op jit(solution)/shard_map/ppermute | solution.py:28
  131.1 1.9 %collective-permute-start.8 = (f32[40,128]{1,0:T(8,128)S(1)}, f32[40,128]{1,0:T(8,128)S(1)}, u32[]{:S(2)}, u32[]{:S(2)}) collective-permute-start(f32[40,128]{1,0:T(8,128)S(1)} %add_add_fusion.1), channel_id=1, source_target_pairs={{0,16},{16,0},{32,48},{48,32},{64,80},{80,64},{96,112},{112,96},{1... | collective-permute-start | bytes 61448 | tf_op jit(solution)/shard_map/ppermute | solution.py:28
  133.1 2.2 %collective-permute-start.7 = (f32[40,128]{1,0:T(8,128)S(1)}, f32[40,128]{1,0:T(8,128)S(1)}, u32[]{:S(2)}, u32[]{:S(2)}) collective-permute-start(f32[40,128]{1,0:T(8,128)S(1)} %add_add_fusion.1), channel_id=1, source_target_pairs={{0,32},{16,48},{32,0},{48,16},{64,96},{80,112},{96,64},{112,80},{1... | collective-permute-start | bytes 61448 | tf_op jit(solution)/shard_map/ppermute | solution.py:28
  135.3 0.0 collective-permute-done.9
  135.3 0.7 collective-permute-done.8
  135.9 2.8 %collective-permute-done.7 = f32[40,128]{1,0:T(8,128)S(1)} collective-permute-done((f32[40,128]{1,0:T(8,128)S(1)}, f32[40,128]{1,0:T(8,128)S(1)}, u32[]{:S(2)}, u32[]{:S(2)}) %collective-permute-start.7) | collective-permute-done | bytes 20512 | tf_op jit(solution)/shard_map/ppermute | solution.py:28
  138.8 4.8 %collective-permute-start.10 = (f32[40,128]{1,0:T(8,128)S(1)}, f32[40,128]{1,0:T(8,128)S(1)}, u32[]{:S(2)}, u32[]{:S(2)}) collective-permute-start(f32[40,128]{1,0:T(8,128)S(1)} %add_add_fusion), channel_id=1, source_target_pairs={{0,64},{16,80},{32,96},{48,112},{64,0},{80,16},{96,32},{112,48},{1... | collective-permute-start | bytes 61448 | tf_op jit(solution)/shard_map/ppermute | solution.py:28
  143.6 3.9 %collective-permute-done.10 = f32[40,128]{1,0:T(8,128)S(1)} collective-permute-done((f32[40,128]{1,0:T(8,128)S(1)}, f32[40,128]{1,0:T(8,128)S(1)}, u32[]{:S(2)}, u32[]{:S(2)}) %collective-permute-start.10) | collective-permute-done | bytes 20512 | tf_op jit(solution)/shard_map/ppermute | solution.py:28
  147.5 4.7 %collective-permute-start.11 = (f32[40,128]{1,0:T(8,128)S(1)}, f32[40,128]{1,0:T(8,128)S(1)}, u32[]{:S(2)}, u32[]{:S(2)}) collective-permute-start(f32[40,128]{1,0:T(8,128)S(1)} %add.56), channel_id=1, source_target_pairs={{0,8},{8,0},{1,9},{9,1},{2,10},{10,2},{3,11},{11,3},{4,12},{12,4},... | collective-permute-start | bytes 61448 | tf_op jit(solution)/shard_map/ppermute | solution.py:515
  152.2 0.8 collective-permute-done.11
  153.0 0.6 broadcast_select_fusion
  153.6 7.6 %factorize.1 = (f32[128,128]{1,0:T(8,128)}, f32[128,128]{1,0:T(8,128)}) custom-call(f32[40,128]{1,0:T(8,128)} %get-tuple-element.49.refs_0_, f32[40,128]{1,0:T(8,128)} %get-tuple-element.48.refs_1_), custom_call_target="tpu_custom_call" | custom-call | tf_op jit(solution)/shard_map/factorize/pallas_call | solution.py:344
  161.3 0.0 all-to-all-done.2.code_ref
  161.3 0.8 copy-done.4
  162.1 4.3 %apply.1 = f32[1,128,5,8,128]{4,3,2,1,0:T(8,128)} custom-call(f32[128,128]{1,0:T(8,128)S(1)} %copy-done.4, f32[8,128]{1,0:T(8,128)S(1)} %fusion.6.scale_ref, s16[8,960,128]{2,1,0:T(8,128)(2,1)S(1)} %all-to-all-done.2.code_ref), custom_call_target="tpu_custom_call" | custom-call | tf_op jit(solution)/shard_map/apply/pallas_call | solution.py:384
  (27 shorter events, 0.2 us)
Async XLA Ops:
  5.2 7.8 %copy-start.5 = (f32[8,128]{1,0:T(8,128)S(1)}, f32[8,128]{1,0:T(8,128)}, u32[]{:S(2)}) copy-start(f32[8,128]{1,0:T(8,128)} %velocity_ref) | copy-start | bytes 12292
  5.2 7.8 %copy-start.3 = (f32[5,5,8,128]{3,2,1,0:T(8,128)S(1)}, f32[5,5,8,128]{3,2,1,0:T(8,128)}, u32[]{:S(2)}) copy-start(f32[5,5,8,128]{3,2,1,0:T(8,128)} %param.5) | copy-start | bytes 307204
  5.3 14.7 %copy-start.6 = (s32[8]{0:T(128)S(1)}, s32[8]{0:T(128)}, u32[]{:S(2)}) copy-start(s32[8]{0:T(128)} %param.7) | copy-start | bytes 100
  5.3 49.6 %all-to-all-start = ((bf16[8,2,400,128]{3,2,1,0:T(8,128)(2,1)}), bf16[8,2,400,128]{3,2,1,0:T(8,128)(2,1)S(1)}, u32[]{:S(2)}, u32[]{:S(2)}) async-start(bf16[8,2,400,128]{3,2,1,0:T(8,128)(2,1)} %spread.1), calls=%async_computation | async-start | bytes 3276800 | tf_op jit(solution)/shard_map/all_to_all | solution.py:487
  13.1 7.5 %collective-permute-start = (f32[26,2,128]{2,1,0:T(2,128)S(1)}, f32[26,2,128]{2,1,0:T(2,128)S(1)}, u32[]{:S(2)}, u32[]{:S(2)}) collective-permute-start(f32[26,2,128]{2,1,0:T(2,128)S(1)} %pad_maximum_fusion), channel_id=1, source_target_pairs={{8,0},{16,8},{24,16},{32,24},{40,32},{48,40},{56,48},{64,56},{72,6... | collective-permute-start | bytes 79880 | tf_op jit(solution)/shard_map/ppermute | solution.py:461
  17.9 3.1 %collective-permute-start.1 = (f32[26,2,128]{2,1,0:T(2,128)S(1)}, f32[26,2,128]{2,1,0:T(2,128)S(1)}, u32[]{:S(2)}, u32[]{:S(2)}) collective-permute-start(f32[26,2,128]{2,1,0:T(2,128)S(1)} %pad_maximum_fusion.1), channel_id=1, source_target_pairs={{0,8},{8,16},{16,24},{24,32},{32,40},{40,48},{48,56},{56,64},{64,7... | collective-permute-start | bytes 79880 | tf_op jit(solution)/shard_map/ppermute | solution.py:462
  26.8 2.1 %copy-start = (f32[29,304,128]{2,1,0:T(8,128)}, f32[29,304,128]{2,1,0:T(8,128)S(1)}, u32[]{:S(2)}) copy-start(f32[29,304,128]{2,1,0:T(8,128)S(1)} %get-tuple-element.36.refs_20_) | copy-start | bytes 13541380
  55.0 13.7 %collective-permute-start.3 = (bf16[8,400,128]{2,1,0:T(8,128)(2,1)S(1)}, bf16[8,400,128]{2,1,0:T(8,128)(2,1)S(1)}, u32[]{:S(2)}, u32[]{:S(2)}) collective-permute-start(bf16[8,400,128]{2,1,0:T(8,128)(2,1)S(1)} %get-tuple-element.44), channel_id=1, source_target_pairs={{0,8},{8,16},{16,24},{24,32},{32,40},{40,48},{48,56},{56,64},{64,7... | collective-permute-start | bytes 2457608 | tf_op jit(solution)/shard_map/ppermute | solution.py:499
  59.4 13.7 %collective-permute-start.2 = (bf16[8,400,128]{2,1,0:T(8,128)(2,1)S(1)}, bf16[8,400,128]{2,1,0:T(8,128)(2,1)S(1)}, u32[]{:S(2)}, u32[]{:S(2)}) collective-permute-start(bf16[8,400,128]{2,1,0:T(8,128)(2,1)S(1)} %get-tuple-element.45), channel_id=1, source_target_pairs={{8,0},{16,8},{24,16},{32,24},{40,32},{48,40},{56,48},{64,56},{72,6... | collective-permute-start | bytes 2457608 | tf_op jit(solution)/shard_map/ppermute | solution.py:498
  61.3 15.0 %copy-start.1 = (f32[29,304,128]{2,1,0:T(8,128)S(1)}, f32[29,304,128]{2,1,0:T(8,128)}, u32[]{:S(2)}) copy-start(f32[29,304,128]{2,1,0:T(8,128)} %copy-done) | copy-start | bytes 13541380
  88.6 1.3 copy-start.2
  104.8 56.5 %all-to-all-start.2 = ((s16[8,960,128]{2,1,0:T(8,128)(2,1)}), s16[8,960,128]{2,1,0:T(8,128)(2,1)S(1)}, u32[]{:S(2)}, u32[]{:S(2)}) async-start(s16[8,960,128]{2,1,0:T(8,128)(2,1)} %copy-done.2), calls=%async_computation.2 | async-start | bytes 3932160 | tf_op jit(solution)/shard_map/all_to_all | solution.py:511
  108.4 14.1 %collective-permute-start.6 = (f32[40,128]{1,0:T(8,128)S(1)}, f32[40,128]{1,0:T(8,128)S(1)}, u32[]{:S(2)}, u32[]{:S(2)}) collective-permute-start(f32[40,128]{1,0:T(8,128)S(1)} %reduce_sum.9), channel_id=1, source_target_pairs={{0,384},{16,400},{32,416},{48,432},{64,448},{80,464},{96,480},{112... | collective-permute-start | bytes 61448 | tf_op jit(solution)/shard_map/ppermute | solution.py:28
  117.5 5.0 %collective-permute-start.5 = (f32[40,128]{1,0:T(8,128)S(1)}, f32[40,128]{1,0:T(8,128)S(1)}, u32[]{:S(2)}, u32[]{:S(2)}) collective-permute-start(f32[40,128]{1,0:T(8,128)S(1)} %reduce_sum.9), channel_id=1, source_target_pairs={{0,128},{16,144},{32,160},{48,176},{64,192},{80,208},{96,224},{112... | collective-permute-start | bytes 61448 | tf_op jit(solution)/shard_map/ppermute | solution.py:28
  119.4 6.4 %collective-permute-start.4 = (f32[40,128]{1,0:T(8,128)S(1)}, f32[40,128]{1,0:T(8,128)S(1)}, u32[]{:S(2)}, u32[]{:S(2)}) collective-permute-start(f32[40,128]{1,0:T(8,128)S(1)} %reduce_sum.9), channel_id=1, source_target_pairs={{0,256},{16,272},{32,288},{48,304},{64,320},{80,336},{96,352},{112... | collective-permute-start | bytes 61448 | tf_op jit(solution)/shard_map/ppermute | solution.py:28
  125.8 9.5 %collective-permute-start.9 = (f32[40,128]{1,0:T(8,128)S(1)}, f32[40,128]{1,0:T(8,128)S(1)}, u32[]{:S(2)}, u32[]{:S(2)}) collective-permute-start(f32[40,128]{1,0:T(8,128)S(1)} %add_add_fusion.1), channel_id=1, source_target_pairs={{0,48},{16,32},{32,16},{48,0},{64,112},{80,96},{96,80},{112,64},{1... | collective-permute-start | bytes 61448 | tf_op jit(solution)/shard_map/ppermute | solution.py:28
  131.1 4.8 %collective-permute-start.8 = (f32[40,128]{1,0:T(8,128)S(1)}, f32[40,128]{1,0:T(8,128)S(1)}, u32[]{:S(2)}, u32[]{:S(2)}) collective-permute-start(f32[40,128]{1,0:T(8,128)S(1)} %add_add_fusion.1), channel_id=1, source_target_pairs={{0,16},{16,0},{32,48},{48,32},{64,80},{80,64},{96,112},{112,96},{1... | collective-permute-start | bytes 61448 | tf_op jit(solution)/shard_map/ppermute | solution.py:28
  133.1 5.7 %collective-permute-start.7 = (f32[40,128]{1,0:T(8,128)S(1)}, f32[40,128]{1,0:T(8,128)S(1)}, u32[]{:S(2)}, u32[]{:S(2)}) collective-permute-start(f32[40,128]{1,0:T(8,128)S(1)} %add_add_fusion.1), channel_id=1, source_target_pairs={{0,32},{16,48},{32,0},{48,16},{64,96},{80,112},{96,64},{112,80},{1... | collective-permute-start | bytes 61448 | tf_op jit(solution)/shard_map/ppermute | solution.py:28
  138.8 8.7 %collective-permute-start.10 = (f32[40,128]{1,0:T(8,128)S(1)}, f32[40,128]{1,0:T(8,128)S(1)}, u32[]{:S(2)}, u32[]{:S(2)}) collective-permute-start(f32[40,128]{1,0:T(8,128)S(1)} %add_add_fusion), channel_id=1, source_target_pairs={{0,64},{16,80},{32,96},{48,112},{64,0},{80,16},{96,32},{112,48},{1... | collective-permute-start | bytes 61448 | tf_op jit(solution)/shard_map/ppermute | solution.py:28
  147.5 5.5 %collective-permute-start.11 = (f32[40,128]{1,0:T(8,128)S(1)}, f32[40,128]{1,0:T(8,128)S(1)}, u32[]{:S(2)}, u32[]{:S(2)}) collective-permute-start(f32[40,128]{1,0:T(8,128)S(1)} %add.56), channel_id=1, source_target_pairs={{0,8},{8,0},{1,9},{9,1},{2,10},{10,2},{3,11},{11,3},{4,12},{12,4},... | collective-permute-start | bytes 61448 | tf_op jit(solution)/shard_map/ppermute | solution.py:515
  161.3 0.8 copy-start.4

commit v8 on v7

--- a/solution.py
+++ b/solution.py
@@ -23,11 +23,14 @@
 VMEM_LIMIT = 28 * 1024 * 1024
 
 
-def xor_sum(value, axis, masks):
+def swap(value, axis, mask):
     count = lax.axis_size(axis)
-    for other in [lax.ppermute(value, axis, [(i, i ^ m) for i in range(count)]) for m in masks]:
-        value = value + other
-    return value
+    return lax.ppermute(value, axis, [(i, i ^ mask) for i in range(count)])
+
+
+def quad_sum(value, axis, one, two):
+    near, far, both = [swap(value, axis, mask) for mask in (one, two, one ^ two)]
+    return (value + near) + (far + both)
 
 
 def spread_body(sketch_ref, out_ref, rows_ref, turned_ref):
@@ -67,10 +70,12 @@
     )(sketch)
 
 
-def fourier_body(parity_ref, one_ref, two_ref, table_ref, z_one, z_two, pair_ref):
+def fourier_body(parity_ref, table_ref, *refs):
+    pair_ref = refs[-1]
+    groups = len(refs) // 2
     size = pair_ref.shape[2]
     first = lax.broadcasted_iota(jnp.int32, (8, LANES), 1) < K
-    for rows_ref, z_ref in ((one_ref, z_one), (two_ref, z_two)):
+    for rows_ref, z_ref in zip(refs[:groups], refs[groups : 2 * groups]):
 
         @pl.loop(0, rows_ref.shape[2] // size)
         def _(step):
@@ -92,26 +97,21 @@
                     )
 
 
-def fourier(parity, one, two, table, parts):
-    slots, _, count, _ = one.shape
+def fourier(parity, rows, parts, table):
+    slots, _, count, _ = rows[0].shape
     size = count // FIELDS
-    z_spec = pl.BlockSpec((F, count, LANES), lambda i: (0, 0, 0))
-    z_shape = jax.ShapeDtypeStruct((F, count, LANES), jnp.float32)
+    block = lambda part: pl.BlockSpec((slots, 1, count, LANES), lambda i: (0, part, 0, 0))
     return pl.pallas_call(
         fourier_body,
         grid=(1,),
-        in_specs=[
-            pl.BlockSpec(memory_space=pltpu.SMEM),
-            pl.BlockSpec((slots, 1, count, LANES), lambda i: (0, parts[0], 0, 0)),
-            pl.BlockSpec((slots, 1, count, LANES), lambda i: (0, parts[1], 0, 0)),
-            pl.BlockSpec(table.shape, lambda i: (0, 0, 0, 0)),
-        ],
-        out_specs=[z_spec, z_spec],
-        out_shape=[z_shape, z_shape],
+        in_specs=[pl.BlockSpec(memory_space=pltpu.SMEM), pl.BlockSpec(table.shape, lambda i: (0, 0, 0, 0))]
+        + [block(part) for part in parts],
+        out_specs=[pl.BlockSpec((F, count, LANES), lambda i: (0, 0, 0))] * len(rows),
+        out_shape=[jax.ShapeDtypeStruct((F, count, LANES), jnp.float32)] * len(rows),
         scratch_shapes=[pltpu.VMEM((2, 4, size, LANES), jnp.float32)],
         compiler_params=pltpu.CompilerParams(vmem_limit_bytes=VMEM_LIMIT),
         name="fourier",
-    )(parity, one, two, table)
+    )(parity, table, *rows)
 
 
 def split(value):
@@ -168,20 +168,21 @@
     wide = per + 2 * RH
 
     for n in range(TOGETHER):
-        low, high, right, left = layers[4 * n : 4 * n + 4]
+        low, high, inner, outer = layers[4 * n : 4 * n + 4]
+        core = order_ref[F]
 
         @pl.loop(0, FIELDS)
         def _(field):
-            for group, ref in enumerate((left, low, high, right)):
+            for group, ref in ((1, low), (2, high), (3 - 3 * core, inner), (3 * core, outer)):
                 for x in range(HALF):
                     source = field * wide * HALF + x
-                    target = 8 + PITCH * (group * HALF + x)
-                    z_ref[n, field, target - RH : target, :] = ref[0, pl.ds(source, RH, stride=HALF), :]
+                    target = pl.multiple_of(8 + PITCH * (group * HALF + x), 8)
+                    z_ref[n, field, pl.ds(target - RH, RH), :] = ref[0, pl.ds(source, RH, stride=HALF), :]
                     for r in range(0, per, 8):
-                        z_ref[n, field, target + r : target + r + 8, :] = ref[
+                        z_ref[n, field, pl.ds(target + r, 8), :] = ref[
                             0, pl.ds(source + (r + RH) * HALF, 8, stride=HALF), :
                         ]
-                    z_ref[n, field, target + per : target + per + RH, :] = ref[
+                    z_ref[n, field, pl.ds(target + per, RH), :] = ref[
                         0, pl.ds(source + (per + RH) * HALF, RH, stride=HALF), :
                     ]
 
@@ -244,8 +245,8 @@
         code_ref[n, 0:count, :], code_ref[n, count : count + count // 2, :] = encode(block, scale)
 
 
-def evolve(order, low, high, right, left, coef, mask, turn):
-    count = order.shape[0]
+def evolve(order, low, high, inner, outer, coef, mask, turn):
+    count = order.shape[0] - 1
     rows = low.shape[1]
     per = rows // (FIELDS * HALF) - 2 * RH
     whole = lambda shape: pl.BlockSpec(shape, lambda i, order: (0,) * len(shape))
@@ -275,16 +276,18 @@
         ],
         compiler_params=pltpu.CompilerParams(vmem_limit_bytes=VMEM_LIMIT),
         name="evolve",
-    )(order, *([low, high, right, left] * TOGETHER), *([turn] * TOGETHER), coef, mask)
-
-
-def factor_body(scale, *refs):
+    )(order, *([low, high, inner, outer] * TOGETHER), *([turn] * TOGETHER), coef, mask)
+
+
+def factor_body(scale, core_ref, *refs):
     parts = refs[:-2]
     inverse_ref, factor_ref = refs[-2:]
     blocks = LANES // 8
     lane = lax.broadcasted_iota(jnp.int32, (8, LANES), 1)
     sub = lax.broadcasted_iota(jnp.int32, (8, LANES), 0)
-    gram = unpack(parts[0][...], parts[1][...])
+    mine, other = parts[0][...] + parts[1][...], parts[2][...] + parts[3][...]
+    lower = jnp.full(mine.shape, core_ref[0], jnp.int32) == 0
+    gram = unpack(jnp.where(lower, mine, other), jnp.where(lower, other, mine))
     w = [gram[8 * b : 8 * b + 8] for b in range(blocks)]
     full = lambda v: jnp.broadcast_to(v, (8, LANES))
     for b in range(blocks):
@@ -338,16 +341,16 @@
     factor_ref[...] = factor_ref[...].T
 
 
-def factorize(parts, scale):
+def factorize(core, parts, scale):
     vmem = pl.BlockSpec(memory_space=pltpu.VMEM)
     shape = jax.ShapeDtypeStruct((LANES, LANES), jnp.float32)
     return pl.pallas_call(
         partial(factor_body, scale),
-        in_specs=[vmem] * len(parts),
+        in_specs=[pl.BlockSpec(memory_space=pltpu.SMEM)] + [vmem] * len(parts),
         out_specs=[vmem, vmem],
         out_shape=[shape, shape],
         name="factorize",
-    )(*parts)
+    )(core[None], *parts)
 
 
 def apply_body(inverse_ref, scale_ref, code_ref, out_ref, rows_ref, all_ref):
@@ -495,13 +498,17 @@
     coef, mask = stencil(coupling, velocity, per)
 
     rows, coef, mask, turn, waves, parity = lax.optimization_barrier((rows, coef, mask, turn, waves, parity))
-    right = lax.ppermute(rows[:, 0], SPACE, [(i + 1, i) for i in range(count - 1)])
-    left = lax.ppermute(rows[:, 1], SPACE, [(i, i + 1) for i in range(count - 1)])
-    low, high = fourier(parity, rows, rows, waves, (0, 1))
-    right, left = fourier(parity, right[:, None], left[:, None], waves, (0, 0))
-
-    columns, grams = evolve(jnp.arange(F, dtype=jnp.int32), low, high, right, left, coef, mask, turn)
     core = lax.axis_index("core")
+    outer = lax.dynamic_index_in_dim(rows, core, 1, keepdims=False)
+    inner = lax.dynamic_index_in_dim(rows, 1 - core, 1, keepdims=False)
+    outer = lax.ppermute(outer, SPACE, [(i, i + 1 if i % 2 else i - 1) for i in range(1, count - 1)])
+    inner = swap(inner, "core", 1)
+    low, high = fourier(parity, [rows, rows], [0, 1], waves)
+    (inner,) = fourier(parity, [inner[:, None]], [0], waves)
+    (outer,) = fourier(parity, [outer[:, None]], [0], waves)
+    order = jnp.concatenate([jnp.arange(F, dtype=jnp.int32), core[None]])
+
+    columns, grams = evolve(order, low, high, inner, outer, coef, mask, turn)
     grams = grams.reshape(groups * 2, HALF_ROWS, LANES)
     parts = lax.all_to_all(grams, ("freq", "core"), split_axis=0, concat_axis=0, tiled=True)
     gram = jnp.sum(parts, axis=0)
@@ -509,13 +516,11 @@
     scales = jnp.where(core == 0, parts[:, 0], parts[:, 1])
     columns, gram = lax.optimization_barrier((columns, gram))
     columns = lax.all_to_all(columns, "freq", split_axis=0, concat_axis=0, tiled=True)
-    gram = xor_sum(gram, "chip", (16, 8, 24))
-    gram = xor_sum(gram, "chip", (2, 1, 3))
-    gram = xor_sum(gram, "chip", (4,))
-    other = lax.ppermute(gram, "core", [(0, 1), (1, 0)])
-    parts = [jnp.where(core == 0, gram, other), jnp.where(core == 0, other, gram)]
+    gram = quad_sum(gram, "chip", 16, 8)
+    gram = quad_sum(gram, "chip", 2, 1)
+    parts = [gram] + [swap(gram, ("chip", "core"), mask) for mask in (8, 1, 9)]
     row_scale = math.sqrt(FIELDS * 8 * count * radial)
-    inverse, factor = factorize(parts, row_scale)
+    inverse, factor = factorize(core, parts, row_scale)
     return apply(inverse, scales, columns), factor[None]
 
 

time: 167 us -> 171 us (1.024)
  starting transfers between devices: 57.4 us -> 63.2 us
  waiting for transfers between devices: 46.4 us -> 43.8 us
    ppermute x10 -> x11, starting transfers between devices: 39.3 us -> 45.1 us  [the longest x10 40.4 us: swap(): return lax.ppermute(value, axis, [(i, i ^ mask) for i in range(count)])]
    ppermute x1, waiting for transfers between devices: 0.01 us -> 2.87 us  [stencil(): right = lax.ppermute(edges[0], SPACE, down)]
    ppermute x1, starting transfers between devices: 4.73 us -> 1.92 us  [stencil(): right = lax.ppermute(edges[0], SPACE, down)]
    ppermute x1, starting transfers between devices: 2.03 us -> 4.84 us  [stencil(): left = lax.ppermute(edges[1], SPACE, up)]
    ppermute x10 -> x11, waiting for transfers between devices: 19.9 us -> 17.4 us  [the longest x10 12.6 us: swap(): return lax.ppermute(value, axis, [(i, i ^ mask) for i in range(count)])]
    all_to_all x1, waiting for transfers between devices: 26.1 us -> 23.6 us  [local(): rows = lax.all_to_all(rows, 'freq', split_axis=0, concat_axis=0, tiled=True)]
    unnamed x15 -> x25, local copies, waits for them, and re-layouts: 4.18 us -> 4.8 us
    pallas_call x2 -> x3, Pallas kernels: 6.54 us -> 7.03 us  [fourier(): pl.pallas_call(fourier_body, grid=(1,), in_specs=[pl.BlockSpec(memory_spa...]
  transfers between devices with their start and end apart: 14 -> 15, of which waited for: 9 -> 7; matrix products, arithmetic and copies ran while one was open for 1% -> 0% of each run, Pallas kernels for 10% -> 11%
where the time goes in v8:
time: 171 us
  starting transfers between devices  63.2 us (37%)
  waiting for transfers between devices  43.8 us (26%)
  Pallas kernels  41.9 us (25%)
  blocking collectives  14.9 us (9%)
  local copies, waits for them, and re-layouts  5.32 us (3%)
    ppermute x10, starting transfers between devices, swap(): return lax.ppermute(value, axis, [(i, i ^ mask) for i in range(count)])  40.4 us
    all_to_all x1, waiting for transfers between devices, local(): rows = lax.all_to_all(rows, 'freq', split_axis=0, concat_axis=0, tiled=True)  23.6 us
    all_to_all x1, blocking collectives, local(): lax.all_to_all(grams, ('freq', 'core'), split_axis=0, concat_axis=0, tile...  14.9 us
    ppermute x10, waiting for transfers between devices, swap(): return lax.ppermute(value, axis, [(i, i ^ mask) for i in range(count)])  12.6 us
    pallas_call x1, Pallas kernels, evolve(): pl.pallas_call(evolve_body, grid_spec=pltpu.PrefetchScalarGridSpec(num_sc...  12.5 us
    all_to_all x1, starting transfers between devices, local(): rows = lax.all_to_all(rows, 'freq', split_axis=0, concat_axis=0, tiled=True)  7.79 us
    pallas_call x1, Pallas kernels, factorize(): pl.pallas_call(partial(factor_body, scale), in_specs=[pl.BlockSpec(memory...  7.68 us
    pallas_call x3, Pallas kernels, fourier(): pl.pallas_call(fourier_body, grid=(1,), in_specs=[pl.BlockSpec(memory_spa...  7.03 us
  transfers between devices with their start and end apart: 15, of which 7 were waited for; matrix products, arithmetic and copies ran while one was open for 0% of the time, Pallas kernels for 11%

profile of v8, /device:TPU:1, one launch (start us, length us, event | category | flops | bytes accessed | tf_op | source)
XLA Modules:
  0.0 170.5 jit_solution(481484926077605208)
XLA Ops:
  0.6 4.6 %spread.1 = bf16[8,2,400,128]{3,2,1,0:T(8,128)(2,1)} custom-call(bf16[2,64,5,8,128]{4,3,2,1,0:T(8,128)(2,1)} %sketch_ref.1), custom_call_target="tpu_custom_call" | custom-call | tf_op jit(solution)/shard_map/spread/pallas_call | solution.py:58
  5.3 7.8 %all-to-all-start = ((bf16[8,2,400,128]{3,2,1,0:T(8,128)(2,1)}), bf16[8,2,400,128]{3,2,1,0:T(8,128)(2,1)S(1)}, u32[]{:S(2)}, u32[]{:S(2)}) async-start(bf16[8,2,400,128]{3,2,1,0:T(8,128)(2,1)} %spread.1), calls=%async_computation | async-start | bytes 3276800 | tf_op jit(solution)/shard_map/all_to_all | solution.py:490
  13.1 4.8 %collective-permute-start.1 = (f32[26,2,128]{2,1,0:T(2,128)S(1)}, f32[26,2,128]{2,1,0:T(2,128)S(1)}, u32[]{:S(2)}, u32[]{:S(2)}) collective-permute-start(f32[26,2,128]{2,1,0:T(2,128)S(1)} %pad_maximum_fusion.1), channel_id=1, source_target_pairs={{0,8},{8,16},{16,24},{24,32},{32,40},{40,48},{48,56},{56,64},{64,7... | collective-permute-start | bytes 79880 | tf_op jit(solution)/shard_map/ppermute | solution.py:465
  18.0 1.9 %collective-permute-start = (f32[26,2,128]{2,1,0:T(2,128)S(1)}, f32[26,2,128]{2,1,0:T(2,128)S(1)}, u32[]{:S(2)}, u32[]{:S(2)}) collective-permute-start(f32[26,2,128]{2,1,0:T(2,128)S(1)} %pad_maximum_fusion), channel_id=1, source_target_pairs={{8,0},{16,8},{24,16},{32,24},{40,32},{48,40},{56,48},{64,56},{72,6... | collective-permute-start | bytes 79880 | tf_op jit(solution)/shard_map/ppermute | solution.py:464
  20.0 0.1 fusion.7
  20.1 0.1 broadcast_multiply_fusion
  20.1 0.1 pad_add_fusion.1.place_ref
  20.2 0.1 copy.7
  20.3 0.1 broadcast_in_dim.46
  20.5 0.1 reshape.145.table_ref
  20.6 0.0 collective-permute-done.1.left_ref
  20.6 2.9 %collective-permute-done.right_ref = f32[26,2,128]{2,1,0:T(2,128)S(1)} collective-permute-done((f32[26,2,128]{2,1,0:T(2,128)S(1)}, f32[26,2,128]{2,1,0:T(2,128)S(1)}, u32[]{:S(2)}, u32[]{:S(2)}) %collective-permute-start) | collective-permute-done | bytes 26656 | tf_op jit(solution)/shard_map/ppermute | solution.py:464
  23.5 5.8 %stencil.1 = (f32[29,304,128]{2,1,0:T(8,128)S(1)}, f32[304,128]{1,0:T(8,128)S(1)}) custom-call(s32[3]{0:T(128)S(1)} %pad_add_fusion.1.place_ref, f32[25,8,128]{2,1,0:T(8,128)S(1)} %bitcast.30, f32[8,128]{1,0:T(8,128)S(1)} %copy-done.4, f32[26,2,128]{2,1,0:T(2,128)S(1)} %collective-permute-done.right_ref, f32[26,2,128]{2,1,0:T(2,128)S(1)} %collective-permute-done.1.left_ref), custom_call_target="tpu_custom_call" | custom-call | tf_op jit(solution)/shard_map/stencil/pallas_call | solution.py:468
  29.2 2.1 %copy-done = f32[29,304,128]{2,1,0:T(8,128)} copy-done((f32[29,304,128]{2,1,0:T(8,128)}, f32[29,304,128]{2,1,0:T(8,128)S(1)}, u32[]{:S(2)}) %copy-start) | copy-done | bytes 4513816
  31.3 23.6 %all-to-all-done.refs_0_.refs_1_ = bf16[8,2,400,128]{3,2,1,0:T(8,128)(2,1)S(1)} async-done(((bf16[8,2,400,128]{3,2,1,0:T(8,128)(2,1)}), bf16[8,2,400,128]{3,2,1,0:T(8,128)(2,1)S(1)}, u32[]{:S(2)}, u32[]{:S(2)}) %all-to-all-start) | async-done | bytes 1638432 | tf_op jit(solution)/shard_map/all_to_all | solution.py:490
  54.9 0.1 dynamic-slice_bitcast_fusion
  55.0 4.6 %collective-permute-start.3 = (bf16[8,400,128]{2,1,0:T(8,128)(2,1)S(1)}, bf16[8,400,128]{2,1,0:T(8,128)(2,1)S(1)}, u32[]{:S(2)}, u32[]{:S(2)}) collective-permute-start(bf16[8,400,128]{2,1,0:T(8,128)(2,1)S(1)} %get-tuple-element.40), channel_id=1, source_target_pairs={{8,16},{16,8},{24,32},{32,24},{40,48},{48,40},{56,64},{64,56},{72,... | collective-permute-start | bytes 2457608 | tf_op jit(solution)/shard_map/ppermute | solution.py:504
  59.6 1.9 %collective-permute-start.2 = (bf16[8,400,128]{2,1,0:T(8,128)(2,1)S(1)}, bf16[8,400,128]{2,1,0:T(8,128)(2,1)S(1)}, u32[]{:S(2)}, u32[]{:S(2)}) collective-permute-start(bf16[8,400,128]{2,1,0:T(8,128)(2,1)S(1)} %get-tuple-element.41), channel_id=1, source_target_pairs={{0,8},{8,0},{1,9},{9,1},{2,10},{10,2},{3,11},{11,3},{4,12},{12,4},... | collective-permute-start | bytes 2457608 | tf_op jit(solution)/shard_map/ppermute | solution.py:28
  61.6 0.1 pad_add_fusion.order_ref
  61.7 3.2 %fourier.3 = (f32[8,400,128]{2,1,0:T(8,128)S(1)}, f32[8,400,128]{2,1,0:T(8,128)S(1)}) custom-call(s32[8]{0:T(128)S(1)} %and_select_fusion.parity_ref, f32[8,2,4,128]{3,2,1,0:T(4,128)S(1)} %reshape.145.table_ref, bf16[8,2,400,128]{3,2,1,0:T(8,128)(2,1)S(1)} %all-to-all-done.refs_0_.refs_1_, bf16[8,2,400,128]{3,2,1,0:T(8,128)(2,1)S(1)} %all-to-all-done.refs_0_.refs_1_), custom_call_target="tpu_custom_call" | custom-call | tf_op jit(solution)/shard_map/fourier/pallas_call | solution.py:104
  64.9 4.7 %collective-permute-done.3 = bf16[8,400,128]{2,1,0:T(8,128)(2,1)S(1)} collective-permute-done((bf16[8,400,128]{2,1,0:T(8,128)(2,1)S(1)}, bf16[8,400,128]{2,1,0:T(8,128)(2,1)S(1)}, u32[]{:S(2)}, u32[]{:S(2)}) %collective-permute-start.3) | collective-permute-done | bytes 819232 | tf_op jit(solution)/shard_map/ppermute | solution.py:504
  69.7 1.9 %fourier.5.refs_3_.refs_7_.refs_11_.refs_15_ = f32[8,400,128]{2,1,0:T(8,128)S(1)} custom-call(s32[8]{0:T(128)S(1)} %and_select_fusion.parity_ref, f32[8,2,4,128]{3,2,1,0:T(4,128)S(1)} %reshape.145.table_ref, bf16[8,1,400,128]{3,2,1,0:T(8,128)(2,1)S(1)} %bitcast.27), custom_call_target="tpu_custom_call" | custom-call | tf_op jit(solution)/shard_map/fourier/pallas_call | solution.py:104
  71.5 0.0 collective-permute-done.2
  71.6 1.9 %fourier.4.refs_2_.refs_6_.refs_10_.refs_14_ = f32[8,400,128]{2,1,0:T(8,128)S(1)} custom-call(s32[8]{0:T(128)S(1)} %and_select_fusion.parity_ref, f32[8,2,4,128]{3,2,1,0:T(4,128)S(1)} %reshape.145.table_ref, bf16[8,1,400,128]{3,2,1,0:T(8,128)(2,1)S(1)} %bitcast.26), custom_call_target="tpu_custom_call" | custom-call | tf_op jit(solution)/shard_map/fourier/pallas_call | solution.py:104
  73.5 12.5 %evolve.1 = (s16[8,960,128]{2,1,0:T(8,128)(2,1)S(1)}, f32[8,2,40,128]{3,2,1,0:T(8,128)S(1)}) custom-call(s32[9]{0:T(128)S(1)} %pad_add_fusion.order_ref, f32[8,400,128]{2,1,0:T(8,128)S(1)} %get-tuple-element.29.refs_0_.refs_4_.refs_8_.refs_12_, f32[8,400,128]{2,1,0:T(8,128)S(1)} %get-tuple-element.30.refs_1_.refs_5_.refs_9_.refs_13_, ...), custom_call_target="tpu_custom_call" | custom-call | tf_op jit(solution)/shard_map/evolve/pallas_call | solution.py:255
  86.0 0.0 copy-start.1
  86.0 1.3 copy-done.1
  87.2 14.9 %all_to_all.15 = f32[16,40,128]{2,1,0:T(8,128)S(1)} all-to-all(f32[16,40,128]{2,1,0:T(8,128)S(1)} %bitcast.28), channel_id=1, replica_groups=mesh['chip'=32,'core'=2,'freq'=8] {'freq','core'}, dimensions={0} | all-to-all | bytes 655360 | tf_op jit(solution)/shard_map/all_to_all | solution.py:513
  102.2 3.6 %all-to-all-start.2 = ((s16[8,960,128]{2,1,0:T(8,128)(2,1)}), s16[8,960,128]{2,1,0:T(8,128)(2,1)S(1)}, u32[]{:S(2)}, u32[]{:S(2)}) async-start(s16[8,960,128]{2,1,0:T(8,128)(2,1)} %copy-done.1), calls=%async_computation.2 | async-start | bytes 3932160 | tf_op jit(solution)/shard_map/all_to_all | solution.py:518
  105.8 10.9 %collective-permute-start.4 = (f32[40,128]{1,0:T(8,128)S(1)}, f32[40,128]{1,0:T(8,128)S(1)}, u32[]{:S(2)}, u32[]{:S(2)}) collective-permute-start(f32[40,128]{1,0:T(8,128)S(1)} %reduce_sum.9), channel_id=1, source_target_pairs={{0,256},{16,272},{32,288},{48,304},{64,320},{80,336},{96,352},{112... | collective-permute-start | bytes 61448 | tf_op jit(solution)/shard_map/ppermute | solution.py:28
  116.7 2.5 %collective-permute-start.5 = (f32[40,128]{1,0:T(8,128)S(1)}, f32[40,128]{1,0:T(8,128)S(1)}, u32[]{:S(2)}, u32[]{:S(2)}) collective-permute-start(f32[40,128]{1,0:T(8,128)S(1)} %reduce_sum.9), channel_id=1, source_target_pairs={{0,128},{16,144},{32,160},{48,176},{64,192},{80,208},{96,224},{112... | collective-permute-start | bytes 61448 | tf_op jit(solution)/shard_map/ppermute | solution.py:28
  119.2 2.2 %collective-permute-start.6 = (f32[40,128]{1,0:T(8,128)S(1)}, f32[40,128]{1,0:T(8,128)S(1)}, u32[]{:S(2)}, u32[]{:S(2)}) collective-permute-start(f32[40,128]{1,0:T(8,128)S(1)} %reduce_sum.9), channel_id=1, source_target_pairs={{0,384},{16,400},{32,416},{48,432},{64,448},{80,464},{96,480},{112... | collective-permute-start | bytes 61448 | tf_op jit(solution)/shard_map/ppermute | solution.py:28
  121.4 0.0 collective-permute-done.4
  121.4 0.2 collective-permute-done.5
  121.6 3.7 %collective-permute-done.6 = f32[40,128]{1,0:T(8,128)S(1)} collective-permute-done((f32[40,128]{1,0:T(8,128)S(1)}, f32[40,128]{1,0:T(8,128)S(1)}, u32[]{:S(2)}, u32[]{:S(2)}) %collective-permute-start.6) | collective-permute-done | bytes 20512 | tf_op jit(solution)/shard_map/ppermute | solution.py:28
  125.2 1.9 %collective-permute-start.7 = (f32[40,128]{1,0:T(8,128)S(1)}, f32[40,128]{1,0:T(8,128)S(1)}, u32[]{:S(2)}, u32[]{:S(2)}) collective-permute-start(f32[40,128]{1,0:T(8,128)S(1)} %add_add_fusion.1), channel_id=1, source_target_pairs={{0,32},{16,48},{32,0},{48,16},{64,96},{80,112},{96,64},{112,80},{1... | collective-permute-start | bytes 61448 | tf_op jit(solution)/shard_map/ppermute | solution.py:28
  127.2 2.6 %collective-permute-start.8 = (f32[40,128]{1,0:T(8,128)S(1)}, f32[40,128]{1,0:T(8,128)S(1)}, u32[]{:S(2)}, u32[]{:S(2)}) collective-permute-start(f32[40,128]{1,0:T(8,128)S(1)} %add_add_fusion.1), channel_id=1, source_target_pairs={{0,16},{16,0},{32,48},{48,32},{64,80},{80,64},{96,112},{112,96},{1... | collective-permute-start | bytes 61448 | tf_op jit(solution)/shard_map/ppermute | solution.py:28
  129.7 4.8 %collective-permute-start.9 = (f32[40,128]{1,0:T(8,128)S(1)}, f32[40,128]{1,0:T(8,128)S(1)}, u32[]{:S(2)}, u32[]{:S(2)}) collective-permute-start(f32[40,128]{1,0:T(8,128)S(1)} %add_add_fusion.1), channel_id=1, source_target_pairs={{0,48},{16,32},{32,16},{48,0},{64,112},{80,96},{96,80},{112,64},{1... | collective-permute-start | bytes 61448 | tf_op jit(solution)/shard_map/ppermute | solution.py:28
  134.6 0.0 collective-permute-done.7
  134.6 1.8 %collective-permute-done.9 = f32[40,128]{1,0:T(8,128)S(1)} collective-permute-done((f32[40,128]{1,0:T(8,128)S(1)}, f32[40,128]{1,0:T(8,128)S(1)}, u32[]{:S(2)}, u32[]{:S(2)}) %collective-permute-start.9) | collective-permute-done | bytes 20512 | tf_op jit(solution)/shard_map/ppermute | solution.py:28
  136.4 7.6 %collective-permute-start.10 = (f32[40,128]{1,0:T(8,128)S(1)}, f32[40,128]{1,0:T(8,128)S(1)}, u32[]{:S(2)}, u32[]{:S(2)}) collective-permute-start(f32[40,128]{1,0:T(8,128)S(1)} %add_add_fusion.refs_0_), channel_id=1, source_target_pairs={{0,64},{8,72},{16,80},{24,88},{32,96},{40,104},{48,112},{56,120},{... | collective-permute-start | bytes 61448 | tf_op jit(solution)/shard_map/ppermute | solution.py:28
  143.9 4.2 %collective-permute-start.11 = (f32[40,128]{1,0:T(8,128)S(1)}, f32[40,128]{1,0:T(8,128)S(1)}, u32[]{:S(2)}, u32[]{:S(2)}) collective-permute-start(f32[40,128]{1,0:T(8,128)S(1)} %add_add_fusion.refs_0_), channel_id=1, source_target_pairs={{0,8},{8,0},{16,24},{24,16},{32,40},{40,32},{48,56},{56,48},{64,72... | collective-permute-start | bytes 61448 | tf_op jit(solution)/shard_map/ppermute | solution.py:28
  148.1 1.9 %collective-permute-start.12 = (f32[40,128]{1,0:T(8,128)S(1)}, f32[40,128]{1,0:T(8,128)S(1)}, u32[]{:S(2)}, u32[]{:S(2)}) collective-permute-start(f32[40,128]{1,0:T(8,128)S(1)} %add_add_fusion.refs_0_), channel_id=1, source_target_pairs={{0,72},{8,64},{16,88},{24,80},{32,104},{40,96},{48,120},{56,112},{... | collective-permute-start | bytes 61448 | tf_op jit(solution)/shard_map/ppermute | solution.py:28
  150.1 7.0 %collective-permute-done.12.refs_3_ = f32[40,128]{1,0:T(8,128)S(1)} collective-permute-done((f32[40,128]{1,0:T(8,128)S(1)}, f32[40,128]{1,0:T(8,128)S(1)}, u32[]{:S(2)}, u32[]{:S(2)}) %collective-permute-start.12) | collective-permute-done | bytes 20512 | tf_op jit(solution)/shard_map/ppermute | solution.py:28
  157.1 0.6 copy-done.8
  157.7 7.7 %factorize.1 = (f32[128,128]{1,0:T(8,128)}, f32[128,128]{1,0:T(8,128)}) custom-call(s32[1]{0:T(128)} %bitcast.core_ref, f32[40,128]{1,0:T(8,128)} %copy-done.5, f32[40,128]{1,0:T(8,128)} %copy-done.6, f32[40,128]{1,0:T(8,128)} %copy-done.7, f32[40,128]{1,0:T(8,128)} %copy-done.8), custom_call_target="tpu_custom_call" | custom-call | tf_op jit(solution)/shard_map/factorize/pallas_call | solution.py:347
  165.4 0.8 copy-done.3
  166.3 4.3 %apply.1 = f32[1,128,5,8,128]{4,3,2,1,0:T(8,128)} custom-call(f32[128,128]{1,0:T(8,128)S(1)} %copy-done.3, f32[8,128]{1,0:T(8,128)S(1)} %fusion.6.scale_ref, s16[8,960,128]{2,1,0:T(8,128)(2,1)S(1)} %all-to-all-done.2.code_ref), custom_call_target="tpu_custom_call" | custom-call | tf_op jit(solution)/shard_map/apply/pallas_call | solution.py:387
  (40 shorter events, 0.2 us)
Async XLA Ops:
  5.2 7.8 %copy-start.4 = (f32[8,128]{1,0:T(8,128)S(1)}, f32[8,128]{1,0:T(8,128)}, u32[]{:S(2)}) copy-start(f32[8,128]{1,0:T(8,128)} %velocity_ref) | copy-start | bytes 12292
  5.2 7.8 %copy-start.2 = (f32[5,5,8,128]{3,2,1,0:T(8,128)S(1)}, f32[5,5,8,128]{3,2,1,0:T(8,128)}, u32[]{:S(2)}) copy-start(f32[5,5,8,128]{3,2,1,0:T(8,128)} %param.5) | copy-start | bytes 307204
  5.3 14.7 %copy-start.9 = (s32[8]{0:T(128)S(1)}, s32[8]{0:T(128)}, u32[]{:S(2)}) copy-start(s32[8]{0:T(128)} %param.7) | copy-start | bytes 100
  5.3 49.6 %all-to-all-start = ((bf16[8,2,400,128]{3,2,1,0:T(8,128)(2,1)}), bf16[8,2,400,128]{3,2,1,0:T(8,128)(2,1)S(1)}, u32[]{:S(2)}, u32[]{:S(2)}) async-start(bf16[8,2,400,128]{3,2,1,0:T(8,128)(2,1)} %spread.1), calls=%async_computation | async-start | bytes 3276800 | tf_op jit(solution)/shard_map/all_to_all | solution.py:490
  13.1 7.5 %collective-permute-start.1 = (f32[26,2,128]{2,1,0:T(2,128)S(1)}, f32[26,2,128]{2,1,0:T(2,128)S(1)}, u32[]{:S(2)}, u32[]{:S(2)}) collective-permute-start(f32[26,2,128]{2,1,0:T(2,128)S(1)} %pad_maximum_fusion.1), channel_id=1, source_target_pairs={{0,8},{8,16},{16,24},{24,32},{32,40},{40,48},{48,56},{56,64},{64,7... | collective-permute-start | bytes 79880 | tf_op jit(solution)/shard_map/ppermute | solution.py:465
  18.0 5.5 %collective-permute-start = (f32[26,2,128]{2,1,0:T(2,128)S(1)}, f32[26,2,128]{2,1,0:T(2,128)S(1)}, u32[]{:S(2)}, u32[]{:S(2)}) collective-permute-start(f32[26,2,128]{2,1,0:T(2,128)S(1)} %pad_maximum_fusion), channel_id=1, source_target_pairs={{8,0},{16,8},{24,16},{32,24},{40,32},{48,40},{56,48},{64,56},{72,6... | collective-permute-start | bytes 79880 | tf_op jit(solution)/shard_map/ppermute | solution.py:464
  29.2 2.1 %copy-start = (f32[29,304,128]{2,1,0:T(8,128)}, f32[29,304,128]{2,1,0:T(8,128)S(1)}, u32[]{:S(2)}) copy-start(f32[29,304,128]{2,1,0:T(8,128)S(1)} %get-tuple-element.32.refs_20_) | copy-start | bytes 13541380
  54.9 18.6 %slice-start = ((s8[4513792]{0:T(1024)(128)(4,1)}), s8[4194304]{0:T(1024)(128)(4,1)S(1)}, s32[]{:S(2)}) async-start(s8[4513792]{0:T(1024)(128)(4,1)} %bitcast.24), calls=%async_computation.3 | async-start | bytes 8388608
  55.0 14.6 %collective-permute-start.3 = (bf16[8,400,128]{2,1,0:T(8,128)(2,1)S(1)}, bf16[8,400,128]{2,1,0:T(8,128)(2,1)S(1)}, u32[]{:S(2)}, u32[]{:S(2)}) collective-permute-start(bf16[8,400,128]{2,1,0:T(8,128)(2,1)S(1)} %get-tuple-element.40), channel_id=1, source_target_pairs={{8,16},{16,8},{24,32},{32,24},{40,48},{48,40},{56,64},{64,56},{72,... | collective-permute-start | bytes 2457608 | tf_op jit(solution)/shard_map/ppermute | solution.py:504
  59.6 11.9 %collective-permute-start.2 = (bf16[8,400,128]{2,1,0:T(8,128)(2,1)S(1)}, bf16[8,400,128]{2,1,0:T(8,128)(2,1)S(1)}, u32[]{:S(2)}, u32[]{:S(2)}) collective-permute-start(bf16[8,400,128]{2,1,0:T(8,128)(2,1)S(1)} %get-tuple-element.41), channel_id=1, source_target_pairs={{0,8},{8,0},{1,9},{9,1},{2,10},{10,2},{3,11},{11,3},{4,12},{12,4},... | collective-permute-start | bytes 2457608 | tf_op jit(solution)/shard_map/ppermute | solution.py:28
  61.7 11.8 %slice-start.1 = ((s8[4513792]{0:T(1024)(128)(4,1)}), s8[319488]{0:T(1024)(128)(4,1)S(1)}, s32[]{:S(2)}) async-start(s8[4513792]{0:T(1024)(128)(4,1)} %bitcast.24), calls=%async_computation.4 | async-start | bytes 638976
  86.0 1.3 copy-start.1
  102.2 63.3 %all-to-all-start.2 = ((s16[8,960,128]{2,1,0:T(8,128)(2,1)}), s16[8,960,128]{2,1,0:T(8,128)(2,1)S(1)}, u32[]{:S(2)}, u32[]{:S(2)}) async-start(s16[8,960,128]{2,1,0:T(8,128)(2,1)} %copy-done.1), calls=%async_computation.2 | async-start | bytes 3932160 | tf_op jit(solution)/shard_map/all_to_all | solution.py:518
  105.8 15.6 %collective-permute-start.4 = (f32[40,128]{1,0:T(8,128)S(1)}, f32[40,128]{1,0:T(8,128)S(1)}, u32[]{:S(2)}, u32[]{:S(2)}) collective-permute-start(f32[40,128]{1,0:T(8,128)S(1)} %reduce_sum.9), channel_id=1, source_target_pairs={{0,256},{16,272},{32,288},{48,304},{64,320},{80,336},{96,352},{112... | collective-permute-start | bytes 61448 | tf_op jit(solution)/shard_map/ppermute | solution.py:28
  116.7 4.9 %collective-permute-start.5 = (f32[40,128]{1,0:T(8,128)S(1)}, f32[40,128]{1,0:T(8,128)S(1)}, u32[]{:S(2)}, u32[]{:S(2)}) collective-permute-start(f32[40,128]{1,0:T(8,128)S(1)} %reduce_sum.9), channel_id=1, source_target_pairs={{0,128},{16,144},{32,160},{48,176},{64,192},{80,208},{96,224},{112... | collective-permute-start | bytes 61448 | tf_op jit(solution)/shard_map/ppermute | solution.py:28
  119.2 6.0 %collective-permute-start.6 = (f32[40,128]{1,0:T(8,128)S(1)}, f32[40,128]{1,0:T(8,128)S(1)}, u32[]{:S(2)}, u32[]{:S(2)}) collective-permute-start(f32[40,128]{1,0:T(8,128)S(1)} %reduce_sum.9), channel_id=1, source_target_pairs={{0,384},{16,400},{32,416},{48,432},{64,448},{80,464},{96,480},{112... | collective-permute-start | bytes 61448 | tf_op jit(solution)/shard_map/ppermute | solution.py:28
  125.2 9.3 %collective-permute-start.7 = (f32[40,128]{1,0:T(8,128)S(1)}, f32[40,128]{1,0:T(8,128)S(1)}, u32[]{:S(2)}, u32[]{:S(2)}) collective-permute-start(f32[40,128]{1,0:T(8,128)S(1)} %add_add_fusion.1), channel_id=1, source_target_pairs={{0,32},{16,48},{32,0},{48,16},{64,96},{80,112},{96,64},{112,80},{1... | collective-permute-start | bytes 61448 | tf_op jit(solution)/shard_map/ppermute | solution.py:28
  127.2 7.4 %collective-permute-start.8 = (f32[40,128]{1,0:T(8,128)S(1)}, f32[40,128]{1,0:T(8,128)S(1)}, u32[]{:S(2)}, u32[]{:S(2)}) collective-permute-start(f32[40,128]{1,0:T(8,128)S(1)} %add_add_fusion.1), channel_id=1, source_target_pairs={{0,16},{16,0},{32,48},{48,32},{64,80},{80,64},{96,112},{112,96},{1... | collective-permute-start | bytes 61448 | tf_op jit(solution)/shard_map/ppermute | solution.py:28
  129.7 6.6 %collective-permute-start.9 = (f32[40,128]{1,0:T(8,128)S(1)}, f32[40,128]{1,0:T(8,128)S(1)}, u32[]{:S(2)}, u32[]{:S(2)}) collective-permute-start(f32[40,128]{1,0:T(8,128)S(1)} %add_add_fusion.1), channel_id=1, source_target_pairs={{0,48},{16,32},{32,16},{48,0},{64,112},{80,96},{96,80},{112,64},{1... | collective-permute-start | bytes 61448 | tf_op jit(solution)/shard_map/ppermute | solution.py:28
  136.4 20.8 %copy-start.5 = (f32[40,128]{1,0:T(8,128)}, f32[40,128]{1,0:T(8,128)S(1)}, u32[]{:S(2)}) copy-start(f32[40,128]{1,0:T(8,128)S(1)} %add_add_fusion.refs_0_) | copy-start | bytes 61444
  136.4 13.7 %collective-permute-start.10 = (f32[40,128]{1,0:T(8,128)S(1)}, f32[40,128]{1,0:T(8,128)S(1)}, u32[]{:S(2)}, u32[]{:S(2)}) collective-permute-start(f32[40,128]{1,0:T(8,128)S(1)} %add_add_fusion.refs_0_), channel_id=1, source_target_pairs={{0,64},{8,72},{16,80},{24,88},{32,96},{40,104},{48,112},{56,120},{... | collective-permute-start | bytes 61448 | tf_op jit(solution)/shard_map/ppermute | solution.py:28
  143.9 6.1 %collective-permute-start.11 = (f32[40,128]{1,0:T(8,128)S(1)}, f32[40,128]{1,0:T(8,128)S(1)}, u32[]{:S(2)}, u32[]{:S(2)}) collective-permute-start(f32[40,128]{1,0:T(8,128)S(1)} %add_add_fusion.refs_0_), channel_id=1, source_target_pairs={{0,8},{8,0},{16,24},{24,16},{32,40},{40,32},{48,56},{56,48},{64,72... | collective-permute-start | bytes 61448 | tf_op jit(solution)/shard_map/ppermute | solution.py:28
  148.1 9.0 %collective-permute-start.12 = (f32[40,128]{1,0:T(8,128)S(1)}, f32[40,128]{1,0:T(8,128)S(1)}, u32[]{:S(2)}, u32[]{:S(2)}) collective-permute-start(f32[40,128]{1,0:T(8,128)S(1)} %add_add_fusion.refs_0_), channel_id=1, source_target_pairs={{0,72},{8,64},{16,88},{24,80},{32,104},{40,96},{48,120},{56,112},{... | collective-permute-start | bytes 61448 | tf_op jit(solution)/shard_map/ppermute | solution.py:28
  150.1 7.1 %copy-start.6 = (f32[40,128]{1,0:T(8,128)}, f32[40,128]{1,0:T(8,128)S(1)}, u32[]{:S(2)}) copy-start(f32[40,128]{1,0:T(8,128)S(1)} %collective-permute-done.10.refs_1_) | copy-start | bytes 61444
  150.1 7.0 %copy-start.7 = (f32[40,128]{1,0:T(8,128)}, f32[40,128]{1,0:T(8,128)S(1)}, u32[]{:S(2)}) copy-start(f32[40,128]{1,0:T(8,128)S(1)} %collective-permute-done.11.refs_2_) | copy-start | bytes 61444
  157.1 0.6 copy-start.8
  165.4 0.8 copy-start.3

commit v9 on v8

--- a/solution.py
+++ b/solution.py
@@ -122,15 +122,20 @@
     return one, two, three
 
 
-CODE = 8388000.0
-
-
-def encode(block, scale):
-    number = jnp.round(block * (CODE / scale)).astype(jnp.int32)
-    half = block.shape[0] // 2
-    low = number & 255
-    both = (low[:half] << 8) + low[half:] - 32768
-    return (number >> 8).astype(jnp.int16), both.astype(jnp.int16)
+CODE = 524200.0
+
+
+def encode(block, scale, ref, n):
+    total = block.shape[0]
+    size = total // FIELDS
+    part = size // 4
+    for i in range(FIELDS):
+        number = jnp.round(block[i * size : (i + 1) * size] * (CODE / scale)).astype(jnp.int32)
+        ref[n, i * size : (i + 1) * size, :] = (number >> 4).astype(jnp.int16)
+        low = number & 15
+        both = (low[:part] << 12) + (low[part : 2 * part] << 8)
+        both = both + (low[2 * part : 3 * part] << 4) + low[3 * part :] - 32768
+        ref[n, total + i * part : total + (i + 1) * part, :] = both.astype(jnp.int16)
 
 
 HALF_ROWS = K // 2 + 8
@@ -163,7 +168,7 @@
 
 def evolve_body(order_ref, *refs):
     layers, turn_refs = refs[: 4 * TOGETHER], refs[4 * TOGETHER : 5 * TOGETHER]
-    coef_ref, mask_ref, code_ref, gram_ref, z_ref, s_ref, out_ref = refs[5 * TOGETHER :]
+    coef_ref, mask_ref, sent_ref, gram_ref, z_ref, s_ref, out_ref, code_ref, sems = refs[5 * TOGETHER :]
     per = out_ref.shape[1] // (8 * FIELDS)
     wide = per + 2 * RH
 
@@ -230,6 +235,7 @@
 
             advance(s_ref, line, line, store)
 
+    copies = []
     for n in range(TOGETHER):
         block = out_ref[n]
         one, two, three = split(block)
@@ -241,8 +247,11 @@
         gram = wide[:LANES, :LANES] + (cross + cross.T + wide[LANES:, LANES:])
         scale = jnp.maximum(jnp.max(jnp.abs(block), axis=0, keepdims=True), 1e-30)
         pack(gram, scale, gram_ref, n)
-        count = block.shape[0]
-        code_ref[n, 0:count, :], code_ref[n, count : count + count // 2, :] = encode(block, scale)
+        encode(block, scale, code_ref, n)
+        copies.append(pltpu.make_async_copy(code_ref.at[n], sent_ref.at[pl.program_id(0) * TOGETHER + n], sems.at[n]))
+        copies[n].start()
+    for copy in copies:
+        copy.wait()
 
 
 def evolve(order, low, high, inner, outer, coef, mask, turn):
@@ -261,17 +270,19 @@
             + [pick((8, LANES), n) for n in range(TOGETHER)]
             + [whole(coef.shape), whole(mask.shape)],
             out_specs=[
-                pl.BlockSpec((TOGETHER, FIELDS * 12 * per, LANES), lambda i, order: (i, 0, 0)),
+                pl.BlockSpec(memory_space=pltpu.HBM),
                 pl.BlockSpec((TOGETHER, 2, HALF_ROWS, LANES), lambda i, order: (i, 0, 0, 0)),
             ],
             scratch_shapes=[
                 pltpu.VMEM((TOGETHER, FIELDS, 16 + 16 * PITCH, LANES), jnp.float32),
                 pltpu.VMEM((TOGETHER, FIELDS, 16 + 12 * PITCH, LANES), jnp.float32),
                 pltpu.VMEM((TOGETHER, FIELDS * 8 * per, LANES), jnp.float32),
+                pltpu.VMEM((TOGETHER, FIELDS * 10 * per, LANES), jnp.int16),
+                pltpu.SemaphoreType.DMA((TOGETHER,)),
             ],
         ),
         out_shape=[
-            jax.ShapeDtypeStruct((count, FIELDS * 12 * per, LANES), jnp.int16),
+            jax.ShapeDtypeStruct((count, FIELDS * 10 * per, LANES), jnp.int16),
             jax.ShapeDtypeStruct((count, 2, HALF_ROWS, LANES), jnp.float32),
         ],
         compiler_params=pltpu.CompilerParams(vmem_limit_bytes=VMEM_LIMIT),
@@ -285,7 +296,7 @@
     blocks = LANES // 8
     lane = lax.broadcasted_iota(jnp.int32, (8, LANES), 1)
     sub = lax.broadcasted_iota(jnp.int32, (8, LANES), 0)
-    mine, other = parts[0][...] + parts[1][...], parts[2][...] + parts[3][...]
+    mine, other = parts[0][...], parts[1][...]
     lower = jnp.full(mine.shape, core_ref[0], jnp.int32) == 0
     gram = unpack(jnp.where(lower, mine, other), jnp.where(lower, other, mine))
     w = [gram[8 * b : 8 * b + 8] for b in range(blocks)]
@@ -349,28 +360,25 @@
         in_specs=[pl.BlockSpec(memory_space=pltpu.SMEM)] + [vmem] * len(parts),
         out_specs=[vmem, vmem],
         out_shape=[shape, shape],
+        compiler_params=pltpu.CompilerParams(vmem_limit_bytes=8 * 1024 * 1024),
         name="factorize",
     )(core[None], *parts)
 
 
-def apply_body(inverse_ref, scale_ref, code_ref, out_ref, rows_ref, all_ref):
-    per = code_ref.shape[1] // (12 * FIELDS)
-    total = 8 * FIELDS * per
-    field = pl.program_id(0)
+def apply_body(inverse_ref, scale_ref, high_ref, low_ref, out_ref, rows_ref, all_ref):
+    per = high_ref.shape[1] // 8
     one, two, three = split(inverse_ref[...].T)
     main = jnp.concatenate([jnp.concatenate([one, two], axis=1)] * 2, axis=0)
     rest = jnp.concatenate([one, three], axis=0)
     for x in range(8):
-        line = (field * 8 + x) * per
-        late = line >= total // 2
-        other = jnp.where(late, line - total // 2, line)
-        shift = jnp.where(late, 0, 8)
+        shift, half = 12 - 4 * (x // 2), x % 2
         for d in range(F):
-            high = code_ref[d, pl.ds(pl.multiple_of(line, 16), per), :].astype(jnp.int32)
-            low = code_ref[d, pl.ds(pl.multiple_of(total + other, 16), per), :].astype(jnp.int32) + 32768
-            low = lax.shift_right_logical(low, jnp.full(low.shape, shift, jnp.int32)) & 255
-            value = ((high << 8) + low).astype(jnp.float32) * (scale_ref[d : d + 1, :] * (1.0 / CODE))
-            all_ref[x, d * per : (d + 1) * per, :] = value
+            high = high_ref[d, x * per : (x + 1) * per, :].astype(jnp.int32)
+            low = low_ref[d, half * per : (half + 1) * per, :].astype(jnp.int32) + 32768
+            number = (high << 4) + ((low >> shift) & 15)
+            all_ref[x, d * per : (d + 1) * per, :] = number.astype(jnp.float32) * (
+                scale_ref[d : d + 1, :] * (1.0 / CODE)
+            )
     for x in range(8):
         a, b, c = split(all_ref[x])
         wide = jnp.dot(jnp.concatenate([a, b], axis=1), main, preferred_element_type=jnp.float32)
@@ -381,13 +389,19 @@
 
 
 def apply(inverse, scales, columns):
-    per = columns.shape[1] // (12 * FIELDS)
+    per = columns.shape[1] // (10 * FIELDS)
     radial = per * F
+    first_low = 8 * FIELDS * per // (2 * per)
     vmem = pl.BlockSpec(memory_space=pltpu.VMEM)
     return pl.pallas_call(
         apply_body,
         grid=(FIELDS,),
-        in_specs=[vmem, vmem, vmem],
+        in_specs=[
+            vmem,
+            vmem,
+            pl.BlockSpec((F, 8 * per, LANES), lambda i: (0, i, 0)),
+            pl.BlockSpec((F, 2 * per, LANES), lambda i: (0, first_low + i, 0)),
+        ],
         out_specs=pl.BlockSpec((1, LANES, 1, 8, radial), lambda i: (0, 0, i, 0, 0)),
         out_shape=jax.ShapeDtypeStruct((1, LANES, FIELDS, 8, radial), jnp.float32),
         scratch_shapes=[
@@ -396,7 +410,7 @@
         ],
         compiler_params=pltpu.CompilerParams(vmem_limit_bytes=VMEM_LIMIT),
         name="apply",
-    )(inverse, scales, columns)
+    )(inverse, scales, columns, columns)
 
 
 def make_table(indices, slots):
@@ -518,7 +532,8 @@
     columns = lax.all_to_all(columns, "freq", split_axis=0, concat_axis=0, tiled=True)
     gram = quad_sum(gram, "chip", 16, 8)
     gram = quad_sum(gram, "chip", 2, 1)
-    parts = [gram] + [swap(gram, ("chip", "core"), mask) for mask in (8, 1, 9)]
+    gram = gram + swap(gram, "chip", 4)
+    parts = [gram, swap(gram, "core", 1)]
     row_scale = math.sqrt(FIELDS * 8 * count * radial)
     inverse, factor = factorize(core, parts, row_scale)
     return apply(inverse, scales, columns), factor[None]

time: 171 us -> 163 us (0.953)
  waiting for transfers between devices: 43.8 us -> 39 us
  local copies, waits for them, and re-layouts: 5.32 us -> 2.61 us
    ppermute x10 -> x9, waiting for transfers between devices: 12.6 us -> 7.87 us  [swap(): return lax.ppermute(value, axis, [(i, i ^ mask) for i in range(count)])]
    unnamed x25 -> x13, local copies, waits for them, and re-layouts: 4.8 us -> 2.08 us
    ppermute x10 -> x9, starting transfers between devices: 40.4 us -> 39.1 us  [swap(): return lax.ppermute(value, axis, [(i, i ^ mask) for i in range(count)])]
  transfers between devices with their start and end apart: 15 -> 14, of which waited for: 7 -> 8; matrix products, arithmetic and copies ran while one was open for 0% -> 0% of each run, Pallas kernels for 11% -> 11%
where the time goes in v9:
time: 163 us; the launch traced here: 162 us
  starting transfers between devices  61.8 us (38%)
  Pallas kernels  42.5 us (26%)
  waiting for transfers between devices  39 us (24%)
  blocking collectives  14.9 us (9%)
  local copies, waits for them, and re-layouts  2.61 us (2%)
    ppermute x9, starting transfers between devices, swap(): return lax.ppermute(value, axis, [(i, i ^ mask) for i in range(count)])  39.1 us
    all_to_all x1, waiting for transfers between devices, local(): rows = lax.all_to_all(rows, 'freq', split_axis=0, concat_axis=0, tiled=True)  23.6 us
    all_to_all x1, blocking collectives, local(): lax.all_to_all(grams, ('freq', 'core'), split_axis=0, concat_axis=0, tile...  14.9 us
    pallas_call x1, Pallas kernels, evolve(): pl.pallas_call(evolve_body, grid_spec=pltpu.PrefetchScalarGridSpec(num_sc...  13.7 us
    ppermute x9, waiting for transfers between devices, swap(): return lax.ppermute(value, axis, [(i, i ^ mask) for i in range(count)])  7.87 us
    all_to_all x1, starting transfers between devices, local(): rows = lax.all_to_all(rows, 'freq', split_axis=0, concat_axis=0, tiled=True)  7.79 us
    pallas_call x3, Pallas kernels, fourier(): pl.pallas_call(fourier_body, grid=(1,), in_specs=[pl.BlockSpec(memory_spa...  7.07 us
    pallas_call x1, Pallas kernels, factorize(): pl.pallas_call(partial(factor_body, scale), in_specs=[pl.BlockSpec(memory...  6.9 us
  transfers between devices with their start and end apart: 14, of which 8 were waited for; matrix products, arithmetic and copies ran while one was open for 0% of the time, Pallas kernels for 11%

profile of v9, /device:TPU:1, one launch (start us, length us, event | category | flops | bytes accessed | tf_op | source)
XLA Modules:
  0.0 162.3 jit_solution(11744779665278441476)
XLA Ops:
  0.6 4.6 %spread.1 = bf16[8,2,400,128]{3,2,1,0:T(8,128)(2,1)} custom-call(bf16[2,64,5,8,128]{4,3,2,1,0:T(8,128)(2,1)} %sketch_ref.1), custom_call_target="tpu_custom_call" | custom-call | tf_op jit(solution)/shard_map/spread/pallas_call | solution.py:58
  5.3 7.8 %all-to-all-start = ((bf16[8,2,400,128]{3,2,1,0:T(8,128)(2,1)}), bf16[8,2,400,128]{3,2,1,0:T(8,128)(2,1)S(1)}, u32[]{:S(2)}, u32[]{:S(2)}) async-start(bf16[8,2,400,128]{3,2,1,0:T(8,128)(2,1)} %spread.1), calls=%async_computation | async-start | bytes 3276800 | tf_op jit(solution)/shard_map/all_to_all | solution.py:504
  13.1 4.8 %collective-permute-start.1 = (f32[26,2,128]{2,1,0:T(2,128)S(1)}, f32[26,2,128]{2,1,0:T(2,128)S(1)}, u32[]{:S(2)}, u32[]{:S(2)}) collective-permute-start(f32[26,2,128]{2,1,0:T(2,128)S(1)} %pad_maximum_fusion.1), channel_id=1, source_target_pairs={{0,8},{8,16},{16,24},{24,32},{32,40},{40,48},{48,56},{56,64},{64,7... | collective-permute-start | bytes 79880 | tf_op jit(solution)/shard_map/ppermute | solution.py:479
  18.0 1.9 %collective-permute-start = (f32[26,2,128]{2,1,0:T(2,128)S(1)}, f32[26,2,128]{2,1,0:T(2,128)S(1)}, u32[]{:S(2)}, u32[]{:S(2)}) collective-permute-start(f32[26,2,128]{2,1,0:T(2,128)S(1)} %pad_maximum_fusion), channel_id=1, source_target_pairs={{8,0},{16,8},{24,16},{32,24},{40,32},{48,40},{56,48},{64,56},{72,6... | collective-permute-start | bytes 79880 | tf_op jit(solution)/shard_map/ppermute | solution.py:478
  20.0 0.1 fusion.7
  20.1 0.1 broadcast_multiply_fusion
  20.1 0.1 pad_add_fusion.1.place_ref
  20.2 0.1 copy.7
  20.3 0.1 broadcast_in_dim.46
  20.5 0.1 reshape.145.table_ref
  20.6 0.0 collective-permute-done.1.left_ref
  20.6 2.9 %collective-permute-done.right_ref = f32[26,2,128]{2,1,0:T(2,128)S(1)} collective-permute-done((f32[26,2,128]{2,1,0:T(2,128)S(1)}, f32[26,2,128]{2,1,0:T(2,128)S(1)}, u32[]{:S(2)}, u32[]{:S(2)}) %collective-permute-start) | collective-permute-done | bytes 26656 | tf_op jit(solution)/shard_map/ppermute | solution.py:478
  23.5 5.8 %stencil.1 = (f32[29,304,128]{2,1,0:T(8,128)S(1)}, f32[304,128]{1,0:T(8,128)S(1)}) custom-call(s32[3]{0:T(128)S(1)} %pad_add_fusion.1.place_ref, f32[25,8,128]{2,1,0:T(8,128)S(1)} %bitcast.30, f32[8,128]{1,0:T(8,128)S(1)} %copy-done.2, f32[26,2,128]{2,1,0:T(2,128)S(1)} %collective-permute-done.right_ref, f32[26,2,128]{2,1,0:T(2,128)S(1)} %collective-permute-done.1.left_ref), custom_call_target="tpu_custom_call" | custom-call | tf_op jit(solution)/shard_map/stencil/pallas_call | solution.py:482
  29.2 0.0 copy-start
  29.2 2.1 %copy-done = f32[29,304,128]{2,1,0:T(8,128)} copy-done((f32[29,304,128]{2,1,0:T(8,128)}, f32[29,304,128]{2,1,0:T(8,128)S(1)}, u32[]{:S(2)}) %copy-start) | copy-done | bytes 4513816
  31.3 23.6 %all-to-all-done.refs_0_.refs_1_ = bf16[8,2,400,128]{3,2,1,0:T(8,128)(2,1)S(1)} async-done(((bf16[8,2,400,128]{3,2,1,0:T(8,128)(2,1)}), bf16[8,2,400,128]{3,2,1,0:T(8,128)(2,1)S(1)}, u32[]{:S(2)}, u32[]{:S(2)}) %all-to-all-start) | async-done | bytes 1638432 | tf_op jit(solution)/shard_map/all_to_all | solution.py:504
  54.9 0.1 dynamic-slice_bitcast_fusion
  55.0 4.6 %collective-permute-start.3 = (bf16[8,400,128]{2,1,0:T(8,128)(2,1)S(1)}, bf16[8,400,128]{2,1,0:T(8,128)(2,1)S(1)}, u32[]{:S(2)}, u32[]{:S(2)}) collective-permute-start(bf16[8,400,128]{2,1,0:T(8,128)(2,1)S(1)} %get-tuple-element.40), channel_id=1, source_target_pairs={{8,16},{16,8},{24,32},{32,24},{40,48},{48,40},{56,64},{64,56},{72,... | collective-permute-start | bytes 2457608 | tf_op jit(solution)/shard_map/ppermute | solution.py:518
  59.6 1.9 %collective-permute-start.2 = (bf16[8,400,128]{2,1,0:T(8,128)(2,1)S(1)}, bf16[8,400,128]{2,1,0:T(8,128)(2,1)S(1)}, u32[]{:S(2)}, u32[]{:S(2)}) collective-permute-start(bf16[8,400,128]{2,1,0:T(8,128)(2,1)S(1)} %get-tuple-element.41), channel_id=1, source_target_pairs={{0,8},{8,0},{1,9},{9,1},{2,10},{10,2},{3,11},{11,3},{4,12},{12,4},... | collective-permute-start | bytes 2457608 | tf_op jit(solution)/shard_map/ppermute | solution.py:28
  61.6 0.1 pad_add_fusion.order_ref
  61.7 3.3 %fourier.3 = (f32[8,400,128]{2,1,0:T(8,128)S(1)}, f32[8,400,128]{2,1,0:T(8,128)S(1)}) custom-call(s32[8]{0:T(128)S(1)} %and_select_fusion.parity_ref, f32[8,2,4,128]{3,2,1,0:T(4,128)S(1)} %reshape.145.table_ref, bf16[8,2,400,128]{3,2,1,0:T(8,128)(2,1)S(1)} %all-to-all-done.refs_0_.refs_1_, bf16[8,2,400,128]{3,2,1,0:T(8,128)(2,1)S(1)} %all-to-all-done.refs_0_.refs_1_), custom_call_target="tpu_custom_call" | custom-call | tf_op jit(solution)/shard_map/fourier/pallas_call | solution.py:104
  64.9 4.7 %collective-permute-done.3 = bf16[8,400,128]{2,1,0:T(8,128)(2,1)S(1)} collective-permute-done((bf16[8,400,128]{2,1,0:T(8,128)(2,1)S(1)}, bf16[8,400,128]{2,1,0:T(8,128)(2,1)S(1)}, u32[]{:S(2)}, u32[]{:S(2)}) %collective-permute-start.3) | collective-permute-done | bytes 819232 | tf_op jit(solution)/shard_map/ppermute | solution.py:518
  69.7 1.9 %fourier.5.refs_3_.refs_7_.refs_11_.refs_15_ = f32[8,400,128]{2,1,0:T(8,128)S(1)} custom-call(s32[8]{0:T(128)S(1)} %and_select_fusion.parity_ref, f32[8,2,4,128]{3,2,1,0:T(4,128)S(1)} %reshape.145.table_ref, bf16[8,1,400,128]{3,2,1,0:T(8,128)(2,1)S(1)} %bitcast.27), custom_call_target="tpu_custom_call" | custom-call | tf_op jit(solution)/shard_map/fourier/pallas_call | solution.py:104
  71.6 0.0 collective-permute-done.2
  71.6 1.9 %fourier.4.refs_2_.refs_6_.refs_10_.refs_14_ = f32[8,400,128]{2,1,0:T(8,128)S(1)} custom-call(s32[8]{0:T(128)S(1)} %and_select_fusion.parity_ref, f32[8,2,4,128]{3,2,1,0:T(4,128)S(1)} %reshape.145.table_ref, bf16[8,1,400,128]{3,2,1,0:T(8,128)(2,1)S(1)} %bitcast.26), custom_call_target="tpu_custom_call" | custom-call | tf_op jit(solution)/shard_map/fourier/pallas_call | solution.py:104
  73.5 0.0 slice-done.1
  73.5 13.7 %evolve.1 = (s16[8,800,128]{2,1,0:T(8,128)(2,1)}, f32[8,2,40,128]{3,2,1,0:T(8,128)S(1)}) custom-call(s32[9]{0:T(128)S(1)} %pad_add_fusion.order_ref, f32[8,400,128]{2,1,0:T(8,128)S(1)} %get-tuple-element.29.refs_0_.refs_4_.refs_8_.refs_12_, f32[8,400,128]{2,1,0:T(8,128)S(1)} %get-tuple-element.30.refs_1_.refs_5_.refs_9_.refs_13_, ...), custom_call_target="tpu_custom_call" | custom-call | tf_op jit(solution)/shard_map/evolve/pallas_call | solution.py:264
  87.2 14.9 %all_to_all.15 = f32[16,40,128]{2,1,0:T(8,128)S(1)} all-to-all(f32[16,40,128]{2,1,0:T(8,128)S(1)} %bitcast.28), channel_id=1, replica_groups=mesh['chip'=32,'core'=2,'freq'=8] {'freq','core'}, dimensions={0} | all-to-all | bytes 655360 | tf_op jit(solution)/shard_map/all_to_all | solution.py:527
  102.1 3.6 %all-to-all-start.2 = ((s16[8,800,128]{2,1,0:T(8,128)(2,1)}), s16[8,800,128]{2,1,0:T(8,128)(2,1)S(1)}, u32[]{:S(2)}, u32[]{:S(2)}) async-start(s16[8,800,128]{2,1,0:T(8,128)(2,1)} %get-tuple-element.38), calls=%async_computation.2 | async-start | bytes 3276800 | tf_op jit(solution)/shard_map/all_to_all | solution.py:532
  105.7 10.9 %collective-permute-start.4 = (f32[40,128]{1,0:T(8,128)S(1)}, f32[40,128]{1,0:T(8,128)S(1)}, u32[]{:S(2)}, u32[]{:S(2)}) collective-permute-start(f32[40,128]{1,0:T(8,128)S(1)} %reduce_sum.9), channel_id=1, source_target_pairs={{0,256},{16,272},{32,288},{48,304},{64,320},{80,336},{96,352},{112... | collective-permute-start | bytes 61448 | tf_op jit(solution)/shard_map/ppermute | solution.py:28
  116.7 2.5 %collective-permute-start.5 = (f32[40,128]{1,0:T(8,128)S(1)}, f32[40,128]{1,0:T(8,128)S(1)}, u32[]{:S(2)}, u32[]{:S(2)}) collective-permute-start(f32[40,128]{1,0:T(8,128)S(1)} %reduce_sum.9), channel_id=1, source_target_pairs={{0,128},{16,144},{32,160},{48,176},{64,192},{80,208},{96,224},{112... | collective-permute-start | bytes 61448 | tf_op jit(solution)/shard_map/ppermute | solution.py:28
  119.2 2.2 %collective-permute-start.6 = (f32[40,128]{1,0:T(8,128)S(1)}, f32[40,128]{1,0:T(8,128)S(1)}, u32[]{:S(2)}, u32[]{:S(2)}) collective-permute-start(f32[40,128]{1,0:T(8,128)S(1)} %reduce_sum.9), channel_id=1, source_target_pairs={{0,384},{16,400},{32,416},{48,432},{64,448},{80,464},{96,480},{112... | collective-permute-start | bytes 61448 | tf_op jit(solution)/shard_map/ppermute | solution.py:28
  121.4 0.0 collective-permute-done.4
  121.4 0.2 collective-permute-done.5
  121.5 3.7 %collective-permute-done.6 = f32[40,128]{1,0:T(8,128)S(1)} collective-permute-done((f32[40,128]{1,0:T(8,128)S(1)}, f32[40,128]{1,0:T(8,128)S(1)}, u32[]{:S(2)}, u32[]{:S(2)}) %collective-permute-start.6) | collective-permute-done | bytes 20512 | tf_op jit(solution)/shard_map/ppermute | solution.py:28
  125.2 1.9 %collective-permute-start.7 = (f32[40,128]{1,0:T(8,128)S(1)}, f32[40,128]{1,0:T(8,128)S(1)}, u32[]{:S(2)}, u32[]{:S(2)}) collective-permute-start(f32[40,128]{1,0:T(8,128)S(1)} %add_add_fusion.1), channel_id=1, source_target_pairs={{0,32},{16,48},{32,0},{48,16},{64,96},{80,112},{96,64},{112,80},{1... | collective-permute-start | bytes 61448 | tf_op jit(solution)/shard_map/ppermute | solution.py:28
  127.1 2.6 %collective-permute-start.8 = (f32[40,128]{1,0:T(8,128)S(1)}, f32[40,128]{1,0:T(8,128)S(1)}, u32[]{:S(2)}, u32[]{:S(2)}) collective-permute-start(f32[40,128]{1,0:T(8,128)S(1)} %add_add_fusion.1), channel_id=1, source_target_pairs={{0,16},{16,0},{32,48},{48,32},{64,80},{80,64},{96,112},{112,96},{1... | collective-permute-start | bytes 61448 | tf_op jit(solution)/shard_map/ppermute | solution.py:28
  129.7 4.8 %collective-permute-start.9 = (f32[40,128]{1,0:T(8,128)S(1)}, f32[40,128]{1,0:T(8,128)S(1)}, u32[]{:S(2)}, u32[]{:S(2)}) collective-permute-start(f32[40,128]{1,0:T(8,128)S(1)} %add_add_fusion.1), channel_id=1, source_target_pairs={{0,48},{16,32},{32,16},{48,0},{64,112},{80,96},{96,80},{112,64},{1... | collective-permute-start | bytes 61448 | tf_op jit(solution)/shard_map/ppermute | solution.py:28
  134.5 0.0 collective-permute-done.7
  134.5 0.0 collective-permute-done.8
  134.5 1.8 %collective-permute-done.9 = f32[40,128]{1,0:T(8,128)S(1)} collective-permute-done((f32[40,128]{1,0:T(8,128)S(1)}, f32[40,128]{1,0:T(8,128)S(1)}, u32[]{:S(2)}, u32[]{:S(2)}) %collective-permute-start.9) | collective-permute-done | bytes 20512 | tf_op jit(solution)/shard_map/ppermute | solution.py:28
  136.3 7.6 %collective-permute-start.10 = (f32[40,128]{1,0:T(8,128)S(1)}, f32[40,128]{1,0:T(8,128)S(1)}, u32[]{:S(2)}, u32[]{:S(2)}) collective-permute-start(f32[40,128]{1,0:T(8,128)S(1)} %add_add_fusion), channel_id=1, source_target_pairs={{0,64},{16,80},{32,96},{48,112},{64,0},{80,16},{96,32},{112,48},{1... | collective-permute-start | bytes 61448 | tf_op jit(solution)/shard_map/ppermute | solution.py:28
  143.9 1.4 collective-permute-done.10
  145.4 4.7 %collective-permute-start.11 = (f32[40,128]{1,0:T(8,128)S(1)}, f32[40,128]{1,0:T(8,128)S(1)}, u32[]{:S(2)}, u32[]{:S(2)}) collective-permute-start(f32[40,128]{1,0:T(8,128)S(1)} %add.66.refs_0_), channel_id=1, source_target_pairs={{0,8},{8,0},{1,9},{9,1},{2,10},{10,2},{3,11},{11,3},{4,12},{12,4},... | collective-permute-start | bytes 61448 | tf_op jit(solution)/shard_map/ppermute | solution.py:28
  150.1 0.8 collective-permute-done.11.refs_1_
  150.9 6.9 %factorize.1 = (f32[128,128]{1,0:T(8,128)S(1)}, f32[128,128]{1,0:T(8,128)}) custom-call(s32[1]{0:T(128)} %bitcast.core_ref, f32[40,128]{1,0:T(8,128)S(1)} %add.66.refs_0_, f32[40,128]{1,0:T(8,128)S(1)} %collective-permute-done.11.refs_1_), custom_call_target="tpu_custom_call" | custom-call | tf_op jit(solution)/shard_map/factorize/pallas_call | solution.py:358
  157.8 0.0 all-to-all-done.2.high_ref.low_ref
  157.8 4.5 %apply.1 = f32[1,128,5,8,128]{4,3,2,1,0:T(8,128)} custom-call(f32[128,128]{1,0:T(8,128)S(1)} %get-tuple-element.37.inverse_ref, f32[8,128]{1,0:T(8,128)S(1)} %fusion.6.scale_ref, s16[8,800,128]{2,1,0:T(8,128)(2,1)S(1)} %all-to-all-done.2.high_ref.low_ref, s16[8,800,128]{2,1,0:T(8,128)(2,1)S(1)} %all-to-all-done.2.high_ref.low_ref), custom_call_target="tpu_custom_call" | custom-call | tf_op jit(solution)/shard_map/apply/pallas_call | solution.py:396
  (27 shorter events, 0.2 us)
Async XLA Ops:
  5.2 7.8 %copy-start.2 = (f32[8,128]{1,0:T(8,128)S(1)}, f32[8,128]{1,0:T(8,128)}, u32[]{:S(2)}) copy-start(f32[8,128]{1,0:T(8,128)} %velocity_ref) | copy-start | bytes 12292
  5.2 7.8 %copy-start.1 = (f32[5,5,8,128]{3,2,1,0:T(8,128)S(1)}, f32[5,5,8,128]{3,2,1,0:T(8,128)}, u32[]{:S(2)}) copy-start(f32[5,5,8,128]{3,2,1,0:T(8,128)} %param.5) | copy-start | bytes 307204
  5.3 14.7 %copy-start.3 = (s32[8]{0:T(128)S(1)}, s32[8]{0:T(128)}, u32[]{:S(2)}) copy-start(s32[8]{0:T(128)} %param.7) | copy-start | bytes 100
  5.3 49.6 %all-to-all-start = ((bf16[8,2,400,128]{3,2,1,0:T(8,128)(2,1)}), bf16[8,2,400,128]{3,2,1,0:T(8,128)(2,1)S(1)}, u32[]{:S(2)}, u32[]{:S(2)}) async-start(bf16[8,2,400,128]{3,2,1,0:T(8,128)(2,1)} %spread.1), calls=%async_computation | async-start | bytes 3276800 | tf_op jit(solution)/shard_map/all_to_all | solution.py:504
  13.1 7.5 %collective-permute-start.1 = (f32[26,2,128]{2,1,0:T(2,128)S(1)}, f32[26,2,128]{2,1,0:T(2,128)S(1)}, u32[]{:S(2)}, u32[]{:S(2)}) collective-permute-start(f32[26,2,128]{2,1,0:T(2,128)S(1)} %pad_maximum_fusion.1), channel_id=1, source_target_pairs={{0,8},{8,16},{16,24},{24,32},{32,40},{40,48},{48,56},{56,64},{64,7... | collective-permute-start | bytes 79880 | tf_op jit(solution)/shard_map/ppermute | solution.py:479
  18.0 5.5 %collective-permute-start = (f32[26,2,128]{2,1,0:T(2,128)S(1)}, f32[26,2,128]{2,1,0:T(2,128)S(1)}, u32[]{:S(2)}, u32[]{:S(2)}) collective-permute-start(f32[26,2,128]{2,1,0:T(2,128)S(1)} %pad_maximum_fusion), channel_id=1, source_target_pairs={{8,0},{16,8},{24,16},{32,24},{40,32},{48,40},{56,48},{64,56},{72,6... | collective-permute-start | bytes 79880 | tf_op jit(solution)/shard_map/ppermute | solution.py:478
  29.2 2.1 %copy-start = (f32[29,304,128]{2,1,0:T(8,128)}, f32[29,304,128]{2,1,0:T(8,128)S(1)}, u32[]{:S(2)}) copy-start(f32[29,304,128]{2,1,0:T(8,128)S(1)} %get-tuple-element.32.refs_20_) | copy-start | bytes 13541380
  54.9 18.6 %slice-start = ((s8[4513792]{0:T(1024)(128)(4,1)}), s8[4194304]{0:T(1024)(128)(4,1)S(1)}, s32[]{:S(2)}) async-start(s8[4513792]{0:T(1024)(128)(4,1)} %bitcast.24), calls=%async_computation.3 | async-start | bytes 8388608
  55.0 14.6 %collective-permute-start.3 = (bf16[8,400,128]{2,1,0:T(8,128)(2,1)S(1)}, bf16[8,400,128]{2,1,0:T(8,128)(2,1)S(1)}, u32[]{:S(2)}, u32[]{:S(2)}) collective-permute-start(bf16[8,400,128]{2,1,0:T(8,128)(2,1)S(1)} %get-tuple-element.40), channel_id=1, source_target_pairs={{8,16},{16,8},{24,32},{32,24},{40,48},{48,40},{56,64},{64,56},{72,... | collective-permute-start | bytes 2457608 | tf_op jit(solution)/shard_map/ppermute | solution.py:518
  59.6 11.9 %collective-permute-start.2 = (bf16[8,400,128]{2,1,0:T(8,128)(2,1)S(1)}, bf16[8,400,128]{2,1,0:T(8,128)(2,1)S(1)}, u32[]{:S(2)}, u32[]{:S(2)}) collective-permute-start(bf16[8,400,128]{2,1,0:T(8,128)(2,1)S(1)} %get-tuple-element.41), channel_id=1, source_target_pairs={{0,8},{8,0},{1,9},{9,1},{2,10},{10,2},{3,11},{11,3},{4,12},{12,4},... | collective-permute-start | bytes 2457608 | tf_op jit(solution)/shard_map/ppermute | solution.py:28
  61.7 11.8 %slice-start.1 = ((s8[4513792]{0:T(1024)(128)(4,1)}), s8[319488]{0:T(1024)(128)(4,1)S(1)}, s32[]{:S(2)}) async-start(s8[4513792]{0:T(1024)(128)(4,1)} %bitcast.24), calls=%async_computation.4 | async-start | bytes 638976
  102.1 55.7 %all-to-all-start.2 = ((s16[8,800,128]{2,1,0:T(8,128)(2,1)}), s16[8,800,128]{2,1,0:T(8,128)(2,1)S(1)}, u32[]{:S(2)}, u32[]{:S(2)}) async-start(s16[8,800,128]{2,1,0:T(8,128)(2,1)} %get-tuple-element.38), calls=%async_computation.2 | async-start | bytes 3276800 | tf_op jit(solution)/shard_map/all_to_all | solution.py:532
  105.7 15.6 %collective-permute-start.4 = (f32[40,128]{1,0:T(8,128)S(1)}, f32[40,128]{1,0:T(8,128)S(1)}, u32[]{:S(2)}, u32[]{:S(2)}) collective-permute-start(f32[40,128]{1,0:T(8,128)S(1)} %reduce_sum.9), channel_id=1, source_target_pairs={{0,256},{16,272},{32,288},{48,304},{64,320},{80,336},{96,352},{112... | collective-permute-start | bytes 61448 | tf_op jit(solution)/shard_map/ppermute | solution.py:28
  116.7 4.9 %collective-permute-start.5 = (f32[40,128]{1,0:T(8,128)S(1)}, f32[40,128]{1,0:T(8,128)S(1)}, u32[]{:S(2)}, u32[]{:S(2)}) collective-permute-start(f32[40,128]{1,0:T(8,128)S(1)} %reduce_sum.9), channel_id=1, source_target_pairs={{0,128},{16,144},{32,160},{48,176},{64,192},{80,208},{96,224},{112... | collective-permute-start | bytes 61448 | tf_op jit(solution)/shard_map/ppermute | solution.py:28
  119.2 6.0 %collective-permute-start.6 = (f32[40,128]{1,0:T(8,128)S(1)}, f32[40,128]{1,0:T(8,128)S(1)}, u32[]{:S(2)}, u32[]{:S(2)}) collective-permute-start(f32[40,128]{1,0:T(8,128)S(1)} %reduce_sum.9), channel_id=1, source_target_pairs={{0,384},{16,400},{32,416},{48,432},{64,448},{80,464},{96,480},{112... | collective-permute-start | bytes 61448 | tf_op jit(solution)/shard_map/ppermute | solution.py:28
  125.2 9.3 %collective-permute-start.7 = (f32[40,128]{1,0:T(8,128)S(1)}, f32[40,128]{1,0:T(8,128)S(1)}, u32[]{:S(2)}, u32[]{:S(2)}) collective-permute-start(f32[40,128]{1,0:T(8,128)S(1)} %add_add_fusion.1), channel_id=1, source_target_pairs={{0,32},{16,48},{32,0},{48,16},{64,96},{80,112},{96,64},{112,80},{1... | collective-permute-start | bytes 61448 | tf_op jit(solution)/shard_map/ppermute | solution.py:28
  127.1 7.4 %collective-permute-start.8 = (f32[40,128]{1,0:T(8,128)S(1)}, f32[40,128]{1,0:T(8,128)S(1)}, u32[]{:S(2)}, u32[]{:S(2)}) collective-permute-start(f32[40,128]{1,0:T(8,128)S(1)} %add_add_fusion.1), channel_id=1, source_target_pairs={{0,16},{16,0},{32,48},{48,32},{64,80},{80,64},{96,112},{112,96},{1... | collective-permute-start | bytes 61448 | tf_op jit(solution)/shard_map/ppermute | solution.py:28
  129.7 6.6 %collective-permute-start.9 = (f32[40,128]{1,0:T(8,128)S(1)}, f32[40,128]{1,0:T(8,128)S(1)}, u32[]{:S(2)}, u32[]{:S(2)}) collective-permute-start(f32[40,128]{1,0:T(8,128)S(1)} %add_add_fusion.1), channel_id=1, source_target_pairs={{0,48},{16,32},{32,16},{48,0},{64,112},{80,96},{96,80},{112,64},{1... | collective-permute-start | bytes 61448 | tf_op jit(solution)/shard_map/ppermute | solution.py:28
  136.3 9.0 %collective-permute-start.10 = (f32[40,128]{1,0:T(8,128)S(1)}, f32[40,128]{1,0:T(8,128)S(1)}, u32[]{:S(2)}, u32[]{:S(2)}) collective-permute-start(f32[40,128]{1,0:T(8,128)S(1)} %add_add_fusion), channel_id=1, source_target_pairs={{0,64},{16,80},{32,96},{48,112},{64,0},{80,16},{96,32},{112,48},{1... | collective-permute-start | bytes 61448 | tf_op jit(solution)/shard_map/ppermute | solution.py:28
  145.4 5.6 %collective-permute-start.11 = (f32[40,128]{1,0:T(8,128)S(1)}, f32[40,128]{1,0:T(8,128)S(1)}, u32[]{:S(2)}, u32[]{:S(2)}) collective-permute-start(f32[40,128]{1,0:T(8,128)S(1)} %add.66.refs_0_), channel_id=1, source_target_pairs={{0,8},{8,0},{1,9},{9,1},{2,10},{10,2},{3,11},{11,3},{4,12},{12,4},... | collective-permute-start | bytes 61448 | tf_op jit(solution)/shard_map/ppermute | solution.py:28

commit v10 on v9

--- a/solution.py
+++ b/solution.py
@@ -235,23 +235,34 @@
 
             advance(s_ref, line, line, store)
 
-    copies = []
+    step = pl.program_id(0)
+    copy = lambda step, n: pltpu.make_async_copy(code_ref.at[n], sent_ref.at[step * TOGETHER + n], sems.at[n])
+
+    @pl.when(step > 0)
+    def _():
+        for n in range(TOGETHER):
+            copy(step - 1, n).wait()
+
+    scales = []
     for n in range(TOGETHER):
         block = out_ref[n]
-        one, two, three = split(block)
+        scales.append(jnp.maximum(jnp.max(jnp.abs(block), axis=0, keepdims=True), 1e-30))
+        encode(block, scales[n], code_ref, n)
+        copy(step, n).start()
+    for n in range(TOGETHER):
+        one, two, three = split(out_ref[n])
         pair = jnp.concatenate([one, two], axis=1)
         contract = (((0,), (0,)), ((), ()))
         wide = lax.dot_general(pair, pair, contract, preferred_element_type=jnp.float32)
         thin = lax.dot_general(one, three, contract, preferred_element_type=jnp.float32)
         cross = wide[:LANES, LANES:] + thin
         gram = wide[:LANES, :LANES] + (cross + cross.T + wide[LANES:, LANES:])
-        scale = jnp.maximum(jnp.max(jnp.abs(block), axis=0, keepdims=True), 1e-30)
-        pack(gram, scale, gram_ref, n)
-        encode(block, scale, code_ref, n)
-        copies.append(pltpu.make_async_copy(code_ref.at[n], sent_ref.at[pl.program_id(0) * TOGETHER + n], sems.at[n]))
-        copies[n].start()
-    for copy in copies:
-        copy.wait()
+        pack(gram, scales[n], gram_ref, n)
+
+    @pl.when(step == pl.num_programs(0) - 1)
+    def _():
+        for n in range(TOGETHER):
+            copy(step, n).wait()
 
 
 def evolve(order, low, high, inner, outer, coef, mask, turn):
@@ -365,22 +376,20 @@
     )(core[None], *parts)
 
 
-def apply_body(inverse_ref, scale_ref, high_ref, low_ref, out_ref, rows_ref, all_ref):
+def apply_body(inverse_ref, scale_ref, high_ref, low_ref, out_ref, rows_ref):
     per = high_ref.shape[1] // 8
     one, two, three = split(inverse_ref[...].T)
     main = jnp.concatenate([jnp.concatenate([one, two], axis=1)] * 2, axis=0)
     rest = jnp.concatenate([one, three], axis=0)
     for x in range(8):
         shift, half = 12 - 4 * (x // 2), x % 2
+        lines = []
         for d in range(F):
             high = high_ref[d, x * per : (x + 1) * per, :].astype(jnp.int32)
             low = low_ref[d, half * per : (half + 1) * per, :].astype(jnp.int32) + 32768
             number = (high << 4) + ((low >> shift) & 15)
-            all_ref[x, d * per : (d + 1) * per, :] = number.astype(jnp.float32) * (
-                scale_ref[d : d + 1, :] * (1.0 / CODE)
-            )
-    for x in range(8):
-        a, b, c = split(all_ref[x])
+            lines.append(number.astype(jnp.float32) * (scale_ref[d : d + 1, :] * (1.0 / CODE)))
+        a, b, c = split(jnp.concatenate(lines, axis=0))
         wide = jnp.dot(jnp.concatenate([a, b], axis=1), main, preferred_element_type=jnp.float32)
         tail = jnp.dot(jnp.concatenate([c, a], axis=1), rest, preferred_element_type=jnp.float32)
         value = wide[:, :LANES] + (wide[:, LANES:] + tail)
@@ -406,7 +415,6 @@
         out_shape=jax.ShapeDtypeStruct((1, LANES, FIELDS, 8, radial), jnp.float32),
         scratch_shapes=[
             pltpu.VMEM((LANES * 8, radial), jnp.float32),
-            pltpu.VMEM((8, radial, LANES), jnp.float32),
         ],
         compiler_params=pltpu.CompilerParams(vmem_limit_bytes=VMEM_LIMIT),
         name="apply",
@@ -517,8 +525,7 @@
     inner = lax.dynamic_index_in_dim(rows, 1 - core, 1, keepdims=False)
     outer = lax.ppermute(outer, SPACE, [(i, i + 1 if i % 2 else i - 1) for i in range(1, count - 1)])
     inner = swap(inner, "core", 1)
-    low, high = fourier(parity, [rows, rows], [0, 1], waves)
-    (inner,) = fourier(parity, [inner[:, None]], [0], waves)
+    low, high, inner = fourier(parity, [rows, rows, inner[:, None]], [0, 1, 0], waves)
     (outer,) = fourier(parity, [outer[:, None]], [0], waves)
     order = jnp.concatenate([jnp.arange(F, dtype=jnp.int32), core[None]])
 

time: 163 us -> 162 us (level)
    ppermute x1, waiting for transfers between devices: 2.87 us -> 0.01 us  [stencil(): right = lax.ppermute(edges[0], SPACE, down)]
    ppermute x1, starting transfers between devices: 1.92 us -> 4.73 us  [stencil(): right = lax.ppermute(edges[0], SPACE, down)]
    ppermute x1, starting transfers between devices: 4.84 us -> 2.03 us  [stencil(): left = lax.ppermute(edges[1], SPACE, up)]
    all_to_all x1, waiting for transfers between devices: 23.6 us -> 26.1 us  [local(): rows = lax.all_to_all(rows, 'freq', split_axis=0, concat_axis=0, tiled=True)]
    pallas_call x3 -> x2, Pallas kernels: 7.07 us -> 6.57 us  [fourier(): pl.pallas_call(fourier_body, grid=(1,), in_specs=[pl.BlockSpec(memory_spa...]
where the time goes in v10:
time: 162 us
  starting transfers between devices  62.2 us (38%)
  Pallas kernels  41.7 us (26%)
  waiting for transfers between devices  38.8 us (24%)
  blocking collectives  14.9 us (9%)
  local copies, waits for them, and re-layouts  2.6 us (2%)
    ppermute x9, starting transfers between devices, swap(): return lax.ppermute(value, axis, [(i, i ^ mask) for i in range(count)])  40.1 us
    all_to_all x1, waiting for transfers between devices, local(): rows = lax.all_to_all(rows, 'freq', split_axis=0, concat_axis=0, tiled=True)  26.1 us
    all_to_all x1, blocking collectives, local(): lax.all_to_all(grams, ('freq', 'core'), split_axis=0, concat_axis=0, tile...  14.9 us
    pallas_call x1, Pallas kernels, evolve(): pl.pallas_call(evolve_body, grid_spec=pltpu.PrefetchScalarGridSpec(num_sc...  13.4 us
    all_to_all x1, starting transfers between devices, local(): rows = lax.all_to_all(rows, 'freq', split_axis=0, concat_axis=0, tiled=True)  7.79 us
    ppermute x9, waiting for transfers between devices, swap(): return lax.ppermute(value, axis, [(i, i ^ mask) for i in range(count)])  7.14 us
    pallas_call x1, Pallas kernels, factorize(): pl.pallas_call(partial(factor_body, scale), in_specs=[pl.BlockSpec(memory...  6.9 us
    pallas_call x2, Pallas kernels, fourier(): pl.pallas_call(fourier_body, grid=(1,), in_specs=[pl.BlockSpec(memory_spa...  6.57 us
  transfers between devices with their start and end apart: 14, of which 8 were waited for; matrix products, arithmetic and copies ran while one was open for 0% of the time, Pallas kernels for 11%

profile of v10, /device:TPU:1, one launch (start us, length us, event | category | flops | bytes accessed | tf_op | source)
XLA Modules:
  0.0 161.6 jit_solution(17426104561510138479)
XLA Ops:
  0.6 4.6 %spread.1 = bf16[8,2,400,128]{3,2,1,0:T(8,128)(2,1)} custom-call(bf16[2,64,5,8,128]{4,3,2,1,0:T(8,128)(2,1)} %sketch_ref.1), custom_call_target="tpu_custom_call" | custom-call | tf_op jit(solution)/shard_map/spread/pallas_call | solution.py:58
  5.3 7.8 %all-to-all-start = ((bf16[8,2,400,128]{3,2,1,0:T(8,128)(2,1)}), bf16[8,2,400,128]{3,2,1,0:T(8,128)(2,1)S(1)}, u32[]{:S(2)}, u32[]{:S(2)}) async-start(bf16[8,2,400,128]{3,2,1,0:T(8,128)(2,1)} %spread.1), calls=%async_computation | async-start | bytes 3276800 | tf_op jit(solution)/shard_map/all_to_all | solution.py:512
  13.0 0.0 copy-done.3
  13.1 0.0 copy-done.2
  13.1 4.7 %collective-permute-start = (f32[26,2,128]{2,1,0:T(2,128)S(1)}, f32[26,2,128]{2,1,0:T(2,128)S(1)}, u32[]{:S(2)}, u32[]{:S(2)}) collective-permute-start(f32[26,2,128]{2,1,0:T(2,128)S(1)} %pad_maximum_fusion), channel_id=1, source_target_pairs={{8,0},{16,8},{24,16},{32,24},{40,32},{48,40},{56,48},{64,56},{72,6... | collective-permute-start | bytes 79880 | tf_op jit(solution)/shard_map/ppermute | solution.py:486
  17.9 2.0 %collective-permute-start.1 = (f32[26,2,128]{2,1,0:T(2,128)S(1)}, f32[26,2,128]{2,1,0:T(2,128)S(1)}, u32[]{:S(2)}, u32[]{:S(2)}) collective-permute-start(f32[26,2,128]{2,1,0:T(2,128)S(1)} %pad_maximum_fusion.1), channel_id=1, source_target_pairs={{0,8},{8,16},{16,24},{24,32},{32,40},{40,48},{48,56},{56,64},{64,7... | collective-permute-start | bytes 79880 | tf_op jit(solution)/shard_map/ppermute | solution.py:487
  19.9 0.0 copy-done.4
  20.0 0.1 fusion.7
  20.1 0.1 broadcast_multiply_fusion
  20.1 0.1 pad_add_fusion.1.place_ref
  20.2 0.1 copy.7
  20.3 0.1 broadcast_in_dim.46
  20.5 0.1 reshape.145.table_ref
  20.6 0.0 collective-permute-done.right_ref
  20.6 0.4 collective-permute-done.1.left_ref
  21.0 5.8 %stencil.1 = (f32[29,304,128]{2,1,0:T(8,128)S(1)}, f32[304,128]{1,0:T(8,128)S(1)}) custom-call(s32[3]{0:T(128)S(1)} %pad_add_fusion.1.place_ref, f32[25,8,128]{2,1,0:T(8,128)S(1)} %bitcast.28, f32[8,128]{1,0:T(8,128)S(1)} %copy-done.3, f32[26,2,128]{2,1,0:T(2,128)S(1)} %collective-permute-done.right_ref, f32[26,2,128]{2,1,0:T(2,128)S(1)} %collective-permute-done.1.left_ref), custom_call_target="tpu_custom_call" | custom-call | tf_op jit(solution)/shard_map/stencil/pallas_call | solution.py:490
  26.8 2.1 %copy-done = f32[29,304,128]{2,1,0:T(8,128)} copy-done((f32[29,304,128]{2,1,0:T(8,128)}, f32[29,304,128]{2,1,0:T(8,128)S(1)}, u32[]{:S(2)}) %copy-start) | copy-done | bytes 4513816
  28.8 26.1 %all-to-all-done.refs_0_.refs_1_ = bf16[8,2,400,128]{3,2,1,0:T(8,128)(2,1)S(1)} async-done(((bf16[8,2,400,128]{3,2,1,0:T(8,128)(2,1)}), bf16[8,2,400,128]{3,2,1,0:T(8,128)(2,1)S(1)}, u32[]{:S(2)}, u32[]{:S(2)}) %all-to-all-start) | async-done | bytes 1638432 | tf_op jit(solution)/shard_map/all_to_all | solution.py:512
  54.9 0.1 dynamic-slice_bitcast_fusion
  55.0 2.4 %collective-permute-start.2 = (bf16[8,400,128]{2,1,0:T(8,128)(2,1)S(1)}, bf16[8,400,128]{2,1,0:T(8,128)(2,1)S(1)}, u32[]{:S(2)}, u32[]{:S(2)}) collective-permute-start(bf16[8,400,128]{2,1,0:T(8,128)(2,1)S(1)} %get-tuple-element.43), channel_id=1, source_target_pairs={{0,8},{8,0},{1,9},{9,1},{2,10},{10,2},{3,11},{11,3},{4,12},{12,4},... | collective-permute-start | bytes 2457608 | tf_op jit(solution)/shard_map/ppermute | solution.py:28
  57.4 3.9 %collective-permute-start.3 = (bf16[8,400,128]{2,1,0:T(8,128)(2,1)S(1)}, bf16[8,400,128]{2,1,0:T(8,128)(2,1)S(1)}, u32[]{:S(2)}, u32[]{:S(2)}) collective-permute-start(bf16[8,400,128]{2,1,0:T(8,128)(2,1)S(1)} %get-tuple-element.42), channel_id=1, source_target_pairs={{8,16},{16,8},{24,32},{32,24},{40,48},{48,40},{56,64},{64,56},{72,... | collective-permute-start | bytes 2457608 | tf_op jit(solution)/shard_map/ppermute | solution.py:526
  61.3 0.1 pad_add_fusion.order_ref
  61.4 0.0 collective-permute-done.2
  61.4 4.7 %fourier.2 = (f32[8,400,128]{2,1,0:T(8,128)S(1)}, f32[8,400,128]{2,1,0:T(8,128)S(1)}, f32[8,400,128]{2,1,0:T(8,128)S(1)}) custom-call(s32[8]{0:T(128)S(1)} %and_select_fusion.parity_ref, f32[8,2,4,128]{3,2,1,0:T(4,128)S(1)} %reshape.145.table_ref, bf16[8,2,400,128]{3,2,1,0:T(8,128)(2,1)S(1)} %all-to-all-done.refs_0_.refs_1_, ...), custom_call_target="tpu_custom_call" | custom-call | tf_op jit(solution)/shard_map/fourier/pallas_call | solution.py:104
  66.1 5.3 %collective-permute-done.3 = bf16[8,400,128]{2,1,0:T(8,128)(2,1)S(1)} collective-permute-done((bf16[8,400,128]{2,1,0:T(8,128)(2,1)S(1)}, bf16[8,400,128]{2,1,0:T(8,128)(2,1)S(1)}, u32[]{:S(2)}, u32[]{:S(2)}) %collective-permute-start.3) | collective-permute-done | bytes 819232 | tf_op jit(solution)/shard_map/ppermute | solution.py:526
  71.3 1.9 %fourier.3.refs_3_.refs_7_.refs_11_.refs_15_ = f32[8,400,128]{2,1,0:T(8,128)S(1)} custom-call(s32[8]{0:T(128)S(1)} %and_select_fusion.parity_ref, f32[8,2,4,128]{3,2,1,0:T(4,128)S(1)} %reshape.145.table_ref, bf16[8,1,400,128]{3,2,1,0:T(8,128)(2,1)S(1)} %bitcast.24), custom_call_target="tpu_custom_call" | custom-call | tf_op jit(solution)/shard_map/fourier/pallas_call | solution.py:104
  73.2 13.4 %evolve.1 = (s16[8,800,128]{2,1,0:T(8,128)(2,1)}, f32[8,2,40,128]{3,2,1,0:T(8,128)S(1)}) custom-call(s32[9]{0:T(128)S(1)} %pad_add_fusion.order_ref, f32[8,400,128]{2,1,0:T(8,128)S(1)} %get-tuple-element.30.refs_0_.refs_4_.refs_8_.refs_12_, f32[8,400,128]{2,1,0:T(8,128)S(1)} %get-tuple-element.31.refs_1_.refs_5_.refs_9_.refs_13_, ...), custom_call_target="tpu_custom_call" | custom-call | tf_op jit(solution)/shard_map/evolve/pallas_call | solution.py:275
  86.6 14.9 %all_to_all.15 = f32[16,40,128]{2,1,0:T(8,128)S(1)} all-to-all(f32[16,40,128]{2,1,0:T(8,128)S(1)} %bitcast.26), channel_id=1, replica_groups=mesh['chip'=32,'core'=2,'freq'=8] {'freq','core'}, dimensions={0} | all-to-all | bytes 655360 | tf_op jit(solution)/shard_map/all_to_all | solution.py:534
  101.5 3.6 %all-to-all-start.2 = ((s16[8,800,128]{2,1,0:T(8,128)(2,1)}), s16[8,800,128]{2,1,0:T(8,128)(2,1)S(1)}, u32[]{:S(2)}, u32[]{:S(2)}) async-start(s16[8,800,128]{2,1,0:T(8,128)(2,1)} %get-tuple-element.40), calls=%async_computation.2 | async-start | bytes 3276800 | tf_op jit(solution)/shard_map/all_to_all | solution.py:539
  105.1 10.8 %collective-permute-start.5 = (f32[40,128]{1,0:T(8,128)S(1)}, f32[40,128]{1,0:T(8,128)S(1)}, u32[]{:S(2)}, u32[]{:S(2)}) collective-permute-start(f32[40,128]{1,0:T(8,128)S(1)} %reduce_sum.9), channel_id=1, source_target_pairs={{0,128},{16,144},{32,160},{48,176},{64,192},{80,208},{96,224},{112... | collective-permute-start | bytes 61448 | tf_op jit(solution)/shard_map/ppermute | solution.py:28
  116.0 3.7 %collective-permute-start.6 = (f32[40,128]{1,0:T(8,128)S(1)}, f32[40,128]{1,0:T(8,128)S(1)}, u32[]{:S(2)}, u32[]{:S(2)}) collective-permute-start(f32[40,128]{1,0:T(8,128)S(1)} %reduce_sum.9), channel_id=1, source_target_pairs={{0,384},{16,400},{32,416},{48,432},{64,448},{80,464},{96,480},{112... | collective-permute-start | bytes 61448 | tf_op jit(solution)/shard_map/ppermute | solution.py:28
  119.7 2.9 %collective-permute-start.4 = (f32[40,128]{1,0:T(8,128)S(1)}, f32[40,128]{1,0:T(8,128)S(1)}, u32[]{:S(2)}, u32[]{:S(2)}) collective-permute-start(f32[40,128]{1,0:T(8,128)S(1)} %reduce_sum.9), channel_id=1, source_target_pairs={{0,256},{16,272},{32,288},{48,304},{64,320},{80,336},{96,352},{112... | collective-permute-start | bytes 61448 | tf_op jit(solution)/shard_map/ppermute | solution.py:28
  122.6 0.0 collective-permute-done.5
  122.6 0.0 collective-permute-done.6
  122.6 3.4 %collective-permute-done.4 = f32[40,128]{1,0:T(8,128)S(1)} collective-permute-done((f32[40,128]{1,0:T(8,128)S(1)}, f32[40,128]{1,0:T(8,128)S(1)}, u32[]{:S(2)}, u32[]{:S(2)}) %collective-permute-start.4) | collective-permute-done | bytes 20512 | tf_op jit(solution)/shard_map/ppermute | solution.py:28
  126.0 1.9 %collective-permute-start.8 = (f32[40,128]{1,0:T(8,128)S(1)}, f32[40,128]{1,0:T(8,128)S(1)}, u32[]{:S(2)}, u32[]{:S(2)}) collective-permute-start(f32[40,128]{1,0:T(8,128)S(1)} %add_add_fusion.1), channel_id=1, source_target_pairs={{0,16},{16,0},{32,48},{48,32},{64,80},{80,64},{96,112},{112,96},{1... | collective-permute-start | bytes 61448 | tf_op jit(solution)/shard_map/ppermute | solution.py:28
  128.0 1.9 %collective-permute-start.9 = (f32[40,128]{1,0:T(8,128)S(1)}, f32[40,128]{1,0:T(8,128)S(1)}, u32[]{:S(2)}, u32[]{:S(2)}) collective-permute-start(f32[40,128]{1,0:T(8,128)S(1)} %add_add_fusion.1), channel_id=1, source_target_pairs={{0,48},{16,32},{32,16},{48,0},{64,112},{80,96},{96,80},{112,64},{1... | collective-permute-start | bytes 61448 | tf_op jit(solution)/shard_map/ppermute | solution.py:28
  129.9 4.5 %collective-permute-start.7 = (f32[40,128]{1,0:T(8,128)S(1)}, f32[40,128]{1,0:T(8,128)S(1)}, u32[]{:S(2)}, u32[]{:S(2)}) collective-permute-start(f32[40,128]{1,0:T(8,128)S(1)} %add_add_fusion.1), channel_id=1, source_target_pairs={{0,32},{16,48},{32,0},{48,16},{64,96},{80,112},{96,64},{112,80},{1... | collective-permute-start | bytes 61448 | tf_op jit(solution)/shard_map/ppermute | solution.py:28
  134.4 0.0 collective-permute-done.8
  134.4 0.1 collective-permute-done.9
  134.6 1.3 collective-permute-done.7
  135.9 7.5 %collective-permute-start.10 = (f32[40,128]{1,0:T(8,128)S(1)}, f32[40,128]{1,0:T(8,128)S(1)}, u32[]{:S(2)}, u32[]{:S(2)}) collective-permute-start(f32[40,128]{1,0:T(8,128)S(1)} %add_add_fusion), channel_id=1, source_target_pairs={{0,64},{16,80},{32,96},{48,112},{64,0},{80,16},{96,32},{112,48},{1... | collective-permute-start | bytes 61448 | tf_op jit(solution)/shard_map/ppermute | solution.py:28
  143.4 1.4 collective-permute-done.10
  144.9 4.5 %collective-permute-start.11 = (f32[40,128]{1,0:T(8,128)S(1)}, f32[40,128]{1,0:T(8,128)S(1)}, u32[]{:S(2)}, u32[]{:S(2)}) collective-permute-start(f32[40,128]{1,0:T(8,128)S(1)} %add.66.refs_0_), channel_id=1, source_target_pairs={{0,8},{8,0},{1,9},{9,1},{2,10},{10,2},{3,11},{11,3},{4,12},{12,4},... | collective-permute-start | bytes 61448 | tf_op jit(solution)/shard_map/ppermute | solution.py:28
  149.4 0.8 collective-permute-done.11.refs_1_
  150.2 6.9 %factorize.1 = (f32[128,128]{1,0:T(8,128)S(1)}, f32[128,128]{1,0:T(8,128)}) custom-call(s32[1]{0:T(128)} %bitcast.core_ref, f32[40,128]{1,0:T(8,128)S(1)} %add.66.refs_0_, f32[40,128]{1,0:T(8,128)S(1)} %collective-permute-done.11.refs_1_), custom_call_target="tpu_custom_call" | custom-call | tf_op jit(solution)/shard_map/factorize/pallas_call | solution.py:369
  157.1 0.0 all-to-all-done.2.high_ref.low_ref
  157.1 4.5 %apply.1 = f32[1,128,5,8,128]{4,3,2,1,0:T(8,128)} custom-call(f32[128,128]{1,0:T(8,128)S(1)} %get-tuple-element.39.inverse_ref, f32[8,128]{1,0:T(8,128)S(1)} %fusion.6.scale_ref, s16[8,800,128]{2,1,0:T(8,128)(2,1)S(1)} %all-to-all-done.2.high_ref.low_ref, s16[8,800,128]{2,1,0:T(8,128)(2,1)S(1)} %all-to-all-done.2.high_ref.low_ref), custom_call_target="tpu_custom_call" | custom-call | tf_op jit(solution)/shard_map/apply/pallas_call | solution.py:405
  (23 shorter events, 0.2 us)
Async XLA Ops:
  5.2 7.8 %copy-start.3 = (f32[8,128]{1,0:T(8,128)S(1)}, f32[8,128]{1,0:T(8,128)}, u32[]{:S(2)}) copy-start(f32[8,128]{1,0:T(8,128)} %velocity_ref) | copy-start | bytes 12292
  5.2 7.8 %copy-start.2 = (f32[5,5,8,128]{3,2,1,0:T(8,128)S(1)}, f32[5,5,8,128]{3,2,1,0:T(8,128)}, u32[]{:S(2)}) copy-start(f32[5,5,8,128]{3,2,1,0:T(8,128)} %param.5) | copy-start | bytes 307204
  5.3 14.7 %copy-start.4 = (s32[8]{0:T(128)S(1)}, s32[8]{0:T(128)}, u32[]{:S(2)}) copy-start(s32[8]{0:T(128)} %param.7) | copy-start | bytes 100
  5.3 49.6 %all-to-all-start = ((bf16[8,2,400,128]{3,2,1,0:T(8,128)(2,1)}), bf16[8,2,400,128]{3,2,1,0:T(8,128)(2,1)S(1)}, u32[]{:S(2)}, u32[]{:S(2)}) async-start(bf16[8,2,400,128]{3,2,1,0:T(8,128)(2,1)} %spread.1), calls=%async_computation | async-start | bytes 3276800 | tf_op jit(solution)/shard_map/all_to_all | solution.py:512
  13.1 7.5 %collective-permute-start = (f32[26,2,128]{2,1,0:T(2,128)S(1)}, f32[26,2,128]{2,1,0:T(2,128)S(1)}, u32[]{:S(2)}, u32[]{:S(2)}) collective-permute-start(f32[26,2,128]{2,1,0:T(2,128)S(1)} %pad_maximum_fusion), channel_id=1, source_target_pairs={{8,0},{16,8},{24,16},{32,24},{40,32},{48,40},{56,48},{64,56},{72,6... | collective-permute-start | bytes 79880 | tf_op jit(solution)/shard_map/ppermute | solution.py:486
  17.9 3.1 %collective-permute-start.1 = (f32[26,2,128]{2,1,0:T(2,128)S(1)}, f32[26,2,128]{2,1,0:T(2,128)S(1)}, u32[]{:S(2)}, u32[]{:S(2)}) collective-permute-start(f32[26,2,128]{2,1,0:T(2,128)S(1)} %pad_maximum_fusion.1), channel_id=1, source_target_pairs={{0,8},{8,16},{16,24},{24,32},{32,40},{40,48},{48,56},{56,64},{64,7... | collective-permute-start | bytes 79880 | tf_op jit(solution)/shard_map/ppermute | solution.py:487
  26.8 2.1 %copy-start = (f32[29,304,128]{2,1,0:T(8,128)}, f32[29,304,128]{2,1,0:T(8,128)S(1)}, u32[]{:S(2)}) copy-start(f32[29,304,128]{2,1,0:T(8,128)S(1)} %get-tuple-element.34.refs_20_) | copy-start | bytes 13541380
  55.0 6.4 %collective-permute-start.2 = (bf16[8,400,128]{2,1,0:T(8,128)(2,1)S(1)}, bf16[8,400,128]{2,1,0:T(8,128)(2,1)S(1)}, u32[]{:S(2)}, u32[]{:S(2)}) collective-permute-start(bf16[8,400,128]{2,1,0:T(8,128)(2,1)S(1)} %get-tuple-element.43), channel_id=1, source_target_pairs={{0,8},{8,0},{1,9},{9,1},{2,10},{10,2},{3,11},{11,3},{4,12},{12,4},... | collective-permute-start | bytes 2457608 | tf_op jit(solution)/shard_map/ppermute | solution.py:28
  57.4 13.9 %collective-permute-start.3 = (bf16[8,400,128]{2,1,0:T(8,128)(2,1)S(1)}, bf16[8,400,128]{2,1,0:T(8,128)(2,1)S(1)}, u32[]{:S(2)}, u32[]{:S(2)}) collective-permute-start(bf16[8,400,128]{2,1,0:T(8,128)(2,1)S(1)} %get-tuple-element.42), channel_id=1, source_target_pairs={{8,16},{16,8},{24,32},{32,24},{40,48},{48,40},{56,64},{64,56},{72,... | collective-permute-start | bytes 2457608 | tf_op jit(solution)/shard_map/ppermute | solution.py:526
  61.4 11.8 %copy-start.1 = (f32[29,304,128]{2,1,0:T(8,128)S(1)}, f32[29,304,128]{2,1,0:T(8,128)}, u32[]{:S(2)}) copy-start(f32[29,304,128]{2,1,0:T(8,128)} %copy-done) | copy-start | bytes 13541380
  101.5 55.6 %all-to-all-start.2 = ((s16[8,800,128]{2,1,0:T(8,128)(2,1)}), s16[8,800,128]{2,1,0:T(8,128)(2,1)S(1)}, u32[]{:S(2)}, u32[]{:S(2)}) async-start(s16[8,800,128]{2,1,0:T(8,128)(2,1)} %get-tuple-element.40), calls=%async_computation.2 | async-start | bytes 3276800 | tf_op jit(solution)/shard_map/all_to_all | solution.py:539
  105.1 17.4 %collective-permute-start.5 = (f32[40,128]{1,0:T(8,128)S(1)}, f32[40,128]{1,0:T(8,128)S(1)}, u32[]{:S(2)}, u32[]{:S(2)}) collective-permute-start(f32[40,128]{1,0:T(8,128)S(1)} %reduce_sum.9), channel_id=1, source_target_pairs={{0,128},{16,144},{32,160},{48,176},{64,192},{80,208},{96,224},{112... | collective-permute-start | bytes 61448 | tf_op jit(solution)/shard_map/ppermute | solution.py:28
  116.0 6.6 %collective-permute-start.6 = (f32[40,128]{1,0:T(8,128)S(1)}, f32[40,128]{1,0:T(8,128)S(1)}, u32[]{:S(2)}, u32[]{:S(2)}) collective-permute-start(f32[40,128]{1,0:T(8,128)S(1)} %reduce_sum.9), channel_id=1, source_target_pairs={{0,384},{16,400},{32,416},{48,432},{64,448},{80,464},{96,480},{112... | collective-permute-start | bytes 61448 | tf_op jit(solution)/shard_map/ppermute | solution.py:28
  119.7 6.3 %collective-permute-start.4 = (f32[40,128]{1,0:T(8,128)S(1)}, f32[40,128]{1,0:T(8,128)S(1)}, u32[]{:S(2)}, u32[]{:S(2)}) collective-permute-start(f32[40,128]{1,0:T(8,128)S(1)} %reduce_sum.9), channel_id=1, source_target_pairs={{0,256},{16,272},{32,288},{48,304},{64,320},{80,336},{96,352},{112... | collective-permute-start | bytes 61448 | tf_op jit(solution)/shard_map/ppermute | solution.py:28
  126.0 8.4 %collective-permute-start.8 = (f32[40,128]{1,0:T(8,128)S(1)}, f32[40,128]{1,0:T(8,128)S(1)}, u32[]{:S(2)}, u32[]{:S(2)}) collective-permute-start(f32[40,128]{1,0:T(8,128)S(1)} %add_add_fusion.1), channel_id=1, source_target_pairs={{0,16},{16,0},{32,48},{48,32},{64,80},{80,64},{96,112},{112,96},{1... | collective-permute-start | bytes 61448 | tf_op jit(solution)/shard_map/ppermute | solution.py:28
  128.0 6.6 %collective-permute-start.9 = (f32[40,128]{1,0:T(8,128)S(1)}, f32[40,128]{1,0:T(8,128)S(1)}, u32[]{:S(2)}, u32[]{:S(2)}) collective-permute-start(f32[40,128]{1,0:T(8,128)S(1)} %add_add_fusion.1), channel_id=1, source_target_pairs={{0,48},{16,32},{32,16},{48,0},{64,112},{80,96},{96,80},{112,64},{1... | collective-permute-start | bytes 61448 | tf_op jit(solution)/shard_map/ppermute | solution.py:28
  129.9 6.0 %collective-permute-start.7 = (f32[40,128]{1,0:T(8,128)S(1)}, f32[40,128]{1,0:T(8,128)S(1)}, u32[]{:S(2)}, u32[]{:S(2)}) collective-permute-start(f32[40,128]{1,0:T(8,128)S(1)} %add_add_fusion.1), channel_id=1, source_target_pairs={{0,32},{16,48},{32,0},{48,16},{64,96},{80,112},{96,64},{112,80},{1... | collective-permute-start | bytes 61448 | tf_op jit(solution)/shard_map/ppermute | solution.py:28
  135.9 9.0 %collective-permute-start.10 = (f32[40,128]{1,0:T(8,128)S(1)}, f32[40,128]{1,0:T(8,128)S(1)}, u32[]{:S(2)}, u32[]{:S(2)}) collective-permute-start(f32[40,128]{1,0:T(8,128)S(1)} %add_add_fusion), channel_id=1, source_target_pairs={{0,64},{16,80},{32,96},{48,112},{64,0},{80,16},{96,32},{112,48},{1... | collective-permute-start | bytes 61448 | tf_op jit(solution)/shard_map/ppermute | solution.py:28
  144.9 5.3 %collective-permute-start.11 = (f32[40,128]{1,0:T(8,128)S(1)}, f32[40,128]{1,0:T(8,128)S(1)}, u32[]{:S(2)}, u32[]{:S(2)}) collective-permute-start(f32[40,128]{1,0:T(8,128)S(1)} %add.66.refs_0_), channel_id=1, source_target_pairs={{0,8},{8,0},{1,9},{9,1},{2,10},{10,2},{3,11},{11,3},{4,12},{12,4},... | collective-permute-start | bytes 61448 | tf_op jit(solution)/shard_map/ppermute | solution.py:28

commit v11 on v10

--- a/solution.py
+++ b/solution.py
@@ -31,6 +31,11 @@
 def quad_sum(value, axis, one, two):
     near, far, both = [swap(value, axis, mask) for mask in (one, two, one ^ two)]
     return (value + near) + (far + both)
+
+
+def eight_sum(value, axis):
+    far = {mask: swap(value, axis, mask) for mask in (4, 7, 3, 5, 2, 6, 1)}
+    return ((value + far[1]) + (far[2] + far[3])) + ((far[4] + far[5]) + (far[6] + far[7]))
 
 
 def spread_body(sketch_ref, out_ref, rows_ref, turned_ref):
@@ -376,11 +381,16 @@
     )(core[None], *parts)
 
 
-def apply_body(inverse_ref, scale_ref, high_ref, low_ref, out_ref, rows_ref):
+def apply_body(inverse_ref, scale_ref, high_ref, low_ref, out_ref, rows_ref, main_ref, rest_ref):
     per = high_ref.shape[1] // 8
-    one, two, three = split(inverse_ref[...].T)
-    main = jnp.concatenate([jnp.concatenate([one, two], axis=1)] * 2, axis=0)
-    rest = jnp.concatenate([one, three], axis=0)
+
+    @pl.when(pl.program_id(0) == 0)
+    def _():
+        one, two, three = split(inverse_ref[...].T)
+        main_ref[...] = jnp.concatenate([jnp.concatenate([one, two], axis=1)] * 2, axis=0)
+        rest_ref[...] = jnp.concatenate([one, three], axis=0)
+
+    main, rest = main_ref[...], rest_ref[...]
     for x in range(8):
         shift, half = 12 - 4 * (x // 2), x % 2
         lines = []
@@ -415,6 +425,8 @@
         out_shape=jax.ShapeDtypeStruct((1, LANES, FIELDS, 8, radial), jnp.float32),
         scratch_shapes=[
             pltpu.VMEM((LANES * 8, radial), jnp.float32),
+            pltpu.VMEM((2 * LANES, 2 * LANES), jnp.bfloat16),
+            pltpu.VMEM((2 * LANES, LANES), jnp.bfloat16),
         ],
         compiler_params=pltpu.CompilerParams(vmem_limit_bytes=VMEM_LIMIT),
         name="apply",
@@ -538,8 +550,7 @@
     columns, gram = lax.optimization_barrier((columns, gram))
     columns = lax.all_to_all(columns, "freq", split_axis=0, concat_axis=0, tiled=True)
     gram = quad_sum(gram, "chip", 16, 8)
-    gram = quad_sum(gram, "chip", 2, 1)
-    gram = gram + swap(gram, "chip", 4)
+    gram = eight_sum(gram, "chip")
     parts = [gram, swap(gram, "core", 1)]
     row_scale = math.sqrt(FIELDS * 8 * count * radial)
     inverse, factor = factorize(core, parts, row_scale)

time: 162 us -> 171 us (1.056)
  starting transfers between devices: 62.2 us -> 72.1 us
    ppermute x9 -> x12, starting transfers between devices: 40.1 us -> 50 us  [swap(): return lax.ppermute(value, axis, [(i, i ^ mask) for i in range(count)])]
    ppermute x9 -> x12, waiting for transfers between devices: 7.14 us -> 5.88 us  [swap(): return lax.ppermute(value, axis, [(i, i ^ mask) for i in range(count)])]
  transfers between devices with their start and end apart: 14 -> 17, of which waited for: 8 -> 7; matrix products, arithmetic and copies ran while one was open for 0% -> 0% of each run, Pallas kernels for 11% -> 10%
where the time goes in v11:
time: 171 us; the launch traced here: 170 us
  starting transfers between devices  72.1 us (42%)
  Pallas kernels  41.6 us (24%)
  waiting for transfers between devices  37.6 us (22%)
  blocking collectives  14.9 us (9%)
  local copies, waits for them, and re-layouts  2.6 us (2%)
    ppermute x12, starting transfers between devices, swap(): return lax.ppermute(value, axis, [(i, i ^ mask) for i in range(count)])  50 us
    all_to_all x1, waiting for transfers between devices, local(): rows = lax.all_to_all(rows, 'freq', split_axis=0, concat_axis=0, tiled=True)  26.1 us
    all_to_all x1, blocking collectives, local(): lax.all_to_all(grams, ('freq', 'core'), split_axis=0, concat_axis=0, tile...  14.9 us
    pallas_call x1, Pallas kernels, evolve(): pl.pallas_call(evolve_body, grid_spec=pltpu.PrefetchScalarGridSpec(num_sc...  13.4 us
    all_to_all x1, starting transfers between devices, local(): rows = lax.all_to_all(rows, 'freq', split_axis=0, concat_axis=0, tiled=True)  7.79 us
    pallas_call x1, Pallas kernels, factorize(): pl.pallas_call(partial(factor_body, scale), in_specs=[pl.BlockSpec(memory...  6.9 us
    pallas_call x2, Pallas kernels, fourier(): pl.pallas_call(fourier_body, grid=(1,), in_specs=[pl.BlockSpec(memory_spa...  6.57 us
    ppermute x12, waiting for transfers between devices, swap(): return lax.ppermute(value, axis, [(i, i ^ mask) for i in range(count)])  5.88 us
  transfers between devices with their start and end apart: 17, of which 7 were waited for; matrix products, arithmetic and copies ran while one was open for 0% of the time, Pallas kernels for 10%

profile of v11, /device:TPU:1, one launch (start us, length us, event | category | flops | bytes accessed | tf_op | source)
XLA Modules:
  0.0 170.2 jit_solution(4565364320544170121)
XLA Ops:
  0.6 4.6 %spread.1 = bf16[8,2,400,128]{3,2,1,0:T(8,128)(2,1)} custom-call(bf16[2,64,5,8,128]{4,3,2,1,0:T(8,128)(2,1)} %sketch_ref.1), custom_call_target="tpu_custom_call" | custom-call | tf_op jit(solution)/shard_map/spread/pallas_call | solution.py:63
  5.3 7.8 %all-to-all-start = ((bf16[8,2,400,128]{3,2,1,0:T(8,128)(2,1)}), bf16[8,2,400,128]{3,2,1,0:T(8,128)(2,1)S(1)}, u32[]{:S(2)}, u32[]{:S(2)}) async-start(bf16[8,2,400,128]{3,2,1,0:T(8,128)(2,1)} %spread.1), calls=%async_computation | async-start | bytes 3276800 | tf_op jit(solution)/shard_map/all_to_all | solution.py:524
  13.1 4.7 %collective-permute-start = (f32[26,2,128]{2,1,0:T(2,128)S(1)}, f32[26,2,128]{2,1,0:T(2,128)S(1)}, u32[]{:S(2)}, u32[]{:S(2)}) collective-permute-start(f32[26,2,128]{2,1,0:T(2,128)S(1)} %pad_maximum_fusion), channel_id=1, source_target_pairs={{8,0},{16,8},{24,16},{32,24},{40,32},{48,40},{56,48},{64,56},{72,6... | collective-permute-start | bytes 79880 | tf_op jit(solution)/shard_map/ppermute | solution.py:498
  17.9 2.0 %collective-permute-start.1 = (f32[26,2,128]{2,1,0:T(2,128)S(1)}, f32[26,2,128]{2,1,0:T(2,128)S(1)}, u32[]{:S(2)}, u32[]{:S(2)}) collective-permute-start(f32[26,2,128]{2,1,0:T(2,128)S(1)} %pad_maximum_fusion.1), channel_id=1, source_target_pairs={{0,8},{8,16},{16,24},{24,32},{32,40},{40,48},{48,56},{56,64},{64,7... | collective-permute-start | bytes 79880 | tf_op jit(solution)/shard_map/ppermute | solution.py:499
  20.0 0.1 fusion.7
  20.1 0.1 broadcast_multiply_fusion
  20.1 0.1 pad_add_fusion.1.place_ref
  20.2 0.1 copy.7
  20.3 0.1 broadcast_in_dim.46
  20.5 0.1 reshape.145.table_ref
  20.6 0.4 collective-permute-done.1.left_ref
  21.0 5.8 %stencil.1 = (f32[29,304,128]{2,1,0:T(8,128)S(1)}, f32[304,128]{1,0:T(8,128)S(1)}) custom-call(s32[3]{0:T(128)S(1)} %pad_add_fusion.1.place_ref, f32[25,8,128]{2,1,0:T(8,128)S(1)} %bitcast.28, f32[8,128]{1,0:T(8,128)S(1)} %copy-done.3, f32[26,2,128]{2,1,0:T(2,128)S(1)} %collective-permute-done.right_ref, f32[26,2,128]{2,1,0:T(2,128)S(1)} %collective-permute-done.1.left_ref), custom_call_target="tpu_custom_call" | custom-call | tf_op jit(solution)/shard_map/stencil/pallas_call | solution.py:502
  26.8 2.1 %copy-done = f32[29,304,128]{2,1,0:T(8,128)} copy-done((f32[29,304,128]{2,1,0:T(8,128)}, f32[29,304,128]{2,1,0:T(8,128)S(1)}, u32[]{:S(2)}) %copy-start) | copy-done | bytes 4513816
  28.8 26.1 %all-to-all-done.refs_0_.refs_1_ = bf16[8,2,400,128]{3,2,1,0:T(8,128)(2,1)S(1)} async-done(((bf16[8,2,400,128]{3,2,1,0:T(8,128)(2,1)}), bf16[8,2,400,128]{3,2,1,0:T(8,128)(2,1)S(1)}, u32[]{:S(2)}, u32[]{:S(2)}) %all-to-all-start) | async-done | bytes 1638432 | tf_op jit(solution)/shard_map/all_to_all | solution.py:524
  54.9 0.1 dynamic-slice_bitcast_fusion
  55.0 2.4 %collective-permute-start.2 = (bf16[8,400,128]{2,1,0:T(8,128)(2,1)S(1)}, bf16[8,400,128]{2,1,0:T(8,128)(2,1)S(1)}, u32[]{:S(2)}, u32[]{:S(2)}) collective-permute-start(bf16[8,400,128]{2,1,0:T(8,128)(2,1)S(1)} %get-tuple-element.43), channel_id=1, source_target_pairs={{0,8},{8,0},{1,9},{9,1},{2,10},{10,2},{3,11},{11,3},{4,12},{12,4},... | collective-permute-start | bytes 2457608 | tf_op jit(solution)/shard_map/ppermute | solution.py:28
  57.4 3.9 %collective-permute-start.3 = (bf16[8,400,128]{2,1,0:T(8,128)(2,1)S(1)}, bf16[8,400,128]{2,1,0:T(8,128)(2,1)S(1)}, u32[]{:S(2)}, u32[]{:S(2)}) collective-permute-start(bf16[8,400,128]{2,1,0:T(8,128)(2,1)S(1)} %get-tuple-element.42), channel_id=1, source_target_pairs={{8,16},{16,8},{24,32},{32,24},{40,48},{48,40},{56,64},{64,56},{72,... | collective-permute-start | bytes 2457608 | tf_op jit(solution)/shard_map/ppermute | solution.py:538
  61.3 0.1 pad_add_fusion.order_ref
  61.4 0.0 collective-permute-done.2
  61.4 4.7 %fourier.2 = (f32[8,400,128]{2,1,0:T(8,128)S(1)}, f32[8,400,128]{2,1,0:T(8,128)S(1)}, f32[8,400,128]{2,1,0:T(8,128)S(1)}) custom-call(s32[8]{0:T(128)S(1)} %and_select_fusion.parity_ref, f32[8,2,4,128]{3,2,1,0:T(4,128)S(1)} %reshape.145.table_ref, bf16[8,2,400,128]{3,2,1,0:T(8,128)(2,1)S(1)} %all-to-all-done.refs_0_.refs_1_, ...), custom_call_target="tpu_custom_call" | custom-call | tf_op jit(solution)/shard_map/fourier/pallas_call | solution.py:109
  66.1 5.3 %collective-permute-done.3 = bf16[8,400,128]{2,1,0:T(8,128)(2,1)S(1)} collective-permute-done((bf16[8,400,128]{2,1,0:T(8,128)(2,1)S(1)}, bf16[8,400,128]{2,1,0:T(8,128)(2,1)S(1)}, u32[]{:S(2)}, u32[]{:S(2)}) %collective-permute-start.3) | collective-permute-done | bytes 819232 | tf_op jit(solution)/shard_map/ppermute | solution.py:538
  71.3 1.9 %fourier.3.refs_3_.refs_7_.refs_11_.refs_15_ = f32[8,400,128]{2,1,0:T(8,128)S(1)} custom-call(s32[8]{0:T(128)S(1)} %and_select_fusion.parity_ref, f32[8,2,4,128]{3,2,1,0:T(4,128)S(1)} %reshape.145.table_ref, bf16[8,1,400,128]{3,2,1,0:T(8,128)(2,1)S(1)} %bitcast.24), custom_call_target="tpu_custom_call" | custom-call | tf_op jit(solution)/shard_map/fourier/pallas_call | solution.py:109
  73.2 13.4 %evolve.1 = (s16[8,800,128]{2,1,0:T(8,128)(2,1)}, f32[8,2,40,128]{3,2,1,0:T(8,128)S(1)}) custom-call(s32[9]{0:T(128)S(1)} %pad_add_fusion.order_ref, f32[8,400,128]{2,1,0:T(8,128)S(1)} %get-tuple-element.30.refs_0_.refs_4_.refs_8_.refs_12_, f32[8,400,128]{2,1,0:T(8,128)S(1)} %get-tuple-element.31.refs_1_.refs_5_.refs_9_.refs_13_, ...), custom_call_target="tpu_custom_call" | custom-call | tf_op jit(solution)/shard_map/evolve/pallas_call | solution.py:280
  86.6 14.9 %all_to_all.15 = f32[16,40,128]{2,1,0:T(8,128)S(1)} all-to-all(f32[16,40,128]{2,1,0:T(8,128)S(1)} %bitcast.26), channel_id=1, replica_groups=mesh['chip'=32,'core'=2,'freq'=8] {'freq','core'}, dimensions={0} | all-to-all | bytes 655360 | tf_op jit(solution)/shard_map/all_to_all | solution.py:546
  101.5 3.6 %all-to-all-start.2 = ((s16[8,800,128]{2,1,0:T(8,128)(2,1)}), s16[8,800,128]{2,1,0:T(8,128)(2,1)S(1)}, u32[]{:S(2)}, u32[]{:S(2)}) async-start(s16[8,800,128]{2,1,0:T(8,128)(2,1)} %get-tuple-element.40), calls=%async_computation.2 | async-start | bytes 3276800 | tf_op jit(solution)/shard_map/all_to_all | solution.py:551
  105.1 10.8 %collective-permute-start.5 = (f32[40,128]{1,0:T(8,128)S(1)}, f32[40,128]{1,0:T(8,128)S(1)}, u32[]{:S(2)}, u32[]{:S(2)}) collective-permute-start(f32[40,128]{1,0:T(8,128)S(1)} %reduce_sum.9), channel_id=1, source_target_pairs={{0,128},{16,144},{32,160},{48,176},{64,192},{80,208},{96,224},{112... | collective-permute-start | bytes 61448 | tf_op jit(solution)/shard_map/ppermute | solution.py:28
  116.0 3.7 %collective-permute-start.6 = (f32[40,128]{1,0:T(8,128)S(1)}, f32[40,128]{1,0:T(8,128)S(1)}, u32[]{:S(2)}, u32[]{:S(2)}) collective-permute-start(f32[40,128]{1,0:T(8,128)S(1)} %reduce_sum.9), channel_id=1, source_target_pairs={{0,384},{16,400},{32,416},{48,432},{64,448},{80,464},{96,480},{112... | collective-permute-start | bytes 61448 | tf_op jit(solution)/shard_map/ppermute | solution.py:28
  119.7 2.9 %collective-permute-start.4 = (f32[40,128]{1,0:T(8,128)S(1)}, f32[40,128]{1,0:T(8,128)S(1)}, u32[]{:S(2)}, u32[]{:S(2)}) collective-permute-start(f32[40,128]{1,0:T(8,128)S(1)} %reduce_sum.9), channel_id=1, source_target_pairs={{0,256},{16,272},{32,288},{48,304},{64,320},{80,336},{96,352},{112... | collective-permute-start | bytes 61448 | tf_op jit(solution)/shard_map/ppermute | solution.py:28
  122.6 0.0 collective-permute-done.5
  122.6 0.0 collective-permute-done.6
  122.6 3.4 %collective-permute-done.4 = f32[40,128]{1,0:T(8,128)S(1)} collective-permute-done((f32[40,128]{1,0:T(8,128)S(1)}, f32[40,128]{1,0:T(8,128)S(1)}, u32[]{:S(2)}, u32[]{:S(2)}) %collective-permute-start.4) | collective-permute-done | bytes 20512 | tf_op jit(solution)/shard_map/ppermute | solution.py:28
  126.0 3.3 %collective-permute-start.12 = (f32[40,128]{1,0:T(8,128)S(1)}, f32[40,128]{1,0:T(8,128)S(1)}, u32[]{:S(2)}, u32[]{:S(2)}) collective-permute-start(f32[40,128]{1,0:T(8,128)S(1)} %add_add_fusion.1), channel_id=1, source_target_pairs={{0,96},{16,112},{32,64},{48,80},{64,32},{80,48},{96,0},{112,16},{1... | collective-permute-start | bytes 61448 | tf_op jit(solution)/shard_map/ppermute | solution.py:28
  129.3 3.5 %collective-permute-start.13 = (f32[40,128]{1,0:T(8,128)S(1)}, f32[40,128]{1,0:T(8,128)S(1)}, u32[]{:S(2)}, u32[]{:S(2)}) collective-permute-start(f32[40,128]{1,0:T(8,128)S(1)} %add_add_fusion.1), channel_id=1, source_target_pairs={{0,112},{16,96},{32,80},{48,64},{64,48},{80,32},{96,16},{112,0},{1... | collective-permute-start | bytes 61448 | tf_op jit(solution)/shard_map/ppermute | solution.py:28
  132.8 4.2 %collective-permute-start.10 = (f32[40,128]{1,0:T(8,128)S(1)}, f32[40,128]{1,0:T(8,128)S(1)}, u32[]{:S(2)}, u32[]{:S(2)}) collective-permute-start(f32[40,128]{1,0:T(8,128)S(1)} %add_add_fusion.1), channel_id=1, source_target_pairs={{0,64},{16,80},{32,96},{48,112},{64,0},{80,16},{96,32},{112,48},{1... | collective-permute-start | bytes 61448 | tf_op jit(solution)/shard_map/ppermute | solution.py:28
  137.0 5.7 %collective-permute-start.11 = (f32[40,128]{1,0:T(8,128)S(1)}, f32[40,128]{1,0:T(8,128)S(1)}, u32[]{:S(2)}, u32[]{:S(2)}) collective-permute-start(f32[40,128]{1,0:T(8,128)S(1)} %add_add_fusion.1), channel_id=1, source_target_pairs={{0,80},{16,64},{32,112},{48,96},{64,16},{80,0},{96,48},{112,32},{1... | collective-permute-start | bytes 61448 | tf_op jit(solution)/shard_map/ppermute | solution.py:28
  142.6 2.4 %collective-permute-start.8 = (f32[40,128]{1,0:T(8,128)S(1)}, f32[40,128]{1,0:T(8,128)S(1)}, u32[]{:S(2)}, u32[]{:S(2)}) collective-permute-start(f32[40,128]{1,0:T(8,128)S(1)} %add_add_fusion.1), channel_id=1, source_target_pairs={{0,32},{16,48},{32,0},{48,16},{64,96},{80,112},{96,64},{112,80},{1... | collective-permute-start | bytes 61448 | tf_op jit(solution)/shard_map/ppermute | solution.py:28
  145.1 0.0 collective-permute-done.12
  145.1 3.1 %collective-permute-start.9 = (f32[40,128]{1,0:T(8,128)S(1)}, f32[40,128]{1,0:T(8,128)S(1)}, u32[]{:S(2)}, u32[]{:S(2)}) collective-permute-start(f32[40,128]{1,0:T(8,128)S(1)} %add_add_fusion.1), channel_id=1, source_target_pairs={{0,48},{16,32},{32,16},{48,0},{64,112},{80,96},{96,80},{112,64},{1... | collective-permute-start | bytes 61448 | tf_op jit(solution)/shard_map/ppermute | solution.py:28
  148.2 2.8 %collective-permute-start.7 = (f32[40,128]{1,0:T(8,128)S(1)}, f32[40,128]{1,0:T(8,128)S(1)}, u32[]{:S(2)}, u32[]{:S(2)}) collective-permute-start(f32[40,128]{1,0:T(8,128)S(1)} %add_add_fusion.1), channel_id=1, source_target_pairs={{0,16},{16,0},{32,48},{48,32},{64,80},{80,64},{96,112},{112,96},{1... | collective-permute-start | bytes 61448 | tf_op jit(solution)/shard_map/ppermute | solution.py:28
  151.1 0.0 collective-permute-done.10
  151.1 0.0 collective-permute-done.8
  151.1 0.3 collective-permute-done.9
  151.4 1.3 collective-permute-done.7
  152.8 5.3 %collective-permute-start.14 = (f32[40,128]{1,0:T(8,128)S(1)}, f32[40,128]{1,0:T(8,128)S(1)}, u32[]{:S(2)}, u32[]{:S(2)}) collective-permute-start(f32[40,128]{1,0:T(8,128)S(1)} %add_add_fusion.refs_0_), channel_id=1, source_target_pairs={{0,8},{8,0},{1,9},{9,1},{2,10},{10,2},{3,11},{11,3},{4,12},{12,4},... | collective-permute-start | bytes 61448 | tf_op jit(solution)/shard_map/ppermute | solution.py:28
  158.1 0.8 collective-permute-done.14.refs_1_
  158.9 6.9 %factorize.1 = (f32[128,128]{1,0:T(8,128)S(1)}, f32[128,128]{1,0:T(8,128)}) custom-call(s32[1]{0:T(128)} %bitcast.core_ref, f32[40,128]{1,0:T(8,128)S(1)} %add_add_fusion.refs_0_, f32[40,128]{1,0:T(8,128)S(1)} %collective-permute-done.14.refs_1_), custom_call_target="tpu_custom_call" | custom-call | tf_op jit(solution)/shard_map/factorize/pallas_call | solution.py:374
  165.8 0.0 all-to-all-done.2.high_ref.low_ref
  165.8 4.4 %apply.1 = f32[1,128,5,8,128]{4,3,2,1,0:T(8,128)} custom-call(f32[128,128]{1,0:T(8,128)S(1)} %get-tuple-element.39.inverse_ref, f32[8,128]{1,0:T(8,128)S(1)} %fusion.6.scale_ref, s16[8,800,128]{2,1,0:T(8,128)(2,1)S(1)} %all-to-all-done.2.high_ref.low_ref, s16[8,800,128]{2,1,0:T(8,128)(2,1)S(1)} %all-to-all-done.2.high_ref.low_ref), custom_call_target="tpu_custom_call" | custom-call | tf_op jit(solution)/shard_map/apply/pallas_call | solution.py:415
  (28 shorter events, 0.2 us)
Async XLA Ops:
  5.2 7.8 %copy-start.3 = (f32[8,128]{1,0:T(8,128)S(1)}, f32[8,128]{1,0:T(8,128)}, u32[]{:S(2)}) copy-start(f32[8,128]{1,0:T(8,128)} %velocity_ref) | copy-start | bytes 12292
  5.2 7.8 %copy-start.2 = (f32[5,5,8,128]{3,2,1,0:T(8,128)S(1)}, f32[5,5,8,128]{3,2,1,0:T(8,128)}, u32[]{:S(2)}) copy-start(f32[5,5,8,128]{3,2,1,0:T(8,128)} %param.5) | copy-start | bytes 307204
  5.3 14.7 %copy-start.4 = (s32[8]{0:T(128)S(1)}, s32[8]{0:T(128)}, u32[]{:S(2)}) copy-start(s32[8]{0:T(128)} %param.7) | copy-start | bytes 100
  5.3 49.6 %all-to-all-start = ((bf16[8,2,400,128]{3,2,1,0:T(8,128)(2,1)}), bf16[8,2,400,128]{3,2,1,0:T(8,128)(2,1)S(1)}, u32[]{:S(2)}, u32[]{:S(2)}) async-start(bf16[8,2,400,128]{3,2,1,0:T(8,128)(2,1)} %spread.1), calls=%async_computation | async-start | bytes 3276800 | tf_op jit(solution)/shard_map/all_to_all | solution.py:524
  13.1 7.5 %collective-permute-start = (f32[26,2,128]{2,1,0:T(2,128)S(1)}, f32[26,2,128]{2,1,0:T(2,128)S(1)}, u32[]{:S(2)}, u32[]{:S(2)}) collective-permute-start(f32[26,2,128]{2,1,0:T(2,128)S(1)} %pad_maximum_fusion), channel_id=1, source_target_pairs={{8,0},{16,8},{24,16},{32,24},{40,32},{48,40},{56,48},{64,56},{72,6... | collective-permute-start | bytes 79880 | tf_op jit(solution)/shard_map/ppermute | solution.py:498
  17.9 3.1 %collective-permute-start.1 = (f32[26,2,128]{2,1,0:T(2,128)S(1)}, f32[26,2,128]{2,1,0:T(2,128)S(1)}, u32[]{:S(2)}, u32[]{:S(2)}) collective-permute-start(f32[26,2,128]{2,1,0:T(2,128)S(1)} %pad_maximum_fusion.1), channel_id=1, source_target_pairs={{0,8},{8,16},{16,24},{24,32},{32,40},{40,48},{48,56},{56,64},{64,7... | collective-permute-start | bytes 79880 | tf_op jit(solution)/shard_map/ppermute | solution.py:499
  26.8 2.1 %copy-start = (f32[29,304,128]{2,1,0:T(8,128)}, f32[29,304,128]{2,1,0:T(8,128)S(1)}, u32[]{:S(2)}) copy-start(f32[29,304,128]{2,1,0:T(8,128)S(1)} %get-tuple-element.34.refs_20_) | copy-start | bytes 13541380
  55.0 6.4 %collective-permute-start.2 = (bf16[8,400,128]{2,1,0:T(8,128)(2,1)S(1)}, bf16[8,400,128]{2,1,0:T(8,128)(2,1)S(1)}, u32[]{:S(2)}, u32[]{:S(2)}) collective-permute-start(bf16[8,400,128]{2,1,0:T(8,128)(2,1)S(1)} %get-tuple-element.43), channel_id=1, source_target_pairs={{0,8},{8,0},{1,9},{9,1},{2,10},{10,2},{3,11},{11,3},{4,12},{12,4},... | collective-permute-start | bytes 2457608 | tf_op jit(solution)/shard_map/ppermute | solution.py:28
  57.4 13.9 %collective-permute-start.3 = (bf16[8,400,128]{2,1,0:T(8,128)(2,1)S(1)}, bf16[8,400,128]{2,1,0:T(8,128)(2,1)S(1)}, u32[]{:S(2)}, u32[]{:S(2)}) collective-permute-start(bf16[8,400,128]{2,1,0:T(8,128)(2,1)S(1)} %get-tuple-element.42), channel_id=1, source_target_pairs={{8,16},{16,8},{24,32},{32,24},{40,48},{48,40},{56,64},{64,56},{72,... | collective-permute-start | bytes 2457608 | tf_op jit(solution)/shard_map/ppermute | solution.py:538
  61.4 11.8 %copy-start.1 = (f32[29,304,128]{2,1,0:T(8,128)S(1)}, f32[29,304,128]{2,1,0:T(8,128)}, u32[]{:S(2)}) copy-start(f32[29,304,128]{2,1,0:T(8,128)} %copy-done) | copy-start | bytes 13541380
  101.5 64.3 %all-to-all-start.2 = ((s16[8,800,128]{2,1,0:T(8,128)(2,1)}), s16[8,800,128]{2,1,0:T(8,128)(2,1)S(1)}, u32[]{:S(2)}, u32[]{:S(2)}) async-start(s16[8,800,128]{2,1,0:T(8,128)(2,1)} %get-tuple-element.40), calls=%async_computation.2 | async-start | bytes 3276800 | tf_op jit(solution)/shard_map/all_to_all | solution.py:551
  105.1 17.4 %collective-permute-start.5 = (f32[40,128]{1,0:T(8,128)S(1)}, f32[40,128]{1,0:T(8,128)S(1)}, u32[]{:S(2)}, u32[]{:S(2)}) collective-permute-start(f32[40,128]{1,0:T(8,128)S(1)} %reduce_sum.9), channel_id=1, source_target_pairs={{0,128},{16,144},{32,160},{48,176},{64,192},{80,208},{96,224},{112... | collective-permute-start | bytes 61448 | tf_op jit(solution)/shard_map/ppermute | solution.py:28
  116.0 6.6 %collective-permute-start.6 = (f32[40,128]{1,0:T(8,128)S(1)}, f32[40,128]{1,0:T(8,128)S(1)}, u32[]{:S(2)}, u32[]{:S(2)}) collective-permute-start(f32[40,128]{1,0:T(8,128)S(1)} %reduce_sum.9), channel_id=1, source_target_pairs={{0,384},{16,400},{32,416},{48,432},{64,448},{80,464},{96,480},{112... | collective-permute-start | bytes 61448 | tf_op jit(solution)/shard_map/ppermute | solution.py:28
  119.7 6.3 %collective-permute-start.4 = (f32[40,128]{1,0:T(8,128)S(1)}, f32[40,128]{1,0:T(8,128)S(1)}, u32[]{:S(2)}, u32[]{:S(2)}) collective-permute-start(f32[40,128]{1,0:T(8,128)S(1)} %reduce_sum.9), channel_id=1, source_target_pairs={{0,256},{16,272},{32,288},{48,304},{64,320},{80,336},{96,352},{112... | collective-permute-start | bytes 61448 | tf_op jit(solution)/shard_map/ppermute | solution.py:28
  126.0 19.1 %collective-permute-start.12 = (f32[40,128]{1,0:T(8,128)S(1)}, f32[40,128]{1,0:T(8,128)S(1)}, u32[]{:S(2)}, u32[]{:S(2)}) collective-permute-start(f32[40,128]{1,0:T(8,128)S(1)} %add_add_fusion.1), channel_id=1, source_target_pairs={{0,96},{16,112},{32,64},{48,80},{64,32},{80,48},{96,0},{112,16},{1... | collective-permute-start | bytes 61448 | tf_op jit(solution)/shard_map/ppermute | solution.py:28
  129.3 18.9 %collective-permute-start.13 = (f32[40,128]{1,0:T(8,128)S(1)}, f32[40,128]{1,0:T(8,128)S(1)}, u32[]{:S(2)}, u32[]{:S(2)}) collective-permute-start(f32[40,128]{1,0:T(8,128)S(1)} %add_add_fusion.1), channel_id=1, source_target_pairs={{0,112},{16,96},{32,80},{48,64},{64,48},{80,32},{96,16},{112,0},{1... | collective-permute-start | bytes 61448 | tf_op jit(solution)/shard_map/ppermute | solution.py:28
  132.8 18.3 %collective-permute-start.10 = (f32[40,128]{1,0:T(8,128)S(1)}, f32[40,128]{1,0:T(8,128)S(1)}, u32[]{:S(2)}, u32[]{:S(2)}) collective-permute-start(f32[40,128]{1,0:T(8,128)S(1)} %add_add_fusion.1), channel_id=1, source_target_pairs={{0,64},{16,80},{32,96},{48,112},{64,0},{80,16},{96,32},{112,48},{1... | collective-permute-start | bytes 61448 | tf_op jit(solution)/shard_map/ppermute | solution.py:28
  137.0 14.1 %collective-permute-start.11 = (f32[40,128]{1,0:T(8,128)S(1)}, f32[40,128]{1,0:T(8,128)S(1)}, u32[]{:S(2)}, u32[]{:S(2)}) collective-permute-start(f32[40,128]{1,0:T(8,128)S(1)} %add_add_fusion.1), channel_id=1, source_target_pairs={{0,80},{16,64},{32,112},{48,96},{64,16},{80,0},{96,48},{112,32},{1... | collective-permute-start | bytes 61448 | tf_op jit(solution)/shard_map/ppermute | solution.py:28
  142.6 8.5 %collective-permute-start.8 = (f32[40,128]{1,0:T(8,128)S(1)}, f32[40,128]{1,0:T(8,128)S(1)}, u32[]{:S(2)}, u32[]{:S(2)}) collective-permute-start(f32[40,128]{1,0:T(8,128)S(1)} %add_add_fusion.1), channel_id=1, source_target_pairs={{0,32},{16,48},{32,0},{48,16},{64,96},{80,112},{96,64},{112,80},{1... | collective-permute-start | bytes 61448 | tf_op jit(solution)/shard_map/ppermute | solution.py:28
  145.1 6.3 %collective-permute-start.9 = (f32[40,128]{1,0:T(8,128)S(1)}, f32[40,128]{1,0:T(8,128)S(1)}, u32[]{:S(2)}, u32[]{:S(2)}) collective-permute-start(f32[40,128]{1,0:T(8,128)S(1)} %add_add_fusion.1), channel_id=1, source_target_pairs={{0,48},{16,32},{32,16},{48,0},{64,112},{80,96},{96,80},{112,64},{1... | collective-permute-start | bytes 61448 | tf_op jit(solution)/shard_map/ppermute | solution.py:28
  148.2 4.5 %collective-permute-start.7 = (f32[40,128]{1,0:T(8,128)S(1)}, f32[40,128]{1,0:T(8,128)S(1)}, u32[]{:S(2)}, u32[]{:S(2)}) collective-permute-start(f32[40,128]{1,0:T(8,128)S(1)} %add_add_fusion.1), channel_id=1, source_target_pairs={{0,16},{16,0},{32,48},{48,32},{64,80},{80,64},{96,112},{112,96},{1... | collective-permute-start | bytes 61448 | tf_op jit(solution)/shard_map/ppermute | solution.py:28
  152.8 6.1 %collective-permute-start.14 = (f32[40,128]{1,0:T(8,128)S(1)}, f32[40,128]{1,0:T(8,128)S(1)}, u32[]{:S(2)}, u32[]{:S(2)}) collective-permute-start(f32[40,128]{1,0:T(8,128)S(1)} %add_add_fusion.refs_0_), channel_id=1, source_target_pairs={{0,8},{8,0},{1,9},{9,1},{2,10},{10,2},{3,11},{11,3},{4,12},{12,4},... | collective-permute-start | bytes 61448 | tf_op jit(solution)/shard_map/ppermute | solution.py:28
